TPU v7x, 32 devices: a whole 2x2x4 slice. The times are simulated.
32 devices in a mesh: macro: 4 (over y, x), tile: 4 (over z), micro: 2 (over core).
Axes of the slice: x: 2, y: 2, z: 4, core: 2. Of those that a mesh axis runs over, the one named last changes fastest.
Arguments:
- velocity: float32 [3, 96, 32, 256], P(None, 'macro', 'tile', 'micro'), may hold values from -6 to 6
- viscosity: float32 [96, 32, 256], P('macro', 'tile', 'micro'), may hold values from 0.3 to 3
- flag_cell: int32 [1024], P(('macro', 'tile', 'micro')), may hold values from 1153 to 23422, as said below
- flag_owner: int32 [1024, 1], P(('macro', 'tile', 'micro')), may hold values from 0 to 7; in each aligned block of 32 rows (0 to 31, 32 to 63, ...) at most 8 rows name the same one
- conformations: float32 [3, 2048, 512], P(None, ('macro', 'tile', 'micro')), may hold values from -3.2 to 3.2
- increments: bfloat16 [16, 3, 2048, 512], P(None, None, ('macro', 'tile', 'micro')), may hold values from -4 to 4
Outputs:
- velocity_next: float32 [3, 96, 32, 256], P(None, 'macro', 'tile', 'micro')
- conformations_next: float32 [3, 2048, 512], P(None, ('macro', 'tile', 'micro'))
- flag_stress: float32 [6, 1024], P(None, ('macro', 'tile', 'micro'))
Inputs may be any that keep to these rules, and one draw needn't show every extreme that they name: `flag_cell`: on each device 32 distinct cells of its own block, none of them on a face of the block. `flag_owner`: among the 32 entries of one device at most 8 name the same owner, and some device has an owner named 8 times.
All inputs are finite; a program needn't handle non-finite values.
Results may differ from a plain program's by a relative error of at most 0.0003.
Values sent between devices are 32-bit elements; how exact they have to be, the bound alone decides.
No kernel may reach another device: no remote copies, remote signals or barrier semaphores. Data moves between devices by JAX's collectives and lax.ppermute only.
A program may use at most 64 MiB of HBM per device.

v0:
```python
import jax
import jax.numpy as jnp
from jax import lax
from jax.sharding import PartitionSpec as P

stress_pairs = ((0, 0), (1, 1), (2, 2), (0, 1), (0, 2), (1, 2))
macro_step = 0.1
micro_step = 0.01
noise_weight = 0.1
relax_rate = 0.5
fene_extent = 30.0
spring_floor = 0.1
polymer_weight = 0.25


def padded_2(block, sides, width):
    for axis, dim in sides:
        count = lax.axis_size(axis)
        forward = [(i, i + 1) for i in range(count - 1)]
        backward = [(target, source) for source, target in forward]
        low = lax.ppermute(
            lax.slice_in_dim(block, block.shape[dim] - width, None, axis=dim), axis, forward
        )
        high = lax.ppermute(lax.slice_in_dim(block, 0, width, axis=dim), axis, backward)
        block = jnp.concatenate([low, block, high], axis=dim)
    return block


def pair_index(left_axis, right_axis):
    return stress_pairs.index((min(left_axis, right_axis), max(left_axis, right_axis)))


def window(source, direction, offset):
    slicers = [slice(None)]
    for spatial in range(3):
        length = source.shape[spatial + 1] - 2
        if spatial == direction:
            slicers.append(slice(offset, offset + length))
        else:
            slicers.append(slice(1, 1 + length))
    return source[tuple(slicers)]


def stress_field(padded, viscous):
    slopes = [
        (window(padded, direction, 2) - window(padded, direction, 0)) * 0.5
        for direction in range(3)
    ]
    components = [
        viscous * (slopes[right_axis][left_axis] + slopes[left_axis][right_axis])
        for left_axis, right_axis in stress_pairs
    ]
    return jnp.stack(components, axis=0)


def divergence(padded_stress):
    result = []
    for left_axis in range(3):
        summed = None
        for right_axis in range(3):
            member = pair_index(left_axis, right_axis)
            column = padded_stress[member : member + 1]
            change = (window(column, right_axis, 2) - window(column, right_axis, 0))[0] * 0.5
            summed = change if summed is None else summed + change
        result.append(summed)
    return jnp.stack(result, axis=0)


def spring_of(current):
    return 1.0 / jnp.maximum(
        1.0
        - (current[0] * current[0] + current[1] * current[1] + current[2] * current[2])
        / fene_extent,
        spring_floor,
    )


def advance(conform, gradient_in, noise):
    rate_table = gradient_in[:, :, None]

    def substep(substep_index, current):
        spring = spring_of(current)
        updated = []
        for left_axis in range(3):
            drift_term = (
                rate_table[3 * left_axis] * current[0]
                + rate_table[3 * left_axis + 1] * current[1]
                + rate_table[3 * left_axis + 2] * current[2]
                - relax_rate * spring * current[left_axis]
            )
            updated.append(
                current[left_axis]
                + micro_step * drift_term
                + noise_weight * noise[substep_index, left_axis].astype(jnp.float32)
            )
        return jnp.stack(updated, axis=0)

    last_state = lax.fori_loop(0, noise.shape[0], substep, conform)
    spring = spring_of(last_state)
    stresses = []
    for left_axis, right_axis in stress_pairs:
        identity_part = 1.0 if left_axis == right_axis else 0.0
        stresses.append(
            polymer_weight
            * (
                jnp.mean(spring * last_state[left_axis] * last_state[right_axis], axis=-1)
                - identity_part
            )
        )
    return (last_state, jnp.stack(stresses, axis=0))


def add_polymer(velocity_next, polymer_rows, flag_cell, strides):
    flattened = velocity_next.reshape(3, -1)
    index_parts = []
    value_parts = [[], [], []]
    for right_axis, stride in enumerate(strides):
        index_parts.append(flag_cell - stride)
        index_parts.append(flag_cell + stride)
        for left_axis in range(3):
            contribution = macro_step * 0.5 * polymer_rows[pair_index(left_axis, right_axis)]
            value_parts[left_axis].append(contribution)
            value_parts[left_axis].append(-contribution)
    targets = jnp.concatenate(index_parts, axis=0)
    updates = jnp.stack([jnp.concatenate(parts, axis=0) for parts in value_parts], axis=0)
    flattened = flattened.at[:, targets].add(updates)
    return flattened.reshape(velocity_next.shape)


def shards(velocity, viscosity, flag_cell, flag_owner, conformations, increments):
    macro_count = lax.axis_size("macro")
    micro_count = lax.axis_size("micro")
    owner_count = macro_count * micro_count
    slot_count = conformations.shape[1]
    capacity = slot_count // owner_count
    size_x, size_y, size_z = viscosity.shape
    strides = (size_y * size_z, size_z, 1)
    flat_velocity = velocity.reshape(3, size_x * size_y * size_z)
    slopes = []
    for stride in strides:
        upper_side = jnp.take(flat_velocity, flag_cell + stride, axis=1)
        lower_side = jnp.take(flat_velocity, flag_cell - stride, axis=1)
        slopes.append((upper_side - lower_side) * 0.5)
    gradient_rows = jnp.stack(slopes, axis=1).reshape(9, flag_cell.shape[0])
    viscous_flag = jnp.take(viscosity.reshape(-1), flag_cell)
    viscous_rows = jnp.stack(
        [
            viscous_flag
            * (
                gradient_rows[3 * left_axis + right_axis]
                + gradient_rows[3 * right_axis + left_axis]
            )
            for left_axis, right_axis in stress_pairs
        ],
        axis=0,
    )
    owner_index = flag_owner[:, 0]
    onehot = (owner_index[:, None] == jnp.arange(owner_count, dtype=jnp.int32)[None, :]).astype(
        jnp.int32
    )
    slot_rank = jnp.sum((jnp.cumsum(onehot, axis=0) - onehot) * onehot, axis=1)
    position = owner_index * capacity + slot_rank
    placing = (position[:, None] == jnp.arange(slot_count, dtype=jnp.int32)[None, :]).astype(
        jnp.float32
    )
    outgoing = jnp.dot(gradient_rows, placing, precision=lax.Precision.HIGHEST)
    gradient_in = lax.all_to_all(
        outgoing, ("macro", "micro"), split_axis=1, concat_axis=1, tiled=True
    )
    last_state, polymer = advance(conformations, gradient_in, increments)
    returned_rows = lax.all_to_all(
        polymer, ("macro", "micro"), split_axis=1, concat_axis=1, tiled=True
    )
    polymer_rows = jnp.dot(returned_rows, placing.T, precision=lax.Precision.HIGHEST)
    flag_stress = viscous_rows + polymer_rows
    padded = padded_2(velocity, (("macro", 1), ("tile", 2), ("micro", 3)), 1)
    stress_all = stress_field(padded, viscosity)
    stress_pad = padded_2(stress_all, (("macro", 1), ("tile", 2), ("micro", 3)), 1)
    velocity_next = velocity + macro_step * divergence(stress_pad)
    velocity_next = add_polymer(velocity_next, polymer_rows, flag_cell, strides)
    return (velocity_next, last_state, flag_stress)


def solution(mesh):
    in_specs = (
        P(None, "macro", "tile", "micro"),
        P("macro", "tile", "micro"),
        P(("macro", "tile", "micro")),
        P(("macro", "tile", "micro"), None),
        P(None, ("macro", "tile", "micro"), None),
        P(None, None, ("macro", "tile", "micro"), None),
    )
    out_specs = (
        P(None, "macro", "tile", "micro"),
        P(None, ("macro", "tile", "micro"), None),
        P(None, ("macro", "tile", "micro")),
    )
    return jax.shard_map(shards, mesh=mesh, in_specs=in_specs, out_specs=out_specs, check_vma=False)
```

profile of v0, /device:TPU:0, one launch (start us, length us, event | category | flops | bytes accessed | tf_op | source)
XLA Modules:
  0.0 211.8 jit_solution(5536115119198874540)
XLA Ops:
  1.4 4.8 %collective-permute-start.1 = (f32[3,1,8,128]{3,2,1,0:T(8,128)S(1)}, f32[3,1,8,128]{3,2,1,0:T(8,128)S(1)}, u32[]{:S(2)}, u32[]{:S(2)}) collective-permute-start(f32[3,1,8,128]{3,2,1,0:T(8,128)S(1)} %get-tuple-element.201), channel_id=1, source_target_pairs={{0,8},{8,16},{16,24},{1,9},{9,17},{17,25},{2,10},{10,18},{18,26},{... | collective-permute-start | bytes 36872 | tf_op jit(solution)/shard_map/ppermute | solution.py:21
  7.6 7.6 %copy.198 = f32[3,24,8,128]{0,3,2,1:T(8,128)} copy(f32[3,24,8,128]{3,2,1,0:T(8,128)} %param.10) | data formatting | bytes 589824 | tf_op args[0]
  15.5 5.1 %gather_fusion.6 = f32[32,3]{1,0:T(8,128)S(1)} fusion(f32[3,24576]{0,1:T(8,128)} %bitcast.223, s32[1024]{0:T(1024)S(1)} %get-tuple-element.239), kind=kCustom, calls=%fused_computation.5.clone | custom fusion | bytes 896 | tf_op jit(solution)/shard_map/jit(_take)/gather | solution.py:142
  20.8 5.2 %gather_fusion.5 = f32[32,3]{1,0:T(8,128)S(1)} fusion(f32[3,24576]{0,1:T(8,128)} %bitcast.224, s32[1024]{0:T(1024)S(1)} %get-tuple-element.240), kind=kCustom, calls=%fused_computation.4.clone | custom fusion | bytes 896 | tf_op jit(solution)/shard_map/jit(_take)/gather | solution.py:141
  26.0 5.2 %gather_fusion.4 = f32[32,3]{1,0:T(8,128)S(1)} fusion(f32[3,24576]{0,1:T(8,128)} %bitcast.225, s32[1024]{0:T(1024)S(1)} %get-tuple-element.241), kind=kCustom, calls=%fused_computation.3.clone | custom fusion | bytes 896 | tf_op jit(solution)/shard_map/jit(_take)/gather | solution.py:142
  31.2 5.2 %gather_fusion.3 = f32[32,3]{1,0:T(8,128)S(1)} fusion(f32[3,24576]{0,1:T(8,128)} %bitcast.226, s32[1024]{0:T(1024)S(1)} %get-tuple-element.242), kind=kCustom, calls=%fused_computation.2.clone | custom fusion | bytes 896 | tf_op jit(solution)/shard_map/jit(_take)/gather | solution.py:141
  36.5 5.2 %gather_fusion.2 = f32[32,3]{1,0:T(8,128)S(1)} fusion(f32[3,24576]{0,1:T(8,128)} %bitcast.227, s32[1024]{0:T(1024)S(1)} %get-tuple-element.243), kind=kCustom, calls=%fused_computation.1.clone | custom fusion | bytes 896 | tf_op jit(solution)/shard_map/jit(_take)/gather | solution.py:142
  41.6 5.1 %gather_fusion.1 = f32[32,3]{1,0:T(8,128)S(1)} fusion(f32[3,24576]{0,1:T(8,128)} %bitcast.228, s32[1024]{0:T(1024)S(1)} %get-tuple-element.244), kind=kCustom, calls=%fused_computation.clone | custom fusion | bytes 896 | tf_op jit(solution)/shard_map/jit(_take)/gather | solution.py:141
  47.8 4.9 %all-to-all-start = ((f32[9,8,8]{0,2,1:T(8,128)}), f32[9,8,8]{0,2,1:T(8,128)S(1)}, u32[]{:S(2)}, u32[]{:S(2)}) async-start(f32[9,8,8]{0,2,1:T(8,128)} %fusion.46), calls=%async_computation | async-start | bytes 65536 | tf_op jit(solution)/shard_map/all_to_all | solution.py:167
  53.6 4.0 %all-to-all-done = f32[9,8,8]{0,2,1:T(8,128)S(1)} async-done(((f32[9,8,8]{0,2,1:T(8,128)}), f32[9,8,8]{0,2,1:T(8,128)S(1)}, u32[]{:S(2)}, u32[]{:S(2)}) %all-to-all-start) | async-done | bytes 2336 | tf_op jit(solution)/shard_map/all_to_all | solution.py:167
  57.6 33.2 %while.13 = (s32[]{:T(128)}, f32[3,64,512]{2,1,0:T(8,128)S(1)}, f32[9,64,1]{1,2,0:T(1,128)S(1)}, bf16[16,3,64,512]{3,2,1,0:T(8,128)(2,1)}, s32[]{:T(128)}) while((s32[]{:T(128)}, f32[3,64,512]{2,1,0:T(8,128)S(1)}, f32[9,64,1]{1,2,0:T(1,128)S(1)}, bf16[16,3,64,512]{3,2,1,0:T(8,128)(2,1)}, s32[]{:T(128)}) %tuple.129), condition=%wide.region_3.5_spmd, body=%wide.region_2.4_spmd.sunk | while | flops 2031618 | bytes 2169677 | solution.py:98
  92.4 3.3 %all-to-all-start.1 = ((f32[6,8,8]{2,0,1:T(8,128)}), f32[6,8,8]{2,0,1:T(8,128)S(1)}, u32[]{:S(2)}, u32[]{:S(2)}) async-start(f32[6,8,8]{2,0,1:T(8,128)} %copy.207), calls=%async_computation.1 | async-start | bytes 65536 | tf_op jit(solution)/shard_map/all_to_all | solution.py:171
  97.3 3.2 %all-to-all-done.1 = f32[6,8,8]{2,0,1:T(8,128)S(1)} async-done(((f32[6,8,8]{2,0,1:T(8,128)}), f32[6,8,8]{2,0,1:T(8,128)S(1)}, u32[]{:S(2)}, u32[]{:S(2)}) %all-to-all-start.1) | async-done | bytes 1568 | tf_op jit(solution)/shard_map/all_to_all | solution.py:171
  104.6 5.2 %collective-permute-start.3 = (f32[3,26,1,128]{1,3,2,0:T(8,128)}, f32[3,26,1,128]{1,3,2,0:T(8,128)}, u32[]{:S(2)}, u32[]{:S(2)}) collective-permute-start(f32[3,26,1,128]{1,3,2,0:T(8,128)} %get-tuple-element.187), channel_id=1, source_target_pairs={{0,2},{2,4},{4,6},{1,3},{3,5},{5,7},{8,10},{10,12},{12,14},{9,11},... | collective-permute-start | bytes 119816 | tf_op jit(solution)/shard_map/ppermute | solution.py:21
  115.9 3.0 %collective-permute-start.5 = (f32[3,26,10,1]{1,3,2,0:T(1,128)S(1)}, f32[3,26,10,1]{1,3,2,0:T(1,128)S(1)}, u32[]{:S(2)}, u32[]{:S(2)}) collective-permute-start(f32[3,26,10,1]{1,3,2,0:T(1,128)S(1)} %get-tuple-element.185), channel_id=1, source_target_pairs={{0,1},{2,3},{4,5},{6,7},{8,9},{10,11},{12,13},{14,15},{16,17},{18,... | collective-permute-start | bytes 9368 | tf_op jit(solution)/shard_map/ppermute | solution.py:21
  119.8 2.8 %fusion.1 = (f32[3,24,8,128]{1,3,2,0:T(8,128)S(1)}, f32[3,24,8,128]{1,3,2,0:T(8,128)S(1)}) fusion(f32[3,26,10,1]{1,3,2,0:T(1,128)S(1)} %collective-permute-done.5, f32[3,26,1,128]{1,3,2,0:T(8,128)} %collective-permute-done.2, f32[3,26,8,128]{1,3,2,0:T(8,128)S(1)} %copy.168, f32[3,26,1,128]{1,3,2,0:T(8,128)} %collective-permute-done.3, ...), kind=kLoop, calls=%fused_computation.24 | loop fusion | flops 884736 | bytes 995424 | tf_op jit(solution)/shard_map/mul | solution.py:46
  129.5 3.0 %collective-permute-done.6 = f32[6,1,8,128]{3,2,1,0:T(8,128)S(1)} collective-permute-done((f32[6,1,8,128]{3,2,1,0:T(8,128)S(1)}, f32[6,1,8,128]{3,2,1,0:T(8,128)S(1)}, u32[]{:S(2)}, u32[]{:S(2)}) %collective-permute-start.6) | collective-permute-done | bytes 24608 | tf_op jit(solution)/shard_map/ppermute | solution.py:24
  136.9 4.1 %collective-permute-start.9 = (f32[6,26,1,128]{1,3,2,0:T(8,128)}, f32[6,26,1,128]{1,3,2,0:T(8,128)S(1)}, u32[]{:S(2)}, u32[]{:S(2)}) collective-permute-start(f32[6,26,1,128]{1,3,2,0:T(8,128)} %get-tuple-element.174), channel_id=1, source_target_pairs={{0,2},{2,4},{4,6},{1,3},{3,5},{5,7},{8,10},{10,12},{12,14},{9,11},... | collective-permute-start | bytes 239624 | tf_op jit(solution)/shard_map/ppermute | solution.py:21
  143.1 5.6 %collective-permute-done.9 = f32[6,26,1,128]{1,3,2,0:T(8,128)S(1)} collective-permute-done((f32[6,26,1,128]{1,3,2,0:T(8,128)}, f32[6,26,1,128]{1,3,2,0:T(8,128)S(1)}, u32[]{:S(2)}, u32[]{:S(2)}) %collective-permute-start.9) | collective-permute-done | bytes 79904 | tf_op jit(solution)/shard_map/ppermute | solution.py:21
  148.7 4.1 %collective-permute-done.8 = f32[6,26,1,128]{1,3,2,0:T(8,128)} collective-permute-done((f32[6,26,1,128]{1,3,2,0:T(8,128)}, f32[6,26,1,128]{1,3,2,0:T(8,128)}, u32[]{:S(2)}, u32[]{:S(2)}) %collective-permute-start.8) | collective-permute-done | bytes 79904 | tf_op jit(solution)/shard_map/ppermute | solution.py:24
  155.6 4.2 %collective-permute-start.11 = (f32[6,26,10,1]{1,3,2,0:T(1,128)}, f32[6,26,10,1]{1,3,2,0:T(1,128)}, u32[]{:S(2)}, u32[]{:S(2)}) collective-permute-start(f32[6,26,10,1]{1,3,2,0:T(1,128)} %get-tuple-element.173), channel_id=1, source_target_pairs={{0,1},{2,3},{4,5},{6,7},{8,9},{10,11},{12,13},{14,15},{16,17},{18,... | collective-permute-start | bytes 18728 | tf_op jit(solution)/shard_map/ppermute | solution.py:21
  186.1 6.8 %copy.197 = f32[3,24,8,128]{0,3,2,1:T(8,128)} copy(f32[3,24,8,128]{3,2,1,0:T(8,128)S(1)} %fusion.33) | data formatting | bytes 589824 | tf_op jit(solution)/shard_map/add | solution.py:179
  192.8 10.9 %scatter_fusion = f32[3,24576]{0,1:T(8,128)} fusion(f32[3,24576]{0,1:T(8,128)} %bitcast.221, s32[192]{0:T(256)S(1)} %bitcast.231, f32[192,3]{1,0:T(8,128)} %copy.209), kind=kCustom, calls=%fused_computation.7 | custom fusion | flops 576 | bytes 7680 | tf_op jit(solution)/shard_map/scatter-add | solution.py:126
  203.7 8.1 %copy.210 = f32[3,24,8,128]{3,2,1,0:T(8,128)} copy(f32[3,24,8,128]{0,3,2,1:T(8,128)} %bitcast.222) | data formatting | bytes 589824
  (224 shorter events, 93.3 us)
Async XLA Ops:
  1.4 100.6 %collective-permute-start.1 = (f32[3,1,8,128]{3,2,1,0:T(8,128)S(1)}, f32[3,1,8,128]{3,2,1,0:T(8,128)S(1)}, u32[]{:S(2)}, u32[]{:S(2)}) collective-permute-start(f32[3,1,8,128]{3,2,1,0:T(8,128)S(1)} %get-tuple-element.201), channel_id=1, source_target_pairs={{0,8},{8,16},{16,24},{1,9},{9,17},{17,25},{2,10},{10,18},{18,26},{... | collective-permute-start | bytes 36872 | tf_op jit(solution)/shard_map/ppermute | solution.py:21
  6.2 95.8 %collective-permute-start = (f32[3,1,8,128]{3,2,1,0:T(8,128)S(1)}, f32[3,1,8,128]{3,2,1,0:T(8,128)S(1)}, u32[]{:S(2)}, u32[]{:S(2)}) collective-permute-start(f32[3,1,8,128]{3,2,1,0:T(8,128)S(1)} %get-tuple-element.202), channel_id=1, source_target_pairs={{8,0},{16,8},{24,16},{9,1},{17,9},{25,17},{10,2},{18,10},{26,18},{... | collective-permute-start | bytes 36872 | tf_op jit(solution)/shard_map/ppermute | solution.py:24
  7.5 7.7 %copy-start.12 = (s32[32]{0:T(128)S(1)}, s32[32]{0:T(128)}, u32[]{:S(2)}) copy-start(s32[32]{0:T(128)} %param.12) | copy-start | bytes 388
  7.5 7.7 %copy-start.16 = (s32[32,1]{0,1:T(1,128)S(1)}, s32[32,1]{0,1:T(1,128)}, u32[]{:S(2)}) copy-start(s32[32,1]{0,1:T(1,128)} %param.13) | copy-start | bytes 388
  7.5 45.2 %copy-start.4 = (f32[24,8,128]{2,1,0:T(8,128)S(1)}, f32[24,8,128]{2,1,0:T(8,128)}, u32[]{:S(2)}) copy-start(f32[24,8,128]{2,1,0:T(8,128)} %param.11) | copy-start | bytes 294916
  7.5 50.1 %copy-start.1 = (f32[3,64,512]{2,1,0:T(8,128)S(1)}, f32[3,64,512]{2,1,0:T(8,128)}, u32[]{:S(2)}) copy-start(f32[3,64,512]{2,1,0:T(8,128)} %param.14) | copy-start | bytes 1179652
  47.8 9.7 %all-to-all-start = ((f32[9,8,8]{0,2,1:T(8,128)}), f32[9,8,8]{0,2,1:T(8,128)S(1)}, u32[]{:S(2)}, u32[]{:S(2)}) async-start(f32[9,8,8]{0,2,1:T(8,128)} %fusion.46), calls=%async_computation | async-start | bytes 65536 | tf_op jit(solution)/shard_map/all_to_all | solution.py:167
  90.9 11.7 %copy-start = (f32[3,64,512]{2,1,0:T(8,128)}, f32[3,64,512]{2,1,0:T(8,128)S(1)}, u32[]{:S(2)}) copy-start(f32[3,64,512]{2,1,0:T(8,128)S(1)} %get-tuple-element.131) | copy-start | bytes 1179652
  90.9 11.1 %copy-start.3 = (f32[3,24,8,128]{3,2,1,0:T(8,128)S(1)}, f32[3,24,8,128]{3,2,1,0:T(8,128)}, u32[]{:S(2)}) copy-start(f32[3,24,8,128]{3,2,1,0:T(8,128)} %param.10) | copy-start | bytes 884740
  92.4 8.1 %all-to-all-start.1 = ((f32[6,8,8]{2,0,1:T(8,128)}), f32[6,8,8]{2,0,1:T(8,128)S(1)}, u32[]{:S(2)}, u32[]{:S(2)}) async-start(f32[6,8,8]{2,0,1:T(8,128)} %copy.207), calls=%async_computation.1 | async-start | bytes 65536 | tf_op jit(solution)/shard_map/all_to_all | solution.py:171
  103.3 10.4 %collective-permute-start.2 = (f32[3,26,1,128]{1,3,2,0:T(8,128)}, f32[3,26,1,128]{1,3,2,0:T(8,128)}, u32[]{:S(2)}, u32[]{:S(2)}) collective-permute-start(f32[3,26,1,128]{1,3,2,0:T(8,128)} %get-tuple-element.186), channel_id=1, source_target_pairs={{2,0},{4,2},{6,4},{3,1},{5,3},{7,5},{10,8},{12,10},{14,12},{11,9},... | collective-permute-start | bytes 119816 | tf_op jit(solution)/shard_map/ppermute | solution.py:24
  104.6 9.1 %collective-permute-start.3 = (f32[3,26,1,128]{1,3,2,0:T(8,128)}, f32[3,26,1,128]{1,3,2,0:T(8,128)}, u32[]{:S(2)}, u32[]{:S(2)}) collective-permute-start(f32[3,26,1,128]{1,3,2,0:T(8,128)} %get-tuple-element.187), channel_id=1, source_target_pairs={{0,2},{2,4},{4,6},{1,3},{3,5},{5,7},{8,10},{10,12},{12,14},{9,11},... | collective-permute-start | bytes 119816 | tf_op jit(solution)/shard_map/ppermute | solution.py:21
  114.6 4.6 %collective-permute-start.4 = (f32[3,26,10,1]{1,3,2,0:T(1,128)S(1)}, f32[3,26,10,1]{1,3,2,0:T(1,128)S(1)}, u32[]{:S(2)}, u32[]{:S(2)}) collective-permute-start(f32[3,26,10,1]{1,3,2,0:T(1,128)S(1)} %get-tuple-element.184), channel_id=1, source_target_pairs={{1,0},{3,2},{5,4},{7,6},{9,8},{11,10},{13,12},{15,14},{17,16},{19,... | collective-permute-start | bytes 9368 | tf_op jit(solution)/shard_map/ppermute | solution.py:24
  115.9 3.9 %collective-permute-start.5 = (f32[3,26,10,1]{1,3,2,0:T(1,128)S(1)}, f32[3,26,10,1]{1,3,2,0:T(1,128)S(1)}, u32[]{:S(2)}, u32[]{:S(2)}) collective-permute-start(f32[3,26,10,1]{1,3,2,0:T(1,128)S(1)} %get-tuple-element.185), channel_id=1, source_target_pairs={{0,1},{2,3},{4,5},{6,7},{8,9},{10,11},{12,13},{14,15},{16,17},{18,... | collective-permute-start | bytes 9368 | tf_op jit(solution)/shard_map/ppermute | solution.py:21
  124.3 8.2 %copy-start.5 = (f32[6,24,8,128]{3,2,1,0:T(8,128)}, f32[6,24,8,128]{3,2,1,0:T(8,128)S(1)}, u32[]{:S(2)}) copy-start(f32[6,24,8,128]{3,2,1,0:T(8,128)S(1)} %constant_dynamic-update-slice_fusion) | copy-start | bytes 1769476
  124.3 5.2 %collective-permute-start.7 = (f32[6,1,8,128]{3,2,1,0:T(8,128)S(1)}, f32[6,1,8,128]{3,2,1,0:T(8,128)S(1)}, u32[]{:S(2)}, u32[]{:S(2)}) collective-permute-start(f32[6,1,8,128]{3,2,1,0:T(8,128)S(1)} %get-tuple-element.197), channel_id=1, source_target_pairs={{0,8},{8,16},{16,24},{1,9},{9,17},{17,25},{2,10},{10,18},{18,26},{... | collective-permute-start | bytes 73736 | tf_op jit(solution)/shard_map/ppermute | solution.py:21
  126.8 5.7 %collective-permute-start.6 = (f32[6,1,8,128]{3,2,1,0:T(8,128)S(1)}, f32[6,1,8,128]{3,2,1,0:T(8,128)S(1)}, u32[]{:S(2)}, u32[]{:S(2)}) collective-permute-start(f32[6,1,8,128]{3,2,1,0:T(8,128)S(1)} %get-tuple-element.198), channel_id=1, source_target_pairs={{8,0},{16,8},{24,16},{9,1},{17,9},{25,17},{10,2},{18,10},{26,18},{... | collective-permute-start | bytes 73736 | tf_op jit(solution)/shard_map/ppermute | solution.py:24
  136.9 11.8 %collective-permute-start.9 = (f32[6,26,1,128]{1,3,2,0:T(8,128)}, f32[6,26,1,128]{1,3,2,0:T(8,128)S(1)}, u32[]{:S(2)}, u32[]{:S(2)}) collective-permute-start(f32[6,26,1,128]{1,3,2,0:T(8,128)} %get-tuple-element.174), channel_id=1, source_target_pairs={{0,2},{2,4},{4,6},{1,3},{3,5},{5,7},{8,10},{10,12},{12,14},{9,11},... | collective-permute-start | bytes 239624 | tf_op jit(solution)/shard_map/ppermute | solution.py:21
  141.0 11.9 %collective-permute-start.8 = (f32[6,26,1,128]{1,3,2,0:T(8,128)}, f32[6,26,1,128]{1,3,2,0:T(8,128)}, u32[]{:S(2)}, u32[]{:S(2)}) collective-permute-start(f32[6,26,1,128]{1,3,2,0:T(8,128)} %get-tuple-element.175), channel_id=1, source_target_pairs={{2,0},{4,2},{6,4},{3,1},{5,3},{7,5},{10,8},{12,10},{14,12},{11,9},... | collective-permute-start | bytes 239624 | tf_op jit(solution)/shard_map/ppermute | solution.py:24
  143.1 16.7 %copy-start.6 = (f32[6,24,8,128]{3,2,1,0:T(8,128)S(1)}, f32[6,24,8,128]{3,2,1,0:T(8,128)}, u32[]{:S(2)}) copy-start(f32[6,24,8,128]{3,2,1,0:T(8,128)} %copy-done.5) | copy-start | bytes 1769476
  143.1 16.7 %copy-start.9 = (f32[6,1,8,128]{3,2,1,0:T(8,128)S(1)}, f32[6,1,8,128]{3,2,1,0:T(8,128)}, u32[]{:S(2)}) copy-start(f32[6,1,8,128]{3,2,1,0:T(8,128)} %copy-done.8) | copy-start | bytes 73732
  143.1 16.7 %copy-start.11 = (f32[6,1,8,128]{3,2,1,0:T(8,128)S(1)}, f32[6,1,8,128]{3,2,1,0:T(8,128)}, u32[]{:S(2)}) copy-start(f32[6,1,8,128]{3,2,1,0:T(8,128)} %copy-done.10) | copy-start | bytes 73732
  154.3 17.7 %collective-permute-start.10 = (f32[6,26,10,1]{1,3,2,0:T(1,128)}, f32[6,26,10,1]{1,3,2,0:T(1,128)}, u32[]{:S(2)}, u32[]{:S(2)}) collective-permute-start(f32[6,26,10,1]{1,3,2,0:T(1,128)} %get-tuple-element.172), channel_id=1, source_target_pairs={{1,0},{3,2},{5,4},{7,6},{9,8},{11,10},{13,12},{15,14},{17,16},{19,... | collective-permute-start | bytes 18728 | tf_op jit(solution)/shard_map/ppermute | solution.py:24
  155.6 16.4 %collective-permute-start.11 = (f32[6,26,10,1]{1,3,2,0:T(1,128)}, f32[6,26,10,1]{1,3,2,0:T(1,128)}, u32[]{:S(2)}, u32[]{:S(2)}) collective-permute-start(f32[6,26,10,1]{1,3,2,0:T(1,128)} %get-tuple-element.173), channel_id=1, source_target_pairs={{0,1},{2,3},{4,5},{6,7},{8,9},{10,11},{12,13},{14,15},{16,17},{18,... | collective-permute-start | bytes 18728 | tf_op jit(solution)/shard_map/ppermute | solution.py:21
  (10 other events, 47.1 us)
where the time goes:
time: 215 us; the launch traced here: 212 us
  local copies, waits for them, and re-layouts  85.4 us (40%)
  other arithmetic  62.6 us (29%)
  starting transfers between devices  39.8 us (19%)
  waiting for transfers between devices  20.4 us (9%)
    add x32, other arithmetic, substep(): current[left_axis] + micro_step * drift_term  32 us
    unnamed x61, local copies, waits for them, and re-layouts  32 us
    ppermute x6, starting transfers between devices, padded_2(): lax.ppermute(lax.slice_in_dim(block, block.shape[dim] - width, None, axis...  23.9 us
    gather x6, local copies, waits for them, and re-layouts, shards(): upper_side = jnp.take(flat_velocity, flag_cell + stride, axis=1)  15.7 us
    gather x6, local copies, waits for them, and re-layouts, shards(): lower_side = jnp.take(flat_velocity, flag_cell - stride, axis=1)  15.7 us
    scatter-add x1, other arithmetic, add_polymer(): flattened = flattened.at[:, targets].add(updates)  10.9 us
    add x3, other arithmetic, divergence(): summed = change if summed is None else summed + change  8.02 us
    ppermute x6, starting transfers between devices, padded_2(): lax.ppermute(lax.slice_in_dim(block, 0, width, axis=dim), axis, backward)  7.73 us
  transfers between devices with their start and end apart: 14, of which 6 were waited for; matrix products, arithmetic and copies ran while one was open for 46% of the time, Pallas kernels for 0%

commit v1 on v0

v1 whole, which is shorter than its diff:
```python
import functools

import jax
import jax.numpy as jnp
from jax import lax
from jax.experimental import pallas as pl
from jax.experimental.pallas import tpu as pltpu
from jax.sharding import PartitionSpec as P

stress_pairs = ((0, 0), (1, 1), (2, 2), (0, 1), (0, 2), (1, 2))
macro_step = 0.1
micro_step = 0.01
noise_weight = 0.1
relax_rate = 0.5
fene_extent = 30.0
spring_floor = 0.1
polymer_weight = 0.25

SMEM = pl.BlockSpec(memory_space=pltpu.SMEM)
VMEM = pl.BlockSpec(memory_space=pltpu.VMEM)


def pair_index(left_axis, right_axis):
    return stress_pairs.index((min(left_axis, right_axis), max(left_axis, right_axis)))


def lanes_of(shape):
    return lax.broadcasted_iota(jnp.int32, shape, len(shape) - 1)


def gather_kernel(
    capacity, size_y, size_z, cell_ref, owner_ref, velocity_ref, viscosity_ref,
    slots_ref, position_ref, viscous_ref, masked, gradients, count,
):
    flags = cell_ref.shape[0]
    for owner in range(count.shape[0]):
        count[owner] = 0
    lane = lanes_of((1, size_z))
    for j in range(flags):
        cell = cell_ref[j]
        row = lax.div(cell, size_z)
        z = cell - row * size_z
        here = (lane == z).astype(jnp.float32)
        along_z = (lane == z + 1).astype(jnp.float32) - (lane == z - 1).astype(jnp.float32)
        for a in range(3):
            along_x = velocity_ref[a, pl.ds(row + size_y, 1), :] - velocity_ref[a, pl.ds(row - size_y, 1), :]
            along_y = velocity_ref[a, pl.ds(row + 1, 1), :] - velocity_ref[a, pl.ds(row - 1, 1), :]
            masked[3 * a, j : j + 1, :] = along_x * here
            masked[3 * a + 1, j : j + 1, :] = along_y * here
            masked[3 * a + 2, j : j + 1, :] = velocity_ref[a, pl.ds(row, 1), :] * along_z
        masked[9, j : j + 1, :] = viscosity_ref[pl.ds(row, 1), :] * here
        owner = owner_ref[j]
        rank = count[owner]
        count[owner] = rank + 1
        position_ref[j] = owner * capacity + rank
    columns = [0.5 * jnp.sum(masked[c], axis=1, keepdims=True) for c in range(9)]
    viscous = jnp.sum(masked[9], axis=1, keepdims=True)
    wide = lanes_of((flags, 128))
    packed = jnp.zeros((flags, 128), jnp.float32)
    for c in range(9):
        packed = jnp.where(wide == c, columns[c], packed)
    gradients[...] = packed
    stress = jnp.zeros((flags, 128), jnp.float32)
    for k, (a, b) in enumerate(stress_pairs):
        stress = jnp.where(wide == k, viscous * (columns[3 * a + b] + columns[3 * b + a]), stress)
    viscous_ref[...] = stress
    slots_ref[...] = jnp.zeros_like(slots_ref)
    for j in range(flags):
        slots_ref[pl.ds(position_ref[j], 1), :] = gradients[j : j + 1, :]


def gather_rows(flag_cell, owner, velocity, viscosity, slot_count, owner_count):
    size_x, size_y, size_z = viscosity.shape
    flags = flag_cell.shape[0]
    return pl.pallas_call(
        functools.partial(gather_kernel, slot_count // owner_count, size_y, size_z),
        out_shape=(
            jax.ShapeDtypeStruct((slot_count, 128), jnp.float32),
            jax.ShapeDtypeStruct((flags,), jnp.int32),
            jax.ShapeDtypeStruct((flags, 128), jnp.float32),
        ),
        in_specs=[SMEM, SMEM, VMEM, VMEM],
        out_specs=(VMEM, SMEM, VMEM),
        scratch_shapes=[
            pltpu.VMEM((10, flags, size_z), jnp.float32),
            pltpu.VMEM((flags, 128), jnp.float32),
            pltpu.SMEM((owner_count,), jnp.int32),
        ],
        cost_estimate=pl.CostEstimate(flops=400000, bytes_accessed=3000000, transcendentals=0),
        name="gather_rows",
    )(
        flag_cell,
        owner,
        velocity.reshape(3, size_x * size_y, size_z),
        viscosity.reshape(size_x * size_y, size_z),
    )


def roll_lanes(value, amount):
    return pltpu.roll(value, amount % value.shape[-1], value.ndim - 1)


def packed_lanes(values, layers, core):
    size = values[0].shape[-1]
    lane = lanes_of(values[0].shape)
    total = jnp.zeros_like(values[0])
    for i, (value, layer) in enumerate(zip(values, layers)):
        if core == 0:
            total = jnp.where(lane == 8 * i, roll_lanes(value, 1 + layer + 8 * i), total)
        else:
            total = jnp.where(lane == size - 1 - 8 * i, roll_lanes(value, -1 - layer - 8 * i), total)
    return total


def unpacked_lanes(packed, item, core):
    if item == 0:
        return packed
    return roll_lanes(packed, -8 * item if core == 0 else 8 * item)


def pack_kernel(
    size_x, size_y, size_z, place_ref, velocity_ref, viscosity_ref, face_y_ref, face_x_ref, face_z_ref, edge_ref
):
    def row_of(ref, a, y):
        if a is None:
            return ref[pl.ds(y, size_x, stride=size_y), :]
        return ref[a, pl.ds(y, size_x, stride=size_y), :]

    def plane_of(x):
        return pl.ds(x * size_y, size_y)

    near = []
    for side in range(2):
        ys = (0, 1) if side == 0 else (size_y - 1, size_y - 2)
        xs = (0, 1) if side == 0 else (size_x - 1, size_x - 2)
        for layer in range(2):
            for a in range(3):
                rows = row_of(velocity_ref, a, ys[layer])
                face_y_ref[7 * side + 3 * layer + a] = rows
                if layer == 0 and a > 0:
                    near.append(rows)
                face_x_ref[7 * side + 3 * layer + a] = velocity_ref[a, plane_of(xs[layer]), :]
        face_y_ref[7 * side + 6] = row_of(viscosity_ref, None, ys[0])
        face_x_ref[7 * side + 6] = viscosity_ref[plane_of(xs[0]), :]
        for other in range(2):
            y = 0 if other == 0 else size_y - 1
            for a in range(2):
                number = 4 * side + 2 * other + a
                edge_ref[number : number + 1, :] = velocity_ref[a, pl.ds(xs[0] * size_y + y, 1), :]
    core = place_ref[2]
    for option in range(2):

        @pl.when(core == option)
        def _(option=option):
            whole = [velocity_ref[a] for a in range(3)]
            face_z_ref[...] = packed_lanes(
                whole + [viscosity_ref[...]] + whole, (0, 0, 0, 0, 1, 1, 1), option
            )
            edge_ref[8:, :] = packed_lanes(near, (0, 0, 0, 0), option)


def pack_faces(place, velocity, viscosity):
    size_x, size_y, size_z = viscosity.shape
    return pl.pallas_call(
        functools.partial(pack_kernel, size_x, size_y, size_z),
        out_shape=(
            jax.ShapeDtypeStruct((14, size_x, size_z), jnp.float32),
            jax.ShapeDtypeStruct((14, size_y, size_z), jnp.float32),
            jax.ShapeDtypeStruct((size_x * size_y, size_z), jnp.float32),
            jax.ShapeDtypeStruct((8 + size_x, size_z), jnp.float32),
        ),
        in_specs=[SMEM, VMEM, VMEM],
        out_specs=(VMEM, VMEM, VMEM, VMEM),
        cost_estimate=pl.CostEstimate(flops=400000, bytes_accessed=3000000, transcendentals=0),
        name="pack_faces",
    )(
        place,
        velocity.reshape(3, size_x * size_y, size_z),
        viscosity.reshape(size_x * size_y, size_z),
    )


def reciprocal(value):
    first = pl.reciprocal(value, approx=True)
    return first * (2.0 - value * first)


def micro_kernel(parts, conform_ref, noise_ref, rate_ref, next_ref, polymer_ref):
    rows = conform_ref.shape[1]
    steps = noise_ref.shape[0]
    dumbbells = conform_ref.shape[2]
    width = dumbbells // parts
    scale = 1.0 / noise_weight
    extent = fene_extent * scale * scale
    rates = [
        [
            jnp.broadcast_to(
                micro_step * rate_ref[:, 3 * a + b : 3 * a + b + 1] + (1.0 if a == b else 0.0), (rows, width)
            )
            for b in range(3)
        ]
        for a in range(3)
    ]

    def inverse_of(q):
        return reciprocal(
            jnp.maximum(extent - (q[0] * q[0] + q[1] * q[1] + q[2] * q[2]), extent * spring_floor)
        )

    def substep(step, state):
        result = []
        for part in range(parts):
            q = state[3 * part : 3 * part + 3]
            spring = (micro_step * relax_rate * extent) * inverse_of(q)
            for a in range(3):
                noise = noise_ref[step, a, :, part * width : (part + 1) * width].astype(jnp.float32)
                terms = [(rates[a][b] - spring if a == b else rates[a][b]) * q[b] for b in range(3)]
                result.append(terms[0] + terms[1] + terms[2] + noise)
        return tuple(result)

    state = tuple(
        conform_ref[a, :, part * width : (part + 1) * width] * scale for part in range(parts) for a in range(3)
    )
    state = lax.fori_loop(0, steps, substep, state, unroll=True)
    lane = lanes_of((rows, 128))
    sums = [None] * 6
    for part in range(parts):
        q = state[3 * part : 3 * part + 3]
        for a in range(3):
            next_ref[a, :, part * width : (part + 1) * width] = q[a] * noise_weight
        inverse = inverse_of(q)
        for k, (a, b) in enumerate(stress_pairs):
            term = inverse * q[a] * q[b]
            sums[k] = term if sums[k] is None else sums[k] + term
    packed = jnp.zeros((rows, 128), jnp.float32)
    weight = extent * noise_weight * noise_weight / dumbbells
    for k, (a, b) in enumerate(stress_pairs):
        mean = jnp.sum(sums[k], axis=1, keepdims=True) * weight
        packed = jnp.where(lane == k, polymer_weight * (mean - (1.0 if a == b else 0.0)), packed)
    polymer_ref[...] = packed


def advance(conformations, increments, rates):
    slots, dumbbells = conformations.shape[1:]
    steps = increments.shape[0]
    rows = 16
    return pl.pallas_call(
        functools.partial(micro_kernel, 4),
        grid=(slots // rows,),
        out_shape=(
            jax.ShapeDtypeStruct(conformations.shape, jnp.float32),
            jax.ShapeDtypeStruct((slots, 128), jnp.float32),
        ),
        in_specs=[
            pl.BlockSpec((3, rows, dumbbells), lambda i: (0, i, 0)),
            pl.BlockSpec((steps, 3, rows, dumbbells), lambda i: (0, 0, i, 0)),
            pl.BlockSpec((rows, 128), lambda i: (i, 0)),
        ],
        out_specs=(
            pl.BlockSpec((3, rows, dumbbells), lambda i: (0, i, 0)),
            pl.BlockSpec((rows, 128), lambda i: (i, 0)),
        ),
        cost_estimate=pl.CostEstimate(flops=20000000, bytes_accessed=5000000, transcendentals=600000),
        name="advance",
    )(conformations, increments, rates)


def flow_kernel(
    size_x, size_y, size_z, place_ref,
    velocity_ref, viscosity_ref, y_low_ref, y_high_ref, x_low_ref, x_high_ref,
    xz_low_ref, xz_high_ref, z_ref, ll_ref, lh_ref, hl_ref, hh_ref, yz_low_ref, yz_high_ref,
    out_ref, stress_ref,
):
    m, t, core = place_ref[0], place_ref[1], place_ref[2]
    x_in = (m > 0, m < place_ref[3] - 1)
    y_in = (t > 0, t < place_ref[4] - 1)

    def kept(value, *conditions):
        weight = jnp.float32(1.0)
        for condition in conditions:
            weight = weight * jnp.where(condition, 1.0, 0.0)
        return value * weight

    def compute(core):
        block = (size_x, size_y, size_z)
        lane3 = lanes_of(block)
        row3 = lax.broadcasted_iota(jnp.int32, block, 1)
        end = size_z - 1 if core == 0 else 0
        sender = 1 - core

        x_face = [[kept(ref[0, i], x_in[s]) for i in range(7)] for s, ref in enumerate((x_low_ref, x_high_ref))]
        y_face = [[kept(ref[0, i], y_in[s]) for i in range(7)] for s, ref in enumerate((y_low_ref, y_high_ref))]
        packed = z_ref[0]
        z_face = [
            unpacked_lanes(packed, item, sender).reshape(block) for item in range(7)
        ]

        def shift_x(value, low, high):
            minus = jnp.concatenate([low[None], value[:-1]], axis=0)
            plus = jnp.concatenate([value[1:], high[None]], axis=0)
            return minus, plus

        def shift_y(value, low, high):
            minus = jnp.where(row3 == 0, low[:, None, :], pltpu.roll(value, 1, 1))
            plus = jnp.where(row3 == size_y - 1, high[:, None, :], pltpu.roll(value, size_y - 1, 1))
            return minus, plus

        def shift_z(value, ghost):
            lane = lanes_of(value.shape)
            minus, plus = roll_lanes(value, 1), roll_lanes(value, -1)
            if core == 0:
                return jnp.where(lane == 0, 0.0, minus), jnp.where(lane == size_z - 1, ghost, plus)
            return jnp.where(lane == 0, ghost, minus), jnp.where(lane == size_z - 1, 0.0, plus)

        velocity = [velocity_ref[a].reshape(block) for a in range(3)]
        viscosity = viscosity_ref[...].reshape(block)
        half = 0.5 * viscosity
        slopes = []
        for a in range(3):
            minus_x, plus_x = shift_x(velocity[a], x_face[0][a], x_face[1][a])
            minus_y, plus_y = shift_y(velocity[a], y_face[0][a], y_face[1][a])
            minus_z, plus_z = shift_z(velocity[a], z_face[a])
            slopes.append((plus_x - minus_x, plus_y - minus_y, plus_z - minus_z))
        for k, (a, b) in enumerate(stress_pairs):
            stress_ref[k] = half * (slopes[a][b] + slopes[b][a])

        corners = ((ll_ref, lh_ref), (hl_ref, hh_ref))
        xz_refs = (xz_low_ref, xz_high_ref)
        yz_refs = (yz_low_ref, yz_high_ref)

        x_ghost = []
        for s in range(2):
            v0, v1, weight = x_face[s][0:3], x_face[s][3:6], 0.5 * x_face[s][6]
            edge_plane = 0 if s == 0 else size_x - 1
            normal = [
                (velocity[a][edge_plane] - v1[a]) * (1.0 if s == 0 else -1.0) for a in range(3)
            ]
            row2 = lax.broadcasted_iota(jnp.int32, (size_y, size_z), 0)
            low = kept(corners[s][0][0, 4 * (1 - s) + 2 : 4 * (1 - s) + 3, :], x_in[s], y_in[0])
            high = kept(corners[s][1][0, 4 * (1 - s) : 4 * (1 - s) + 1, :], x_in[s], y_in[1])
            minus = jnp.where(row2 == 0, low, pltpu.roll(v0[0], 1, 0))
            plus = jnp.where(row2 == size_y - 1, high, pltpu.roll(v0[0], size_y - 1, 0))
            slope_y = plus - minus
            ghost = kept(roll_lanes(xz_refs[s][0, 0], 1 if core == 1 else -1), x_in[s])
            minus, plus = shift_z(v0[0], ghost)
            slope_z = plus - minus
            x_ghost.append(
                (weight * (2.0 * normal[0]), weight * (normal[1] + slope_y), weight * (normal[2] + slope_z))
            )

        y_ghost = []
        for s in range(2):
            v0, v1, weight = y_face[s][0:3], y_face[s][3:6], 0.5 * y_face[s][6]
            y = 0 if s == 0 else size_y - 1
            own = [velocity_ref[a, pl.ds(y, size_x, stride=size_y), :] for a in range(3)]
            normal = [(own[a] - v1[a]) * (1.0 if s == 0 else -1.0) for a in range(3)]
            row2 = lax.broadcasted_iota(jnp.int32, (size_x, size_z), 0)
            line = 2 * (1 - s) + 1
            low = kept(corners[0][s][0, 4 + line : 5 + line, :], x_in[0], y_in[s])
            high = kept(corners[1][s][0, line : 1 + line, :], x_in[1], y_in[s])
            minus = jnp.where(row2 == 0, low, pltpu.roll(v0[1], 1, 0))
            plus = jnp.where(row2 == size_x - 1, high, pltpu.roll(v0[1], size_x - 1, 0))
            slope_x = plus - minus
            packed_edge = yz_refs[s][0, 8:, :]
            ghost = kept(unpacked_lanes(packed_edge, 2 * (1 - s), sender), y_in[s])
            minus, plus = shift_z(v0[1], ghost)
            slope_z = plus - minus
            y_ghost.append(
                (weight * (normal[0] + slope_x), weight * (2.0 * normal[1]), weight * (normal[2] + slope_z))
            )

        v0, weight, v1 = z_face[0:3], 0.5 * z_face[3], z_face[4:7]
        sign = -1.0 if core == 0 else 1.0
        normal = [(velocity[a] - v1[a]) * sign for a in range(3)]
        low, high = [
            kept(roll_lanes(xz_refs[s][0, 2], 1 if core == 1 else -1), x_in[s]) for s in range(2)
        ]
        minus, plus = shift_x(v0[2], low, high)
        slope_x = plus - minus
        low, high = [
            kept(unpacked_lanes(yz_refs[s][0, 8:, :], 2 * (1 - s) + 1, sender), y_in[s]) for s in range(2)
        ]
        minus, plus = shift_y(v0[2], low, high)
        slope_y = plus - minus
        z_ghost = (weight * (normal[0] + slope_x), weight * (normal[1] + slope_y), weight * (2.0 * normal[2]))

        for a in range(3):
            column = stress_ref[pair_index(a, 0)]
            minus, plus = shift_x(column, x_ghost[0][a], x_ghost[1][a])
            total = plus - minus
            column = stress_ref[pair_index(a, 1)]
            minus, plus = shift_y(column, y_ghost[0][a], y_ghost[1][a])
            total = total + (plus - minus)
            column = stress_ref[pair_index(a, 2)]
            minus, plus = shift_z(column, z_ghost[a])
            total = total + (plus - minus)
            out_ref[a] = (velocity[a] + (0.5 * macro_step) * total).reshape(size_x * size_y, size_z)

    for option in range(2):

        @pl.when(core == option)
        def _(option=option):
            compute(option)


def flow_step(place, velocity, viscosity, faces_y, faces_x, faces_z, edges, counts):
    size_x, size_y, size_z = viscosity.shape
    macro_count, tile_count = counts

    def low(index):
        return jnp.maximum(index - 1, 0)

    def high(index, count):
        return jnp.minimum(index + 1, count - 1)

    def neighbour(index, side, count):
        return low(index) if side == 0 else high(index, count)

    def y_spec(side):
        return pl.BlockSpec(
            (1, 7, size_x, size_z), lambda i, p: (neighbour(p[1], side, tile_count), 1 - side, 0, 0)
        )

    def x_spec(side, other):
        return pl.BlockSpec(
            (1, 7, size_y, size_z),
            lambda i, p: (
                2 * neighbour(p[0], side, macro_count) + (1 - p[2] if other else p[2]), 1 - side, 0, 0
            ),
        )

    def device(m, t, c):
        return (m * tile_count + t) * 2 + c

    def corner_spec(x_side, y_side):
        return pl.BlockSpec(
            (1, 8, size_z),
            lambda i, p: (
                device(neighbour(p[0], x_side, macro_count), neighbour(p[1], y_side, tile_count), p[2]), 0, 0
            ),
        )

    def edge_spec(y_side):
        return pl.BlockSpec(
            (1, 8 + size_x, size_z),
            lambda i, p: (device(p[0], neighbour(p[1], y_side, tile_count), 1 - p[2]), 0, 0),
        )

    whole3 = pl.BlockSpec((3, size_x * size_y, size_z), lambda i, p: (0, 0, 0))
    return pl.pallas_call(
        functools.partial(flow_kernel, size_x, size_y, size_z),
        grid_spec=pltpu.PrefetchScalarGridSpec(
            num_scalar_prefetch=1,
            grid=(1,),
            in_specs=[
                whole3,
                pl.BlockSpec((size_x * size_y, size_z), lambda i, p: (0, 0)),
                y_spec(0), y_spec(1),
                x_spec(0, False), x_spec(1, False), x_spec(0, True), x_spec(1, True),
                pl.BlockSpec((1, size_x * size_y, size_z), lambda i, p: (1 - p[2], 0, 0)),
                corner_spec(0, 0), corner_spec(0, 1), corner_spec(1, 0), corner_spec(1, 1),
                edge_spec(0), edge_spec(1),
            ],
            out_specs=whole3,
            scratch_shapes=[pltpu.VMEM((6, size_x, size_y, size_z), jnp.float32)],
        ),
        out_shape=jax.ShapeDtypeStruct((3, size_x * size_y, size_z), jnp.float32),
        cost_estimate=pl.CostEstimate(flops=4000000, bytes_accessed=3000000, transcendentals=0),
        name="flow_step",
    )(
        place,
        velocity.reshape(3, size_x * size_y, size_z),
        viscosity.reshape(size_x * size_y, size_z),
        faces_y, faces_y, faces_x, faces_x, faces_x, faces_x, faces_z,
        edges, edges, edges, edges, edges, edges,
    )


def polymer_kernel(
    size_y, size_z, cell_ref, position_ref, slots_ref, viscous_ref, partial_ref,
    out_ref, flag_ref, polymer, lines, shifted,
):
    flags = cell_ref.shape[0]
    out_ref[...] = partial_ref[...]
    lane = lanes_of((1, size_z))
    for j in range(flags):
        polymer[j : j + 1, :] = slots_ref[pl.ds(position_ref[j], 1), :]
        cell = cell_ref[j]
        z = cell - lax.div(cell, size_z) * size_z
        lines[0, j : j + 1, :] = jnp.where(lane == z, 0.5 * macro_step, 0.0)
        lines[1, j : j + 1, :] = jnp.where(
            lane == z - 1, 0.5 * macro_step, jnp.where(lane == z + 1, -0.5 * macro_step, 0.0)
        )
    values = polymer[...]
    flag_ref[...] = (viscous_ref[...] + values).T[0:6, :]
    here, beside = lines[0], lines[1]
    for k in range(6):
        column = jnp.broadcast_to(values[:, k : k + 1], (flags, size_z))
        shifted[k] = column * here
        if stress_pairs[k][1] == 2:
            shifted[6 + stress_pairs[k][0]] = column * beside
    for j in range(flags):
        row = lax.div(cell_ref[j], size_z)
        targets = []
        for a in range(3):
            line_x = shifted[pair_index(a, 0), j : j + 1, :]
            line_y = shifted[pair_index(a, 1), j : j + 1, :]
            line_z = shifted[6 + a, j : j + 1, :]
            targets += [
                (a, row - size_y, line_x), (a, row + size_y, -line_x),
                (a, row - 1, line_y), (a, row + 1, -line_y), (a, row, line_z),
            ]
        updated = [out_ref[a, pl.ds(at, 1), :] + line for a, at, line in targets]
        for (a, at, _), line in zip(targets, updated):
            out_ref[a, pl.ds(at, 1), :] = line


def add_polymer(flag_cell, position, slots, viscous, partial, size_y):
    flags = flag_cell.shape[0]
    size_z = partial.shape[2]
    return pl.pallas_call(
        functools.partial(polymer_kernel, size_y, size_z),
        out_shape=(
            jax.ShapeDtypeStruct(partial.shape, jnp.float32),
            jax.ShapeDtypeStruct((6, flags), jnp.float32),
        ),
        in_specs=[SMEM, SMEM, VMEM, VMEM, VMEM],
        out_specs=(VMEM, VMEM),
        scratch_shapes=[
            pltpu.VMEM((flags, 128), jnp.float32),
            pltpu.VMEM((2, flags, size_z), jnp.float32),
            pltpu.VMEM((9, flags, size_z), jnp.float32),
        ],
        cost_estimate=pl.CostEstimate(flops=400000, bytes_accessed=3000000, transcendentals=0),
        name="add_polymer",
    )(flag_cell, position, slots, viscous, partial)


def shards(velocity, viscosity, flag_cell, flag_owner, conformations, increments):
    macro_count = lax.axis_size("macro")
    tile_count = lax.axis_size("tile")
    micro_count = lax.axis_size("micro")
    assert micro_count == 2
    owner_count = macro_count * micro_count
    slot_count = conformations.shape[1]
    capacity = slot_count // owner_count
    size_x, size_y, size_z = viscosity.shape
    place = jnp.stack(
        [
            lax.axis_index("macro"), lax.axis_index("tile"), lax.axis_index("micro"),
            jnp.int32(macro_count), jnp.int32(tile_count),
        ]
    ).astype(jnp.int32)
    slots, position, viscous = gather_rows(
        flag_cell, flag_owner.reshape(-1), velocity, viscosity, slot_count, owner_count
    )

    def exchange(rows):
        rows = rows.reshape(owner_count, capacity, 128)
        rows = lax.all_to_all(rows, ("macro", "micro"), split_axis=0, concat_axis=0, tiled=True)
        return rows.reshape(slot_count, 128)

    rates = exchange(slots)
    face_y, face_x, face_z, edge = pack_faces(place, velocity, viscosity)
    faces_y = lax.all_gather(face_y, "tile")
    faces_x = lax.all_gather(face_x, ("macro", "micro"))
    faces_z = lax.all_gather(face_z, "micro")
    edges = lax.all_gather(edge, ("macro", "tile", "micro"))
    last_state, polymer = advance(conformations, increments, rates)
    returned = exchange(polymer)
    partial = flow_step(
        place, velocity, viscosity, faces_y, faces_x, faces_z, edges, (macro_count, tile_count)
    )
    velocity_next, flag_stress = add_polymer(flag_cell, position, returned, viscous, partial, size_y)
    return (velocity_next.reshape(velocity.shape), last_state, flag_stress)


def solution(mesh):
    in_specs = (
        P(None, "macro", "tile", "micro"),
        P("macro", "tile", "micro"),
        P(("macro", "tile", "micro")),
        P(("macro", "tile", "micro"), None),
        P(None, ("macro", "tile", "micro"), None),
        P(None, None, ("macro", "tile", "micro"), None),
    )
    out_specs = (
        P(None, "macro", "tile", "micro"),
        P(None, ("macro", "tile", "micro"), None),
        P(None, ("macro", "tile", "micro")),
    )
    return jax.shard_map(shards, mesh=mesh, in_specs=in_specs, out_specs=out_specs, check_vma=False)
```

time: 215 us -> 105 us (0.49); the launches traced: 212 us -> 104 us
  local copies, waits for them, and re-layouts: 85.4 us -> 1.23 us
  blocking collectives: 0 us -> 78.1 us
  other arithmetic: 62.6 us -> 0.59 us
  starting transfers between devices: 39.8 us -> 8.51 us
  waiting for transfers between devices: 20.4 us -> 0.01 us
  Pallas kernels: 0 us -> 15 us
    all_gather x0 -> x4, blocking collectives: none -> 78.1 us  [the longest x1 45 us: shards(): edges = lax.all_gather(edge, ('macro', 'tile', 'micro'))]
    add x36 -> x0, other arithmetic: 41.1 us -> none  [the longest x32 32 us: substep(): current[left_axis] + micro_step * drift_term]
    gather x13 -> x0, local copies, waits for them, and re-layouts: 32.1 us -> none  [the longest x6 15.7 us: shards(): upper_side = jnp.take(flat_velocity, flag_cell + stride, axis=1)]
    ppermute x12 -> x0, starting transfers between devices: 31.6 us -> none  [the longest x6 23.9 us: padded_2(): lax.ppermute(lax.slice_in_dim(block, block.shape[dim] - width, None, axis...]
    unnamed x61 -> x6, local copies, waits for them, and re-layouts: 32 us -> 1.23 us
    pallas_call x0 -> x5, Pallas kernels: none -> 15 us  [the longest x1 5.69 us: advance(): pl.pallas_call(functools.partial(micro_kernel, 4), grid=(slots // rows,),...]
    ppermute x12 -> x0, waiting for transfers between devices: 13.3 us -> none  [the longest x6 7.13 us: padded_2(): lax.ppermute(lax.slice_in_dim(block, 0, width, axis=dim), axis, backward)]
    add x4 -> x0, local copies, waits for them, and re-layouts: 11.7 us -> none  [the longest x1 6.76 us: shards(): velocity_next = velocity + macro_step * divergence(stress_pad)]
  transfers between devices with their start and end apart: 14 -> 2, of which waited for: 6 -> 0; matrix products, arithmetic and copies ran while one was open for 46% -> 0% of each run, Pallas kernels for 0% -> 5%
where the time goes in v1:
time: 105 us; the launch traced here: 104 us
  blocking collectives  78.1 us (74%)
  Pallas kernels  15 us (14%)
  starting transfers between devices  8.51 us (8%)
  local copies, waits for them, and re-layouts  1.23 us (1%)
    all_gather x1, blocking collectives, shards(): edges = lax.all_gather(edge, ('macro', 'tile', 'micro'))  45 us
    all_gather x1, blocking collectives, shards(): faces_y = lax.all_gather(face_y, 'tile')  20.4 us
    all_gather x1, blocking collectives, shards(): faces_x = lax.all_gather(face_x, ('macro', 'micro'))  10.6 us
    all_to_all x2, starting transfers between devices, exchange(): lax.all_to_all(rows, ('macro', 'micro'), split_axis=0, concat_axis=0, til...  8.51 us
    pallas_call x1, Pallas kernels, advance(): pl.pallas_call(functools.partial(micro_kernel, 4), grid=(slots // rows,),...  5.69 us
    pallas_call x1, Pallas kernels, flow_step(): pl.pallas_call(functools.partial(flow_kernel, size_x, size_y, size_z), gr...  3.22 us
    all_gather x1, blocking collectives, shards(): faces_z = lax.all_gather(face_z, 'micro')  2.11 us
  transfers between devices with their start and end apart: 2, of which 0 were waited for; matrix products, arithmetic and copies ran while one was open for 0% of the time, Pallas kernels for 5%

profile of v1, /device:TPU:0, one launch (start us, length us, event | category | flops | bytes accessed | tf_op | source)
XLA Modules:
  0.0 104.1 jit_solution(457330064533608216)
XLA Ops:
  0.6 0.6 pad_add_fusion.place_ref
  1.2 2.0 %gather_rows.1 = (f32[64,128]{1,0:T(8,128)}, s32[32]{0:T(128)}, f32[32,128]{1,0:T(8,128)}) custom-call(s32[32]{0:T(128)} %cell_ref.3, s32[32]{0:T(128)} %bitcast.38, f32[3,192,128]{2,1,0:T(8,128)} %bitcast.27, f32[192,128]{1,0:T(8,128)} %bitcast.30), custom_call_target="tpu_custom_call" | custom-call | flops 400000 | bytes 3000000 | tf_op jit(solution)/shard_map/gather_rows/pallas_call | solution.py:75
  3.2 5.2 %all-to-all-start = ((f32[8,8,128]{2,1,0:T(8,128)}), f32[8,8,128]{2,1,0:T(8,128)S(1)}, u32[]{:S(2)}, u32[]{:S(2)}) async-start(f32[8,8,128]{2,1,0:T(8,128)} %bitcast.36), calls=%async_computation | async-start | bytes 65536 | tf_op jit(solution)/shard_map/all_to_all | solution.py:560
  8.4 2.0 %pack_faces.1 = (f32[14,24,128]{2,1,0:T(8,128)}, f32[14,8,128]{2,1,0:T(8,128)}, f32[192,128]{1,0:T(8,128)}, f32[32,128]{1,0:T(8,128)}) custom-call(s32[5]{0:T(128)} %pad_add_fusion.place_ref, f32[3,192,128]{2,1,0:T(8,128)} %bitcast.28, f32[192,128]{1,0:T(8,128)} %bitcast.31), custom_call_target="tpu_custom_call" | custom-call | flops 400000 | bytes 3000000 | tf_op jit(solution)/shard_map/pack_faces/pallas_call | solution.py:164
  10.4 0.0 copy-start.2
  10.4 20.4 %all-gather = f32[56,24,128]{2,1,0:T(8,128)} all-gather(f32[14,24,128]{2,1,0:T(8,128)} %get-tuple-element.18), channel_id=2, replica_groups=mesh['macro'=4,'tile'=4,'micro'=2] {'tile'}, dimensions={0}, use_global_device_ids=true | all-gather | bytes 860160 | tf_op jit(solution)/shard_map/all_gather | solution.py:565
  30.8 45.0 %all-gather.3 = f32[1024,128]{1,0:T(8,128)} all-gather(f32[32,128]{1,0:T(8,128)} %get-tuple-element.21), channel_id=5, replica_groups=mesh['macro'=4,'tile'=4,'micro'=2] {'macro','tile','micro'}, dimensions={0}, use_global_device_ids=true | all-gather | bytes 540672 | tf_op jit(solution)/shard_map/all_gather | solution.py:568
  75.8 10.6 %all-gather.1 = f32[112,8,128]{2,1,0:T(8,128)} all-gather(f32[14,8,128]{2,1,0:T(8,128)} %get-tuple-element.19), channel_id=3, replica_groups=mesh['macro'=4,'tile'=4,'micro'=2] {'macro','micro'}, dimensions={0}, use_global_device_ids=true | all-gather | bytes 516096 | tf_op jit(solution)/shard_map/all_gather | solution.py:566
  86.4 0.0 all-to-all-done
  86.4 0.0 copy-start
  86.4 0.6 copy-done
  87.0 5.7 %advance.1 = (f32[3,64,512]{2,1,0:T(8,128)}, f32[64,128]{1,0:T(8,128)}) custom-call(f32[3,64,512]{2,1,0:T(8,128)} %conform_ref.1, bf16[16,3,64,512]{3,2,1,0:T(8,128)(2,1)} %noise_ref.1, f32[64,128]{1,0:T(8,128)} %bitcast.34), custom_call_target="tpu_custom_call" | custom-call | flops 20000000 | bytes 5000000 | tf_op jit(solution)/shard_map/advance/pallas_call | solution.py:247
  92.7 3.3 %all-to-all-start.1 = ((f32[8,8,128]{2,1,0:T(8,128)}), f32[8,8,128]{2,1,0:T(8,128)S(1)}, u32[]{:S(2)}, u32[]{:S(2)}) async-start(f32[8,8,128]{2,1,0:T(8,128)} %bitcast.37), calls=%async_computation.1 | async-start | bytes 65536 | tf_op jit(solution)/shard_map/all_to_all | solution.py:560
  96.0 0.0 copy-done.2
  96.1 2.1 %all-gather.2 = f32[384,128]{1,0:T(8,128)} all-gather(f32[192,128]{1,0:T(8,128)S(1)} %copy-done.2), channel_id=4, replica_groups=mesh['macro'=4,'tile'=4,'micro'=2] {'micro'}, dimensions={0}, use_global_device_ids=true | all-gather | bytes 294912 | tf_op jit(solution)/shard_map/all_gather | solution.py:567
  98.2 3.2 %flow_step.1.partial_ref = f32[3,192,128]{2,1,0:T(8,128)} custom-call(s32[5]{0:T(128)} %pad_add_fusion.place_ref, f32[3,192,128]{2,1,0:T(8,128)} %bitcast.29, f32[192,128]{1,0:T(8,128)} %bitcast.32, f32[4,14,24,128]{3,2,1,0:T(8,128)} %bitcast.25, f32[4,14,24,128]{3,2,1,0:T(8,128)} %bitcast.26, f32[8,14,8,128]{3,2,1,0:T(8,128)} %bitcast.21, ...), custom_call_target="tpu_custom_call" | custom-call | flops 4000000 | bytes 3000000 | tf_op jit(solution)/shard_map/flow_step/pallas_call | solution.py:450
  101.4 0.0 all-to-all-done.1
  101.4 0.0 copy-start.1
  101.4 0.6 copy-done.1
  102.0 2.1 %add_polymer.1 = (f32[3,192,128]{2,1,0:T(8,128)}, f32[6,32]{1,0:T(8,128)}) custom-call(s32[32]{0:T(128)} %cell_ref.3, s32[32]{0:T(128)} %get-tuple-element.14.position_ref, f32[64,128]{1,0:T(8,128)} %bitcast.35, f32[32,128]{1,0:T(8,128)} %get-tuple-element.17.viscous_ref, f32[3,192,128]{2,1,0:T(8,128)} %flow_step.1.partial_ref), custom_call_target="tpu_custom_call" | custom-call | flops 400000 | bytes 3000000 | tf_op jit(solution)/shard_map/add_polymer/pallas_call | solution.py:521
  (1 shorter events, 0.0 us)
Async XLA Ops:
  3.2 83.2 %all-to-all-start = ((f32[8,8,128]{2,1,0:T(8,128)}), f32[8,8,128]{2,1,0:T(8,128)S(1)}, u32[]{:S(2)}, u32[]{:S(2)}) async-start(f32[8,8,128]{2,1,0:T(8,128)} %bitcast.36), calls=%async_computation | async-start | bytes 65536 | tf_op jit(solution)/shard_map/all_to_all | solution.py:560
  10.4 85.6 %copy-start.2 = (f32[192,128]{1,0:T(8,128)S(1)}, f32[192,128]{1,0:T(8,128)}, u32[]{:S(2)}) copy-start(f32[192,128]{1,0:T(8,128)} %get-tuple-element.20) | copy-start | bytes 294916
  86.4 0.6 copy-start
  92.7 8.7 %all-to-all-start.1 = ((f32[8,8,128]{2,1,0:T(8,128)}), f32[8,8,128]{2,1,0:T(8,128)S(1)}, u32[]{:S(2)}, u32[]{:S(2)}) async-start(f32[8,8,128]{2,1,0:T(8,128)} %bitcast.37), calls=%async_computation.1 | async-start | bytes 65536 | tf_op jit(solution)/shard_map/all_to_all | solution.py:560
  101.4 0.6 copy-start.1

commit v2 on v0

v2 whole, which is shorter than its diff:
```python
import functools

import jax
import jax.numpy as jnp
from jax import lax
from jax.experimental import pallas as pl
from jax.experimental.pallas import tpu as pltpu
from jax.sharding import PartitionSpec as P

stress_pairs = ((0, 0), (1, 1), (2, 2), (0, 1), (0, 2), (1, 2))
macro_step = 0.1
micro_step = 0.01
noise_weight = 0.1
relax_rate = 0.5
fene_extent = 30.0
spring_floor = 0.1
polymer_weight = 0.25

SMEM = pl.BlockSpec(memory_space=pltpu.SMEM)
VMEM = pl.BlockSpec(memory_space=pltpu.VMEM)


def pair_index(left_axis, right_axis):
    return stress_pairs.index((min(left_axis, right_axis), max(left_axis, right_axis)))


def lanes_of(shape):
    return lax.broadcasted_iota(jnp.int32, shape, len(shape) - 1)


slot_rows = 8
item_count = 7
line_rows = 8


def limit(mebibytes):
    return pltpu.CompilerParams(vmem_limit_bytes=mebibytes * 1024 * 1024)


def place_of():
    return lax.axis_index("macro"), lax.axis_index("micro")


def rolled(value, amount):
    size = value.shape[-1]
    if isinstance(amount, int):
        return pltpu.roll(value, amount % size, value.ndim - 1)
    return pltpu.roll(value, lax.rem(amount + 2 * size, size), value.ndim - 1)


def gather_kernel(
    capacity, size_x, size_y, size_z, macro_count, cell_ref, owner_ref, velocity_ref, viscosity_ref,
    chunk_ref, position_ref, viscous_ref, y_low_ref, y_high_ref, masked, gradients, target, count,
):
    flags = cell_ref.shape[0]
    chunk_rows = slot_rows + item_count * size_y
    macro, core = place_of()
    lane = lanes_of((1, size_z))

    def clear(owner, carry):
        count[owner] = 0
        chunk_ref[pl.ds(pl.multiple_of(owner * chunk_rows, 8), slot_rows), :] = jnp.zeros(
            (slot_rows, 128), jnp.float32
        )
        return carry

    lax.fori_loop(0, count.shape[0], clear, 0, unroll=True)

    def read(j, carry):
        cell = cell_ref[j]
        row = lax.div(cell, size_z)
        z = cell - row * size_z
        here = (lane == z).astype(jnp.float32)
        along_z = (lane == z + 1).astype(jnp.float32) - (lane == z - 1).astype(jnp.float32)
        for a in range(3):
            along_x = velocity_ref[a, pl.ds(row + size_y, 1), :] - velocity_ref[a, pl.ds(row - size_y, 1), :]
            along_y = velocity_ref[a, pl.ds(row + 1, 1), :] - velocity_ref[a, pl.ds(row - 1, 1), :]
            masked[3 * a, pl.ds(j, 1), :] = along_x * here
            masked[3 * a + 1, pl.ds(j, 1), :] = along_y * here
            masked[3 * a + 2, pl.ds(j, 1), :] = velocity_ref[a, pl.ds(row, 1), :] * along_z
        masked[9, pl.ds(j, 1), :] = viscosity_ref[pl.ds(row, 1), :] * here
        owner = owner_ref[j]
        rank = count[owner]
        count[owner] = rank + 1
        target[j] = owner * chunk_rows + rank
        position_ref[j] = owner * (slot_rows + line_rows) + rank
        return carry

    lax.fori_loop(0, flags, read, 0, unroll=4)

    for side, ref in enumerate((y_low_ref, y_high_ref)):
        for layer in range(2):
            y = layer if side == 0 else size_y - 1 - layer
            for a in range(3):
                ref[3 * layer + a] = velocity_ref[a, pl.ds(y, size_x, stride=size_y), :]
        y = 0 if side == 0 else size_y - 1
        ref[6] = viscosity_ref[pl.ds(y, size_x, stride=size_y), :]

    for side in range(2):
        beside = macro - 1 if side == 0 else macro + 1

        @pl.when(beside >= 0 if side == 0 else beside < macro_count)
        def _(side=side, beside=beside):
            first = pl.multiple_of((2 * beside + core) * chunk_rows + slot_rows, 8)
            other = pl.multiple_of((2 * beside + 1 - core) * chunk_rows + slot_rows, 8)
            for layer in range(2):
                x = layer if side == 0 else size_x - 1 - layer
                for a in range(3):
                    chunk_ref[pl.ds(first + (3 * layer + a) * size_y, size_y), :] = velocity_ref[
                        a, x * size_y : (x + 1) * size_y, :
                    ]
            x = 0 if side == 0 else size_x - 1
            chunk_ref[pl.ds(first + 6 * size_y, size_y), :] = viscosity_ref[x * size_y : (x + 1) * size_y, :]
            for number, a in enumerate((0, 2)):
                chunk_ref[pl.ds(other + number * size_y, size_y), :] = velocity_ref[
                    a, x * size_y : (x + 1) * size_y, :
                ]

    group = size_z // 8
    lane2 = lanes_of((size_y, size_z))
    first = pl.multiple_of((2 * macro + 1 - core) * chunk_rows + slot_rows, 8)
    sources = [jnp.where(core == 0, size_z - 1 - layer, layer) for layer in range(2)]
    for block in range(-(-size_x // group)):

        def add_plane(x, total):
            rows = pl.ds(pl.multiple_of(x * size_y, 8), size_y)
            start = 8 * (x - block * group)
            for q in range(item_count):
                layer, a = (0, q) if q < 4 else (1, q - 4)
                value = viscosity_ref[rows, :] if q == 3 else velocity_ref[a, rows, :]
                total = jnp.where(lane2 == start + q, rolled(value, start + q - sources[layer]), total)
            return total

        total = lax.fori_loop(
            block * group, min(size_x, (block + 1) * group), add_plane,
            jnp.zeros((size_y, size_z), jnp.float32), unroll=4,
        )
        chunk_ref[pl.ds(first + block * size_y, size_y), :] = total

    columns = [0.5 * jnp.sum(masked[c], axis=1, keepdims=True) for c in range(9)]
    viscous = jnp.sum(masked[9], axis=1, keepdims=True)
    wide = lanes_of((flags, 128))
    packed = jnp.zeros((flags, 128), jnp.float32)
    for c in range(9):
        packed = jnp.where(wide == c, columns[c], packed)
    gradients[...] = packed
    stress = jnp.zeros((flags, 128), jnp.float32)
    for k, (a, b) in enumerate(stress_pairs):
        stress = jnp.where(wide == k, viscous * (columns[3 * a + b] + columns[3 * b + a]), stress)
    viscous_ref[...] = stress

    def place(j, carry):
        chunk_ref[pl.ds(target[j], 1), :] = gradients[pl.ds(j, 1), :]
        return carry

    lax.fori_loop(0, flags, place, 0, unroll=8)


def gather_rows(flag_cell, owner, velocity, viscosity, capacity, owner_count):
    size_x, size_y, size_z = viscosity.shape
    flags = flag_cell.shape[0]
    chunk_rows = slot_rows + item_count * size_y
    face = jax.ShapeDtypeStruct((item_count, size_x, size_z), jnp.float32)
    return pl.pallas_call(
        functools.partial(gather_kernel, capacity, size_x, size_y, size_z, owner_count // 2),
        out_shape=(
            jax.ShapeDtypeStruct((owner_count * chunk_rows, 128), jnp.float32),
            jax.ShapeDtypeStruct((flags,), jnp.int32),
            jax.ShapeDtypeStruct((flags, 128), jnp.float32),
            face,
            face,
        ),
        in_specs=[SMEM, SMEM, VMEM, VMEM],
        out_specs=(VMEM, SMEM, VMEM, VMEM, VMEM),
        scratch_shapes=[
            pltpu.VMEM((10, flags, size_z), jnp.float32),
            pltpu.VMEM((flags, 128), jnp.float32),
            pltpu.SMEM((flags,), jnp.int32),
            pltpu.SMEM((owner_count,), jnp.int32),
        ],
        compiler_params=limit(8),
        cost_estimate=pl.CostEstimate(flops=400000, bytes_accessed=3000000, transcendentals=0),
        name="gather_rows",
    )(
        flag_cell,
        owner,
        velocity.reshape(3, size_x * size_y, size_z),
        viscosity.reshape(size_x * size_y, size_z),
    )


def reciprocal(value):
    first = pl.reciprocal(value, approx=True)
    return first * (2.0 - value * first)


def micro_kernel(
    capacity, parts, rows, macro_count, conform_ref, noise_ref, rate_ref, y_low_ref, y_high_ref,
    next_ref, chunk_ref, conform, noise, result, rate, sums_ref, read_sem, noise_sem, write_sem,
):
    steps, _, slots, dumbbells = noise_ref.shape
    blocks = slots // rows
    width = dumbbells // parts
    owners = slots // capacity
    scale = 1.0 / noise_weight
    extent = fene_extent * scale * scale

    def block_rows(block):
        return pl.ds(pl.multiple_of(block * rows, rows), rows)

    def copies(block):
        at = block_rows(block)
        return (
            pltpu.make_async_copy(conform_ref.at[:, at, :], conform.at[:, at, :], read_sem.at[block]),
            pltpu.make_async_copy(noise_ref.at[:, :, at, :], noise.at[:, :, at, :], noise_sem.at[block]),
        )

    def write(block):
        at = block_rows(block)
        return pltpu.make_async_copy(result.at[:, at, :], next_ref.at[:, at, :], write_sem.at[block])

    for block in range(blocks):
        for copy in copies(block):
            copy.start()

    for owner in range(owners):
        rate[owner * capacity : (owner + 1) * capacity, :] = rate_ref[owner, 0:capacity, :]

    macro, core = place_of()
    size_x, size_z = y_low_ref.shape[1:]
    sides = (y_low_ref, y_high_ref)
    for side in range(2):
        beside = macro - 1 if side == 0 else macro + 1

        @pl.when(beside >= 0 if side == 0 else beside < macro_count)
        def _(side=side, beside=beside):
            x = 0 if side == 0 else size_x - 1
            for u in range(2):
                for a in range(2):
                    at = slot_rows + 2 * u + a
                    chunk_ref[2 * beside + core, at : at + 1, :] = sides[u][a, x : x + 1, :]

    lane = lanes_of((8, size_z))
    source = jnp.where(core == 0, size_z - 1, 0)
    total = jnp.zeros((8, size_z), jnp.float32)
    for i in range(size_x // 8):
        for u in range(2):
            for a in range(2):
                at = 4 * i + 2 * u + a
                total = jnp.where(
                    lane == at, rolled(sides[u][1 + a, 8 * i : 8 * i + 8, :], at - source), total
                )
    chunk_ref[2 * macro + 1 - core, slot_rows:, :] = total

    def inverse_of(q):
        return reciprocal(
            jnp.maximum(extent - (q[0] * q[0] + q[1] * q[1] + q[2] * q[2]), extent * spring_floor)
        )

    def advance_block(block, carry):
        at = block_rows(block)
        for copy in copies(block):
            copy.wait()
        table = rate[at, :]
        rates = [
            [
                jnp.broadcast_to(
                    micro_step * table[:, 3 * a + b : 3 * a + b + 1] + (1.0 if a == b else 0.0), (rows, width)
                )
                for b in range(3)
            ]
            for a in range(3)
        ]

        def substep(step, state):
            updated = []
            for part in range(parts):
                q = state[3 * part : 3 * part + 3]
                spring = (micro_step * relax_rate * extent) * inverse_of(q)
                for a in range(3):
                    kick = noise[step, a, at, part * width : (part + 1) * width].astype(jnp.float32)
                    terms = [(rates[a][b] - spring if a == b else rates[a][b]) * q[b] for b in range(3)]
                    updated.append(terms[0] + terms[1] + terms[2] + kick)
            return tuple(updated)

        state = tuple(
            conform[a, at, part * width : (part + 1) * width] * scale
            for part in range(parts)
            for a in range(3)
        )
        state = lax.fori_loop(0, steps, substep, state, unroll=4)
        sums = [None] * 6
        for part in range(parts):
            q = state[3 * part : 3 * part + 3]
            for a in range(3):
                result[a, at, part * width : (part + 1) * width] = q[a] * noise_weight
            inverse = inverse_of(q)
            for k, (a, b) in enumerate(stress_pairs):
                term = inverse * q[a] * q[b]
                sums[k] = term if sums[k] is None else sums[k] + term
        write(block).start()
        for k in range(6):
            sums_ref[k, at, :] = sums[k]
        return carry

    lax.fori_loop(0, blocks, advance_block, 0)
    lane = lanes_of((slots, 128))
    packed = jnp.zeros((slots, 128), jnp.float32)
    weight = extent * noise_weight * noise_weight / dumbbells
    for k, (a, b) in enumerate(stress_pairs):
        mean = jnp.sum(sums_ref[k], axis=1, keepdims=True) * weight
        packed = jnp.where(lane == k, polymer_weight * (mean - (1.0 if a == b else 0.0)), packed)
    for owner in range(owners):
        chunk_ref[owner, 0:capacity, :] = packed[owner * capacity : (owner + 1) * capacity]
    for block in range(blocks):
        write(block).wait()


def advance(conformations, increments, chunks, y_low, y_high, capacity):
    slots, dumbbells = conformations.shape[1:]
    steps = increments.shape[0]
    owners = slots // capacity
    rows, parts = 16, 4
    blocks = slots // rows
    whole = pl.BlockSpec(memory_space=pl.ANY)
    return pl.pallas_call(
        functools.partial(micro_kernel, capacity, parts, rows, owners // 2),
        out_shape=(
            jax.ShapeDtypeStruct(conformations.shape, jnp.float32),
            jax.ShapeDtypeStruct((owners, slot_rows + line_rows, 128), jnp.float32),
        ),
        in_specs=[
            pl.BlockSpec(memory_space=pltpu.HBM), pl.BlockSpec(memory_space=pltpu.HBM), VMEM, VMEM, VMEM
        ],
        out_specs=(pl.BlockSpec(memory_space=pltpu.HBM), VMEM),
        scratch_shapes=[
            pltpu.VMEM(conformations.shape, jnp.float32),
            pltpu.VMEM(increments.shape, jnp.bfloat16),
            pltpu.VMEM(conformations.shape, jnp.float32),
            pltpu.VMEM((slots, 128), jnp.float32),
            pltpu.VMEM((6, slots, dumbbells // parts), jnp.float32),
            pltpu.SemaphoreType.DMA((blocks,)),
            pltpu.SemaphoreType.DMA((blocks,)),
            pltpu.SemaphoreType.DMA((blocks,)),
        ],
        compiler_params=limit(12),
        cost_estimate=pl.CostEstimate(flops=20000000, bytes_accessed=5000000, transcendentals=600000),
        name="advance",
    )(conformations, increments, chunks, y_low, y_high)


def flow_kernel(
    size_x, size_y, size_z, macro_count, velocity_ref, viscosity_ref, chunk_ref, y_low_ref, y_high_ref,
    out_ref, corner_ref, edge_ref, padded, stress_x, stress_rest, faces, ghost_y, ghost_z,
):
    macro, core = place_of()
    inside = (macro > 0, macro < macro_count - 1)
    sign_z = jnp.where(core == 0, 1.0, -1.0)
    end = jnp.where(core == 0, size_z - 1, 0)
    shape = (size_y, size_z)
    lane, row = lanes_of(shape), lax.broadcasted_iota(jnp.int32, shape, 0)
    at_end = jnp.where(lane == end, sign_z, 0.0)

    def kept(value, condition):
        return jnp.where(condition, value, 0.0)

    def plane(x):
        return pl.ds(pl.multiple_of(x * size_y, 8), size_y)

    def difference_z(value):
        lane = lanes_of(value.shape)
        return jnp.where(lane == size_z - 1, 0.0, rolled(value, -1)) - jnp.where(
            lane == 0, 0.0, rolled(value, 1)
        )

    def difference_rows(value, low=0.0, high=0.0):
        count = value.shape[0]
        row = lax.broadcasted_iota(jnp.int32, value.shape, 0)
        return jnp.where(row == count - 1, high, pltpu.roll(value, count - 1, 0)) - jnp.where(
            row == 0, low, pltpu.roll(value, 1, 0)
        )

    x_faces, x_others = [], []
    for s in range(2):
        beside = jnp.maximum(macro - 1, 0) if s == 0 else jnp.minimum(macro + 1, macro_count - 1)
        x_faces.append(
            [
                kept(chunk_ref[2 * beside + core, slot_rows + i * size_y : slot_rows + (i + 1) * size_y, :], inside[s])
                for i in range(item_count)
            ]
        )
        x_others.append(
            [
                kept(
                    rolled(
                        chunk_ref[
                            2 * beside + 1 - core, slot_rows + i * size_y : slot_rows + (i + 1) * size_y, :
                        ],
                        2 * end + 1,
                    ),
                    inside[s],
                )
                for i in range(2)
            ]
        )

    group = size_z // 8
    packed = [
        chunk_ref[2 * macro + 1 - core, slot_rows + i * size_y : slot_rows + (i + 1) * size_y, :]
        for i in range(-(-size_x // group))
    ]
    for i, value in enumerate(packed):

        def unpack(x, carry):
            for q in range(item_count):
                faces[q, x + 1] = rolled(value, end - (8 * (x - i * group) + q))
            return carry

        lax.fori_loop(i * group, min(size_x, (i + 1) * group), unpack, 0, unroll=2)
    faces[2, 0] = x_others[0][1]
    faces[2, size_x + 1] = x_others[1][1]

    for a in range(3):
        padded[a, 0] = x_faces[0][a]
        padded[a, size_x + 1] = x_faces[1][a]

    def fill(x, carry):
        for a in range(3):
            padded[a, x + 1] = velocity_ref[a, plane(x), :]
        return carry

    lax.fori_loop(0, size_x, fill, 0, unroll=4)

    rest = {(1, 1): 0, (2, 2): 1, (1, 2): 2}

    def stress_plane(x, carry):
        along_x, along_y, along_z, centre = [], [], [], []
        for a in range(3):
            value = padded[a, x + 1]
            centre.append(value)
            along_x.append(padded[a, x + 2] - padded[a, x])
            along_y.append(
                difference_rows(value, y_low_ref[a, pl.ds(x, 1), :], y_high_ref[a, pl.ds(x, 1), :])
            )
            along_z.append(difference_z(value) + faces[a, x + 1] * at_end)
        slopes = (along_x, along_y, along_z)
        half = 0.5 * viscosity_ref[plane(x), :]
        for a, b in stress_pairs:
            value = half * (slopes[b][a] + slopes[a][b])
            if a == 0:
                stress_x[b, x + 1] = value
            else:
                stress_rest[rest[a, b], x] = value
        weight = (0.5 * faces[3, x + 1]) * at_end
        normal = [(faces[4 + a, x + 1] - centre[a]) * sign_z for a in range(3)]
        ghost_z[0, x] = weight * (normal[0] + (faces[2, x + 2] - faces[2, x]))
        ghost_z[1, x] = weight * (normal[1] + difference_rows(faces[2, x + 1]))
        ghost_z[2, x] = weight * (2.0 * normal[2])
        return carry

    lax.fori_loop(0, size_x, stress_plane, 0, unroll=2)

    for s in range(2):
        near, far, weight = x_faces[s][0:3], x_faces[s][3:6], 0.5 * x_faces[s][6]
        sign = -1.0 if s == 0 else 1.0
        normal = [(far[a] - padded[a, 1 if s == 0 else size_x]) * sign for a in range(3)]
        slope_y = difference_rows(near[0])
        slope_z = difference_z(near[0]) + x_others[s][0] * at_end
        at = 0 if s == 0 else size_x + 1
        stress_x[0, at] = weight * (2.0 * normal[0])
        stress_x[1, at] = weight * (normal[1] + slope_y)
        stress_x[2, at] = weight * (normal[2] + slope_z)
        for u in range(2):
            y, sign_y = (0, -1.0) if u == 0 else (size_y - 1, 1.0)
            number = 4 * s + 2 * u
            corner_ref[number : number + 1, :] = (0.5 * macro_step * sign * sign_y) * weight[y : y + 1, :]

    for u, ref in enumerate((y_low_ref, y_high_ref)):
        y, sign = (0, -1.0) if u == 0 else (size_y - 1, 1.0)
        weight = 0.5 * ref[6]
        normal = [
            (ref[3 + a] - velocity_ref[a, pl.ds(y, size_x, stride=size_y), :]) * sign for a in range(3)
        ]
        ghost_y[3 * u] = weight * (normal[0] + difference_rows(ref[1]))
        ghost_y[3 * u + 1] = weight * (2.0 * normal[1])
        ghost_y[3 * u + 2] = weight * (normal[2] + difference_z(ref[1]))
        for s in range(2):
            x, sign_x = (0, -1.0) if s == 0 else (size_x - 1, 1.0)
            number = 4 * s + 2 * u + 1
            corner_ref[number : number + 1, :] = (0.5 * macro_step * sign * sign_x) * weight[x : x + 1, :]
        wide = lanes_of((size_x, size_z))
        scale = jnp.where(wide == end, (0.5 * macro_step * sign) * sign_z, 0.0)
        edge_ref[2 * u] = scale * weight
        for x in range(size_x):
            edge_ref[2 * u + 1, x : x + 1, :] = scale[x : x + 1, :] * (0.5 * faces[3, x + 1, y : y + 1, :])

    columns = {(0, 1): (stress_x, 1, 1), (1, 1): (stress_rest, 0, 0), (2, 1): (stress_rest, 2, 0)}
    columns_z = {0: (stress_x, 2, 1), 1: (stress_rest, 2, 0), 2: (stress_rest, 1, 0)}

    def step_plane(x, carry):
        for a in range(3):
            total = stress_x[a, x + 2] - stress_x[a, x]
            ref, number, shift = columns[a, 1]
            total = total + difference_rows(
                ref[number, x + shift], ghost_y[a, pl.ds(x, 1), :], ghost_y[3 + a, pl.ds(x, 1), :]
            )
            ref, number, shift = columns_z[a]
            total = total + (difference_z(ref[number, x + shift]) + ghost_z[a, x])
            out_ref[a, plane(x), :] = padded[a, x + 1] + (0.5 * macro_step) * total
        return carry

    lax.fori_loop(0, size_x, step_plane, 0, unroll=2)


def flow_step(velocity, viscosity, chunks, y_low, y_high):
    size_x, size_y, size_z = viscosity.shape
    planes = (size_x, size_y, size_z)
    wide = (size_x + 2, size_y, size_z)
    return pl.pallas_call(
        functools.partial(flow_kernel, size_x, size_y, size_z, chunks.shape[0] // 2),
        out_shape=(
            jax.ShapeDtypeStruct((3, size_x * size_y, size_z), jnp.float32),
            jax.ShapeDtypeStruct((8, size_z), jnp.float32),
            jax.ShapeDtypeStruct((4, size_x, size_z), jnp.float32),
        ),
        in_specs=[VMEM] * 5,
        out_specs=(VMEM, VMEM, VMEM),
        scratch_shapes=[
            pltpu.VMEM((3, *wide), jnp.float32),
            pltpu.VMEM((3, *wide), jnp.float32),
            pltpu.VMEM((3, *planes), jnp.float32),
            pltpu.VMEM((item_count, *wide), jnp.float32),
            pltpu.VMEM((6, size_x, size_z), jnp.float32),
            pltpu.VMEM((3, *planes), jnp.float32),
        ],
        compiler_params=limit(12),
        cost_estimate=pl.CostEstimate(flops=4000000, bytes_accessed=3000000, transcendentals=0),
        name="flow_step",
    )(
        velocity.reshape(3, size_x * size_y, size_z),
        viscosity.reshape(size_x * size_y, size_z),
        chunks, y_low, y_high,
    )


def polymer_kernel(
    size_x, size_y, size_z, macro_count, cell_ref, position_ref, chunk_ref, viscous_ref, corner_ref,
    edge_ref, partial_ref, out_ref, flag_ref, polymer, lines, shifted,
):
    flags = cell_ref.shape[0]
    chunk_rows = slot_rows + line_rows
    macro, core = place_of()
    lane = lanes_of((1, size_z))
    weight = 0.5 * macro_step
    out_ref[...] = partial_ref[...]

    def read(j, carry):
        polymer[pl.ds(j, 1), :] = chunk_ref[pl.ds(position_ref[j], 1), :]
        cell = cell_ref[j]
        z = cell - lax.div(cell, size_z) * size_z
        lines[0, pl.ds(j, 1), :] = jnp.where(lane == z, weight, 0.0)
        lines[1, pl.ds(j, 1), :] = jnp.where(lane == z - 1, weight, jnp.where(lane == z + 1, -weight, 0.0))
        return carry

    lax.fori_loop(0, flags, read, 0, unroll=8)
    values = polymer[...]
    here, beside_z = lines[0], lines[1]
    for k in range(6):
        column = jnp.broadcast_to(values[:, k : k + 1], (flags, size_z))
        shifted[k] = column * here
        if stress_pairs[k][1] == 2:
            shifted[6 + stress_pairs[k][0]] = column * beside_z
    flag_ref[...] = (viscous_ref[...] + values).T[0:6, :]

    for s in range(2):
        inside = macro > 0 if s == 0 else macro < macro_count - 1
        beside = jnp.maximum(macro - 1, 0) if s == 0 else jnp.minimum(macro + 1, macro_count - 1)
        start = (2 * beside + core) * chunk_rows + slot_rows
        x = 0 if s == 0 else size_x - 1
        for u in range(2):
            at = x * size_y + (0 if u == 0 else size_y - 1)
            for a in range(2):
                number = 4 * s + 2 * u + a
                line = corner_ref[number : number + 1, :] * chunk_ref[pl.ds(start + 2 * u + a, 1), :]
                out_ref[1 - a, at : at + 1, :] += jnp.where(inside, line, 0.0)
    start = pl.multiple_of((2 * macro + 1 - core) * chunk_rows + slot_rows, 8)
    packed = chunk_ref[pl.ds(start, line_rows), :]
    end = jnp.where(core == 0, size_z - 1, 0)
    for u in range(2):
        y = 0 if u == 0 else size_y - 1
        for a in range(2):
            for i in range(size_x // 8):
                line = rolled(packed, end - (4 * i + 2 * u + a)) * edge_ref[2 * u + a, 8 * i : 8 * i + 8, :]
                at = pl.ds(8 * i * size_y + y, 8, stride=size_y)
                out_ref[2 - a, at, :] += line

    def add(j, carry):
        row = lax.div(cell_ref[j], size_z)
        targets = []
        for a in range(3):
            line_x = shifted[pair_index(a, 0), pl.ds(j, 1), :]
            line_y = shifted[pair_index(a, 1), pl.ds(j, 1), :]
            line_z = shifted[6 + a, pl.ds(j, 1), :]
            targets += [
                (a, row - size_y, line_x), (a, row + size_y, -line_x),
                (a, row - 1, line_y), (a, row + 1, -line_y), (a, row, line_z),
            ]
        updated = [out_ref[a, pl.ds(at, 1), :] + line for a, at, line in targets]
        for (a, at, _), line in zip(targets, updated):
            out_ref[a, pl.ds(at, 1), :] = line
        return carry

    lax.fori_loop(0, flags, add, 0, unroll=2)


def add_polymer(flag_cell, position, chunks, viscous, corners, edges, partial, shape):
    flags = flag_cell.shape[0]
    size_x, size_y, size_z = shape
    return pl.pallas_call(
        functools.partial(polymer_kernel, size_x, size_y, size_z, chunks.shape[0] // 2),
        out_shape=(
            jax.ShapeDtypeStruct(partial.shape, jnp.float32),
            jax.ShapeDtypeStruct((6, flags), jnp.float32),
        ),
        in_specs=[SMEM, SMEM, VMEM, VMEM, VMEM, VMEM, VMEM],
        out_specs=(VMEM, VMEM),
        scratch_shapes=[
            pltpu.VMEM((flags, 128), jnp.float32),
            pltpu.VMEM((2, flags, size_z), jnp.float32),
            pltpu.VMEM((9, flags, size_z), jnp.float32),
        ],
        compiler_params=limit(8),
        cost_estimate=pl.CostEstimate(flops=400000, bytes_accessed=3000000, transcendentals=0),
        name="add_polymer",
    )(flag_cell, position, chunks.reshape(-1, 128), viscous, corners, edges, partial)


def shards(velocity, viscosity, flag_cell, flag_owner, conformations, increments):
    macro_count = lax.axis_size("macro")
    tile_count = lax.axis_size("tile")
    assert lax.axis_size("micro") == 2
    owner_count = 2 * macro_count
    capacity = conformations.shape[1] // owner_count
    size_x, size_y, size_z = viscosity.shape
    assert capacity <= slot_rows and size_y == 8 and size_z == 128 and size_x % 8 == 0 and size_x <= 48
    chunks, position, viscous, y_first, y_last = gather_rows(
        flag_cell, flag_owner.reshape(-1), velocity, viscosity, capacity, owner_count
    )

    def exchange(rows):
        return lax.all_to_all(rows, ("macro", "micro"), split_axis=0, concat_axis=0, tiled=True)

    received = exchange(chunks.reshape(owner_count, -1, 128))
    up = [(i, i + 1) for i in range(tile_count - 1)]
    down = [(target, source) for source, target in up]
    y_low = lax.ppermute(y_last, "tile", up)
    y_high = lax.ppermute(y_first, "tile", down)
    last_state, polymer = advance(conformations, increments, received, y_low, y_high, capacity)
    returned = exchange(polymer)
    partial, corners, edges = flow_step(velocity, viscosity, received, y_low, y_high)
    velocity_next, flag_stress = add_polymer(
        flag_cell, position, returned, viscous, corners, edges, partial, viscosity.shape
    )
    return (velocity_next.reshape(velocity.shape), last_state, flag_stress)


def solution(mesh):
    in_specs = (
        P(None, "macro", "tile", "micro"),
        P("macro", "tile", "micro"),
        P(("macro", "tile", "micro")),
        P(("macro", "tile", "micro"), None),
        P(None, ("macro", "tile", "micro"), None),
        P(None, None, ("macro", "tile", "micro"), None),
    )
    out_specs = (
        P(None, "macro", "tile", "micro"),
        P(None, ("macro", "tile", "micro"), None),
        P(None, ("macro", "tile", "micro")),
    )
    return jax.shard_map(shards, mesh=mesh, in_specs=in_specs, out_specs=out_specs, check_vma=False)
```

time: 215 us -> 41.1 us (0.19); the launches traced: 212 us -> 40.6 us
  local copies, waits for them, and re-layouts: 85.4 us -> 6.06 us
  other arithmetic: 62.6 us -> 0 us
  starting transfers between devices: 39.8 us -> 14 us
  waiting for transfers between devices: 20.4 us -> 6.86 us
  Pallas kernels: 0 us -> 13 us
    add x36 -> x0, other arithmetic: 41.1 us -> none  [the longest x32 32 us: substep(): current[left_axis] + micro_step * drift_term]
    gather x13 -> x0, local copies, waits for them, and re-layouts: 32.1 us -> none  [the longest x6 15.7 us: shards(): upper_side = jnp.take(flat_velocity, flag_cell + stride, axis=1)]
    ppermute x12 -> x2, starting transfers between devices: 31.6 us -> 4.77 us  [the longest x1 3.47 us: shards(): y_low = lax.ppermute(y_last, 'tile', up)]
    unnamed x61 -> x18, local copies, waits for them, and re-layouts: 32 us -> 6.06 us
    pallas_call x0 -> x4, Pallas kernels: none -> 13 us  [the longest x1 5.15 us: advance(): pl.pallas_call(functools.partial(micro_kernel, capacity, parts, rows, own...]
    add x4 -> x0, local copies, waits for them, and re-layouts: 11.7 us -> none  [the longest x1 6.76 us: shards(): velocity_next = velocity + macro_step * divergence(stress_pad)]
    scatter-add x1 -> x0, other arithmetic: 10.9 us -> none  [add_polymer(): flattened = flattened.at[:, targets].add(updates)]
    ppermute x12 -> x2, waiting for transfers between devices: 13.3 us -> 5.26 us  [the longest x1 4.12 us: shards(): y_high = lax.ppermute(y_first, 'tile', down)]
  transfers between devices with their start and end apart: 14 -> 4, of which waited for: 6 -> 3; matrix products, arithmetic and copies ran while one was open for 46% -> 0% of each run, Pallas kernels for 0% -> 8%
where the time goes in v2:
time: 41.1 us; the launch traced here: 40.6 us
  starting transfers between devices  14 us (34%)
  Pallas kernels  13 us (32%)
  waiting for transfers between devices  6.86 us (17%)
  local copies, waits for them, and re-layouts  6.06 us (15%)
  between operations  0.71 us (2%)
    all_to_all x2, starting transfers between devices, exchange(): lax.all_to_all(rows, ('macro', 'micro'), split_axis=0, concat_axis=0, til...  9.22 us
    unnamed x18, local copies, waits for them, and re-layouts  6.06 us
    pallas_call x1, Pallas kernels, advance(): pl.pallas_call(functools.partial(micro_kernel, capacity, parts, rows, own...  5.15 us
    ppermute x1, waiting for transfers between devices, shards(): y_high = lax.ppermute(y_first, 'tile', down)  4.12 us
    ppermute x1, starting transfers between devices, shards(): y_low = lax.ppermute(y_last, 'tile', up)  3.47 us
    pallas_call x1, Pallas kernels, flow_step(): pl.pallas_call(functools.partial(flow_kernel, size_x, size_y, size_z, chu...  3.4 us
    pallas_call x1, Pallas kernels, gather_rows(): pl.pallas_call(functools.partial(gather_kernel, capacity, size_x, size_y,...  2.61 us
    pallas_call x1, Pallas kernels, add_polymer(): pl.pallas_call(functools.partial(polymer_kernel, size_x, size_y, size_z,...  1.86 us
  transfers between devices with their start and end apart: 4, of which 3 were waited for; matrix products, arithmetic and copies ran while one was open for 0% of the time, Pallas kernels for 8%

profile of v2, /device:TPU:0, one launch (start us, length us, event | category | flops | bytes accessed | tf_op | source)
XLA Modules:
  0.0 40.6 jit_solution(16029914465875237999)
XLA Ops:
  0.6 0.0 copy-start.7
  0.6 0.0 copy-start.1
  0.7 1.0 %copy-done.1 = f32[3,24,8,128]{3,2,1,0:T(8,128)S(1)} copy-done((f32[3,24,8,128]{3,2,1,0:T(8,128)S(1)}, f32[3,24,8,128]{3,2,1,0:T(8,128)}, u32[]{:S(2)}) %copy-start.1) | copy-done | bytes 294936
  1.6 0.0 copy-start.3
  1.6 0.9 %copy-done.3 = f32[24,8,128]{2,1,0:T(8,128)S(1)} copy-done((f32[24,8,128]{2,1,0:T(8,128)S(1)}, f32[24,8,128]{2,1,0:T(8,128)}, u32[]{:S(2)}) %copy-start.3) | copy-done | bytes 98328
  2.5 0.7 %copy-done.6 = s32[32]{0:T(128)S(1)} copy-done((s32[32]{0:T(128)S(1)}, s32[32]{0:T(128)}, u32[]{:S(2)}) %copy-start.6) | copy-done | bytes 152
  3.2 0.7 %copy-done.8 = s32[32,1]{0,1:T(1,128)S(1)} copy-done((s32[32,1]{0,1:T(1,128)S(1)}, s32[32,1]{0,1:T(1,128)}, u32[]{:S(2)}) %copy-start.8) | copy-done | bytes 152
  3.8 2.6 %gather_rows.1 = (f32[512,128]{1,0:T(8,128)}, s32[32]{0:T(128)S(1)}, f32[32,128]{1,0:T(8,128)S(1)}, f32[7,24,128]{2,1,0:T(8,128)S(1)}, f32[7,24,128]{2,1,0:T(8,128)S(1)}) custom-call(s32[32]{0:T(128)S(1)} %copy-done.6, s32[32]{0:T(128)S(1)} %bitcast.11, f32[3,192,128]{2,1,0:T(8,128)S(1)} %bitcast.6, f32[192,128]{1,0:T(8,128)S(1)} %bitcast.8), custom_call_target="tpu_custom_call" | custom-call | flops 400000 | bytes 3000000 | tf_op jit(solution)/shard_map/gather_rows/pallas_call | solution.py:164
  6.4 5.2 %all-to-all-start = ((f32[8,64,128]{2,1,0:T(8,128)}), f32[8,64,128]{2,1,0:T(8,128)S(1)}, u32[]{:S(2)}, u32[]{:S(2)}) async-start(f32[8,64,128]{2,1,0:T(8,128)} %bitcast.3), calls=%async_computation | async-start | bytes 524288 | tf_op jit(solution)/shard_map/all_to_all | solution.py:651
  11.6 3.5 %collective-permute-start = (f32[7,24,128]{2,1,0:T(8,128)S(1)}, f32[7,24,128]{2,1,0:T(8,128)S(1)}, u32[]{:S(2)}, u32[]{:S(2)}) collective-permute-start(f32[7,24,128]{2,1,0:T(8,128)S(1)} %get-tuple-element.17), channel_id=1, source_target_pairs={{0,2},{2,4},{4,6},{1,3},{3,5},{5,7},{8,10},{10,12},{12,14},{9,11},... | collective-permute-start | bytes 258056 | tf_op jit(solution)/shard_map/ppermute | solution.py:656
  15.1 1.3 %collective-permute-start.1 = (f32[7,24,128]{2,1,0:T(8,128)S(1)}, f32[7,24,128]{2,1,0:T(8,128)S(1)}, u32[]{:S(2)}, u32[]{:S(2)}) collective-permute-start(f32[7,24,128]{2,1,0:T(8,128)S(1)} %get-tuple-element.18), channel_id=1, source_target_pairs={{2,0},{4,2},{6,4},{3,1},{5,3},{7,5},{10,8},{12,10},{14,12},{11,9},... | collective-permute-start | bytes 258056 | tf_op jit(solution)/shard_map/ppermute | solution.py:657
  16.4 1.1 %collective-permute-done.y_low_ref = f32[7,24,128]{2,1,0:T(8,128)S(1)} collective-permute-done((f32[7,24,128]{2,1,0:T(8,128)S(1)}, f32[7,24,128]{2,1,0:T(8,128)S(1)}, u32[]{:S(2)}, u32[]{:S(2)}) %collective-permute-start) | collective-permute-done | bytes 86048 | tf_op jit(solution)/shard_map/ppermute | solution.py:656
  17.5 4.1 %collective-permute-done.1.y_high_ref = f32[7,24,128]{2,1,0:T(8,128)S(1)} collective-permute-done((f32[7,24,128]{2,1,0:T(8,128)S(1)}, f32[7,24,128]{2,1,0:T(8,128)S(1)}, u32[]{:S(2)}, u32[]{:S(2)}) %collective-permute-start.1) | collective-permute-done | bytes 86048 | tf_op jit(solution)/shard_map/ppermute | solution.py:657
  21.7 0.0 all-to-all-done.rate_ref.chunk_ref
  21.7 1.9 %copy-done = bf16[16,3,64,512]{3,2,1,0:T(8,128)(2,1)S(1)} copy-done((bf16[16,3,64,512]{3,2,1,0:T(8,128)(2,1)S(1)}, bf16[16,3,64,512]{3,2,1,0:T(8,128)(2,1)}, u32[]{:S(2)}) %copy-start) | copy-done | bytes 3145752
  23.6 1.0 %copy-done.5 = f32[3,64,512]{2,1,0:T(8,128)S(1)} copy-done((f32[3,64,512]{2,1,0:T(8,128)S(1)}, f32[3,64,512]{2,1,0:T(8,128)}, u32[]{:S(2)}) %copy-start.5) | copy-done | bytes 393240
  24.5 5.1 %advance.1 = (f32[3,64,512]{2,1,0:T(8,128)}, f32[8,16,128]{2,1,0:T(8,128)}) custom-call(f32[3,64,512]{2,1,0:T(8,128)S(1)} %copy-done.5, bf16[16,3,64,512]{3,2,1,0:T(8,128)(2,1)S(1)} %copy-done, f32[8,64,128]{2,1,0:T(8,128)S(1)} %all-to-all-done.rate_ref.chunk_ref, f32[7,24,128]{2,1,0:T(8,128)S(1)} %collective-permute-done.y_low_ref, ...), custom_call_target="tpu_custom_call" | custom-call | flops 20000000 | bytes 5000000 | tf_op jit(solution)/shard_map/advance/pallas_call | solution.py:326
  29.7 4.0 %all-to-all-start.1 = ((f32[8,16,128]{2,1,0:T(8,128)}), f32[8,16,128]{2,1,0:T(8,128)S(1)}, u32[]{:S(2)}, u32[]{:S(2)}) async-start(f32[8,16,128]{2,1,0:T(8,128)} %get-tuple-element.19), calls=%async_computation.1 | async-start | bytes 131072 | tf_op jit(solution)/shard_map/all_to_all | solution.py:651
  33.7 0.0 copy-done.2
  33.7 0.0 copy-done.4
  33.8 3.4 %flow_step.1 = (f32[3,192,128]{2,1,0:T(8,128)S(1)}, f32[8,128]{1,0:T(8,128)S(1)}, f32[4,24,128]{2,1,0:T(8,128)S(1)}) custom-call(f32[3,192,128]{2,1,0:T(8,128)S(1)} %bitcast.7, f32[192,128]{1,0:T(8,128)S(1)} %bitcast.9, f32[8,64,128]{2,1,0:T(8,128)S(1)} %all-to-all-done.rate_ref.chunk_ref, f32[7,24,128]{2,1,0:T(8,128)S(1)} %collective-permute-done.y_low_ref, ...), custom_call_target="tpu_custom_call" | custom-call | flops 4000000 | bytes 3000000 | tf_op jit(solution)/shard_map/flow_step/pallas_call | solution.py:519
  37.2 1.6 %all-to-all-done.1 = f32[8,16,128]{2,1,0:T(8,128)S(1)} async-done(((f32[8,16,128]{2,1,0:T(8,128)}), f32[8,16,128]{2,1,0:T(8,128)S(1)}, u32[]{:S(2)}, u32[]{:S(2)}) %all-to-all-start.1) | async-done | bytes 65568 | tf_op jit(solution)/shard_map/all_to_all | solution.py:651
  38.8 0.0 copy-done.7
  38.8 1.9 %add_polymer.1 = (f32[3,192,128]{2,1,0:T(8,128)}, f32[6,32]{1,0:T(8,128)}) custom-call(s32[32]{0:T(128)S(1)} %copy-done.7, s32[32]{0:T(128)S(1)} %get-tuple-element.15.position_ref, f32[128,128]{1,0:T(8,128)S(1)} %bitcast.10, f32[32,128]{1,0:T(8,128)S(1)} %get-tuple-element.20.viscous_ref, f32[8,128]{1,0:T(8,128)S(1)} %get-tuple-element.21.corner_ref, ...), custom_call_target="tpu_custom_call" | custom-call | flops 400000 | bytes 3000000 | tf_op jit(solution)/shard_map/add_polymer/pallas_call | solution.py:619
  (6 shorter events, 0.0 us)
Async XLA Ops:
  0.6 38.1 %copy-start.7 = (s32[32]{0:T(128)S(1)}, s32[32]{0:T(128)}, u32[]{:S(2)}) copy-start(s32[32]{0:T(128)} %cell_ref.3) | copy-start | bytes 388
  0.6 1.0 %copy-start.1 = (f32[3,24,8,128]{3,2,1,0:T(8,128)S(1)}, f32[3,24,8,128]{3,2,1,0:T(8,128)}, u32[]{:S(2)}) copy-start(f32[3,24,8,128]{3,2,1,0:T(8,128)} %param.6) | copy-start | bytes 884740
  1.6 0.9 %copy-start.3 = (f32[24,8,128]{2,1,0:T(8,128)S(1)}, f32[24,8,128]{2,1,0:T(8,128)}, u32[]{:S(2)}) copy-start(f32[24,8,128]{2,1,0:T(8,128)} %param.7) | copy-start | bytes 294916
  2.5 0.7 %copy-start.6 = (s32[32]{0:T(128)S(1)}, s32[32]{0:T(128)}, u32[]{:S(2)}) copy-start(s32[32]{0:T(128)} %cell_ref.3) | copy-start | bytes 388
  3.2 0.7 %copy-start.8 = (s32[32,1]{0,1:T(1,128)S(1)}, s32[32,1]{0,1:T(1,128)}, u32[]{:S(2)}) copy-start(s32[32,1]{0,1:T(1,128)} %param.9) | copy-start | bytes 388
  3.8 29.9 %copy-start.2 = (f32[3,24,8,128]{3,2,1,0:T(8,128)S(1)}, f32[3,24,8,128]{3,2,1,0:T(8,128)}, u32[]{:S(2)}) copy-start(f32[3,24,8,128]{3,2,1,0:T(8,128)} %param.6) | copy-start | bytes 884740
  3.8 29.9 %copy-start.4 = (f32[24,8,128]{2,1,0:T(8,128)S(1)}, f32[24,8,128]{2,1,0:T(8,128)}, u32[]{:S(2)}) copy-start(f32[24,8,128]{2,1,0:T(8,128)} %param.7) | copy-start | bytes 294916
  6.4 15.2 %all-to-all-start = ((f32[8,64,128]{2,1,0:T(8,128)}), f32[8,64,128]{2,1,0:T(8,128)S(1)}, u32[]{:S(2)}, u32[]{:S(2)}) async-start(f32[8,64,128]{2,1,0:T(8,128)} %bitcast.3), calls=%async_computation | async-start | bytes 524288 | tf_op jit(solution)/shard_map/all_to_all | solution.py:651
  11.6 5.9 %collective-permute-start = (f32[7,24,128]{2,1,0:T(8,128)S(1)}, f32[7,24,128]{2,1,0:T(8,128)S(1)}, u32[]{:S(2)}, u32[]{:S(2)}) collective-permute-start(f32[7,24,128]{2,1,0:T(8,128)S(1)} %get-tuple-element.17), channel_id=1, source_target_pairs={{0,2},{2,4},{4,6},{1,3},{3,5},{5,7},{8,10},{10,12},{12,14},{9,11},... | collective-permute-start | bytes 258056 | tf_op jit(solution)/shard_map/ppermute | solution.py:656
  15.1 6.6 %collective-permute-start.1 = (f32[7,24,128]{2,1,0:T(8,128)S(1)}, f32[7,24,128]{2,1,0:T(8,128)S(1)}, u32[]{:S(2)}, u32[]{:S(2)}) collective-permute-start(f32[7,24,128]{2,1,0:T(8,128)S(1)} %get-tuple-element.18), channel_id=1, source_target_pairs={{2,0},{4,2},{6,4},{3,1},{5,3},{7,5},{10,8},{12,10},{14,12},{11,9},... | collective-permute-start | bytes 258056 | tf_op jit(solution)/shard_map/ppermute | solution.py:657
  21.7 1.9 %copy-start = (bf16[16,3,64,512]{3,2,1,0:T(8,128)(2,1)S(1)}, bf16[16,3,64,512]{3,2,1,0:T(8,128)(2,1)}, u32[]{:S(2)}) copy-start(bf16[16,3,64,512]{3,2,1,0:T(8,128)(2,1)} %noise_ref.1) | copy-start | bytes 9437188
  23.6 1.0 %copy-start.5 = (f32[3,64,512]{2,1,0:T(8,128)S(1)}, f32[3,64,512]{2,1,0:T(8,128)}, u32[]{:S(2)}) copy-start(f32[3,64,512]{2,1,0:T(8,128)} %conform_ref.1) | copy-start | bytes 1179652
  29.7 9.1 %all-to-all-start.1 = ((f32[8,16,128]{2,1,0:T(8,128)}), f32[8,16,128]{2,1,0:T(8,128)S(1)}, u32[]{:S(2)}, u32[]{:S(2)}) async-start(f32[8,16,128]{2,1,0:T(8,128)} %get-tuple-element.19), calls=%async_computation.1 | async-start | bytes 131072 | tf_op jit(solution)/shard_map/all_to_all | solution.py:651

commit v3 on v2

--- a/solution.py
+++ b/solution.py
@@ -37,6 +37,10 @@
     return pltpu.CompilerParams(vmem_limit_bytes=mebibytes * 1024 * 1024)
 
 
+def far(value):
+    return pltpu.with_memory_space_constraint(value, pltpu.HBM)
+
+
 def place_of():
     return lax.axis_index("macro"), lax.axis_index("micro")
 
@@ -57,16 +61,10 @@
     macro, core = place_of()
     lane = lanes_of((1, size_z))
 
-    def clear(owner, carry):
+    for owner in range(count.shape[0]):
         count[owner] = 0
-        chunk_ref[pl.ds(pl.multiple_of(owner * chunk_rows, 8), slot_rows), :] = jnp.zeros(
-            (slot_rows, 128), jnp.float32
-        )
-        return carry
-
-    lax.fori_loop(0, count.shape[0], clear, 0, unroll=True)
-
-    def read(j, carry):
+        chunk_ref[owner * chunk_rows : owner * chunk_rows + slot_rows, :] = jnp.zeros((slot_rows, 128), jnp.float32)
+    for j in range(flags):
         cell = cell_ref[j]
         row = lax.div(cell, size_z)
         z = cell - row * size_z
@@ -75,18 +73,15 @@
         for a in range(3):
             along_x = velocity_ref[a, pl.ds(row + size_y, 1), :] - velocity_ref[a, pl.ds(row - size_y, 1), :]
             along_y = velocity_ref[a, pl.ds(row + 1, 1), :] - velocity_ref[a, pl.ds(row - 1, 1), :]
-            masked[3 * a, pl.ds(j, 1), :] = along_x * here
-            masked[3 * a + 1, pl.ds(j, 1), :] = along_y * here
-            masked[3 * a + 2, pl.ds(j, 1), :] = velocity_ref[a, pl.ds(row, 1), :] * along_z
-        masked[9, pl.ds(j, 1), :] = viscosity_ref[pl.ds(row, 1), :] * here
+            masked[3 * a, j : j + 1, :] = along_x * here
+            masked[3 * a + 1, j : j + 1, :] = along_y * here
+            masked[3 * a + 2, j : j + 1, :] = velocity_ref[a, pl.ds(row, 1), :] * along_z
+        masked[9, j : j + 1, :] = viscosity_ref[pl.ds(row, 1), :] * here
         owner = owner_ref[j]
         rank = count[owner]
         count[owner] = rank + 1
         target[j] = owner * chunk_rows + rank
         position_ref[j] = owner * (slot_rows + line_rows) + rank
-        return carry
-
-    lax.fori_loop(0, flags, read, 0, unroll=4)
 
     for side, ref in enumerate((y_low_ref, y_high_ref)):
         for layer in range(2):
@@ -119,22 +114,15 @@
     group = size_z // 8
     lane2 = lanes_of((size_y, size_z))
     first = pl.multiple_of((2 * macro + 1 - core) * chunk_rows + slot_rows, 8)
-    sources = [jnp.where(core == 0, size_z - 1 - layer, layer) for layer in range(2)]
+    source = jnp.where(core == 0, size_z - 2, 0)
     for block in range(-(-size_x // group)):
-
-        def add_plane(x, total):
-            rows = pl.ds(pl.multiple_of(x * size_y, 8), size_y)
-            start = 8 * (x - block * group)
-            for q in range(item_count):
-                layer, a = (0, q) if q < 4 else (1, q - 4)
-                value = viscosity_ref[rows, :] if q == 3 else velocity_ref[a, rows, :]
-                total = jnp.where(lane2 == start + q, rolled(value, start + q - sources[layer]), total)
-            return total
-
-        total = lax.fori_loop(
-            block * group, min(size_x, (block + 1) * group), add_plane,
-            jnp.zeros((size_y, size_z), jnp.float32), unroll=4,
-        )
+        total = jnp.zeros((size_y, size_z), jnp.float32)
+        for x in range(block * group, min(size_x, (block + 1) * group)):
+            rows = slice(x * size_y, (x + 1) * size_y)
+            for a in range(4):
+                at = 8 * (x - block * group) + 2 * a
+                value = viscosity_ref[rows, :] if a == 3 else velocity_ref[a, rows, :]
+                total = jnp.where((lane2 == at) | (lane2 == at + 1), rolled(value, at - source), total)
         chunk_ref[pl.ds(first + block * size_y, size_y), :] = total
 
     columns = [0.5 * jnp.sum(masked[c], axis=1, keepdims=True) for c in range(9)]
@@ -149,11 +137,8 @@
         stress = jnp.where(wide == k, viscous * (columns[3 * a + b] + columns[3 * b + a]), stress)
     viscous_ref[...] = stress
 
-    def place(j, carry):
-        chunk_ref[pl.ds(target[j], 1), :] = gradients[pl.ds(j, 1), :]
-        return carry
-
-    lax.fori_loop(0, flags, place, 0, unroll=8)
+    for j in range(flags):
+        chunk_ref[pl.ds(target[j], 1), :] = gradients[j : j + 1, :]
 
 
 def gather_rows(flag_cell, owner, velocity, viscosity, capacity, owner_count):
@@ -182,24 +167,20 @@
         cost_estimate=pl.CostEstimate(flops=400000, bytes_accessed=3000000, transcendentals=0),
         name="gather_rows",
     )(
-        flag_cell,
-        owner,
-        velocity.reshape(3, size_x * size_y, size_z),
-        viscosity.reshape(size_x * size_y, size_z),
+        far(flag_cell),
+        far(owner),
+        far(velocity.reshape(3, size_x * size_y, size_z)),
+        far(viscosity.reshape(size_x * size_y, size_z)),
     )
 
 
-def reciprocal(value):
-    first = pl.reciprocal(value, approx=True)
-    return first * (2.0 - value * first)
-
-
 def micro_kernel(
-    capacity, parts, rows, macro_count, conform_ref, noise_ref, rate_ref, y_low_ref, y_high_ref,
+    capacity, parts, rows, groups, conform_ref, noise_ref, rate_ref,
     next_ref, chunk_ref, conform, noise, result, rate, sums_ref, read_sem, noise_sem, write_sem,
 ):
     steps, _, slots, dumbbells = noise_ref.shape
     blocks = slots // rows
+    span = steps // groups
     width = dumbbells // parts
     owners = slots // capacity
     scale = 1.0 / noise_weight
@@ -208,11 +189,14 @@
     def block_rows(block):
         return pl.ds(pl.multiple_of(block * rows, rows), rows)
 
-    def copies(block):
+    def read(block):
         at = block_rows(block)
-        return (
-            pltpu.make_async_copy(conform_ref.at[:, at, :], conform.at[:, at, :], read_sem.at[block]),
-            pltpu.make_async_copy(noise_ref.at[:, :, at, :], noise.at[:, :, at, :], noise_sem.at[block]),
+        return pltpu.make_async_copy(conform_ref.at[:, at, :], conform.at[:, at, :], read_sem.at[block])
+
+    def read_noise(block, group):
+        at, when = block_rows(block), pl.ds(group * span, span)
+        return pltpu.make_async_copy(
+            noise_ref.at[when, :, at, :], noise.at[when, :, at, :], noise_sem.at[block, group]
         )
 
     def write(block):
@@ -220,47 +204,19 @@
         return pltpu.make_async_copy(result.at[:, at, :], next_ref.at[:, at, :], write_sem.at[block])
 
     for block in range(blocks):
-        for copy in copies(block):
-            copy.start()
-
+        read(block).start()
+        for group in range(groups):
+            read_noise(block, group).start()
     for owner in range(owners):
         rate[owner * capacity : (owner + 1) * capacity, :] = rate_ref[owner, 0:capacity, :]
-
-    macro, core = place_of()
-    size_x, size_z = y_low_ref.shape[1:]
-    sides = (y_low_ref, y_high_ref)
-    for side in range(2):
-        beside = macro - 1 if side == 0 else macro + 1
-
-        @pl.when(beside >= 0 if side == 0 else beside < macro_count)
-        def _(side=side, beside=beside):
-            x = 0 if side == 0 else size_x - 1
-            for u in range(2):
-                for a in range(2):
-                    at = slot_rows + 2 * u + a
-                    chunk_ref[2 * beside + core, at : at + 1, :] = sides[u][a, x : x + 1, :]
-
-    lane = lanes_of((8, size_z))
-    source = jnp.where(core == 0, size_z - 1, 0)
-    total = jnp.zeros((8, size_z), jnp.float32)
-    for i in range(size_x // 8):
-        for u in range(2):
-            for a in range(2):
-                at = 4 * i + 2 * u + a
-                total = jnp.where(
-                    lane == at, rolled(sides[u][1 + a, 8 * i : 8 * i + 8, :], at - source), total
-                )
-    chunk_ref[2 * macro + 1 - core, slot_rows:, :] = total
+        chunk_ref[owner, slot_rows:, :] = jnp.zeros((line_rows, 128), jnp.float32)
 
     def inverse_of(q):
-        return reciprocal(
-            jnp.maximum(extent - (q[0] * q[0] + q[1] * q[1] + q[2] * q[2]), extent * spring_floor)
-        )
+        room = (extent - q[0] * q[0]) - (q[1] * q[1] + q[2] * q[2])
+        return pl.reciprocal(jnp.maximum(room, extent * spring_floor), approx=True)
 
     def advance_block(block, carry):
         at = block_rows(block)
-        for copy in copies(block):
-            copy.wait()
         table = rate[at, :]
         rates = [
             [
@@ -278,17 +234,25 @@
                 q = state[3 * part : 3 * part + 3]
                 spring = (micro_step * relax_rate * extent) * inverse_of(q)
                 for a in range(3):
+                    b, c = [other for other in range(3) if other != a]
                     kick = noise[step, a, at, part * width : (part + 1) * width].astype(jnp.float32)
-                    terms = [(rates[a][b] - spring if a == b else rates[a][b]) * q[b] for b in range(3)]
-                    updated.append(terms[0] + terms[1] + terms[2] + kick)
+                    rest = (rates[a][b] * q[b] + rates[a][c] * q[c]) + kick
+                    updated.append((rates[a][a] - spring) * q[a] + rest)
             return tuple(updated)
 
+        def advance_group(group, state):
+            read_noise(block, group).wait()
+            for step in range(span):
+                state = substep(group * span + step, state)
+            return state
+
+        read(block).wait()
         state = tuple(
             conform[a, at, part * width : (part + 1) * width] * scale
             for part in range(parts)
             for a in range(3)
         )
-        state = lax.fori_loop(0, steps, substep, state, unroll=4)
+        state = lax.fori_loop(0, groups, advance_group, state)
         sums = [None] * 6
         for part in range(parts):
             q = state[3 * part : 3 * part + 3]
@@ -296,7 +260,7 @@
                 result[a, at, part * width : (part + 1) * width] = q[a] * noise_weight
             inverse = inverse_of(q)
             for k, (a, b) in enumerate(stress_pairs):
-                term = inverse * q[a] * q[b]
+                term = (inverse * q[a]) * q[b]
                 sums[k] = term if sums[k] is None else sums[k] + term
         write(block).start()
         for k in range(6):
@@ -316,23 +280,21 @@
         write(block).wait()
 
 
-def advance(conformations, increments, chunks, y_low, y_high, capacity):
+def advance(conformations, increments, chunks, capacity):
     slots, dumbbells = conformations.shape[1:]
     steps = increments.shape[0]
     owners = slots // capacity
-    rows, parts = 16, 4
+    rows, parts, groups = 16, 4, 4
     blocks = slots // rows
-    whole = pl.BlockSpec(memory_space=pl.ANY)
+    whole = pl.BlockSpec(memory_space=pltpu.HBM)
     return pl.pallas_call(
-        functools.partial(micro_kernel, capacity, parts, rows, owners // 2),
+        functools.partial(micro_kernel, capacity, parts, rows, groups),
         out_shape=(
             jax.ShapeDtypeStruct(conformations.shape, jnp.float32),
             jax.ShapeDtypeStruct((owners, slot_rows + line_rows, 128), jnp.float32),
         ),
-        in_specs=[
-            pl.BlockSpec(memory_space=pltpu.HBM), pl.BlockSpec(memory_space=pltpu.HBM), VMEM, VMEM, VMEM
-        ],
-        out_specs=(pl.BlockSpec(memory_space=pltpu.HBM), VMEM),
+        in_specs=[whole, whole, VMEM],
+        out_specs=(whole, VMEM),
         scratch_shapes=[
             pltpu.VMEM(conformations.shape, jnp.float32),
             pltpu.VMEM(increments.shape, jnp.bfloat16),
@@ -340,13 +302,54 @@
             pltpu.VMEM((slots, 128), jnp.float32),
             pltpu.VMEM((6, slots, dumbbells // parts), jnp.float32),
             pltpu.SemaphoreType.DMA((blocks,)),
-            pltpu.SemaphoreType.DMA((blocks,)),
+            pltpu.SemaphoreType.DMA((blocks, groups)),
             pltpu.SemaphoreType.DMA((blocks,)),
         ],
         compiler_params=limit(12),
         cost_estimate=pl.CostEstimate(flops=20000000, bytes_accessed=5000000, transcendentals=600000),
         name="advance",
-    )(conformations, increments, chunks, y_low, y_high)
+    )(far(conformations), far(increments), chunks)
+
+
+def lines_kernel(macro_count, chunk_ref, y_low_ref, y_high_ref, out_ref):
+    out_ref[...] = chunk_ref[...]
+    macro, core = place_of()
+    size_x, size_z = y_low_ref.shape[1:]
+    sides = (y_low_ref, y_high_ref)
+    for side in range(2):
+        beside = macro - 1 if side == 0 else macro + 1
+
+        @pl.when(beside >= 0 if side == 0 else beside < macro_count)
+        def _(side=side, beside=beside):
+            x = 0 if side == 0 else size_x - 1
+            for u in range(2):
+                for a in range(2):
+                    at = slot_rows + 2 * u + a
+                    out_ref[2 * beside + core, at : at + 1, :] = sides[u][a, x : x + 1, :]
+
+    lane = lanes_of((8, size_z))
+    source = jnp.where(core == 0, size_z - 1, 0)
+    total = jnp.zeros((8, size_z), jnp.float32)
+    for i in range(size_x // 8):
+        for u in range(2):
+            for a in range(2):
+                at = 4 * i + 2 * u + a
+                total = jnp.where(
+                    lane == at, rolled(sides[u][1 + a, 8 * i : 8 * i + 8, :], at - source), total
+                )
+    out_ref[2 * macro + 1 - core, slot_rows:, :] = total
+
+
+def add_lines(chunks, y_low, y_high):
+    return pl.pallas_call(
+        functools.partial(lines_kernel, chunks.shape[0] // 2),
+        out_shape=jax.ShapeDtypeStruct(chunks.shape, jnp.float32),
+        in_specs=[VMEM, VMEM, VMEM],
+        out_specs=VMEM,
+        compiler_params=limit(4),
+        cost_estimate=pl.CostEstimate(flops=20000, bytes_accessed=400000, transcendentals=0),
+        name="add_lines",
+    )(chunks, y_low, y_high)
 
 
 def flow_kernel(
@@ -413,7 +416,9 @@
 
         def unpack(x, carry):
             for q in range(item_count):
-                faces[q, x + 1] = rolled(value, end - (8 * (x - i * group) + q))
+                a, layer = (q, 0) if q < 4 else (q - 4, 1)
+                at = 8 * (x - i * group) + 2 * a + (core if layer == 0 else 1 - core)
+                faces[q, x + 1] = rolled(value, end - at)
             return carry
 
         lax.fori_loop(i * group, min(size_x, (i + 1) * group), unpack, 0, unroll=2)
@@ -545,24 +550,22 @@
 
 def polymer_kernel(
     size_x, size_y, size_z, macro_count, cell_ref, position_ref, chunk_ref, viscous_ref, corner_ref,
-    edge_ref, partial_ref, out_ref, flag_ref, polymer, lines, shifted,
+    edge_ref, partial_ref, out_ref, flag_ref, polymer, lines, shifted, field_x, field_y, field_z, write_sem,
 ):
     flags = cell_ref.shape[0]
     chunk_rows = slot_rows + line_rows
     macro, core = place_of()
     lane = lanes_of((1, size_z))
     weight = 0.5 * macro_step
-    out_ref[...] = partial_ref[...]
-
-    def read(j, carry):
-        polymer[pl.ds(j, 1), :] = chunk_ref[pl.ds(position_ref[j], 1), :]
+    fields = (field_x, field_y, field_z)
+    for j in range(flags):
+        polymer[j : j + 1, :] = chunk_ref[pl.ds(position_ref[j], 1), :]
         cell = cell_ref[j]
         z = cell - lax.div(cell, size_z) * size_z
-        lines[0, pl.ds(j, 1), :] = jnp.where(lane == z, weight, 0.0)
-        lines[1, pl.ds(j, 1), :] = jnp.where(lane == z - 1, weight, jnp.where(lane == z + 1, -weight, 0.0))
-        return carry
-
-    lax.fori_loop(0, flags, read, 0, unroll=8)
+        lines[0, j : j + 1, :] = jnp.where(lane == z, weight, 0.0)
+        lines[1, j : j + 1, :] = jnp.where(lane == z - 1, weight, jnp.where(lane == z + 1, -weight, 0.0))
+    for a in range(3):
+        fields[a][...] = partial_ref[a]
     values = polymer[...]
     here, beside_z = lines[0], lines[1]
     for k in range(6):
@@ -582,7 +585,7 @@
             for a in range(2):
                 number = 4 * s + 2 * u + a
                 line = corner_ref[number : number + 1, :] * chunk_ref[pl.ds(start + 2 * u + a, 1), :]
-                out_ref[1 - a, at : at + 1, :] += jnp.where(inside, line, 0.0)
+                fields[1 - a][at : at + 1, :] += jnp.where(inside, line, 0.0)
     start = pl.multiple_of((2 * macro + 1 - core) * chunk_rows + slot_rows, 8)
     packed = chunk_ref[pl.ds(start, line_rows), :]
     end = jnp.where(core == 0, size_z - 1, 0)
@@ -592,25 +595,27 @@
             for i in range(size_x // 8):
                 line = rolled(packed, end - (4 * i + 2 * u + a)) * edge_ref[2 * u + a, 8 * i : 8 * i + 8, :]
                 at = pl.ds(8 * i * size_y + y, 8, stride=size_y)
-                out_ref[2 - a, at, :] += line
-
-    def add(j, carry):
+                fields[2 - a][at, :] += line
+
+    for j in range(flags):
         row = lax.div(cell_ref[j], size_z)
         targets = []
         for a in range(3):
-            line_x = shifted[pair_index(a, 0), pl.ds(j, 1), :]
-            line_y = shifted[pair_index(a, 1), pl.ds(j, 1), :]
-            line_z = shifted[6 + a, pl.ds(j, 1), :]
+            line_x = shifted[pair_index(a, 0), j : j + 1, :]
+            line_y = shifted[pair_index(a, 1), j : j + 1, :]
+            line_z = shifted[6 + a, j : j + 1, :]
             targets += [
                 (a, row - size_y, line_x), (a, row + size_y, -line_x),
                 (a, row - 1, line_y), (a, row + 1, -line_y), (a, row, line_z),
             ]
-        updated = [out_ref[a, pl.ds(at, 1), :] + line for a, at, line in targets]
+        updated = [fields[a][pl.ds(at, 1), :] + line for a, at, line in targets]
         for (a, at, _), line in zip(targets, updated):
-            out_ref[a, pl.ds(at, 1), :] = line
-        return carry
-
-    lax.fori_loop(0, flags, add, 0, unroll=2)
+            fields[a][pl.ds(at, 1), :] = line
+    copies = [pltpu.make_async_copy(fields[a], out_ref.at[a], write_sem.at[a]) for a in range(3)]
+    for copy in copies:
+        copy.start()
+    for copy in copies:
+        copy.wait()
 
 
 def add_polymer(flag_cell, position, chunks, viscous, corners, edges, partial, shape):
@@ -623,11 +628,15 @@
             jax.ShapeDtypeStruct((6, flags), jnp.float32),
         ),
         in_specs=[SMEM, SMEM, VMEM, VMEM, VMEM, VMEM, VMEM],
-        out_specs=(VMEM, VMEM),
+        out_specs=(pl.BlockSpec(memory_space=pltpu.HBM), VMEM),
         scratch_shapes=[
             pltpu.VMEM((flags, 128), jnp.float32),
             pltpu.VMEM((2, flags, size_z), jnp.float32),
             pltpu.VMEM((9, flags, size_z), jnp.float32),
+            pltpu.VMEM(partial.shape[1:], jnp.float32),
+            pltpu.VMEM(partial.shape[1:], jnp.float32),
+            pltpu.VMEM(partial.shape[1:], jnp.float32),
+            pltpu.SemaphoreType.DMA((3,)),
         ],
         compiler_params=limit(8),
         cost_estimate=pl.CostEstimate(flops=400000, bytes_accessed=3000000, transcendentals=0),
@@ -655,8 +664,8 @@
     down = [(target, source) for source, target in up]
     y_low = lax.ppermute(y_last, "tile", up)
     y_high = lax.ppermute(y_first, "tile", down)
-    last_state, polymer = advance(conformations, increments, received, y_low, y_high, capacity)
-    returned = exchange(polymer)
+    last_state, polymer = advance(conformations, increments, received, capacity)
+    returned = exchange(add_lines(polymer, y_low, y_high))
     partial, corners, edges = flow_step(velocity, viscosity, received, y_low, y_high)
     velocity_next, flag_stress = add_polymer(
         flag_cell, position, returned, viscous, corners, edges, partial, viscosity.shape

time: 41.1 us -> 32.3 us (0.79)
  local copies, waits for them, and re-layouts: 6.06 us -> 0.01 us
  waiting for transfers between devices: 6.86 us -> 3.67 us
  Pallas kernels: 13 us -> 14.2 us
  starting transfers between devices: 14 us -> 13.3 us
    unnamed x18 -> x6, local copies, waits for them, and re-layouts: 6.06 us -> 0.01 us
    ppermute x1, waiting for transfers between devices: 4.12 us -> 0.01 us  [shards(): y_high = lax.ppermute(y_first, 'tile', down)]
    all_to_all x2, waiting for transfers between devices: 1.6 us -> 3.66 us  [exchange(): lax.all_to_all(rows, ('macro', 'micro'), split_axis=0, concat_axis=0, til...]
    ppermute x1, waiting for transfers between devices: 1.14 us -> 0.01 us  [shards(): y_low = lax.ppermute(y_last, 'tile', up)]
    pallas_call x1 -> x2, Pallas kernels: 5.15 us -> 6.1 us  [the longest x1 5.36 us: advance(): pl.pallas_call(functools.partial(micro_kernel, capacity, parts, rows, gro...]
    all_to_all x2, starting transfers between devices: 9.22 us -> 8.53 us  [exchange(): lax.all_to_all(rows, ('macro', 'micro'), split_axis=0, concat_axis=0, til...]
  transfers between devices with their start and end apart: 4 -> 4, of which waited for: 3 -> 2; matrix products, arithmetic and copies ran while one was open for 0% -> 0% of each run, Pallas kernels for 8% -> 28%
where the time goes in v3:
time: 32.3 us; the launch traced here: 31.9 us
  Pallas kernels  14.2 us (44%)
  starting transfers between devices  13.3 us (41%)
  waiting for transfers between devices  3.67 us (11%)
  between operations  0.74 us (2%)
    all_to_all x2, starting transfers between devices, exchange(): lax.all_to_all(rows, ('macro', 'micro'), split_axis=0, concat_axis=0, til...  8.53 us
    pallas_call x1, Pallas kernels, advance(): pl.pallas_call(functools.partial(micro_kernel, capacity, parts, rows, gro...  5.36 us
    all_to_all x2, waiting for transfers between devices, exchange(): lax.all_to_all(rows, ('macro', 'micro'), split_axis=0, concat_axis=0, til...  3.66 us
    ppermute x1, starting transfers between devices, shards(): y_low = lax.ppermute(y_last, 'tile', up)  3.47 us
    pallas_call x1, Pallas kernels, flow_step(): pl.pallas_call(functools.partial(flow_kernel, size_x, size_y, size_z, chu...  3.41 us
    pallas_call x1, Pallas kernels, gather_rows(): pl.pallas_call(functools.partial(gather_kernel, capacity, size_x, size_y,...  2.43 us
    pallas_call x1, Pallas kernels, add_polymer(): pl.pallas_call(functools.partial(polymer_kernel, size_x, size_y, size_z,...  2.27 us
    ppermute x1, starting transfers between devices, shards(): y_high = lax.ppermute(y_first, 'tile', down)  1.29 us
  transfers between devices with their start and end apart: 4, of which 2 were waited for; matrix products, arithmetic and copies ran while one was open for 0% of the time, Pallas kernels for 28%

profile of v3, /device:TPU:0, one launch (start us, length us, event | category | flops | bytes accessed | tf_op | source)
XLA Modules:
  0.0 31.9 jit_solution(1640599904188310832)
XLA Ops:
  0.6 0.0 copy-start.2
  0.6 0.0 copy-start.1
  0.7 0.0 copy-start
  0.7 2.4 %gather_rows.1 = (f32[512,128]{1,0:T(8,128)}, s32[32]{0:T(128)S(1)}, f32[32,128]{1,0:T(8,128)S(1)}, f32[7,24,128]{2,1,0:T(8,128)S(1)}, f32[7,24,128]{2,1,0:T(8,128)S(1)}) custom-call(s32[32]{0:T(128)} %cell_ref.3, s32[32]{0:T(128)} %bitcast.11, f32[3,192,128]{2,1,0:T(8,128)} %bitcast.6, f32[192,128]{1,0:T(8,128)} %bitcast.8), custom_call_target="tpu_custom_call" | custom-call | flops 400000 | bytes 3000000 | tf_op jit(solution)/shard_map/gather_rows/pallas_call | solution.py:149
  3.1 5.2 %all-to-all-start = ((f32[8,64,128]{2,1,0:T(8,128)}), f32[8,64,128]{2,1,0:T(8,128)S(1)}, u32[]{:S(2)}, u32[]{:S(2)}) async-start(f32[8,64,128]{2,1,0:T(8,128)} %bitcast.3), calls=%async_computation | async-start | bytes 524288 | tf_op jit(solution)/shard_map/all_to_all | solution.py:660
  8.3 3.5 %collective-permute-start = (f32[7,24,128]{2,1,0:T(8,128)S(1)}, f32[7,24,128]{2,1,0:T(8,128)S(1)}, u32[]{:S(2)}, u32[]{:S(2)}) collective-permute-start(f32[7,24,128]{2,1,0:T(8,128)S(1)} %get-tuple-element.18), channel_id=1, source_target_pairs={{0,2},{2,4},{4,6},{1,3},{3,5},{5,7},{8,10},{10,12},{12,14},{9,11},... | collective-permute-start | bytes 258056 | tf_op jit(solution)/shard_map/ppermute | solution.py:665
  11.8 1.3 %collective-permute-start.1 = (f32[7,24,128]{2,1,0:T(8,128)S(1)}, f32[7,24,128]{2,1,0:T(8,128)S(1)}, u32[]{:S(2)}, u32[]{:S(2)}) collective-permute-start(f32[7,24,128]{2,1,0:T(8,128)S(1)} %get-tuple-element.19), channel_id=1, source_target_pairs={{2,0},{4,2},{6,4},{3,1},{5,3},{7,5},{10,8},{12,10},{14,12},{11,9},... | collective-permute-start | bytes 258056 | tf_op jit(solution)/shard_map/ppermute | solution.py:666
  13.1 2.2 %all-to-all-done.rate_ref.chunk_ref = f32[8,64,128]{2,1,0:T(8,128)S(1)} async-done(((f32[8,64,128]{2,1,0:T(8,128)}), f32[8,64,128]{2,1,0:T(8,128)S(1)}, u32[]{:S(2)}, u32[]{:S(2)}) %all-to-all-start) | async-done | bytes 262176 | tf_op jit(solution)/shard_map/all_to_all | solution.py:660
  15.2 5.4 %advance.1 = (f32[3,64,512]{2,1,0:T(8,128)}, f32[8,16,128]{2,1,0:T(8,128)S(1)}) custom-call(f32[3,64,512]{2,1,0:T(8,128)} %conform_ref.1, bf16[16,3,64,512]{3,2,1,0:T(8,128)(2,1)} %noise_ref.1, f32[8,64,128]{2,1,0:T(8,128)S(1)} %all-to-all-done.rate_ref.chunk_ref), custom_call_target="tpu_custom_call" | custom-call | flops 20000000 | bytes 5000000 | tf_op jit(solution)/shard_map/advance/pallas_call | solution.py:290
  20.6 0.0 collective-permute-done.y_low_ref
  20.6 0.0 collective-permute-done.1.y_high_ref
  20.6 0.7 %add_lines.1 = f32[8,16,128]{2,1,0:T(8,128)} custom-call(f32[8,16,128]{2,1,0:T(8,128)S(1)} %get-tuple-element.17.chunk_ref, f32[7,24,128]{2,1,0:T(8,128)S(1)} %collective-permute-done.y_low_ref, f32[7,24,128]{2,1,0:T(8,128)S(1)} %collective-permute-done.1.y_high_ref), custom_call_target="tpu_custom_call" | custom-call | flops 20000 | bytes 400000 | tf_op jit(solution)/shard_map/add_lines/pallas_call | solution.py:344
  21.3 3.4 %all-to-all-start.1 = ((f32[8,16,128]{2,1,0:T(8,128)}), f32[8,16,128]{2,1,0:T(8,128)S(1)}, u32[]{:S(2)}, u32[]{:S(2)}) async-start(f32[8,16,128]{2,1,0:T(8,128)} %add_lines.1), calls=%async_computation.1 | async-start | bytes 131072 | tf_op jit(solution)/shard_map/all_to_all | solution.py:660
  24.7 0.0 copy-done.1
  24.7 0.0 copy-done
  24.7 3.4 %flow_step.1 = (f32[3,192,128]{2,1,0:T(8,128)S(1)}, f32[8,128]{1,0:T(8,128)S(1)}, f32[4,24,128]{2,1,0:T(8,128)S(1)}) custom-call(f32[3,192,128]{2,1,0:T(8,128)S(1)} %bitcast.7, f32[192,128]{1,0:T(8,128)S(1)} %bitcast.9, f32[8,64,128]{2,1,0:T(8,128)S(1)} %all-to-all-done.rate_ref.chunk_ref, f32[7,24,128]{2,1,0:T(8,128)S(1)} %collective-permute-done.y_low_ref, ...), custom_call_target="tpu_custom_call" | custom-call | flops 4000000 | bytes 3000000 | tf_op jit(solution)/shard_map/flow_step/pallas_call | solution.py:524
  28.1 1.5 %all-to-all-done.1 = f32[8,16,128]{2,1,0:T(8,128)S(1)} async-done(((f32[8,16,128]{2,1,0:T(8,128)}), f32[8,16,128]{2,1,0:T(8,128)S(1)}, u32[]{:S(2)}, u32[]{:S(2)}) %all-to-all-start.1) | async-done | bytes 65568 | tf_op jit(solution)/shard_map/all_to_all | solution.py:660
  29.7 0.0 copy-done.2
  29.7 2.3 %add_polymer.1 = (f32[3,192,128]{2,1,0:T(8,128)}, f32[6,32]{1,0:T(8,128)}) custom-call(s32[32]{0:T(128)S(1)} %copy-done.2, s32[32]{0:T(128)S(1)} %get-tuple-element.15.position_ref, f32[128,128]{1,0:T(8,128)S(1)} %bitcast.10, f32[32,128]{1,0:T(8,128)S(1)} %get-tuple-element.20.viscous_ref, f32[8,128]{1,0:T(8,128)S(1)} %get-tuple-element.21.corner_ref, ...), custom_call_target="tpu_custom_call" | custom-call | flops 400000 | bytes 3000000 | tf_op jit(solution)/shard_map/add_polymer/pallas_call | solution.py:624
Async XLA Ops:
  0.6 29.0 %copy-start.2 = (s32[32]{0:T(128)S(1)}, s32[32]{0:T(128)}, u32[]{:S(2)}) copy-start(s32[32]{0:T(128)} %cell_ref.3) | copy-start | bytes 388
  0.6 24.1 %copy-start.1 = (f32[24,8,128]{2,1,0:T(8,128)S(1)}, f32[24,8,128]{2,1,0:T(8,128)}, u32[]{:S(2)}) copy-start(f32[24,8,128]{2,1,0:T(8,128)} %param.7) | copy-start | bytes 294916
  0.7 24.1 %copy-start = (f32[3,24,8,128]{3,2,1,0:T(8,128)S(1)}, f32[3,24,8,128]{3,2,1,0:T(8,128)}, u32[]{:S(2)}) copy-start(f32[3,24,8,128]{3,2,1,0:T(8,128)} %param.6) | copy-start | bytes 884740
  3.1 12.1 %all-to-all-start = ((f32[8,64,128]{2,1,0:T(8,128)}), f32[8,64,128]{2,1,0:T(8,128)S(1)}, u32[]{:S(2)}, u32[]{:S(2)}) async-start(f32[8,64,128]{2,1,0:T(8,128)} %bitcast.3), calls=%async_computation | async-start | bytes 524288 | tf_op jit(solution)/shard_map/all_to_all | solution.py:660
  8.3 12.3 %collective-permute-start = (f32[7,24,128]{2,1,0:T(8,128)S(1)}, f32[7,24,128]{2,1,0:T(8,128)S(1)}, u32[]{:S(2)}, u32[]{:S(2)}) collective-permute-start(f32[7,24,128]{2,1,0:T(8,128)S(1)} %get-tuple-element.18), channel_id=1, source_target_pairs={{0,2},{2,4},{4,6},{1,3},{3,5},{5,7},{8,10},{10,12},{12,14},{9,11},... | collective-permute-start | bytes 258056 | tf_op jit(solution)/shard_map/ppermute | solution.py:665
  11.8 8.8 %collective-permute-start.1 = (f32[7,24,128]{2,1,0:T(8,128)S(1)}, f32[7,24,128]{2,1,0:T(8,128)S(1)}, u32[]{:S(2)}, u32[]{:S(2)}) collective-permute-start(f32[7,24,128]{2,1,0:T(8,128)S(1)} %get-tuple-element.19), channel_id=1, source_target_pairs={{2,0},{4,2},{6,4},{3,1},{5,3},{7,5},{10,8},{12,10},{14,12},{11,9},... | collective-permute-start | bytes 258056 | tf_op jit(solution)/shard_map/ppermute | solution.py:666
  21.3 8.3 %all-to-all-start.1 = ((f32[8,16,128]{2,1,0:T(8,128)}), f32[8,16,128]{2,1,0:T(8,128)S(1)}, u32[]{:S(2)}, u32[]{:S(2)}) async-start(f32[8,16,128]{2,1,0:T(8,128)} %add_lines.1), calls=%async_computation.1 | async-start | bytes 131072 | tf_op jit(solution)/shard_map/all_to_all | solution.py:660

commit v4 on v3

--- a/solution.py
+++ b/solution.py
@@ -252,7 +252,7 @@
             for part in range(parts)
             for a in range(3)
         )
-        state = lax.fori_loop(0, groups, advance_group, state)
+        state = lax.fori_loop(0, groups, advance_group, state, unroll=True)
         sums = [None] * 6
         for part in range(parts):
             q = state[3 * part : 3 * part + 3]
@@ -421,7 +421,7 @@
                 faces[q, x + 1] = rolled(value, end - at)
             return carry
 
-        lax.fori_loop(i * group, min(size_x, (i + 1) * group), unpack, 0, unroll=2)
+        lax.fori_loop(i * group, min(size_x, (i + 1) * group), unpack, 0, unroll=8)
     faces[2, 0] = x_others[0][1]
     faces[2, size_x + 1] = x_others[1][1]
 
@@ -434,7 +434,7 @@
             padded[a, x + 1] = velocity_ref[a, plane(x), :]
         return carry
 
-    lax.fori_loop(0, size_x, fill, 0, unroll=4)
+    lax.fori_loop(0, size_x, fill, 0, unroll=True)
 
     rest = {(1, 1): 0, (2, 2): 1, (1, 2): 2}
 
@@ -463,7 +463,7 @@
         ghost_z[2, x] = weight * (2.0 * normal[2])
         return carry
 
-    lax.fori_loop(0, size_x, stress_plane, 0, unroll=2)
+    lax.fori_loop(0, size_x, stress_plane, 0, unroll=6)
 
     for s in range(2):
         near, far, weight = x_faces[s][0:3], x_faces[s][3:6], 0.5 * x_faces[s][6]
@@ -514,7 +514,7 @@
             out_ref[a, plane(x), :] = padded[a, x + 1] + (0.5 * macro_step) * total
         return carry
 
-    lax.fori_loop(0, size_x, step_plane, 0, unroll=2)
+    lax.fori_loop(0, size_x, step_plane, 0, unroll=6)
 
 
 def flow_step(velocity, viscosity, chunks, y_low, y_high):

time: 32.3 us -> 32.3 us (level)
  Pallas kernels: 14.2 us -> 12.4 us
  waiting for transfers between devices: 3.67 us -> 5.43 us
    all_to_all x2, waiting for transfers between devices: 3.66 us -> 5.43 us  [exchange(): lax.all_to_all(rows, ('macro', 'micro'), split_axis=0, concat_axis=0, til...]
    pallas_call x1, Pallas kernels: 3.41 us -> 1.65 us  [flow_step(): pl.pallas_call(functools.partial(flow_kernel, size_x, size_y, size_z, chu...]
  transfers between devices with their start and end apart: 4 -> 4, of which waited for: 2 -> 2; matrix products, arithmetic and copies ran while one was open for 0% -> 0% of each run, Pallas kernels for 28% -> 22%
where the time goes in v4:
time: 32.3 us; the launch traced here: 31.9 us
  starting transfers between devices  13.3 us (41%)
  Pallas kernels  12.4 us (38%)
  waiting for transfers between devices  5.43 us (17%)
  between operations  0.73 us (2%)
    all_to_all x2, starting transfers between devices, exchange(): lax.all_to_all(rows, ('macro', 'micro'), split_axis=0, concat_axis=0, til...  8.53 us
    all_to_all x2, waiting for transfers between devices, exchange(): lax.all_to_all(rows, ('macro', 'micro'), split_axis=0, concat_axis=0, til...  5.43 us
    pallas_call x1, Pallas kernels, advance(): pl.pallas_call(functools.partial(micro_kernel, capacity, parts, rows, gro...  5.36 us
    ppermute x1, starting transfers between devices, shards(): y_low = lax.ppermute(y_last, 'tile', up)  3.47 us
    pallas_call x1, Pallas kernels, gather_rows(): pl.pallas_call(functools.partial(gather_kernel, capacity, size_x, size_y,...  2.43 us
    pallas_call x1, Pallas kernels, add_polymer(): pl.pallas_call(functools.partial(polymer_kernel, size_x, size_y, size_z,...  2.26 us
    pallas_call x1, Pallas kernels, flow_step(): pl.pallas_call(functools.partial(flow_kernel, size_x, size_y, size_z, chu...  1.65 us
    ppermute x1, starting transfers between devices, shards(): y_high = lax.ppermute(y_first, 'tile', down)  1.29 us
  transfers between devices with their start and end apart: 4, of which 2 were waited for; matrix products, arithmetic and copies ran while one was open for 0% of the time, Pallas kernels for 22%

profile of v4, /device:TPU:0, one launch (start us, length us, event | category | flops | bytes accessed | tf_op | source)
XLA Modules:
  0.0 31.9 jit_solution(1304387645631723843)
XLA Ops:
  0.6 0.0 copy-start.2
  0.6 0.0 copy-start.1
  0.7 0.0 copy-start
  0.7 2.4 %gather_rows.1 = (f32[512,128]{1,0:T(8,128)}, s32[32]{0:T(128)S(1)}, f32[32,128]{1,0:T(8,128)S(1)}, f32[7,24,128]{2,1,0:T(8,128)S(1)}, f32[7,24,128]{2,1,0:T(8,128)S(1)}) custom-call(s32[32]{0:T(128)} %cell_ref.3, s32[32]{0:T(128)} %bitcast.11, f32[3,192,128]{2,1,0:T(8,128)} %bitcast.6, f32[192,128]{1,0:T(8,128)} %bitcast.8), custom_call_target="tpu_custom_call" | custom-call | flops 400000 | bytes 3000000 | tf_op jit(solution)/shard_map/gather_rows/pallas_call | solution.py:149
  3.1 5.2 %all-to-all-start = ((f32[8,64,128]{2,1,0:T(8,128)}), f32[8,64,128]{2,1,0:T(8,128)S(1)}, u32[]{:S(2)}, u32[]{:S(2)}) async-start(f32[8,64,128]{2,1,0:T(8,128)} %bitcast.3), calls=%async_computation | async-start | bytes 524288 | tf_op jit(solution)/shard_map/all_to_all | solution.py:660
  8.3 3.5 %collective-permute-start = (f32[7,24,128]{2,1,0:T(8,128)S(1)}, f32[7,24,128]{2,1,0:T(8,128)S(1)}, u32[]{:S(2)}, u32[]{:S(2)}) collective-permute-start(f32[7,24,128]{2,1,0:T(8,128)S(1)} %get-tuple-element.18), channel_id=1, source_target_pairs={{0,2},{2,4},{4,6},{1,3},{3,5},{5,7},{8,10},{10,12},{12,14},{9,11},... | collective-permute-start | bytes 258056 | tf_op jit(solution)/shard_map/ppermute | solution.py:665
  11.8 1.3 %collective-permute-start.1 = (f32[7,24,128]{2,1,0:T(8,128)S(1)}, f32[7,24,128]{2,1,0:T(8,128)S(1)}, u32[]{:S(2)}, u32[]{:S(2)}) collective-permute-start(f32[7,24,128]{2,1,0:T(8,128)S(1)} %get-tuple-element.19), channel_id=1, source_target_pairs={{2,0},{4,2},{6,4},{3,1},{5,3},{7,5},{10,8},{12,10},{14,12},{11,9},... | collective-permute-start | bytes 258056 | tf_op jit(solution)/shard_map/ppermute | solution.py:666
  13.1 2.2 %all-to-all-done.rate_ref.chunk_ref = f32[8,64,128]{2,1,0:T(8,128)S(1)} async-done(((f32[8,64,128]{2,1,0:T(8,128)}), f32[8,64,128]{2,1,0:T(8,128)S(1)}, u32[]{:S(2)}, u32[]{:S(2)}) %all-to-all-start) | async-done | bytes 262176 | tf_op jit(solution)/shard_map/all_to_all | solution.py:660
  15.2 5.4 %advance.1 = (f32[3,64,512]{2,1,0:T(8,128)}, f32[8,16,128]{2,1,0:T(8,128)S(1)}) custom-call(f32[3,64,512]{2,1,0:T(8,128)} %conform_ref.1, bf16[16,3,64,512]{3,2,1,0:T(8,128)(2,1)} %noise_ref.1, f32[8,64,128]{2,1,0:T(8,128)S(1)} %all-to-all-done.rate_ref.chunk_ref), custom_call_target="tpu_custom_call" | custom-call | flops 20000000 | bytes 5000000 | tf_op jit(solution)/shard_map/advance/pallas_call | solution.py:290
  20.6 0.0 collective-permute-done.y_low_ref
  20.6 0.0 collective-permute-done.1.y_high_ref
  20.6 0.7 %add_lines.1 = f32[8,16,128]{2,1,0:T(8,128)} custom-call(f32[8,16,128]{2,1,0:T(8,128)S(1)} %get-tuple-element.17.chunk_ref, f32[7,24,128]{2,1,0:T(8,128)S(1)} %collective-permute-done.y_low_ref, f32[7,24,128]{2,1,0:T(8,128)S(1)} %collective-permute-done.1.y_high_ref), custom_call_target="tpu_custom_call" | custom-call | flops 20000 | bytes 400000 | tf_op jit(solution)/shard_map/add_lines/pallas_call | solution.py:344
  21.3 3.4 %all-to-all-start.1 = ((f32[8,16,128]{2,1,0:T(8,128)}), f32[8,16,128]{2,1,0:T(8,128)S(1)}, u32[]{:S(2)}, u32[]{:S(2)}) async-start(f32[8,16,128]{2,1,0:T(8,128)} %add_lines.1), calls=%async_computation.1 | async-start | bytes 131072 | tf_op jit(solution)/shard_map/all_to_all | solution.py:660
  24.7 0.0 copy-done.1
  24.7 0.0 copy-done
  24.7 1.7 %flow_step.1 = (f32[3,192,128]{2,1,0:T(8,128)S(1)}, f32[8,128]{1,0:T(8,128)S(1)}, f32[4,24,128]{2,1,0:T(8,128)S(1)}) custom-call(f32[3,192,128]{2,1,0:T(8,128)S(1)} %bitcast.7, f32[192,128]{1,0:T(8,128)S(1)} %bitcast.9, f32[8,64,128]{2,1,0:T(8,128)S(1)} %all-to-all-done.rate_ref.chunk_ref, f32[7,24,128]{2,1,0:T(8,128)S(1)} %collective-permute-done.y_low_ref, ...), custom_call_target="tpu_custom_call" | custom-call | flops 4000000 | bytes 3000000 | tf_op jit(solution)/shard_map/flow_step/pallas_call | solution.py:524
  26.4 3.3 %all-to-all-done.1 = f32[8,16,128]{2,1,0:T(8,128)S(1)} async-done(((f32[8,16,128]{2,1,0:T(8,128)}), f32[8,16,128]{2,1,0:T(8,128)S(1)}, u32[]{:S(2)}, u32[]{:S(2)}) %all-to-all-start.1) | async-done | bytes 65568 | tf_op jit(solution)/shard_map/all_to_all | solution.py:660
  29.7 0.0 copy-done.2
  29.7 2.3 %add_polymer.1 = (f32[3,192,128]{2,1,0:T(8,128)}, f32[6,32]{1,0:T(8,128)}) custom-call(s32[32]{0:T(128)S(1)} %copy-done.2, s32[32]{0:T(128)S(1)} %get-tuple-element.15.position_ref, f32[128,128]{1,0:T(8,128)S(1)} %bitcast.10, f32[32,128]{1,0:T(8,128)S(1)} %get-tuple-element.20.viscous_ref, f32[8,128]{1,0:T(8,128)S(1)} %get-tuple-element.21.corner_ref, ...), custom_call_target="tpu_custom_call" | custom-call | flops 400000 | bytes 3000000 | tf_op jit(solution)/shard_map/add_polymer/pallas_call | solution.py:624
Async XLA Ops:
  0.6 29.0 %copy-start.2 = (s32[32]{0:T(128)S(1)}, s32[32]{0:T(128)}, u32[]{:S(2)}) copy-start(s32[32]{0:T(128)} %cell_ref.3) | copy-start | bytes 388
  0.6 24.1 %copy-start.1 = (f32[24,8,128]{2,1,0:T(8,128)S(1)}, f32[24,8,128]{2,1,0:T(8,128)}, u32[]{:S(2)}) copy-start(f32[24,8,128]{2,1,0:T(8,128)} %param.7) | copy-start | bytes 294916
  0.7 24.1 %copy-start = (f32[3,24,8,128]{3,2,1,0:T(8,128)S(1)}, f32[3,24,8,128]{3,2,1,0:T(8,128)}, u32[]{:S(2)}) copy-start(f32[3,24,8,128]{3,2,1,0:T(8,128)} %param.6) | copy-start | bytes 884740
  3.1 12.1 %all-to-all-start = ((f32[8,64,128]{2,1,0:T(8,128)}), f32[8,64,128]{2,1,0:T(8,128)S(1)}, u32[]{:S(2)}, u32[]{:S(2)}) async-start(f32[8,64,128]{2,1,0:T(8,128)} %bitcast.3), calls=%async_computation | async-start | bytes 524288 | tf_op jit(solution)/shard_map/all_to_all | solution.py:660
  8.3 12.3 %collective-permute-start = (f32[7,24,128]{2,1,0:T(8,128)S(1)}, f32[7,24,128]{2,1,0:T(8,128)S(1)}, u32[]{:S(2)}, u32[]{:S(2)}) collective-permute-start(f32[7,24,128]{2,1,0:T(8,128)S(1)} %get-tuple-element.18), channel_id=1, source_target_pairs={{0,2},{2,4},{4,6},{1,3},{3,5},{5,7},{8,10},{10,12},{12,14},{9,11},... | collective-permute-start | bytes 258056 | tf_op jit(solution)/shard_map/ppermute | solution.py:665
  11.8 8.8 %collective-permute-start.1 = (f32[7,24,128]{2,1,0:T(8,128)S(1)}, f32[7,24,128]{2,1,0:T(8,128)S(1)}, u32[]{:S(2)}, u32[]{:S(2)}) collective-permute-start(f32[7,24,128]{2,1,0:T(8,128)S(1)} %get-tuple-element.19), channel_id=1, source_target_pairs={{2,0},{4,2},{6,4},{3,1},{5,3},{7,5},{10,8},{12,10},{14,12},{11,9},... | collective-permute-start | bytes 258056 | tf_op jit(solution)/shard_map/ppermute | solution.py:666
  21.3 8.3 %all-to-all-start.1 = ((f32[8,16,128]{2,1,0:T(8,128)}), f32[8,16,128]{2,1,0:T(8,128)S(1)}, u32[]{:S(2)}, u32[]{:S(2)}) async-start(f32[8,16,128]{2,1,0:T(8,128)} %add_lines.1), calls=%async_computation.1 | async-start | bytes 131072 | tf_op jit(solution)/shard_map/all_to_all | solution.py:660

commit v5 on v4

--- a/solution.py
+++ b/solution.py
@@ -53,10 +53,22 @@
 
 
 def gather_kernel(
-    capacity, size_x, size_y, size_z, macro_count, cell_ref, owner_ref, velocity_ref, viscosity_ref,
-    chunk_ref, position_ref, viscous_ref, y_low_ref, y_high_ref, masked, gradients, target, count,
+    capacity, size_x, size_y, size_z, macro_count, cell_in, owner_in, velocity_in, viscosity_in,
+    chunk_ref, position_ref, viscous_ref, y_low_ref, y_high_ref,
+    cell_ref, owner_ref, velocity_ref, viscosity_ref, masked, gradients, target, count, sems,
 ):
     flags = cell_ref.shape[0]
+    copies = [
+        pltpu.make_async_copy(source, into, sems.at[number])
+        for number, (source, into) in enumerate(
+            (
+                (cell_in, cell_ref), (owner_in, owner_ref), (velocity_in, velocity_ref),
+                (viscosity_in, viscosity_ref),
+            )
+        )
+    ]
+    for copy in copies:
+        copy.start()
     chunk_rows = slot_rows + item_count * size_y
     macro, core = place_of()
     lane = lanes_of((1, size_z))
@@ -64,6 +76,16 @@
     for owner in range(count.shape[0]):
         count[owner] = 0
         chunk_ref[owner * chunk_rows : owner * chunk_rows + slot_rows, :] = jnp.zeros((slot_rows, 128), jnp.float32)
+    for copy in copies[:2]:
+        copy.wait()
+    for j in range(flags):
+        owner = owner_ref[j]
+        rank = count[owner]
+        count[owner] = rank + 1
+        target[j] = owner * chunk_rows + rank
+        position_ref[j] = owner * (slot_rows + line_rows) + rank
+    for copy in copies[2:]:
+        copy.wait()
     for j in range(flags):
         cell = cell_ref[j]
         row = lax.div(cell, size_z)
@@ -77,11 +99,6 @@
             masked[3 * a + 1, j : j + 1, :] = along_y * here
             masked[3 * a + 2, j : j + 1, :] = velocity_ref[a, pl.ds(row, 1), :] * along_z
         masked[9, j : j + 1, :] = viscosity_ref[pl.ds(row, 1), :] * here
-        owner = owner_ref[j]
-        rank = count[owner]
-        count[owner] = rank + 1
-        target[j] = owner * chunk_rows + rank
-        position_ref[j] = owner * (slot_rows + line_rows) + rank
 
     for side, ref in enumerate((y_low_ref, y_high_ref)):
         for layer in range(2):
@@ -155,13 +172,18 @@
             face,
             face,
         ),
-        in_specs=[SMEM, SMEM, VMEM, VMEM],
+        in_specs=[pl.BlockSpec(memory_space=pltpu.HBM)] * 4,
         out_specs=(VMEM, SMEM, VMEM, VMEM, VMEM),
         scratch_shapes=[
+            pltpu.SMEM((flags,), jnp.int32),
+            pltpu.SMEM((flags,), jnp.int32),
+            pltpu.VMEM((3, size_x * size_y, size_z), jnp.float32),
+            pltpu.VMEM((size_x * size_y, size_z), jnp.float32),
             pltpu.VMEM((10, flags, size_z), jnp.float32),
             pltpu.VMEM((flags, 128), jnp.float32),
             pltpu.SMEM((flags,), jnp.int32),
             pltpu.SMEM((owner_count,), jnp.int32),
+            pltpu.SemaphoreType.DMA((4,)),
         ],
         compiler_params=limit(8),
         cost_estimate=pl.CostEstimate(flops=400000, bytes_accessed=3000000, transcendentals=0),
@@ -176,7 +198,7 @@
 
 def micro_kernel(
     capacity, parts, rows, groups, conform_ref, noise_ref, rate_ref,
-    next_ref, chunk_ref, conform, noise, result, rate, sums_ref, read_sem, noise_sem, write_sem,
+    next_ref, chunk_ref, conform, noise, rate, rate_wide, sums_ref, read_sem, noise_sem,
 ):
     steps, _, slots, dumbbells = noise_ref.shape
     blocks = slots // rows
@@ -199,17 +221,17 @@
             noise_ref.at[when, :, at, :], noise.at[when, :, at, :], noise_sem.at[block, group]
         )
 
-    def write(block):
-        at = block_rows(block)
-        return pltpu.make_async_copy(result.at[:, at, :], next_ref.at[:, at, :], write_sem.at[block])
-
     for block in range(blocks):
         read(block).start()
         for group in range(groups):
             read_noise(block, group).start()
     for owner in range(owners):
         rate[owner * capacity : (owner + 1) * capacity, :] = rate_ref[owner, 0:capacity, :]
-        chunk_ref[owner, slot_rows:, :] = jnp.zeros((line_rows, 128), jnp.float32)
+        chunk_ref[owner] = jnp.zeros(chunk_ref.shape[1:], jnp.float32)
+    for a in range(3):
+        for b in range(3):
+            column = micro_step * rate[:, 3 * a + b : 3 * a + b + 1] + (1.0 if a == b else 0.0)
+            rate_wide[3 * a + b] = jnp.broadcast_to(column, (slots, width))
 
     def inverse_of(q):
         room = (extent - q[0] * q[0]) - (q[1] * q[1] + q[2] * q[2])
@@ -217,16 +239,7 @@
 
     def advance_block(block, carry):
         at = block_rows(block)
-        table = rate[at, :]
-        rates = [
-            [
-                jnp.broadcast_to(
-                    micro_step * table[:, 3 * a + b : 3 * a + b + 1] + (1.0 if a == b else 0.0), (rows, width)
-                )
-                for b in range(3)
-            ]
-            for a in range(3)
-        ]
+        rates = [[rate_wide.at[3 * a + b, at, :] for b in range(3)] for a in range(3)]
 
         def substep(step, state):
             updated = []
@@ -236,8 +249,8 @@
                 for a in range(3):
                     b, c = [other for other in range(3) if other != a]
                     kick = noise[step, a, at, part * width : (part + 1) * width].astype(jnp.float32)
-                    rest = (rates[a][b] * q[b] + rates[a][c] * q[c]) + kick
-                    updated.append((rates[a][a] - spring) * q[a] + rest)
+                    rest = (rates[a][b][...] * q[b] + rates[a][c][...] * q[c]) + kick
+                    updated.append((rates[a][a][...] - spring) * q[a] + rest)
             return tuple(updated)
 
         def advance_group(group, state):
@@ -257,12 +270,11 @@
         for part in range(parts):
             q = state[3 * part : 3 * part + 3]
             for a in range(3):
-                result[a, at, part * width : (part + 1) * width] = q[a] * noise_weight
+                next_ref[a, at, part * width : (part + 1) * width] = q[a] * noise_weight
             inverse = inverse_of(q)
             for k, (a, b) in enumerate(stress_pairs):
                 term = (inverse * q[a]) * q[b]
                 sums[k] = term if sums[k] is None else sums[k] + term
-        write(block).start()
         for k in range(6):
             sums_ref[k, at, :] = sums[k]
         return carry
@@ -276,8 +288,6 @@
         packed = jnp.where(lane == k, polymer_weight * (mean - (1.0 if a == b else 0.0)), packed)
     for owner in range(owners):
         chunk_ref[owner, 0:capacity, :] = packed[owner * capacity : (owner + 1) * capacity]
-    for block in range(blocks):
-        write(block).wait()
 
 
 def advance(conformations, increments, chunks, capacity):
@@ -290,20 +300,19 @@
     return pl.pallas_call(
         functools.partial(micro_kernel, capacity, parts, rows, groups),
         out_shape=(
-            jax.ShapeDtypeStruct(conformations.shape, jnp.float32),
+            pltpu.VMEM(conformations.shape, jnp.float32),
             jax.ShapeDtypeStruct((owners, slot_rows + line_rows, 128), jnp.float32),
         ),
         in_specs=[whole, whole, VMEM],
-        out_specs=(whole, VMEM),
+        out_specs=(VMEM, VMEM),
         scratch_shapes=[
             pltpu.VMEM(conformations.shape, jnp.float32),
             pltpu.VMEM(increments.shape, jnp.bfloat16),
-            pltpu.VMEM(conformations.shape, jnp.float32),
             pltpu.VMEM((slots, 128), jnp.float32),
+            pltpu.VMEM((9, slots, dumbbells // parts), jnp.float32),
             pltpu.VMEM((6, slots, dumbbells // parts), jnp.float32),
             pltpu.SemaphoreType.DMA((blocks,)),
             pltpu.SemaphoreType.DMA((blocks, groups)),
-            pltpu.SemaphoreType.DMA((blocks,)),
         ],
         compiler_params=limit(12),
         cost_estimate=pl.CostEstimate(flops=20000000, bytes_accessed=5000000, transcendentals=600000),
@@ -346,17 +355,55 @@
         out_shape=jax.ShapeDtypeStruct(chunks.shape, jnp.float32),
         in_specs=[VMEM, VMEM, VMEM],
         out_specs=VMEM,
+        input_output_aliases={0: 0},
         compiler_params=limit(4),
         cost_estimate=pl.CostEstimate(flops=20000, bytes_accessed=400000, transcendentals=0),
         name="add_lines",
     )(chunks, y_low, y_high)
 
 
+product_depth = 128
+
+
+def one_hots(size_y, size_z, cell_ref, position_ref, lines_ref, pick_ref, spread_ref, rows):
+    flags = cell_ref.shape[0]
+    weight = 0.5 * macro_step
+    row_count = spread_ref.shape[0]
+    back_rows = pick_ref.shape[1] // 3
+    lane = lanes_of((1, size_z))
+    row_lane = lanes_of((1, rows.shape[1]))
+    slot_lane = lanes_of((flags, back_rows))
+    flag_row = lax.broadcasted_iota(jnp.int32, (flags, back_rows), 0)
+    rows[3 * flags :, :] = jnp.zeros((product_depth - 3 * flags, rows.shape[1]), jnp.float32)
+    slot = jnp.zeros((flags, back_rows), jnp.int32)
+    for j in range(flags):
+        cell = cell_ref[j]
+        row = lax.div(cell, size_z)
+        z = cell - row * size_z
+        lines_ref[0, j : j + 1, :] = jnp.where(lane == z, weight, 0.0)
+        lines_ref[1, j : j + 1, :] = jnp.where(
+            lane == z - 1, weight, jnp.where(lane == z + 1, -weight, 0.0)
+        )
+        for number, shift in enumerate((size_y, 1)):
+            rows[number * flags + j : number * flags + j + 1, :] = jnp.where(
+                row_lane == row - shift, 1.0, jnp.where(row_lane == row + shift, -1.0, 0.0)
+            )
+        rows[2 * flags + j : 2 * flags + j + 1, :] = jnp.where(row_lane == row, 1.0, 0.0)
+        slot = jnp.where(flag_row == j, position_ref[j], slot)
+    spread = rows[...].T[:row_count].astype(jnp.bfloat16)
+    pick = jnp.where(slot_lane == slot, 1.0, 0.0).astype(jnp.bfloat16)
+    for piece in range(3):
+        spread_ref[:, piece * product_depth : (piece + 1) * product_depth] = spread
+        pick_ref[:, piece * back_rows : (piece + 1) * back_rows] = pick
+
+
 def flow_kernel(
-    size_x, size_y, size_z, macro_count, velocity_ref, viscosity_ref, chunk_ref, y_low_ref, y_high_ref,
-    out_ref, corner_ref, edge_ref, padded, stress_x, stress_rest, faces, ghost_y, ghost_z,
+    size_x, size_y, size_z, macro_count, cell_ref, position_ref, velocity_ref, viscosity_ref, chunk_ref,
+    y_low_ref, y_high_ref, out_ref, corner_ref, edge_ref, lines_ref, pick_ref, spread_ref,
+    padded, stress_x, stress_rest, faces, ghost_y, ghost_z, rows,
 ):
     macro, core = place_of()
+    one_hots(size_y, size_z, cell_ref, position_ref, lines_ref, pick_ref, spread_ref, rows)
     inside = (macro > 0, macro < macro_count - 1)
     sign_z = jnp.where(core == 0, 1.0, -1.0)
     end = jnp.where(core == 0, size_z - 1, 0)
@@ -517,8 +564,11 @@
     lax.fori_loop(0, size_x, step_plane, 0, unroll=6)
 
 
-def flow_step(velocity, viscosity, chunks, y_low, y_high):
+def flow_step(flag_cell, position, velocity, viscosity, chunks, y_low, y_high):
     size_x, size_y, size_z = viscosity.shape
+    flags = flag_cell.shape[0]
+    back_rows = chunks.shape[0] * (slot_rows + line_rows)
+    row_count = size_x * size_y
     planes = (size_x, size_y, size_z)
     wide = (size_x + 2, size_y, size_z)
     return pl.pallas_call(
@@ -527,9 +577,12 @@
             jax.ShapeDtypeStruct((3, size_x * size_y, size_z), jnp.float32),
             jax.ShapeDtypeStruct((8, size_z), jnp.float32),
             jax.ShapeDtypeStruct((4, size_x, size_z), jnp.float32),
+            jax.ShapeDtypeStruct((2, flags, size_z), jnp.float32),
+            jax.ShapeDtypeStruct((flags, 3 * back_rows), jnp.bfloat16),
+            jax.ShapeDtypeStruct((row_count, 3 * product_depth), jnp.bfloat16),
         ),
-        in_specs=[VMEM] * 5,
-        out_specs=(VMEM, VMEM, VMEM),
+        in_specs=[SMEM] * 2 + [VMEM] * 5,
+        out_specs=(VMEM,) * 6,
         scratch_shapes=[
             pltpu.VMEM((3, *wide), jnp.float32),
             pltpu.VMEM((3, *wide), jnp.float32),
@@ -537,44 +590,54 @@
             pltpu.VMEM((item_count, *wide), jnp.float32),
             pltpu.VMEM((6, size_x, size_z), jnp.float32),
             pltpu.VMEM((3, *planes), jnp.float32),
+            pltpu.VMEM((product_depth, -(-row_count // 128) * 128), jnp.float32),
         ],
         compiler_params=limit(12),
         cost_estimate=pl.CostEstimate(flops=4000000, bytes_accessed=3000000, transcendentals=0),
         name="flow_step",
     )(
+        flag_cell, position,
         velocity.reshape(3, size_x * size_y, size_z),
         viscosity.reshape(size_x * size_y, size_z),
         chunks, y_low, y_high,
     )
 
 
+def pieces(value):
+    high = value.astype(jnp.bfloat16)
+    rest = value - high.astype(jnp.float32)
+    middle = rest.astype(jnp.bfloat16)
+    return high, middle, (rest - middle.astype(jnp.float32)).astype(jnp.bfloat16)
+
+
 def polymer_kernel(
-    size_x, size_y, size_z, macro_count, cell_ref, position_ref, chunk_ref, viscous_ref, corner_ref,
-    edge_ref, partial_ref, out_ref, flag_ref, polymer, lines, shifted, field_x, field_y, field_z, write_sem,
+    size_x, size_y, size_z, macro_count, chunk_ref, viscous_ref, corner_ref, edge_ref, lines_ref, pick_ref,
+    spread_ref, partial_ref, out_ref, flag_ref, field, write_sem,
 ):
-    flags = cell_ref.shape[0]
+    flags = viscous_ref.shape[0]
     chunk_rows = slot_rows + line_rows
     macro, core = place_of()
-    lane = lanes_of((1, size_z))
-    weight = 0.5 * macro_step
-    fields = (field_x, field_y, field_z)
-    for j in range(flags):
-        polymer[j : j + 1, :] = chunk_ref[pl.ds(position_ref[j], 1), :]
-        cell = cell_ref[j]
-        z = cell - lax.div(cell, size_z) * size_z
-        lines[0, j : j + 1, :] = jnp.where(lane == z, weight, 0.0)
-        lines[1, j : j + 1, :] = jnp.where(lane == z - 1, weight, jnp.where(lane == z + 1, -weight, 0.0))
-    for a in range(3):
-        fields[a][...] = partial_ref[a]
-    values = polymer[...]
-    here, beside_z = lines[0], lines[1]
-    for k in range(6):
-        column = jnp.broadcast_to(values[:, k : k + 1], (flags, size_z))
-        shifted[k] = column * here
-        if stress_pairs[k][1] == 2:
-            shifted[6 + stress_pairs[k][0]] = column * beside_z
+    values = jnp.dot(
+        pick_ref[...], jnp.concatenate(pieces(chunk_ref[...]), axis=0), preferred_element_type=jnp.float32
+    )
+    here, beside_z = lines_ref[0], lines_ref[1]
+    columns = [jnp.broadcast_to(values[:, k : k + 1], (flags, size_z)) for k in range(6)]
+    unused = jnp.zeros((product_depth - 3 * flags, size_z), jnp.float32)
+    split = [
+        pieces(
+            jnp.concatenate(
+                [
+                    columns[pair_index(a, 0)] * here, columns[pair_index(a, 1)] * here,
+                    columns[pair_index(a, 2)] * beside_z, unused,
+                ],
+                axis=0,
+            )
+        )
+        for a in range(3)
+    ]
     flag_ref[...] = (viscous_ref[...] + values).T[0:6, :]
 
+    field[...] = partial_ref[...]
     for s in range(2):
         inside = macro > 0 if s == 0 else macro < macro_count - 1
         beside = jnp.maximum(macro - 1, 0) if s == 0 else jnp.minimum(macro + 1, macro_count - 1)
@@ -585,7 +648,7 @@
             for a in range(2):
                 number = 4 * s + 2 * u + a
                 line = corner_ref[number : number + 1, :] * chunk_ref[pl.ds(start + 2 * u + a, 1), :]
-                fields[1 - a][at : at + 1, :] += jnp.where(inside, line, 0.0)
+                field[1 - a, at : at + 1, :] += jnp.where(inside, line, 0.0)
     start = pl.multiple_of((2 * macro + 1 - core) * chunk_rows + slot_rows, 8)
     packed = chunk_ref[pl.ds(start, line_rows), :]
     end = jnp.where(core == 0, size_z - 1, 0)
@@ -595,31 +658,19 @@
             for i in range(size_x // 8):
                 line = rolled(packed, end - (4 * i + 2 * u + a)) * edge_ref[2 * u + a, 8 * i : 8 * i + 8, :]
                 at = pl.ds(8 * i * size_y + y, 8, stride=size_y)
-                fields[2 - a][at, :] += line
-
-    for j in range(flags):
-        row = lax.div(cell_ref[j], size_z)
-        targets = []
-        for a in range(3):
-            line_x = shifted[pair_index(a, 0), j : j + 1, :]
-            line_y = shifted[pair_index(a, 1), j : j + 1, :]
-            line_z = shifted[6 + a, j : j + 1, :]
-            targets += [
-                (a, row - size_y, line_x), (a, row + size_y, -line_x),
-                (a, row - 1, line_y), (a, row + 1, -line_y), (a, row, line_z),
-            ]
-        updated = [fields[a][pl.ds(at, 1), :] + line for a, at, line in targets]
-        for (a, at, _), line in zip(targets, updated):
-            fields[a][pl.ds(at, 1), :] = line
-    copies = [pltpu.make_async_copy(fields[a], out_ref.at[a], write_sem.at[a]) for a in range(3)]
-    for copy in copies:
-        copy.start()
+                field[2 - a, at, :] += line
+    copies = [pltpu.make_async_copy(field.at[a], out_ref.at[a], write_sem.at[a]) for a in range(3)]
+    for a in range(3):
+        field[a] += jnp.dot(
+            spread_ref[...], jnp.concatenate(split[a], axis=0), preferred_element_type=jnp.float32
+        )
+        copies[a].start()
     for copy in copies:
         copy.wait()
 
 
-def add_polymer(flag_cell, position, chunks, viscous, corners, edges, partial, shape):
-    flags = flag_cell.shape[0]
+def add_polymer(chunks, viscous, corners, edges, lines, pick, spread, partial, shape):
+    flags = viscous.shape[0]
     size_x, size_y, size_z = shape
     return pl.pallas_call(
         functools.partial(polymer_kernel, size_x, size_y, size_z, chunks.shape[0] // 2),
@@ -627,21 +678,13 @@
             jax.ShapeDtypeStruct(partial.shape, jnp.float32),
             jax.ShapeDtypeStruct((6, flags), jnp.float32),
         ),
-        in_specs=[SMEM, SMEM, VMEM, VMEM, VMEM, VMEM, VMEM],
+        in_specs=[VMEM] * 8,
         out_specs=(pl.BlockSpec(memory_space=pltpu.HBM), VMEM),
-        scratch_shapes=[
-            pltpu.VMEM((flags, 128), jnp.float32),
-            pltpu.VMEM((2, flags, size_z), jnp.float32),
-            pltpu.VMEM((9, flags, size_z), jnp.float32),
-            pltpu.VMEM(partial.shape[1:], jnp.float32),
-            pltpu.VMEM(partial.shape[1:], jnp.float32),
-            pltpu.VMEM(partial.shape[1:], jnp.float32),
-            pltpu.SemaphoreType.DMA((3,)),
-        ],
+        scratch_shapes=[pltpu.VMEM(partial.shape, jnp.float32), pltpu.SemaphoreType.DMA((3,))],
         compiler_params=limit(8),
         cost_estimate=pl.CostEstimate(flops=400000, bytes_accessed=3000000, transcendentals=0),
         name="add_polymer",
-    )(flag_cell, position, chunks.reshape(-1, 128), viscous, corners, edges, partial)
+    )(chunks.reshape(-1, 128), viscous, corners, edges, lines, pick, spread, partial)
 
 
 def shards(velocity, viscosity, flag_cell, flag_owner, conformations, increments):
@@ -666,9 +709,11 @@
     y_high = lax.ppermute(y_first, "tile", down)
     last_state, polymer = advance(conformations, increments, received, capacity)
     returned = exchange(add_lines(polymer, y_low, y_high))
-    partial, corners, edges = flow_step(velocity, viscosity, received, y_low, y_high)
+    partial, corners, edges, lines, pick, spread = flow_step(
+        flag_cell, position, velocity, viscosity, received, y_low, y_high
+    )
     velocity_next, flag_stress = add_polymer(
-        flag_cell, position, returned, viscous, corners, edges, partial, viscosity.shape
+        returned, viscous, corners, edges, lines, pick, spread, partial, viscosity.shape
     )
     return (velocity_next.reshape(velocity.shape), last_state, flag_stress)
 

time: 32.3 us -> 32.5 us (level)
  waiting for transfers between devices: 5.43 us -> 3.89 us
  Pallas kernels: 12.4 us -> 13.4 us
  local copies, waits for them, and re-layouts: 0.01 us -> 0.76 us
    all_to_all x2, waiting for transfers between devices: 5.43 us -> 3.88 us  [exchange(): lax.all_to_all(rows, ('macro', 'micro'), split_axis=0, concat_axis=0, til...]
    pallas_call x1, Pallas kernels: 0.73 us -> 1.56 us  [add_lines(): pl.pallas_call(functools.partial(lines_kernel, chunks.shape[0] // 2), out...]
    pallas_call x1, Pallas kernels: 1.65 us -> 2.46 us  [flow_step(): pl.pallas_call(functools.partial(flow_kernel, size_x, size_y, size_z, chu...]
    unnamed x6 -> x7, local copies, waits for them, and re-layouts: 0.01 us -> 0.76 us
    pallas_call x1, Pallas kernels: 2.26 us -> 1.79 us  [add_polymer(): pl.pallas_call(functools.partial(polymer_kernel, size_x, size_y, size_z,...]
  transfers between devices with their start and end apart: 4 -> 4, of which waited for: 2 -> 2; matrix products, arithmetic and copies ran while one was open for 0% -> 2% of each run, Pallas kernels for 22% -> 24%
where the time goes in v5:
time: 32.5 us; the launch traced here: 32 us
  Pallas kernels  13.4 us (41%)
  starting transfers between devices  13.3 us (41%)
  waiting for transfers between devices  3.89 us (12%)
  local copies, waits for them, and re-layouts  0.76 us (2%)
  between operations  0.72 us (2%)
    all_to_all x2, starting transfers between devices, exchange(): lax.all_to_all(rows, ('macro', 'micro'), split_axis=0, concat_axis=0, til...  8.53 us
    pallas_call x1, Pallas kernels, advance(): pl.pallas_call(functools.partial(micro_kernel, capacity, parts, rows, gro...  5.23 us
    all_to_all x2, waiting for transfers between devices, exchange(): lax.all_to_all(rows, ('macro', 'micro'), split_axis=0, concat_axis=0, til...  3.88 us
    ppermute x1, starting transfers between devices, shards(): y_low = lax.ppermute(y_last, 'tile', up)  3.47 us
    pallas_call x1, Pallas kernels, flow_step(): pl.pallas_call(functools.partial(flow_kernel, size_x, size_y, size_z, chu...  2.46 us
    pallas_call x1, Pallas kernels, gather_rows(): pl.pallas_call(functools.partial(gather_kernel, capacity, size_x, size_y,...  2.34 us
    pallas_call x1, Pallas kernels, add_polymer(): pl.pallas_call(functools.partial(polymer_kernel, size_x, size_y, size_z,...  1.79 us
    pallas_call x1, Pallas kernels, add_lines(): pl.pallas_call(functools.partial(lines_kernel, chunks.shape[0] // 2), out...  1.56 us
  transfers between devices with their start and end apart: 4, of which 2 were waited for; matrix products, arithmetic and copies ran while one was open for 2% of the time, Pallas kernels for 24%

profile of v5, /device:TPU:0, one launch (start us, length us, event | category | flops | bytes accessed | tf_op | source)
XLA Modules:
  0.0 32.0 jit_solution(10582914277959508362)
XLA Ops:
  0.6 0.0 copy-start
  0.6 0.0 copy-start.1
  0.7 0.0 copy-start.2
  0.7 2.3 %gather_rows.1 = (f32[512,128]{1,0:T(8,128)}, s32[32]{0:T(128)S(1)}, f32[32,128]{1,0:T(8,128)S(1)}, f32[7,24,128]{2,1,0:T(8,128)S(1)}, f32[7,24,128]{2,1,0:T(8,128)S(1)}) custom-call(s32[32]{0:T(128)} %cell_ref.1, s32[32]{0:T(128)} %bitcast.11, f32[3,192,128]{2,1,0:T(8,128)} %bitcast.6, f32[192,128]{1,0:T(8,128)} %bitcast.8), custom_call_target="tpu_custom_call" | custom-call | flops 400000 | bytes 3000000 | tf_op jit(solution)/shard_map/gather_rows/pallas_call | solution.py:166
  3.0 5.2 %all-to-all-start = ((f32[8,64,128]{2,1,0:T(8,128)}), f32[8,64,128]{2,1,0:T(8,128)S(1)}, u32[]{:S(2)}, u32[]{:S(2)}) async-start(f32[8,64,128]{2,1,0:T(8,128)} %bitcast.3), calls=%async_computation | async-start | bytes 524288 | tf_op jit(solution)/shard_map/all_to_all | solution.py:703
  8.2 3.5 %collective-permute-start = (f32[7,24,128]{2,1,0:T(8,128)S(1)}, f32[7,24,128]{2,1,0:T(8,128)S(1)}, u32[]{:S(2)}, u32[]{:S(2)}) collective-permute-start(f32[7,24,128]{2,1,0:T(8,128)S(1)} %get-tuple-element.20), channel_id=1, source_target_pairs={{0,2},{2,4},{4,6},{1,3},{3,5},{5,7},{8,10},{10,12},{12,14},{9,11},... | collective-permute-start | bytes 258056 | tf_op jit(solution)/shard_map/ppermute | solution.py:708
  11.7 1.3 %collective-permute-start.1 = (f32[7,24,128]{2,1,0:T(8,128)S(1)}, f32[7,24,128]{2,1,0:T(8,128)S(1)}, u32[]{:S(2)}, u32[]{:S(2)}) collective-permute-start(f32[7,24,128]{2,1,0:T(8,128)S(1)} %get-tuple-element.21), channel_id=1, source_target_pairs={{2,0},{4,2},{6,4},{3,1},{5,3},{7,5},{10,8},{12,10},{14,12},{11,9},... | collective-permute-start | bytes 258056 | tf_op jit(solution)/shard_map/ppermute | solution.py:709
  13.0 2.2 %all-to-all-done.rate_ref.chunk_ref = f32[8,64,128]{2,1,0:T(8,128)S(1)} async-done(((f32[8,64,128]{2,1,0:T(8,128)}), f32[8,64,128]{2,1,0:T(8,128)S(1)}, u32[]{:S(2)}, u32[]{:S(2)}) %all-to-all-start) | async-done | bytes 262176 | tf_op jit(solution)/shard_map/all_to_all | solution.py:703
  15.1 5.2 %advance.1 = (f32[3,64,512]{2,1,0:T(8,128)S(1)}, f32[8,16,128]{2,1,0:T(8,128)}) custom-call(f32[3,64,512]{2,1,0:T(8,128)} %conform_ref.1, bf16[16,3,64,512]{3,2,1,0:T(8,128)(2,1)} %noise_ref.1, f32[8,64,128]{2,1,0:T(8,128)S(1)} %all-to-all-done.rate_ref.chunk_ref), custom_call_target="tpu_custom_call" | custom-call | flops 20000000 | bytes 5000000 | tf_op jit(solution)/shard_map/advance/pallas_call | solution.py:300
  20.4 0.0 collective-permute-done.y_low_ref
  20.4 0.0 collective-permute-done.1.y_high_ref
  20.4 1.6 %add_lines.1 = f32[8,16,128]{2,1,0:T(8,128)} custom-call(f32[8,16,128]{2,1,0:T(8,128)} %get-tuple-element.19.chunk_ref, f32[7,24,128]{2,1,0:T(8,128)S(1)} %collective-permute-done.y_low_ref, f32[7,24,128]{2,1,0:T(8,128)S(1)} %collective-permute-done.1.y_high_ref), custom_call_target="tpu_custom_call", output_to_operand_aliasing={{}: (0, {})} | custom-call | flops 20000 | bytes 400000 | tf_op jit(solution)/shard_map/add_lines/pallas_call | solution.py:353
  21.9 3.4 %all-to-all-start.1 = ((f32[8,16,128]{2,1,0:T(8,128)}), f32[8,16,128]{2,1,0:T(8,128)S(1)}, u32[]{:S(2)}, u32[]{:S(2)}) async-start(f32[8,16,128]{2,1,0:T(8,128)} %add_lines.1), calls=%async_computation.1 | async-start | bytes 131072 | tf_op jit(solution)/shard_map/all_to_all | solution.py:703
  25.3 0.7 %copy.11 = f32[3,64,512]{2,1,0:T(8,128)} copy(f32[3,64,512]{2,1,0:T(8,128)S(1)} %get-tuple-element.34) | data formatting | bytes 786432
  26.1 0.0 copy-done
  26.1 0.0 copy-done.1
  26.1 0.0 copy-done.2
  26.1 2.5 %flow_step.1 = (f32[3,192,128]{2,1,0:T(8,128)S(1)}, f32[8,128]{1,0:T(8,128)S(1)}, f32[4,24,128]{2,1,0:T(8,128)S(1)}, f32[2,32,128]{2,1,0:T(8,128)S(1)}, bf16[32,...) custom-call(s32[32]{0:T(128)S(1)} %copy-done.2, s32[32]{0:T(128)S(1)} %get-tuple-element.23.position_ref, ...), custom_call_target="tpu_custom_call" | custom-call | flops 4000000 | bytes 3000000 | tf_op jit(solution)/shard_map/flow_step/pallas_call | solution.py:574
  28.5 1.7 %all-to-all-done.1 = f32[8,16,128]{2,1,0:T(8,128)S(1)} async-done(((f32[8,16,128]{2,1,0:T(8,128)}), f32[8,16,128]{2,1,0:T(8,128)S(1)}, u32[]{:S(2)}, u32[]{:S(2)}) %all-to-all-start.1) | async-done | bytes 65568 | tf_op jit(solution)/shard_map/all_to_all | solution.py:703
  30.3 1.8 %add_polymer.1 = (f32[3,192,128]{2,1,0:T(8,128)}, f32[6,32]{1,0:T(8,128)}) custom-call(f32[128,128]{1,0:T(8,128)S(1)} %bitcast.10, f32[32,128]{1,0:T(8,128)S(1)} %get-tuple-element.22.viscous_ref, f32[8,128]{1,0:T(8,128)S(1)} %get-tuple-element.24.corner_ref, f32[4,24,128]{2,1,0:T(8,128)S(1)} %get-tuple-element.25.edge_ref, ...), custom_call_target="tpu_custom_call" | custom-call | flops 400000 | bytes 3000000 | tf_op jit(solution)/shard_map/add_polymer/pallas_call | solution.py:675
Async XLA Ops:
  0.6 25.4 %copy-start = (f32[3,24,8,128]{3,2,1,0:T(8,128)S(1)}, f32[3,24,8,128]{3,2,1,0:T(8,128)}, u32[]{:S(2)}) copy-start(f32[3,24,8,128]{3,2,1,0:T(8,128)} %param.6) | copy-start | bytes 884740
  0.6 25.4 %copy-start.1 = (f32[24,8,128]{2,1,0:T(8,128)S(1)}, f32[24,8,128]{2,1,0:T(8,128)}, u32[]{:S(2)}) copy-start(f32[24,8,128]{2,1,0:T(8,128)} %param.7) | copy-start | bytes 294916
  0.7 25.4 %copy-start.2 = (s32[32]{0:T(128)S(1)}, s32[32]{0:T(128)}, u32[]{:S(2)}) copy-start(s32[32]{0:T(128)} %cell_ref.1) | copy-start | bytes 388
  3.0 12.1 %all-to-all-start = ((f32[8,64,128]{2,1,0:T(8,128)}), f32[8,64,128]{2,1,0:T(8,128)S(1)}, u32[]{:S(2)}, u32[]{:S(2)}) async-start(f32[8,64,128]{2,1,0:T(8,128)} %bitcast.3), calls=%async_computation | async-start | bytes 524288 | tf_op jit(solution)/shard_map/all_to_all | solution.py:703
  8.2 12.2 %collective-permute-start = (f32[7,24,128]{2,1,0:T(8,128)S(1)}, f32[7,24,128]{2,1,0:T(8,128)S(1)}, u32[]{:S(2)}, u32[]{:S(2)}) collective-permute-start(f32[7,24,128]{2,1,0:T(8,128)S(1)} %get-tuple-element.20), channel_id=1, source_target_pairs={{0,2},{2,4},{4,6},{1,3},{3,5},{5,7},{8,10},{10,12},{12,14},{9,11},... | collective-permute-start | bytes 258056 | tf_op jit(solution)/shard_map/ppermute | solution.py:708
  11.7 8.7 %collective-permute-start.1 = (f32[7,24,128]{2,1,0:T(8,128)S(1)}, f32[7,24,128]{2,1,0:T(8,128)S(1)}, u32[]{:S(2)}, u32[]{:S(2)}) collective-permute-start(f32[7,24,128]{2,1,0:T(8,128)S(1)} %get-tuple-element.21), channel_id=1, source_target_pairs={{2,0},{4,2},{6,4},{3,1},{5,3},{7,5},{10,8},{12,10},{14,12},{11,9},... | collective-permute-start | bytes 258056 | tf_op jit(solution)/shard_map/ppermute | solution.py:709
  21.9 8.3 %all-to-all-start.1 = ((f32[8,16,128]{2,1,0:T(8,128)}), f32[8,16,128]{2,1,0:T(8,128)S(1)}, u32[]{:S(2)}, u32[]{:S(2)}) async-start(f32[8,16,128]{2,1,0:T(8,128)} %add_lines.1), calls=%async_computation.1 | async-start | bytes 131072 | tf_op jit(solution)/shard_map/all_to_all | solution.py:703

commit v6 on v5

--- a/solution.py
+++ b/solution.py
@@ -233,9 +233,17 @@
             column = micro_step * rate[:, 3 * a + b : 3 * a + b + 1] + (1.0 if a == b else 0.0)
             rate_wide[3 * a + b] = jnp.broadcast_to(column, (slots, width))
 
-    def inverse_of(q):
-        room = (extent - q[0] * q[0]) - (q[1] * q[1] + q[2] * q[2])
-        return pl.reciprocal(jnp.maximum(room, extent * spring_floor), approx=True)
+    def inverses(state):
+        rooms = []
+        for part in range(parts):
+            q = state[3 * part : 3 * part + 3]
+            room = (extent - q[0] * q[0]) - (q[1] * q[1] + q[2] * q[2])
+            rooms.append(jnp.maximum(room, extent * spring_floor))
+        result = []
+        for part in range(0, parts, 2):
+            both = pl.reciprocal(rooms[part] * rooms[part + 1], approx=True)
+            result += [both * rooms[part + 1], both * rooms[part]]
+        return result
 
     def advance_block(block, carry):
         at = block_rows(block)
@@ -243,9 +251,10 @@
 
         def substep(step, state):
             updated = []
+            inverse = inverses(state)
             for part in range(parts):
                 q = state[3 * part : 3 * part + 3]
-                spring = (micro_step * relax_rate * extent) * inverse_of(q)
+                spring = (micro_step * relax_rate * extent) * inverse[part]
                 for a in range(3):
                     b, c = [other for other in range(3) if other != a]
                     kick = noise[step, a, at, part * width : (part + 1) * width].astype(jnp.float32)
@@ -267,13 +276,13 @@
         )
         state = lax.fori_loop(0, groups, advance_group, state, unroll=True)
         sums = [None] * 6
+        inverse = inverses(state)
         for part in range(parts):
             q = state[3 * part : 3 * part + 3]
             for a in range(3):
                 next_ref[a, at, part * width : (part + 1) * width] = q[a] * noise_weight
-            inverse = inverse_of(q)
             for k, (a, b) in enumerate(stress_pairs):
-                term = (inverse * q[a]) * q[b]
+                term = (inverse[part] * q[a]) * q[b]
                 sums[k] = term if sums[k] is None else sums[k] + term
         for k in range(6):
             sums_ref[k, at, :] = sums[k]
@@ -355,7 +364,6 @@
         out_shape=jax.ShapeDtypeStruct(chunks.shape, jnp.float32),
         in_specs=[VMEM, VMEM, VMEM],
         out_specs=VMEM,
-        input_output_aliases={0: 0},
         compiler_params=limit(4),
         cost_estimate=pl.CostEstimate(flops=20000, bytes_accessed=400000, transcendentals=0),
         name="add_lines",

time: 32.5 us -> 31 us (0.954)
  Pallas kernels: 13.4 us -> 12 us
    pallas_call x1, Pallas kernels: 1.56 us -> 0.73 us  [add_lines(): pl.pallas_call(functools.partial(lines_kernel, chunks.shape[0] // 2), out...]
    pallas_call x1, Pallas kernels: 5.23 us -> 4.66 us  [advance(): pl.pallas_call(functools.partial(micro_kernel, capacity, parts, rows, gro...]
  transfers between devices with their start and end apart: 4 -> 4, of which waited for: 2 -> 2; matrix products, arithmetic and copies ran while one was open for 2% -> 2% of each run, Pallas kernels for 24% -> 23%
where the time goes in v6:
time: 31 us; the launch traced here: 30.6 us
  starting transfers between devices  13.3 us (43%)
  Pallas kernels  12 us (39%)
  waiting for transfers between devices  3.89 us (13%)
  local copies, waits for them, and re-layouts  0.76 us (2%)
  between operations  0.72 us (2%)
    all_to_all x2, starting transfers between devices, exchange(): lax.all_to_all(rows, ('macro', 'micro'), split_axis=0, concat_axis=0, til...  8.53 us
    pallas_call x1, Pallas kernels, advance(): pl.pallas_call(functools.partial(micro_kernel, capacity, parts, rows, gro...  4.66 us
    all_to_all x2, waiting for transfers between devices, exchange(): lax.all_to_all(rows, ('macro', 'micro'), split_axis=0, concat_axis=0, til...  3.88 us
    ppermute x1, starting transfers between devices, shards(): y_low = lax.ppermute(y_last, 'tile', up)  3.47 us
    pallas_call x1, Pallas kernels, flow_step(): pl.pallas_call(functools.partial(flow_kernel, size_x, size_y, size_z, chu...  2.46 us
    pallas_call x1, Pallas kernels, gather_rows(): pl.pallas_call(functools.partial(gather_kernel, capacity, size_x, size_y,...  2.34 us
    pallas_call x1, Pallas kernels, add_polymer(): pl.pallas_call(functools.partial(polymer_kernel, size_x, size_y, size_z,...  1.78 us
    ppermute x1, starting transfers between devices, shards(): y_high = lax.ppermute(y_first, 'tile', down)  1.29 us
  transfers between devices with their start and end apart: 4, of which 2 were waited for; matrix products, arithmetic and copies ran while one was open for 2% of the time, Pallas kernels for 23%

profile of v6, /device:TPU:0, one launch (start us, length us, event | category | flops | bytes accessed | tf_op | source)
XLA Modules:
  0.0 30.6 jit_solution(11732839962845565077)
XLA Ops:
  0.6 0.0 copy-start
  0.6 0.0 copy-start.1
  0.7 0.0 copy-start.2
  0.7 2.3 %gather_rows.1 = (f32[512,128]{1,0:T(8,128)}, s32[32]{0:T(128)S(1)}, f32[32,128]{1,0:T(8,128)S(1)}, f32[7,24,128]{2,1,0:T(8,128)S(1)}, f32[7,24,128]{2,1,0:T(8,128)S(1)}) custom-call(s32[32]{0:T(128)} %cell_ref.1, s32[32]{0:T(128)} %bitcast.11, f32[3,192,128]{2,1,0:T(8,128)} %bitcast.6, f32[192,128]{1,0:T(8,128)} %bitcast.8), custom_call_target="tpu_custom_call" | custom-call | flops 400000 | bytes 3000000 | tf_op jit(solution)/shard_map/gather_rows/pallas_call | solution.py:166
  3.0 5.2 %all-to-all-start = ((f32[8,64,128]{2,1,0:T(8,128)}), f32[8,64,128]{2,1,0:T(8,128)S(1)}, u32[]{:S(2)}, u32[]{:S(2)}) async-start(f32[8,64,128]{2,1,0:T(8,128)} %bitcast.3), calls=%async_computation | async-start | bytes 524288 | tf_op jit(solution)/shard_map/all_to_all | solution.py:711
  8.2 3.5 %collective-permute-start = (f32[7,24,128]{2,1,0:T(8,128)S(1)}, f32[7,24,128]{2,1,0:T(8,128)S(1)}, u32[]{:S(2)}, u32[]{:S(2)}) collective-permute-start(f32[7,24,128]{2,1,0:T(8,128)S(1)} %get-tuple-element.20), channel_id=1, source_target_pairs={{0,2},{2,4},{4,6},{1,3},{3,5},{5,7},{8,10},{10,12},{12,14},{9,11},... | collective-permute-start | bytes 258056 | tf_op jit(solution)/shard_map/ppermute | solution.py:716
  11.7 1.3 %collective-permute-start.1 = (f32[7,24,128]{2,1,0:T(8,128)S(1)}, f32[7,24,128]{2,1,0:T(8,128)S(1)}, u32[]{:S(2)}, u32[]{:S(2)}) collective-permute-start(f32[7,24,128]{2,1,0:T(8,128)S(1)} %get-tuple-element.21), channel_id=1, source_target_pairs={{2,0},{4,2},{6,4},{3,1},{5,3},{7,5},{10,8},{12,10},{14,12},{11,9},... | collective-permute-start | bytes 258056 | tf_op jit(solution)/shard_map/ppermute | solution.py:717
  13.0 2.2 %all-to-all-done.rate_ref.chunk_ref = f32[8,64,128]{2,1,0:T(8,128)S(1)} async-done(((f32[8,64,128]{2,1,0:T(8,128)}), f32[8,64,128]{2,1,0:T(8,128)S(1)}, u32[]{:S(2)}, u32[]{:S(2)}) %all-to-all-start) | async-done | bytes 262176 | tf_op jit(solution)/shard_map/all_to_all | solution.py:711
  15.1 4.7 %advance.1 = (f32[3,64,512]{2,1,0:T(8,128)S(1)}, f32[8,16,128]{2,1,0:T(8,128)S(1)}) custom-call(f32[3,64,512]{2,1,0:T(8,128)} %conform_ref.1, bf16[16,3,64,512]{3,2,1,0:T(8,128)(2,1)} %noise_ref.1, f32[8,64,128]{2,1,0:T(8,128)S(1)} %all-to-all-done.rate_ref.chunk_ref), custom_call_target="tpu_custom_call" | custom-call | flops 20000000 | bytes 5000000 | tf_op jit(solution)/shard_map/advance/pallas_call | solution.py:309
  19.8 0.0 collective-permute-done.y_low_ref
  19.8 0.0 collective-permute-done.1.y_high_ref
  19.8 0.7 %add_lines.1 = f32[8,16,128]{2,1,0:T(8,128)} custom-call(f32[8,16,128]{2,1,0:T(8,128)S(1)} %get-tuple-element.19.chunk_ref, f32[7,24,128]{2,1,0:T(8,128)S(1)} %collective-permute-done.y_low_ref, f32[7,24,128]{2,1,0:T(8,128)S(1)} %collective-permute-done.1.y_high_ref), custom_call_target="tpu_custom_call" | custom-call | flops 20000 | bytes 400000 | tf_op jit(solution)/shard_map/add_lines/pallas_call | solution.py:362
  20.6 3.4 %all-to-all-start.1 = ((f32[8,16,128]{2,1,0:T(8,128)}), f32[8,16,128]{2,1,0:T(8,128)S(1)}, u32[]{:S(2)}, u32[]{:S(2)}) async-start(f32[8,16,128]{2,1,0:T(8,128)} %add_lines.1), calls=%async_computation.1 | async-start | bytes 131072 | tf_op jit(solution)/shard_map/all_to_all | solution.py:711
  23.9 0.7 %copy.9 = f32[3,64,512]{2,1,0:T(8,128)} copy(f32[3,64,512]{2,1,0:T(8,128)S(1)} %get-tuple-element.34) | data formatting | bytes 786432
  24.7 0.0 copy-done
  24.7 0.0 copy-done.1
  24.7 0.0 copy-done.2
  24.7 2.5 %flow_step.1 = (f32[3,192,128]{2,1,0:T(8,128)S(1)}, f32[8,128]{1,0:T(8,128)S(1)}, f32[4,24,128]{2,1,0:T(8,128)S(1)}, f32[2,32,128]{2,1,0:T(8,128)S(1)}, bf16[32,...) custom-call(s32[32]{0:T(128)S(1)} %copy-done.2, s32[32]{0:T(128)S(1)} %get-tuple-element.23.position_ref, ...), custom_call_target="tpu_custom_call" | custom-call | flops 4000000 | bytes 3000000 | tf_op jit(solution)/shard_map/flow_step/pallas_call | solution.py:582
  27.1 1.7 %all-to-all-done.1 = f32[8,16,128]{2,1,0:T(8,128)S(1)} async-done(((f32[8,16,128]{2,1,0:T(8,128)}), f32[8,16,128]{2,1,0:T(8,128)S(1)}, u32[]{:S(2)}, u32[]{:S(2)}) %all-to-all-start.1) | async-done | bytes 65568 | tf_op jit(solution)/shard_map/all_to_all | solution.py:711
  28.9 1.8 %add_polymer.1 = (f32[3,192,128]{2,1,0:T(8,128)}, f32[6,32]{1,0:T(8,128)}) custom-call(f32[128,128]{1,0:T(8,128)S(1)} %bitcast.10, f32[32,128]{1,0:T(8,128)S(1)} %get-tuple-element.22.viscous_ref, f32[8,128]{1,0:T(8,128)S(1)} %get-tuple-element.24.corner_ref, f32[4,24,128]{2,1,0:T(8,128)S(1)} %get-tuple-element.25.edge_ref, ...), custom_call_target="tpu_custom_call" | custom-call | flops 400000 | bytes 3000000 | tf_op jit(solution)/shard_map/add_polymer/pallas_call | solution.py:683
Async XLA Ops:
  0.6 24.0 %copy-start = (f32[3,24,8,128]{3,2,1,0:T(8,128)S(1)}, f32[3,24,8,128]{3,2,1,0:T(8,128)}, u32[]{:S(2)}) copy-start(f32[3,24,8,128]{3,2,1,0:T(8,128)} %param.6) | copy-start | bytes 884740
  0.6 24.0 %copy-start.1 = (f32[24,8,128]{2,1,0:T(8,128)S(1)}, f32[24,8,128]{2,1,0:T(8,128)}, u32[]{:S(2)}) copy-start(f32[24,8,128]{2,1,0:T(8,128)} %param.7) | copy-start | bytes 294916
  0.7 24.0 %copy-start.2 = (s32[32]{0:T(128)S(1)}, s32[32]{0:T(128)}, u32[]{:S(2)}) copy-start(s32[32]{0:T(128)} %cell_ref.1) | copy-start | bytes 388
  3.0 12.1 %all-to-all-start = ((f32[8,64,128]{2,1,0:T(8,128)}), f32[8,64,128]{2,1,0:T(8,128)S(1)}, u32[]{:S(2)}, u32[]{:S(2)}) async-start(f32[8,64,128]{2,1,0:T(8,128)} %bitcast.3), calls=%async_computation | async-start | bytes 524288 | tf_op jit(solution)/shard_map/all_to_all | solution.py:711
  8.2 11.6 %collective-permute-start = (f32[7,24,128]{2,1,0:T(8,128)S(1)}, f32[7,24,128]{2,1,0:T(8,128)S(1)}, u32[]{:S(2)}, u32[]{:S(2)}) collective-permute-start(f32[7,24,128]{2,1,0:T(8,128)S(1)} %get-tuple-element.20), channel_id=1, source_target_pairs={{0,2},{2,4},{4,6},{1,3},{3,5},{5,7},{8,10},{10,12},{12,14},{9,11},... | collective-permute-start | bytes 258056 | tf_op jit(solution)/shard_map/ppermute | solution.py:716
  11.7 8.1 %collective-permute-start.1 = (f32[7,24,128]{2,1,0:T(8,128)S(1)}, f32[7,24,128]{2,1,0:T(8,128)S(1)}, u32[]{:S(2)}, u32[]{:S(2)}) collective-permute-start(f32[7,24,128]{2,1,0:T(8,128)S(1)} %get-tuple-element.21), channel_id=1, source_target_pairs={{2,0},{4,2},{6,4},{3,1},{5,3},{7,5},{10,8},{12,10},{14,12},{11,9},... | collective-permute-start | bytes 258056 | tf_op jit(solution)/shard_map/ppermute | solution.py:717
  20.6 8.3 %all-to-all-start.1 = ((f32[8,16,128]{2,1,0:T(8,128)}), f32[8,16,128]{2,1,0:T(8,128)S(1)}, u32[]{:S(2)}, u32[]{:S(2)}) async-start(f32[8,16,128]{2,1,0:T(8,128)} %add_lines.1), calls=%async_computation.1 | async-start | bytes 131072 | tf_op jit(solution)/shard_map/all_to_all | solution.py:711

commit v7 on v6

--- a/solution.py
+++ b/solution.py
@@ -197,7 +197,7 @@
 
 
 def micro_kernel(
-    capacity, parts, rows, groups, conform_ref, noise_ref, rate_ref,
+    capacity, parts, rows, groups, conform_ref, noise_ref, rate_ref, first_conform_ref, first_noise_ref,
     next_ref, chunk_ref, conform, noise, rate, rate_wide, sums_ref, read_sem, noise_sem,
 ):
     steps, _, slots, dumbbells = noise_ref.shape
@@ -221,10 +221,14 @@
             noise_ref.at[when, :, at, :], noise.at[when, :, at, :], noise_sem.at[block, group]
         )
 
-    for block in range(blocks):
+    assert parts == 4
+    for block in range(1, blocks):
         read(block).start()
         for group in range(groups):
             read_noise(block, group).start()
+    conform[:, 0:rows, :] = first_conform_ref[...]
+    for step in range(steps):
+        noise[step, :, 0:rows, :] = first_noise_ref[step]
     for owner in range(owners):
         rate[owner * capacity : (owner + 1) * capacity, :] = rate_ref[owner, 0:capacity, :]
         chunk_ref[owner] = jnp.zeros(chunk_ref.shape[1:], jnp.float32)
@@ -233,17 +237,16 @@
             column = micro_step * rate[:, 3 * a + b : 3 * a + b + 1] + (1.0 if a == b else 0.0)
             rate_wide[3 * a + b] = jnp.broadcast_to(column, (slots, width))
 
-    def inverses(state):
+    def inverses(state, scale):
         rooms = []
         for part in range(parts):
             q = state[3 * part : 3 * part + 3]
             room = (extent - q[0] * q[0]) - (q[1] * q[1] + q[2] * q[2])
             rooms.append(jnp.maximum(room, extent * spring_floor))
-        result = []
-        for part in range(0, parts, 2):
-            both = pl.reciprocal(rooms[part] * rooms[part + 1], approx=True)
-            result += [both * rooms[part + 1], both * rooms[part]]
-        return result
+        first, second = rooms[0] * rooms[1], rooms[2] * rooms[3]
+        all_four = scale * pl.reciprocal(first * second)
+        first, second = all_four * second, all_four * first
+        return first * rooms[1], first * rooms[0], second * rooms[3], second * rooms[2]
 
     def advance_block(block, carry):
         at = block_rows(block)
@@ -251,10 +254,10 @@
 
         def substep(step, state):
             updated = []
-            inverse = inverses(state)
+            springs = inverses(state, micro_step * relax_rate * extent)
             for part in range(parts):
                 q = state[3 * part : 3 * part + 3]
-                spring = (micro_step * relax_rate * extent) * inverse[part]
+                spring = springs[part]
                 for a in range(3):
                     b, c = [other for other in range(3) if other != a]
                     kick = noise[step, a, at, part * width : (part + 1) * width].astype(jnp.float32)
@@ -263,12 +266,18 @@
             return tuple(updated)
 
         def advance_group(group, state):
-            read_noise(block, group).wait()
+            @pl.when(block > 0)
+            def _():
+                read_noise(block, group).wait()
+
             for step in range(span):
                 state = substep(group * span + step, state)
             return state
 
-        read(block).wait()
+        @pl.when(block > 0)
+        def _():
+            read(block).wait()
+
         state = tuple(
             conform[a, at, part * width : (part + 1) * width] * scale
             for part in range(parts)
@@ -276,7 +285,7 @@
         )
         state = lax.fori_loop(0, groups, advance_group, state, unroll=True)
         sums = [None] * 6
-        inverse = inverses(state)
+        inverse = inverses(state, 1.0)
         for part in range(parts):
             q = state[3 * part : 3 * part + 3]
             for a in range(3):
@@ -299,11 +308,43 @@
         chunk_ref[owner, 0:capacity, :] = packed[owner * capacity : (owner + 1) * capacity]
 
 
-def advance(conformations, increments, chunks, capacity):
+block_slots = 16
+
+
+def first_kernel(rows, after_ref, conform_ref, noise_ref, conform_out, noise_out, sems):
+    copies = (
+        pltpu.make_async_copy(conform_ref.at[:, 0:rows, :], conform_out, sems.at[0]),
+        pltpu.make_async_copy(noise_ref.at[:, :, 0:rows, :], noise_out, sems.at[1]),
+    )
+    for copy in copies:
+        copy.start()
+    for copy in copies:
+        copy.wait()
+
+
+def first_block(after, conformations, increments):
+    steps, _, _, dumbbells = increments.shape
+    whole = pl.BlockSpec(memory_space=pltpu.HBM)
+    return pl.pallas_call(
+        functools.partial(first_kernel, block_slots),
+        out_shape=(
+            pltpu.VMEM((3, block_slots, dumbbells), jnp.float32),
+            pltpu.VMEM((steps, 3, block_slots, dumbbells), jnp.bfloat16),
+        ),
+        in_specs=[pl.BlockSpec(memory_space=pl.ANY), whole, whole],
+        out_specs=(VMEM, VMEM),
+        scratch_shapes=[pltpu.SemaphoreType.DMA((2,))],
+        compiler_params=limit(4),
+        cost_estimate=pl.CostEstimate(flops=0, bytes_accessed=3000000, transcendentals=0),
+        name="first_block",
+    )(after, far(conformations), far(increments))
+
+
+def advance(conformations, increments, chunks, first_conform, first_noise, capacity):
     slots, dumbbells = conformations.shape[1:]
     steps = increments.shape[0]
     owners = slots // capacity
-    rows, parts, groups = 16, 4, 4
+    rows, parts, groups = block_slots, 4, 4
     blocks = slots // rows
     whole = pl.BlockSpec(memory_space=pltpu.HBM)
     return pl.pallas_call(
@@ -312,7 +353,7 @@
             pltpu.VMEM(conformations.shape, jnp.float32),
             jax.ShapeDtypeStruct((owners, slot_rows + line_rows, 128), jnp.float32),
         ),
-        in_specs=[whole, whole, VMEM],
+        in_specs=[whole, whole, VMEM, VMEM, VMEM],
         out_specs=(VMEM, VMEM),
         scratch_shapes=[
             pltpu.VMEM(conformations.shape, jnp.float32),
@@ -326,7 +367,7 @@
         compiler_params=limit(12),
         cost_estimate=pl.CostEstimate(flops=20000000, bytes_accessed=5000000, transcendentals=600000),
         name="advance",
-    )(far(conformations), far(increments), chunks)
+    )(far(conformations), far(increments), chunks, first_conform, first_noise)
 
 
 def lines_kernel(macro_count, chunk_ref, y_low_ref, y_high_ref, out_ref):
@@ -715,7 +756,10 @@
     down = [(target, source) for source, target in up]
     y_low = lax.ppermute(y_last, "tile", up)
     y_high = lax.ppermute(y_first, "tile", down)
-    last_state, polymer = advance(conformations, increments, received, capacity)
+    first_conform, first_noise = first_block(position, conformations, increments)
+    last_state, polymer = advance(
+        conformations, increments, received, first_conform, first_noise, capacity
+    )
     returned = exchange(add_lines(polymer, y_low, y_high))
     partial, corners, edges, lines, pick, spread = flow_step(
         flag_cell, position, velocity, viscosity, received, y_low, y_high

time: 31 us -> 30.2 us (0.974)
  waiting for transfers between devices: 3.89 us -> 2.69 us
    pallas_call x0 -> x1, Pallas kernels: none -> 1.21 us  [first_block(): pl.pallas_call(functools.partial(first_kernel, block_slots), out_shape=(p...]
    all_to_all x2, waiting for transfers between devices: 3.88 us -> 2.68 us  [exchange(): lax.all_to_all(rows, ('macro', 'micro'), split_axis=0, concat_axis=0, til...]
    pallas_call x1, Pallas kernels: 4.66 us -> 3.84 us  [advance(): pl.pallas_call(functools.partial(micro_kernel, capacity, parts, rows, gro...]
  transfers between devices with their start and end apart: 4 -> 4, of which waited for: 2 -> 2; matrix products, arithmetic and copies ran while one was open for 2% -> 3% of each run, Pallas kernels for 23% -> 25%
where the time goes in v7:
time: 30.2 us; the launch traced here: 29.8 us
  starting transfers between devices  13.3 us (44%)
  Pallas kernels  12.3 us (41%)
  waiting for transfers between devices  2.69 us (9%)
  local copies, waits for them, and re-layouts  0.77 us (3%)
  between operations  0.73 us (2%)
    all_to_all x2, starting transfers between devices, exchange(): lax.all_to_all(rows, ('macro', 'micro'), split_axis=0, concat_axis=0, til...  8.53 us
    pallas_call x1, Pallas kernels, advance(): pl.pallas_call(functools.partial(micro_kernel, capacity, parts, rows, gro...  3.84 us
    ppermute x1, starting transfers between devices, shards(): y_low = lax.ppermute(y_last, 'tile', up)  3.47 us
    all_to_all x2, waiting for transfers between devices, exchange(): lax.all_to_all(rows, ('macro', 'micro'), split_axis=0, concat_axis=0, til...  2.68 us
    pallas_call x1, Pallas kernels, flow_step(): pl.pallas_call(functools.partial(flow_kernel, size_x, size_y, size_z, chu...  2.46 us
    pallas_call x1, Pallas kernels, gather_rows(): pl.pallas_call(functools.partial(gather_kernel, capacity, size_x, size_y,...  2.3 us
    pallas_call x1, Pallas kernels, add_polymer(): pl.pallas_call(functools.partial(polymer_kernel, size_x, size_y, size_z,...  1.78 us
    ppermute x1, starting transfers between devices, shards(): y_high = lax.ppermute(y_first, 'tile', down)  1.29 us
  transfers between devices with their start and end apart: 4, of which 2 were waited for; matrix products, arithmetic and copies ran while one was open for 3% of the time, Pallas kernels for 25%

profile of v7, /device:TPU:0, one launch (start us, length us, event | category | flops | bytes accessed | tf_op | source)
XLA Modules:
  0.0 29.8 jit_solution(15987302552058521672)
XLA Ops:
  0.6 2.3 %gather_rows.1 = (f32[512,128]{1,0:T(8,128)}, s32[32]{0:T(128)S(1)}, f32[32,128]{1,0:T(8,128)S(1)}, f32[7,24,128]{2,1,0:T(8,128)S(1)}, f32[7,24,128]{2,1,0:T(8,128)S(1)}) custom-call(s32[32]{0:T(128)} %cell_ref.1, s32[32]{0:T(128)} %bitcast.11, f32[3,192,128]{2,1,0:T(8,128)} %bitcast.6, f32[192,128]{1,0:T(8,128)} %bitcast.8), custom_call_target="tpu_custom_call" | custom-call | flops 400000 | bytes 3000000 | tf_op jit(solution)/shard_map/gather_rows/pallas_call | solution.py:166
  2.9 5.2 %all-to-all-start = ((f32[8,64,128]{2,1,0:T(8,128)}), f32[8,64,128]{2,1,0:T(8,128)S(1)}, u32[]{:S(2)}, u32[]{:S(2)}) async-start(f32[8,64,128]{2,1,0:T(8,128)} %bitcast.3), calls=%async_computation | async-start | bytes 524288 | tf_op jit(solution)/shard_map/all_to_all | solution.py:752
  8.1 3.5 %collective-permute-start = (f32[7,24,128]{2,1,0:T(8,128)S(1)}, f32[7,24,128]{2,1,0:T(8,128)S(1)}, u32[]{:S(2)}, u32[]{:S(2)}) collective-permute-start(f32[7,24,128]{2,1,0:T(8,128)S(1)} %get-tuple-element.25), channel_id=1, source_target_pairs={{0,2},{2,4},{4,6},{1,3},{3,5},{5,7},{8,10},{10,12},{12,14},{9,11},... | collective-permute-start | bytes 258056 | tf_op jit(solution)/shard_map/ppermute | solution.py:757
  11.6 1.3 %collective-permute-start.1 = (f32[7,24,128]{2,1,0:T(8,128)S(1)}, f32[7,24,128]{2,1,0:T(8,128)S(1)}, u32[]{:S(2)}, u32[]{:S(2)}) collective-permute-start(f32[7,24,128]{2,1,0:T(8,128)S(1)} %get-tuple-element.26), channel_id=1, source_target_pairs={{2,0},{4,2},{6,4},{3,1},{5,3},{7,5},{10,8},{12,10},{14,12},{11,9},... | collective-permute-start | bytes 258056 | tf_op jit(solution)/shard_map/ppermute | solution.py:758
  12.9 1.2 %first_block.1 = (f32[3,16,512]{2,1,0:T(8,128)S(1)}, bf16[16,3,16,512]{3,2,1,0:T(8,128)(2,1)S(1)}) custom-call(s32[32]{0:T(128)S(1)} %get-tuple-element.21.after_ref.position_ref, f32[3,64,512]{2,1,0:T(8,128)} %conform_ref.3, bf16[16,3,64,512]{3,2,1,0:T(8,128)(2,1)} %noise_ref.3), custom_call_target="tpu_custom_call" | custom-call | bytes 3000000 | tf_op jit(solution)/shard_map/first_block/pallas_call | solution.py:328
  14.1 0.0 copy-start
  14.1 0.0 copy-start.1
  14.1 0.0 copy-start.2
  14.2 0.9 %all-to-all-done.rate_ref.chunk_ref = f32[8,64,128]{2,1,0:T(8,128)S(1)} async-done(((f32[8,64,128]{2,1,0:T(8,128)}), f32[8,64,128]{2,1,0:T(8,128)S(1)}, u32[]{:S(2)}, u32[]{:S(2)}) %all-to-all-start) | async-done | bytes 262176 | tf_op jit(solution)/shard_map/all_to_all | solution.py:752
  15.1 3.8 %advance.1 = (f32[3,64,512]{2,1,0:T(8,128)S(1)}, f32[8,16,128]{2,1,0:T(8,128)S(1)}) custom-call(f32[3,64,512]{2,1,0:T(8,128)} %conform_ref.3, bf16[16,3,64,512]{3,2,1,0:T(8,128)(2,1)} %noise_ref.3, f32[8,64,128]{2,1,0:T(8,128)S(1)} %all-to-all-done.rate_ref.chunk_ref, f32[3,16,512]{2,1,0:T(8,128)S(1)} %get-tuple-element.22.first_conform_ref, ...), custom_call_target="tpu_custom_call" | custom-call | flops 20000000 | bytes 5000000 | tf_op jit(solution)/shard_map/advance/pallas_call | solution.py:350
  18.9 0.0 collective-permute-done.y_low_ref
  18.9 0.0 collective-permute-done.1.y_high_ref
  18.9 0.7 %add_lines.1 = f32[8,16,128]{2,1,0:T(8,128)} custom-call(f32[8,16,128]{2,1,0:T(8,128)S(1)} %get-tuple-element.24.chunk_ref, f32[7,24,128]{2,1,0:T(8,128)S(1)} %collective-permute-done.y_low_ref, f32[7,24,128]{2,1,0:T(8,128)S(1)} %collective-permute-done.1.y_high_ref), custom_call_target="tpu_custom_call" | custom-call | flops 20000 | bytes 400000 | tf_op jit(solution)/shard_map/add_lines/pallas_call | solution.py:403
  19.7 3.4 %all-to-all-start.1 = ((f32[8,16,128]{2,1,0:T(8,128)}), f32[8,16,128]{2,1,0:T(8,128)S(1)}, u32[]{:S(2)}, u32[]{:S(2)}) async-start(f32[8,16,128]{2,1,0:T(8,128)} %add_lines.1), calls=%async_computation.1 | async-start | bytes 131072 | tf_op jit(solution)/shard_map/all_to_all | solution.py:752
  23.0 0.7 %copy.9 = f32[3,64,512]{2,1,0:T(8,128)} copy(f32[3,64,512]{2,1,0:T(8,128)S(1)} %get-tuple-element.38) | data formatting | bytes 786432
  23.8 0.0 copy-done
  23.8 0.0 copy-done.1
  23.8 0.0 copy-done.2
  23.8 2.5 %flow_step.1 = (f32[3,192,128]{2,1,0:T(8,128)S(1)}, f32[8,128]{1,0:T(8,128)S(1)}, f32[4,24,128]{2,1,0:T(8,128)S(1)}, f32[2,32,128]{2,1,0:T(8,128)S(1)}, bf16[32,...) custom-call(s32[32]{0:T(128)S(1)} %copy-done.2, s32[32]{0:T(128)S(1)} %get-tuple-element.21.after_ref.position_ref, ...), custom_call_target="tpu_custom_call" | custom-call | flops 4000000 | bytes 3000000 | tf_op jit(solution)/shard_map/flow_step/pallas_call | solution.py:623
  26.2 1.8 %all-to-all-done.1 = f32[8,16,128]{2,1,0:T(8,128)S(1)} async-done(((f32[8,16,128]{2,1,0:T(8,128)}), f32[8,16,128]{2,1,0:T(8,128)S(1)}, u32[]{:S(2)}, u32[]{:S(2)}) %all-to-all-start.1) | async-done | bytes 65568 | tf_op jit(solution)/shard_map/all_to_all | solution.py:752
  28.0 1.8 %add_polymer.1 = (f32[3,192,128]{2,1,0:T(8,128)}, f32[6,32]{1,0:T(8,128)}) custom-call(f32[128,128]{1,0:T(8,128)S(1)} %bitcast.10, f32[32,128]{1,0:T(8,128)S(1)} %get-tuple-element.27.viscous_ref, f32[8,128]{1,0:T(8,128)S(1)} %get-tuple-element.28.corner_ref, f32[4,24,128]{2,1,0:T(8,128)S(1)} %get-tuple-element.29.edge_ref, ...), custom_call_target="tpu_custom_call" | custom-call | flops 400000 | bytes 3000000 | tf_op jit(solution)/shard_map/add_polymer/pallas_call | solution.py:724
Async XLA Ops:
  2.9 12.1 %all-to-all-start = ((f32[8,64,128]{2,1,0:T(8,128)}), f32[8,64,128]{2,1,0:T(8,128)S(1)}, u32[]{:S(2)}, u32[]{:S(2)}) async-start(f32[8,64,128]{2,1,0:T(8,128)} %bitcast.3), calls=%async_computation | async-start | bytes 524288 | tf_op jit(solution)/shard_map/all_to_all | solution.py:752
  8.1 10.8 %collective-permute-start = (f32[7,24,128]{2,1,0:T(8,128)S(1)}, f32[7,24,128]{2,1,0:T(8,128)S(1)}, u32[]{:S(2)}, u32[]{:S(2)}) collective-permute-start(f32[7,24,128]{2,1,0:T(8,128)S(1)} %get-tuple-element.25), channel_id=1, source_target_pairs={{0,2},{2,4},{4,6},{1,3},{3,5},{5,7},{8,10},{10,12},{12,14},{9,11},... | collective-permute-start | bytes 258056 | tf_op jit(solution)/shard_map/ppermute | solution.py:757
  11.6 7.3 %collective-permute-start.1 = (f32[7,24,128]{2,1,0:T(8,128)S(1)}, f32[7,24,128]{2,1,0:T(8,128)S(1)}, u32[]{:S(2)}, u32[]{:S(2)}) collective-permute-start(f32[7,24,128]{2,1,0:T(8,128)S(1)} %get-tuple-element.26), channel_id=1, source_target_pairs={{2,0},{4,2},{6,4},{3,1},{5,3},{7,5},{10,8},{12,10},{14,12},{11,9},... | collective-permute-start | bytes 258056 | tf_op jit(solution)/shard_map/ppermute | solution.py:758
  14.1 9.7 %copy-start = (f32[3,24,8,128]{3,2,1,0:T(8,128)S(1)}, f32[3,24,8,128]{3,2,1,0:T(8,128)}, u32[]{:S(2)}) copy-start(f32[3,24,8,128]{3,2,1,0:T(8,128)} %param.6) | copy-start | bytes 884740
  14.1 9.6 %copy-start.1 = (f32[24,8,128]{2,1,0:T(8,128)S(1)}, f32[24,8,128]{2,1,0:T(8,128)}, u32[]{:S(2)}) copy-start(f32[24,8,128]{2,1,0:T(8,128)} %param.7) | copy-start | bytes 294916
  14.1 9.6 %copy-start.2 = (s32[32]{0:T(128)S(1)}, s32[32]{0:T(128)}, u32[]{:S(2)}) copy-start(s32[32]{0:T(128)} %cell_ref.1) | copy-start | bytes 388
  19.7 8.4 %all-to-all-start.1 = ((f32[8,16,128]{2,1,0:T(8,128)}), f32[8,16,128]{2,1,0:T(8,128)S(1)}, u32[]{:S(2)}, u32[]{:S(2)}) async-start(f32[8,16,128]{2,1,0:T(8,128)} %add_lines.1), calls=%async_computation.1 | async-start | bytes 131072 | tf_op jit(solution)/shard_map/all_to_all | solution.py:752

commit v8 on v7

--- a/solution.py
+++ b/solution.py
@@ -86,19 +86,23 @@
         position_ref[j] = owner * (slot_rows + line_rows) + rank
     for copy in copies[2:]:
         copy.wait()
+    planes = velocity_ref.reshape(3, size_x, size_y, size_z)
+    layers = viscosity_ref.reshape(size_x, size_y, size_z)
     for j in range(flags):
         cell = cell_ref[j]
-        row = lax.div(cell, size_z)
-        z = cell - row * size_z
+        x = lax.shift_right_logical(cell, 10)
+        y = lax.shift_right_logical(cell, 7) & (size_y - 1)
+        z = cell & (size_z - 1)
         here = (lane == z).astype(jnp.float32)
         along_z = (lane == z + 1).astype(jnp.float32) - (lane == z - 1).astype(jnp.float32)
+        at = pl.ds(y, 1)
         for a in range(3):
-            along_x = velocity_ref[a, pl.ds(row + size_y, 1), :] - velocity_ref[a, pl.ds(row - size_y, 1), :]
-            along_y = velocity_ref[a, pl.ds(row + 1, 1), :] - velocity_ref[a, pl.ds(row - 1, 1), :]
+            along_x = planes[a, x + 1, at, :] - planes[a, x - 1, at, :]
+            along_y = planes[a, x, pl.ds(y + 1, 1), :] - planes[a, x, pl.ds(y - 1, 1), :]
             masked[3 * a, j : j + 1, :] = along_x * here
             masked[3 * a + 1, j : j + 1, :] = along_y * here
-            masked[3 * a + 2, j : j + 1, :] = velocity_ref[a, pl.ds(row, 1), :] * along_z
-        masked[9, j : j + 1, :] = viscosity_ref[pl.ds(row, 1), :] * here
+            masked[3 * a + 2, j : j + 1, :] = planes[a, x, at, :] * along_z
+        masked[9, j : j + 1, :] = layers[x, at, :] * here
 
     for side, ref in enumerate((y_low_ref, y_high_ref)):
         for layer in range(2):
@@ -222,12 +226,14 @@
         )
 
     assert parts == 4
-    for block in range(1, blocks):
-        read(block).start()
-        for group in range(groups):
+    early = groups // first_share
+    for block in range(blocks):
+        if block > 0:
+            read(block).start()
+        for group in range(early if block == 0 else 0, groups):
             read_noise(block, group).start()
     conform[:, 0:rows, :] = first_conform_ref[...]
-    for step in range(steps):
+    for step in range(steps // first_share):
         noise[step, :, 0:rows, :] = first_noise_ref[step]
     for owner in range(owners):
         rate[owner * capacity : (owner + 1) * capacity, :] = rate_ref[owner, 0:capacity, :]
@@ -266,10 +272,14 @@
             return tuple(updated)
 
         def advance_group(group, state):
-            @pl.when(block > 0)
-            def _():
+            if group < early:
+
+                @pl.when(block > 0)
+                def _():
+                    read_noise(block, group).wait()
+
+            else:
                 read_noise(block, group).wait()
-
             for step in range(span):
                 state = substep(group * span + step, state)
             return state
@@ -283,7 +293,8 @@
             for part in range(parts)
             for a in range(3)
         )
-        state = lax.fori_loop(0, groups, advance_group, state, unroll=True)
+        for group in range(groups):
+            state = advance_group(group, state)
         sums = [None] * 6
         inverse = inverses(state, 1.0)
         for part in range(parts):
@@ -308,13 +319,14 @@
         chunk_ref[owner, 0:capacity, :] = packed[owner * capacity : (owner + 1) * capacity]
 
 
-block_slots = 16
+block_slots = 32
+first_share = 2
 
 
 def first_kernel(rows, after_ref, conform_ref, noise_ref, conform_out, noise_out, sems):
     copies = (
         pltpu.make_async_copy(conform_ref.at[:, 0:rows, :], conform_out, sems.at[0]),
-        pltpu.make_async_copy(noise_ref.at[:, :, 0:rows, :], noise_out, sems.at[1]),
+        pltpu.make_async_copy(noise_ref.at[0 : noise_out.shape[0], :, 0:rows, :], noise_out, sems.at[1]),
     )
     for copy in copies:
         copy.start()
@@ -329,7 +341,7 @@
         functools.partial(first_kernel, block_slots),
         out_shape=(
             pltpu.VMEM((3, block_slots, dumbbells), jnp.float32),
-            pltpu.VMEM((steps, 3, block_slots, dumbbells), jnp.bfloat16),
+            pltpu.VMEM((steps // first_share, 3, block_slots, dumbbells), jnp.bfloat16),
         ),
         in_specs=[pl.BlockSpec(memory_space=pl.ANY), whole, whole],
         out_specs=(VMEM, VMEM),

time: 30.2 us -> 30.1 us (level)
  Pallas kernels: 12.3 us -> 11.8 us
  starting transfers between devices: 13.3 us -> 13.8 us
    pallas_call x1, Pallas kernels: 3.84 us -> 3.2 us  [advance(): pl.pallas_call(functools.partial(micro_kernel, capacity, parts, rows, gro...]
    all_to_all x2, starting transfers between devices: 8.53 us -> 9.06 us  [exchange(): lax.all_to_all(rows, ('macro', 'micro'), split_axis=0, concat_axis=0, til...]
  transfers between devices with their start and end apart: 4 -> 4, of which waited for: 2 -> 2; matrix products, arithmetic and copies ran while one was open for 3% -> 3% of each run, Pallas kernels for 25% -> 23%
where the time goes in v8:
time: 30.1 us; the launch traced here: 29.7 us
  starting transfers between devices  13.8 us (46%)
  Pallas kernels  11.8 us (39%)
  waiting for transfers between devices  2.65 us (9%)
  local copies, waits for them, and re-layouts  0.76 us (3%)
  between operations  0.72 us (2%)
    all_to_all x2, starting transfers between devices, exchange(): lax.all_to_all(rows, ('macro', 'micro'), split_axis=0, concat_axis=0, til...  9.06 us
    ppermute x1, starting transfers between devices, shards(): y_low = lax.ppermute(y_last, 'tile', up)  3.47 us
    pallas_call x1, Pallas kernels, advance(): pl.pallas_call(functools.partial(micro_kernel, capacity, parts, rows, gro...  3.2 us
    all_to_all x2, waiting for transfers between devices, exchange(): lax.all_to_all(rows, ('macro', 'micro'), split_axis=0, concat_axis=0, til...  2.65 us
    pallas_call x1, Pallas kernels, flow_step(): pl.pallas_call(functools.partial(flow_kernel, size_x, size_y, size_z, chu...  2.46 us
    pallas_call x1, Pallas kernels, gather_rows(): pl.pallas_call(functools.partial(gather_kernel, capacity, size_x, size_y,...  2.31 us
    pallas_call x1, Pallas kernels, add_polymer(): pl.pallas_call(functools.partial(polymer_kernel, size_x, size_y, size_z,...  1.78 us
    ppermute x1, starting transfers between devices, shards(): y_high = lax.ppermute(y_first, 'tile', down)  1.29 us
  transfers between devices with their start and end apart: 4, of which 2 were waited for; matrix products, arithmetic and copies ran while one was open for 3% of the time, Pallas kernels for 23%

profile of v8, /device:TPU:0, one launch (start us, length us, event | category | flops | bytes accessed | tf_op | source)
XLA Modules:
  0.0 29.7 jit_solution(18277209168769827809)
XLA Ops:
  0.6 2.3 %gather_rows.1 = (f32[512,128]{1,0:T(8,128)}, s32[32]{0:T(128)S(1)}, f32[32,128]{1,0:T(8,128)S(1)}, f32[7,24,128]{2,1,0:T(8,128)S(1)}, f32[7,24,128]{2,1,0:T(8,128)S(1)}) custom-call(s32[32]{0:T(128)} %cell_ref.1, s32[32]{0:T(128)} %bitcast.11, f32[3,192,128]{2,1,0:T(8,128)} %bitcast.6, f32[192,128]{1,0:T(8,128)} %bitcast.8), custom_call_target="tpu_custom_call" | custom-call | flops 400000 | bytes 3000000 | tf_op jit(solution)/shard_map/gather_rows/pallas_call | solution.py:170
  2.9 5.2 %all-to-all-start = ((f32[8,64,128]{2,1,0:T(8,128)}), f32[8,64,128]{2,1,0:T(8,128)S(1)}, u32[]{:S(2)}, u32[]{:S(2)}) async-start(f32[8,64,128]{2,1,0:T(8,128)} %bitcast.3), calls=%async_computation | async-start | bytes 524288 | tf_op jit(solution)/shard_map/all_to_all | solution.py:764
  8.1 3.5 %collective-permute-start = (f32[7,24,128]{2,1,0:T(8,128)S(1)}, f32[7,24,128]{2,1,0:T(8,128)S(1)}, u32[]{:S(2)}, u32[]{:S(2)}) collective-permute-start(f32[7,24,128]{2,1,0:T(8,128)S(1)} %get-tuple-element.25), channel_id=1, source_target_pairs={{0,2},{2,4},{4,6},{1,3},{3,5},{5,7},{8,10},{10,12},{12,14},{9,11},... | collective-permute-start | bytes 258056 | tf_op jit(solution)/shard_map/ppermute | solution.py:769
  11.6 1.3 %collective-permute-start.1 = (f32[7,24,128]{2,1,0:T(8,128)S(1)}, f32[7,24,128]{2,1,0:T(8,128)S(1)}, u32[]{:S(2)}, u32[]{:S(2)}) collective-permute-start(f32[7,24,128]{2,1,0:T(8,128)S(1)} %get-tuple-element.26), channel_id=1, source_target_pairs={{2,0},{4,2},{6,4},{3,1},{5,3},{7,5},{10,8},{12,10},{14,12},{11,9},... | collective-permute-start | bytes 258056 | tf_op jit(solution)/shard_map/ppermute | solution.py:770
  12.9 1.3 %first_block.1 = (f32[3,32,512]{2,1,0:T(8,128)S(1)}, bf16[8,3,32,512]{3,2,1,0:T(8,128)(2,1)S(1)}) custom-call(s32[32]{0:T(128)S(1)} %get-tuple-element.21.after_ref.position_ref, f32[3,64,512]{2,1,0:T(8,128)} %conform_ref.3, bf16[16,3,64,512]{3,2,1,0:T(8,128)(2,1)} %noise_ref.3), custom_call_target="tpu_custom_call" | custom-call | bytes 3000000 | tf_op jit(solution)/shard_map/first_block/pallas_call | solution.py:340
  14.2 0.0 copy-start
  14.2 0.0 copy-start.1
  14.2 0.0 copy-start.2
  14.2 0.8 %all-to-all-done.rate_ref.chunk_ref = f32[8,64,128]{2,1,0:T(8,128)S(1)} async-done(((f32[8,64,128]{2,1,0:T(8,128)}), f32[8,64,128]{2,1,0:T(8,128)S(1)}, u32[]{:S(2)}, u32[]{:S(2)}) %all-to-all-start) | async-done | bytes 262176 | tf_op jit(solution)/shard_map/all_to_all | solution.py:764
  15.1 3.2 %advance.1 = (f32[3,64,512]{2,1,0:T(8,128)S(1)}, f32[8,16,128]{2,1,0:T(8,128)S(1)}) custom-call(f32[3,64,512]{2,1,0:T(8,128)} %conform_ref.3, bf16[16,3,64,512]{3,2,1,0:T(8,128)(2,1)} %noise_ref.3, f32[8,64,128]{2,1,0:T(8,128)S(1)} %all-to-all-done.rate_ref.chunk_ref, f32[3,32,512]{2,1,0:T(8,128)S(1)} %get-tuple-element.22.first_conform_ref, ...), custom_call_target="tpu_custom_call" | custom-call | flops 20000000 | bytes 5000000 | tf_op jit(solution)/shard_map/advance/pallas_call | solution.py:362
  18.3 0.0 collective-permute-done.y_low_ref
  18.3 0.0 collective-permute-done.1.y_high_ref
  18.3 0.7 %add_lines.1 = f32[8,16,128]{2,1,0:T(8,128)} custom-call(f32[8,16,128]{2,1,0:T(8,128)S(1)} %get-tuple-element.24.chunk_ref, f32[7,24,128]{2,1,0:T(8,128)S(1)} %collective-permute-done.y_low_ref, f32[7,24,128]{2,1,0:T(8,128)S(1)} %collective-permute-done.1.y_high_ref), custom_call_target="tpu_custom_call" | custom-call | flops 20000 | bytes 400000 | tf_op jit(solution)/shard_map/add_lines/pallas_call | solution.py:415
  19.0 3.9 %all-to-all-start.1 = ((f32[8,16,128]{2,1,0:T(8,128)}), f32[8,16,128]{2,1,0:T(8,128)S(1)}, u32[]{:S(2)}, u32[]{:S(2)}) async-start(f32[8,16,128]{2,1,0:T(8,128)} %add_lines.1), calls=%async_computation.1 | async-start | bytes 131072 | tf_op jit(solution)/shard_map/all_to_all | solution.py:764
  22.9 0.7 %copy.9 = f32[3,64,512]{2,1,0:T(8,128)} copy(f32[3,64,512]{2,1,0:T(8,128)S(1)} %get-tuple-element.38) | data formatting | bytes 786432
  23.7 0.0 copy-done
  23.7 0.0 copy-done.1
  23.7 0.0 copy-done.2
  23.7 2.5 %flow_step.1 = (f32[3,192,128]{2,1,0:T(8,128)S(1)}, f32[8,128]{1,0:T(8,128)S(1)}, f32[4,24,128]{2,1,0:T(8,128)S(1)}, f32[2,32,128]{2,1,0:T(8,128)S(1)}, bf16[32,...) custom-call(s32[32]{0:T(128)S(1)} %copy-done.2, s32[32]{0:T(128)S(1)} %get-tuple-element.21.after_ref.position_ref, ...), custom_call_target="tpu_custom_call" | custom-call | flops 4000000 | bytes 3000000 | tf_op jit(solution)/shard_map/flow_step/pallas_call | solution.py:635
  26.1 1.8 %all-to-all-done.1 = f32[8,16,128]{2,1,0:T(8,128)S(1)} async-done(((f32[8,16,128]{2,1,0:T(8,128)}), f32[8,16,128]{2,1,0:T(8,128)S(1)}, u32[]{:S(2)}, u32[]{:S(2)}) %all-to-all-start.1) | async-done | bytes 65568 | tf_op jit(solution)/shard_map/all_to_all | solution.py:764
  27.9 1.8 %add_polymer.1 = (f32[3,192,128]{2,1,0:T(8,128)}, f32[6,32]{1,0:T(8,128)}) custom-call(f32[128,128]{1,0:T(8,128)S(1)} %bitcast.10, f32[32,128]{1,0:T(8,128)S(1)} %get-tuple-element.27.viscous_ref, f32[8,128]{1,0:T(8,128)S(1)} %get-tuple-element.28.corner_ref, f32[4,24,128]{2,1,0:T(8,128)S(1)} %get-tuple-element.29.edge_ref, ...), custom_call_target="tpu_custom_call" | custom-call | flops 400000 | bytes 3000000 | tf_op jit(solution)/shard_map/add_polymer/pallas_call | solution.py:736
Async XLA Ops:
  2.9 12.1 %all-to-all-start = ((f32[8,64,128]{2,1,0:T(8,128)}), f32[8,64,128]{2,1,0:T(8,128)S(1)}, u32[]{:S(2)}, u32[]{:S(2)}) async-start(f32[8,64,128]{2,1,0:T(8,128)} %bitcast.3), calls=%async_computation | async-start | bytes 524288 | tf_op jit(solution)/shard_map/all_to_all | solution.py:764
  8.1 10.1 %collective-permute-start = (f32[7,24,128]{2,1,0:T(8,128)S(1)}, f32[7,24,128]{2,1,0:T(8,128)S(1)}, u32[]{:S(2)}, u32[]{:S(2)}) collective-permute-start(f32[7,24,128]{2,1,0:T(8,128)S(1)} %get-tuple-element.25), channel_id=1, source_target_pairs={{0,2},{2,4},{4,6},{1,3},{3,5},{5,7},{8,10},{10,12},{12,14},{9,11},... | collective-permute-start | bytes 258056 | tf_op jit(solution)/shard_map/ppermute | solution.py:769
  11.6 6.7 %collective-permute-start.1 = (f32[7,24,128]{2,1,0:T(8,128)S(1)}, f32[7,24,128]{2,1,0:T(8,128)S(1)}, u32[]{:S(2)}, u32[]{:S(2)}) collective-permute-start(f32[7,24,128]{2,1,0:T(8,128)S(1)} %get-tuple-element.26), channel_id=1, source_target_pairs={{2,0},{4,2},{6,4},{3,1},{5,3},{7,5},{10,8},{12,10},{14,12},{11,9},... | collective-permute-start | bytes 258056 | tf_op jit(solution)/shard_map/ppermute | solution.py:770
  14.2 9.5 %copy-start = (f32[3,24,8,128]{3,2,1,0:T(8,128)S(1)}, f32[3,24,8,128]{3,2,1,0:T(8,128)}, u32[]{:S(2)}) copy-start(f32[3,24,8,128]{3,2,1,0:T(8,128)} %param.6) | copy-start | bytes 884740
  14.2 9.5 %copy-start.1 = (f32[24,8,128]{2,1,0:T(8,128)S(1)}, f32[24,8,128]{2,1,0:T(8,128)}, u32[]{:S(2)}) copy-start(f32[24,8,128]{2,1,0:T(8,128)} %param.7) | copy-start | bytes 294916
  14.2 9.5 %copy-start.2 = (s32[32]{0:T(128)S(1)}, s32[32]{0:T(128)}, u32[]{:S(2)}) copy-start(s32[32]{0:T(128)} %cell_ref.1) | copy-start | bytes 388
  19.0 8.9 %all-to-all-start.1 = ((f32[8,16,128]{2,1,0:T(8,128)}), f32[8,16,128]{2,1,0:T(8,128)S(1)}, u32[]{:S(2)}, u32[]{:S(2)}) async-start(f32[8,16,128]{2,1,0:T(8,128)} %add_lines.1), calls=%async_computation.1 | async-start | bytes 131072 | tf_op jit(solution)/shard_map/all_to_all | solution.py:764

commit v9 on v8

--- a/solution.py
+++ b/solution.py
@@ -45,6 +45,10 @@
     return lax.axis_index("macro"), lax.axis_index("micro")
 
 
+def neighbour(index, side, count):
+    return jnp.maximum(index - 1, 0) if side == 0 else jnp.minimum(index + 1, count - 1)
+
+
 def rolled(value, amount):
     size = value.shape[-1]
     if isinstance(amount, int):
@@ -54,7 +58,7 @@
 
 def gather_kernel(
     capacity, size_x, size_y, size_z, macro_count, cell_in, owner_in, velocity_in, viscosity_in,
-    chunk_ref, position_ref, viscous_ref, y_low_ref, y_high_ref,
+    chunk_ref, position_ref, viscous_ref, face_ref,
     cell_ref, owner_ref, velocity_ref, viscosity_ref, masked, gradients, target, count, sems,
 ):
     flags = cell_ref.shape[0]
@@ -104,33 +108,32 @@
             masked[3 * a + 2, j : j + 1, :] = planes[a, x, at, :] * along_z
         masked[9, j : j + 1, :] = layers[x, at, :] * here
 
-    for side, ref in enumerate((y_low_ref, y_high_ref)):
+    tile, tile_count = lax.axis_index("tile"), face_ref.shape[0]
+    for side in range(2):
+        into = neighbour(tile, side, tile_count)
         for layer in range(2):
             y = layer if side == 0 else size_y - 1 - layer
             for a in range(3):
-                ref[3 * layer + a] = velocity_ref[a, pl.ds(y, size_x, stride=size_y), :]
+                face_ref[into, 3 * layer + a] = velocity_ref[a, pl.ds(y, size_x, stride=size_y), :]
         y = 0 if side == 0 else size_y - 1
-        ref[6] = viscosity_ref[pl.ds(y, size_x, stride=size_y), :]
+        face_ref[into, 6] = viscosity_ref[pl.ds(y, size_x, stride=size_y), :]
 
     for side in range(2):
-        beside = macro - 1 if side == 0 else macro + 1
-
-        @pl.when(beside >= 0 if side == 0 else beside < macro_count)
-        def _(side=side, beside=beside):
-            first = pl.multiple_of((2 * beside + core) * chunk_rows + slot_rows, 8)
-            other = pl.multiple_of((2 * beside + 1 - core) * chunk_rows + slot_rows, 8)
-            for layer in range(2):
-                x = layer if side == 0 else size_x - 1 - layer
-                for a in range(3):
-                    chunk_ref[pl.ds(first + (3 * layer + a) * size_y, size_y), :] = velocity_ref[
-                        a, x * size_y : (x + 1) * size_y, :
-                    ]
-            x = 0 if side == 0 else size_x - 1
-            chunk_ref[pl.ds(first + 6 * size_y, size_y), :] = viscosity_ref[x * size_y : (x + 1) * size_y, :]
-            for number, a in enumerate((0, 2)):
-                chunk_ref[pl.ds(other + number * size_y, size_y), :] = velocity_ref[
+        beside = neighbour(macro, side, macro_count)
+        first = pl.multiple_of((2 * beside + core) * chunk_rows + slot_rows, 8)
+        other = pl.multiple_of((2 * beside + 1 - core) * chunk_rows + slot_rows, 8)
+        for layer in range(2):
+            x = layer if side == 0 else size_x - 1 - layer
+            for a in range(3):
+                chunk_ref[pl.ds(first + (3 * layer + a) * size_y, size_y), :] = velocity_ref[
                     a, x * size_y : (x + 1) * size_y, :
                 ]
+        x = 0 if side == 0 else size_x - 1
+        chunk_ref[pl.ds(first + 6 * size_y, size_y), :] = viscosity_ref[x * size_y : (x + 1) * size_y, :]
+        for number, a in enumerate((0, 2)):
+            chunk_ref[pl.ds(other + number * size_y, size_y), :] = velocity_ref[
+                a, x * size_y : (x + 1) * size_y, :
+            ]
 
     group = size_z // 8
     lane2 = lanes_of((size_y, size_z))
@@ -162,22 +165,20 @@
         chunk_ref[pl.ds(target[j], 1), :] = gradients[j : j + 1, :]
 
 
-def gather_rows(flag_cell, owner, velocity, viscosity, capacity, owner_count):
+def gather_rows(flag_cell, owner, velocity, viscosity, capacity, owner_count, tile_count):
     size_x, size_y, size_z = viscosity.shape
     flags = flag_cell.shape[0]
     chunk_rows = slot_rows + item_count * size_y
-    face = jax.ShapeDtypeStruct((item_count, size_x, size_z), jnp.float32)
     return pl.pallas_call(
         functools.partial(gather_kernel, capacity, size_x, size_y, size_z, owner_count // 2),
         out_shape=(
             jax.ShapeDtypeStruct((owner_count * chunk_rows, 128), jnp.float32),
             jax.ShapeDtypeStruct((flags,), jnp.int32),
             jax.ShapeDtypeStruct((flags, 128), jnp.float32),
-            face,
-            face,
+            jax.ShapeDtypeStruct((tile_count, item_count, size_x, size_z), jnp.float32),
         ),
         in_specs=[pl.BlockSpec(memory_space=pltpu.HBM)] * 4,
-        out_specs=(VMEM, SMEM, VMEM, VMEM, VMEM),
+        out_specs=(VMEM, SMEM, VMEM, VMEM),
         scratch_shapes=[
             pltpu.SMEM((flags,), jnp.int32),
             pltpu.SMEM((flags,), jnp.int32),
@@ -225,7 +226,10 @@
             noise_ref.at[when, :, at, :], noise.at[when, :, at, :], noise_sem.at[block, group]
         )
 
-    assert parts == 4
+    pieces = [
+        (half, slice(part * width, (part + 1) * width)) for half in range(rows // 16) for part in range(parts)
+    ]
+    assert len(pieces) == 8
     early = groups // first_share
     for block in range(blocks):
         if block > 0:
@@ -245,30 +249,35 @@
 
     def inverses(state, scale):
         rooms = []
-        for part in range(parts):
-            q = state[3 * part : 3 * part + 3]
+        for piece in range(len(pieces)):
+            q = state[3 * piece : 3 * piece + 3]
             room = (extent - q[0] * q[0]) - (q[1] * q[1] + q[2] * q[2])
             rooms.append(jnp.maximum(room, extent * spring_floor))
-        first, second = rooms[0] * rooms[1], rooms[2] * rooms[3]
-        all_four = scale * pl.reciprocal(first * second)
-        first, second = all_four * second, all_four * first
-        return first * rooms[1], first * rooms[0], second * rooms[3], second * rooms[2]
+        levels = [rooms]
+        while len(levels[-1]) > 1:
+            levels.append([low * high for low, high in zip(levels[-1][0::2], levels[-1][1::2])])
+        result = [scale * pl.reciprocal(levels[-1][0])]
+        for level in reversed(levels[:-1]):
+            result = [result[i // 2] * level[i ^ 1] for i in range(len(level))]
+        return result
 
     def advance_block(block, carry):
-        at = block_rows(block)
-        rates = [[rate_wide.at[3 * a + b, at, :] for b in range(3)] for a in range(3)]
+        ats = [pl.ds(pl.multiple_of(block * rows + 16 * half, 16), 16) for half in range(rows // 16)]
+        rates = [
+            [[rate_wide.at[3 * a + b, at, :] for b in range(3)] for a in range(3)] for at in ats
+        ]
 
         def substep(step, state):
             updated = []
             springs = inverses(state, micro_step * relax_rate * extent)
-            for part in range(parts):
-                q = state[3 * part : 3 * part + 3]
-                spring = springs[part]
+            for piece, (half, lanes) in enumerate(pieces):
+                q = state[3 * piece : 3 * piece + 3]
+                table = rates[half]
                 for a in range(3):
                     b, c = [other for other in range(3) if other != a]
-                    kick = noise[step, a, at, part * width : (part + 1) * width].astype(jnp.float32)
-                    rest = (rates[a][b][...] * q[b] + rates[a][c][...] * q[c]) + kick
-                    updated.append((rates[a][a][...] - spring) * q[a] + rest)
+                    kick = noise[step, a, ats[half], lanes].astype(jnp.float32)
+                    rest = (table[a][b][...] * q[b] + table[a][c][...] * q[c]) + kick
+                    updated.append((table[a][a][...] - springs[piece]) * q[a] + rest)
             return tuple(updated)
 
         def advance_group(group, state):
@@ -288,24 +297,23 @@
         def _():
             read(block).wait()
 
-        state = tuple(
-            conform[a, at, part * width : (part + 1) * width] * scale
-            for part in range(parts)
-            for a in range(3)
-        )
+        state = tuple(conform[a, ats[half], lanes] * scale for half, lanes in pieces for a in range(3))
         for group in range(groups):
             state = advance_group(group, state)
-        sums = [None] * 6
         inverse = inverses(state, 1.0)
-        for part in range(parts):
-            q = state[3 * part : 3 * part + 3]
-            for a in range(3):
-                next_ref[a, at, part * width : (part + 1) * width] = q[a] * noise_weight
-            for k, (a, b) in enumerate(stress_pairs):
-                term = (inverse[part] * q[a]) * q[b]
-                sums[k] = term if sums[k] is None else sums[k] + term
-        for k in range(6):
-            sums_ref[k, at, :] = sums[k]
+        for half, at in enumerate(ats):
+            sums = [None] * 6
+            for piece, (other, lanes) in enumerate(pieces):
+                if other != half:
+                    continue
+                q = state[3 * piece : 3 * piece + 3]
+                for a in range(3):
+                    next_ref[a, at, lanes] = q[a] * noise_weight
+                for k, (a, b) in enumerate(stress_pairs):
+                    term = (inverse[piece] * q[a]) * q[b]
+                    sums[k] = term if sums[k] is None else sums[k] + term
+            for k in range(6):
+                sums_ref[k, at, :] = sums[k]
         return carry
 
     lax.fori_loop(0, blocks, advance_block, 0)
@@ -382,21 +390,24 @@
     )(far(conformations), far(increments), chunks, first_conform, first_noise)
 
 
-def lines_kernel(macro_count, chunk_ref, y_low_ref, y_high_ref, out_ref):
+def lines_kernel(macro_count, chunk_ref, face_ref, out_ref, y_low_ref, y_high_ref):
     out_ref[...] = chunk_ref[...]
     macro, core = place_of()
+    tile, tile_count = lax.axis_index("tile"), face_ref.shape[0]
+    inside = (tile > 0, tile < tile_count - 1)
+    sides = (y_low_ref, y_high_ref)
+    for u in range(2):
+        at = neighbour(tile, u, tile_count)
+        for i in range(item_count):
+            sides[u][i] = jnp.where(inside[u], face_ref[at, i], 0.0)
     size_x, size_z = y_low_ref.shape[1:]
-    sides = (y_low_ref, y_high_ref)
     for side in range(2):
-        beside = macro - 1 if side == 0 else macro + 1
-
-        @pl.when(beside >= 0 if side == 0 else beside < macro_count)
-        def _(side=side, beside=beside):
-            x = 0 if side == 0 else size_x - 1
-            for u in range(2):
-                for a in range(2):
-                    at = slot_rows + 2 * u + a
-                    out_ref[2 * beside + core, at : at + 1, :] = sides[u][a, x : x + 1, :]
+        beside = neighbour(macro, side, macro_count)
+        x = 0 if side == 0 else size_x - 1
+        for u in range(2):
+            for a in range(2):
+                at = slot_rows + 2 * u + a
+                out_ref[2 * beside + core, at : at + 1, :] = sides[u][a, x : x + 1, :]
 
     lane = lanes_of((8, size_z))
     source = jnp.where(core == 0, size_z - 1, 0)
@@ -411,16 +422,17 @@
     out_ref[2 * macro + 1 - core, slot_rows:, :] = total
 
 
-def add_lines(chunks, y_low, y_high):
+def add_lines(chunks, faces):
+    face = jax.ShapeDtypeStruct(faces.shape[1:], jnp.float32)
     return pl.pallas_call(
         functools.partial(lines_kernel, chunks.shape[0] // 2),
-        out_shape=jax.ShapeDtypeStruct(chunks.shape, jnp.float32),
-        in_specs=[VMEM, VMEM, VMEM],
-        out_specs=VMEM,
+        out_shape=(jax.ShapeDtypeStruct(chunks.shape, jnp.float32), face, face),
+        in_specs=[VMEM, VMEM],
+        out_specs=(VMEM, VMEM, VMEM),
         compiler_params=limit(4),
         cost_estimate=pl.CostEstimate(flops=20000, bytes_accessed=400000, transcendentals=0),
         name="add_lines",
-    )(chunks, y_low, y_high)
+    )(chunks, faces)
 
 
 product_depth = 128
@@ -756,23 +768,22 @@
     capacity = conformations.shape[1] // owner_count
     size_x, size_y, size_z = viscosity.shape
     assert capacity <= slot_rows and size_y == 8 and size_z == 128 and size_x % 8 == 0 and size_x <= 48
-    chunks, position, viscous, y_first, y_last = gather_rows(
-        flag_cell, flag_owner.reshape(-1), velocity, viscosity, capacity, owner_count
-    )
-
-    def exchange(rows):
-        return lax.all_to_all(rows, ("macro", "micro"), split_axis=0, concat_axis=0, tiled=True)
-
-    received = exchange(chunks.reshape(owner_count, -1, 128))
-    up = [(i, i + 1) for i in range(tile_count - 1)]
-    down = [(target, source) for source, target in up]
-    y_low = lax.ppermute(y_last, "tile", up)
-    y_high = lax.ppermute(y_first, "tile", down)
+    chunks, position, viscous, faces = gather_rows(
+        flag_cell, flag_owner.reshape(-1), velocity, viscosity, capacity, owner_count, tile_count
+    )
+
+    def exchange(rows, axes):
+        return lax.all_to_all(rows, axes, split_axis=0, concat_axis=0, tiled=True)
+
+    owners = ("macro", "micro")
+    received = exchange(chunks.reshape(owner_count, -1, 128), owners)
+    faces = exchange(faces, "tile")
     first_conform, first_noise = first_block(position, conformations, increments)
     last_state, polymer = advance(
         conformations, increments, received, first_conform, first_noise, capacity
     )
-    returned = exchange(add_lines(polymer, y_low, y_high))
+    polymer, y_low, y_high = add_lines(polymer, faces)
+    returned = exchange(polymer, owners)
     partial, corners, edges, lines, pick, spread = flow_step(
         flag_cell, position, velocity, viscosity, received, y_low, y_high
     )

time: 30.1 us -> 40.8 us (1.36)
  blocking collectives: 0 us -> 11.9 us
  starting transfers between devices: 13.8 us -> 8.22 us
  waiting for transfers between devices: 2.65 us -> 7.17 us
    all_to_all x0 -> x1, blocking collectives: none -> 11.9 us  [exchange(): return lax.all_to_all(rows, axes, split_axis=0, concat_axis=0, tiled=True)]
    ppermute x2 -> x0, starting transfers between devices: 4.76 us -> none  [the longest x1 3.47 us: shards(): y_low = lax.ppermute(y_last, 'tile', up)]
    all_to_all x2, waiting for transfers between devices: 2.65 us -> 7.17 us  [exchange(): return lax.all_to_all(rows, axes, split_axis=0, concat_axis=0, tiled=True)]
    all_to_all x2, starting transfers between devices: 9.06 us -> 8.22 us  [exchange(): return lax.all_to_all(rows, axes, split_axis=0, concat_axis=0, tiled=True)]
  transfers between devices with their start and end apart: 4 -> 2, of which waited for: 2 -> 2; matrix products, arithmetic and copies ran while one was open for 3% -> 2% of each run, Pallas kernels for 23% -> 17%
where the time goes in v9:
time: 40.8 us; the launch traced here: 40.4 us
  blocking collectives  11.9 us (29%)
  Pallas kernels  11.7 us (29%)
  starting transfers between devices  8.22 us (20%)
  waiting for transfers between devices  7.17 us (18%)
  local copies, waits for them, and re-layouts  0.77 us (2%)
  between operations  0.7 us (2%)
    all_to_all x1, blocking collectives, exchange(): return lax.all_to_all(rows, axes, split_axis=0, concat_axis=0, tiled=True)  11.9 us
    all_to_all x2, starting transfers between devices, exchange(): return lax.all_to_all(rows, axes, split_axis=0, concat_axis=0, tiled=True)  8.22 us
    all_to_all x2, waiting for transfers between devices, exchange(): return lax.all_to_all(rows, axes, split_axis=0, concat_axis=0, tiled=True)  7.17 us
    pallas_call x1, Pallas kernels, advance(): pl.pallas_call(functools.partial(micro_kernel, capacity, parts, rows, gro...  3.22 us
    pallas_call x1, Pallas kernels, flow_step(): pl.pallas_call(functools.partial(flow_kernel, size_x, size_y, size_z, chu...  2.46 us
    pallas_call x1, Pallas kernels, gather_rows(): pl.pallas_call(functools.partial(gather_kernel, capacity, size_x, size_y,...  2.19 us
    pallas_call x1, Pallas kernels, add_polymer(): pl.pallas_call(functools.partial(polymer_kernel, size_x, size_y, size_z,...  1.78 us
    pallas_call x1, Pallas kernels, first_block(): pl.pallas_call(functools.partial(first_kernel, block_slots), out_shape=(p...  1.26 us
  transfers between devices with their start and end apart: 2, of which 2 were waited for; matrix products, arithmetic and copies ran while one was open for 2% of the time, Pallas kernels for 17%

profile of v9, /device:TPU:0, one launch (start us, length us, event | category | flops | bytes accessed | tf_op | source)
XLA Modules:
  0.0 40.4 jit_solution(11699963049816923426)
XLA Ops:
  0.6 2.2 %gather_rows.1 = (f32[512,128]{1,0:T(8,128)S(1)}, s32[32]{0:T(128)S(1)}, f32[32,128]{1,0:T(8,128)S(1)}, f32[4,7,24,128]{3,2,1,0:T(8,128)}) custom-call(s32[32]{0:T(128)} %cell_ref.1, s32[32]{0:T(128)} %bitcast.12, f32[3,192,128]{2,1,0:T(8,128)} %bitcast.6, f32[192,128]{1,0:T(8,128)} %bitcast.8), custom_call_target="tpu_custom_call" | custom-call | flops 400000 | bytes 3000000 | tf_op jit(solution)/shard_map/gather_rows/pallas_call | solution.py:172
  2.8 11.9 %all_to_all.15.rate_ref.chunk_ref = f32[8,64,128]{2,1,0:T(8,128)S(1)} all-to-all(f32[8,64,128]{2,1,0:T(8,128)S(1)} %bitcast.11), channel_id=1, replica_groups=mesh['macro'=4,'tile'=4,'micro'=2] {'macro','micro'}, dimensions={0} | all-to-all | bytes 524288 | tf_op jit(solution)/shard_map/all_to_all | solution.py:776
  14.7 4.9 %all-to-all-start.1 = ((f32[4,7,24,128]{3,2,1,0:T(8,128)}), f32[4,7,24,128]{3,2,1,0:T(8,128)S(1)}, u32[]{:S(2)}, u32[]{:S(2)}) async-start(f32[4,7,24,128]{3,2,1,0:T(8,128)} %get-tuple-element.27), calls=%async_computation.1 | async-start | bytes 688128 | tf_op jit(solution)/shard_map/all_to_all | solution.py:776
  19.6 1.3 %first_block.1 = (f32[3,32,512]{2,1,0:T(8,128)S(1)}, bf16[8,3,32,512]{3,2,1,0:T(8,128)(2,1)S(1)}) custom-call(s32[32]{0:T(128)S(1)} %get-tuple-element.23.after_ref.position_ref, f32[3,64,512]{2,1,0:T(8,128)} %conform_ref.3, bf16[16,3,64,512]{3,2,1,0:T(8,128)(2,1)} %noise_ref.3), custom_call_target="tpu_custom_call" | custom-call | bytes 3000000 | tf_op jit(solution)/shard_map/first_block/pallas_call | solution.py:348
  20.9 0.0 copy-start
  20.9 0.0 copy-start.1
  20.9 0.0 copy-start.2
  20.9 3.2 %advance.1 = (f32[3,64,512]{2,1,0:T(8,128)S(1)}, f32[8,16,128]{2,1,0:T(8,128)S(1)}) custom-call(f32[3,64,512]{2,1,0:T(8,128)} %conform_ref.3, bf16[16,3,64,512]{3,2,1,0:T(8,128)(2,1)} %noise_ref.3, f32[8,64,128]{2,1,0:T(8,128)S(1)} %all_to_all.15.rate_ref.chunk_ref, f32[3,32,512]{2,1,0:T(8,128)S(1)} %get-tuple-element.24.first_conform_ref, ...), custom_call_target="tpu_custom_call" | custom-call | flops 20000000 | bytes 5000000 | tf_op jit(solution)/shard_map/advance/pallas_call | solution.py:370
  24.1 5.4 %all-to-all-done.1.face_ref = f32[4,7,24,128]{3,2,1,0:T(8,128)S(1)} async-done(((f32[4,7,24,128]{3,2,1,0:T(8,128)}), f32[4,7,24,128]{3,2,1,0:T(8,128)S(1)}, u32[]{:S(2)}, u32[]{:S(2)}) %all-to-all-start.1) | async-done | bytes 344096 | tf_op jit(solution)/shard_map/all_to_all | solution.py:776
  29.6 0.7 %add_lines.1 = (f32[8,16,128]{2,1,0:T(8,128)}, f32[7,24,128]{2,1,0:T(8,128)S(1)}, f32[7,24,128]{2,1,0:T(8,128)S(1)}) custom-call(f32[8,16,128]{2,1,0:T(8,128)S(1)} %get-tuple-element.26.chunk_ref, f32[4,7,24,128]{3,2,1,0:T(8,128)S(1)} %all-to-all-done.1.face_ref), custom_call_target="tpu_custom_call" | custom-call | flops 20000 | bytes 400000 | tf_op jit(solution)/shard_map/add_lines/pallas_call | solution.py:427
  30.3 3.4 %all-to-all-start.2 = ((f32[8,16,128]{2,1,0:T(8,128)}), f32[8,16,128]{2,1,0:T(8,128)S(1)}, u32[]{:S(2)}, u32[]{:S(2)}) async-start(f32[8,16,128]{2,1,0:T(8,128)} %get-tuple-element.28), calls=%async_computation.2 | async-start | bytes 131072 | tf_op jit(solution)/shard_map/all_to_all | solution.py:776
  33.7 0.7 %copy.9 = f32[3,64,512]{2,1,0:T(8,128)} copy(f32[3,64,512]{2,1,0:T(8,128)S(1)} %get-tuple-element.42) | data formatting | bytes 786432
  34.4 0.0 copy-done
  34.4 0.0 copy-done.1
  34.4 0.0 copy-done.2
  34.4 2.5 %flow_step.1 = (f32[3,192,128]{2,1,0:T(8,128)S(1)}, f32[8,128]{1,0:T(8,128)S(1)}, f32[4,24,128]{2,1,0:T(8,128)S(1)}, f32[2,32,128]{2,1,0:T(8,128)S(1)}, bf16[32,...) custom-call(s32[32]{0:T(128)S(1)} %copy-done.2, s32[32]{0:T(128)S(1)} %get-tuple-element.23.after_ref.position_ref, ...), custom_call_target="tpu_custom_call" | custom-call | flops 4000000 | bytes 3000000 | tf_op jit(solution)/shard_map/flow_step/pallas_call | solution.py:647
  36.9 1.7 %all-to-all-done.2 = f32[8,16,128]{2,1,0:T(8,128)S(1)} async-done(((f32[8,16,128]{2,1,0:T(8,128)}), f32[8,16,128]{2,1,0:T(8,128)S(1)}, u32[]{:S(2)}, u32[]{:S(2)}) %all-to-all-start.2) | async-done | bytes 65568 | tf_op jit(solution)/shard_map/all_to_all | solution.py:776
  38.6 1.8 %add_polymer.1 = (f32[3,192,128]{2,1,0:T(8,128)}, f32[6,32]{1,0:T(8,128)}) custom-call(f32[128,128]{1,0:T(8,128)S(1)} %bitcast.10, f32[32,128]{1,0:T(8,128)S(1)} %get-tuple-element.29.viscous_ref, f32[8,128]{1,0:T(8,128)S(1)} %get-tuple-element.32.corner_ref, f32[4,24,128]{2,1,0:T(8,128)S(1)} %get-tuple-element.33.edge_ref, ...), custom_call_target="tpu_custom_call" | custom-call | flops 400000 | bytes 3000000 | tf_op jit(solution)/shard_map/add_polymer/pallas_call | solution.py:748
Async XLA Ops:
  14.7 14.8 %all-to-all-start.1 = ((f32[4,7,24,128]{3,2,1,0:T(8,128)}), f32[4,7,24,128]{3,2,1,0:T(8,128)S(1)}, u32[]{:S(2)}, u32[]{:S(2)}) async-start(f32[4,7,24,128]{3,2,1,0:T(8,128)} %get-tuple-element.27), calls=%async_computation.1 | async-start | bytes 688128 | tf_op jit(solution)/shard_map/all_to_all | solution.py:776
  20.9 13.6 %copy-start = (f32[3,24,8,128]{3,2,1,0:T(8,128)S(1)}, f32[3,24,8,128]{3,2,1,0:T(8,128)}, u32[]{:S(2)}) copy-start(f32[3,24,8,128]{3,2,1,0:T(8,128)} %param.6) | copy-start | bytes 884740
  20.9 13.6 %copy-start.1 = (f32[24,8,128]{2,1,0:T(8,128)S(1)}, f32[24,8,128]{2,1,0:T(8,128)}, u32[]{:S(2)}) copy-start(f32[24,8,128]{2,1,0:T(8,128)} %param.7) | copy-start | bytes 294916
  20.9 13.5 %copy-start.2 = (s32[32]{0:T(128)S(1)}, s32[32]{0:T(128)}, u32[]{:S(2)}) copy-start(s32[32]{0:T(128)} %cell_ref.1) | copy-start | bytes 388
  30.3 8.3 %all-to-all-start.2 = ((f32[8,16,128]{2,1,0:T(8,128)}), f32[8,16,128]{2,1,0:T(8,128)S(1)}, u32[]{:S(2)}, u32[]{:S(2)}) async-start(f32[8,16,128]{2,1,0:T(8,128)} %get-tuple-element.28), calls=%async_computation.2 | async-start | bytes 131072 | tf_op jit(solution)/shard_map/all_to_all | solution.py:776

commit v10 on v9

--- a/solution.py
+++ b/solution.py
@@ -58,7 +58,7 @@
 
 def gather_kernel(
     capacity, size_x, size_y, size_z, macro_count, cell_in, owner_in, velocity_in, viscosity_in,
-    chunk_ref, position_ref, viscous_ref, face_ref,
+    chunk_ref, position_ref, viscous_ref, y_low_ref, y_high_ref,
     cell_ref, owner_ref, velocity_ref, viscosity_ref, masked, gradients, target, count, sems,
 ):
     flags = cell_ref.shape[0]
@@ -108,15 +108,13 @@
             masked[3 * a + 2, j : j + 1, :] = planes[a, x, at, :] * along_z
         masked[9, j : j + 1, :] = layers[x, at, :] * here
 
-    tile, tile_count = lax.axis_index("tile"), face_ref.shape[0]
-    for side in range(2):
-        into = neighbour(tile, side, tile_count)
+    for side, ref in enumerate((y_low_ref, y_high_ref)):
         for layer in range(2):
             y = layer if side == 0 else size_y - 1 - layer
             for a in range(3):
-                face_ref[into, 3 * layer + a] = velocity_ref[a, pl.ds(y, size_x, stride=size_y), :]
+                ref[3 * layer + a] = velocity_ref[a, pl.ds(y, size_x, stride=size_y), :]
         y = 0 if side == 0 else size_y - 1
-        face_ref[into, 6] = viscosity_ref[pl.ds(y, size_x, stride=size_y), :]
+        ref[6] = viscosity_ref[pl.ds(y, size_x, stride=size_y), :]
 
     for side in range(2):
         beside = neighbour(macro, side, macro_count)
@@ -165,20 +163,22 @@
         chunk_ref[pl.ds(target[j], 1), :] = gradients[j : j + 1, :]
 
 
-def gather_rows(flag_cell, owner, velocity, viscosity, capacity, owner_count, tile_count):
+def gather_rows(flag_cell, owner, velocity, viscosity, capacity, owner_count):
     size_x, size_y, size_z = viscosity.shape
     flags = flag_cell.shape[0]
     chunk_rows = slot_rows + item_count * size_y
+    face = jax.ShapeDtypeStruct((item_count, size_x, size_z), jnp.float32)
     return pl.pallas_call(
         functools.partial(gather_kernel, capacity, size_x, size_y, size_z, owner_count // 2),
         out_shape=(
-            jax.ShapeDtypeStruct((owner_count * chunk_rows, 128), jnp.float32),
+            pltpu.VMEM((owner_count * chunk_rows, 128), jnp.float32),
             jax.ShapeDtypeStruct((flags,), jnp.int32),
             jax.ShapeDtypeStruct((flags, 128), jnp.float32),
-            jax.ShapeDtypeStruct((tile_count, item_count, size_x, size_z), jnp.float32),
+            face,
+            face,
         ),
         in_specs=[pl.BlockSpec(memory_space=pltpu.HBM)] * 4,
-        out_specs=(VMEM, SMEM, VMEM, VMEM),
+        out_specs=(VMEM, SMEM, VMEM, VMEM, VMEM),
         scratch_shapes=[
             pltpu.SMEM((flags,), jnp.int32),
             pltpu.SMEM((flags,), jnp.int32),
@@ -390,16 +390,10 @@
     )(far(conformations), far(increments), chunks, first_conform, first_noise)
 
 
-def lines_kernel(macro_count, chunk_ref, face_ref, out_ref, y_low_ref, y_high_ref):
+def lines_kernel(macro_count, chunk_ref, y_low_ref, y_high_ref, out_ref):
     out_ref[...] = chunk_ref[...]
     macro, core = place_of()
-    tile, tile_count = lax.axis_index("tile"), face_ref.shape[0]
-    inside = (tile > 0, tile < tile_count - 1)
     sides = (y_low_ref, y_high_ref)
-    for u in range(2):
-        at = neighbour(tile, u, tile_count)
-        for i in range(item_count):
-            sides[u][i] = jnp.where(inside[u], face_ref[at, i], 0.0)
     size_x, size_z = y_low_ref.shape[1:]
     for side in range(2):
         beside = neighbour(macro, side, macro_count)
@@ -422,17 +416,16 @@
     out_ref[2 * macro + 1 - core, slot_rows:, :] = total
 
 
-def add_lines(chunks, faces):
-    face = jax.ShapeDtypeStruct(faces.shape[1:], jnp.float32)
+def add_lines(chunks, y_low, y_high):
     return pl.pallas_call(
         functools.partial(lines_kernel, chunks.shape[0] // 2),
-        out_shape=(jax.ShapeDtypeStruct(chunks.shape, jnp.float32), face, face),
-        in_specs=[VMEM, VMEM],
-        out_specs=(VMEM, VMEM, VMEM),
+        out_shape=pltpu.VMEM(chunks.shape, jnp.float32),
+        in_specs=[VMEM, VMEM, VMEM],
+        out_specs=VMEM,
         compiler_params=limit(4),
         cost_estimate=pl.CostEstimate(flops=20000, bytes_accessed=400000, transcendentals=0),
         name="add_lines",
-    )(chunks, faces)
+    )(chunks, y_low, y_high)
 
 
 product_depth = 128
@@ -768,22 +761,23 @@
     capacity = conformations.shape[1] // owner_count
     size_x, size_y, size_z = viscosity.shape
     assert capacity <= slot_rows and size_y == 8 and size_z == 128 and size_x % 8 == 0 and size_x <= 48
-    chunks, position, viscous, faces = gather_rows(
-        flag_cell, flag_owner.reshape(-1), velocity, viscosity, capacity, owner_count, tile_count
-    )
-
-    def exchange(rows, axes):
-        return lax.all_to_all(rows, axes, split_axis=0, concat_axis=0, tiled=True)
-
-    owners = ("macro", "micro")
-    received = exchange(chunks.reshape(owner_count, -1, 128), owners)
-    faces = exchange(faces, "tile")
+    chunks, position, viscous, y_first, y_last = gather_rows(
+        flag_cell, flag_owner.reshape(-1), velocity, viscosity, capacity, owner_count
+    )
+
+    def exchange(rows):
+        return lax.all_to_all(rows, ("macro", "micro"), split_axis=0, concat_axis=0, tiled=True)
+
+    received = exchange(chunks.reshape(owner_count, -1, 128))
+    up = [(i, i + 1) for i in range(tile_count - 1)]
+    down = [(target, source) for source, target in up]
+    y_low = lax.ppermute(y_last, "tile", up)
+    y_high = lax.ppermute(y_first, "tile", down)
     first_conform, first_noise = first_block(position, conformations, increments)
     last_state, polymer = advance(
         conformations, increments, received, first_conform, first_noise, capacity
     )
-    polymer, y_low, y_high = add_lines(polymer, faces)
-    returned = exchange(polymer, owners)
+    returned = exchange(add_lines(polymer, y_low, y_high))
     partial, corners, edges, lines, pick, spread = flow_step(
         flag_cell, position, velocity, viscosity, received, y_low, y_high
     )

time: 40.8 us -> 30 us (0.74)
  blocking collectives: 11.9 us -> 0 us
  starting transfers between devices: 8.22 us -> 13.9 us
  waiting for transfers between devices: 7.17 us -> 2.65 us
    all_to_all x1 -> x0, blocking collectives: 11.9 us -> none  [exchange(): return lax.all_to_all(rows, axes, split_axis=0, concat_axis=0, tiled=True)]
    ppermute x0 -> x2, starting transfers between devices: none -> 4.77 us  [the longest x1 3.48 us: shards(): y_low = lax.ppermute(y_last, 'tile', up)]
    all_to_all x2, waiting for transfers between devices: 7.17 us -> 2.64 us  [exchange(): lax.all_to_all(rows, ('macro', 'micro'), split_axis=0, concat_axis=0, til...]
    all_to_all x2, starting transfers between devices: 8.22 us -> 9.1 us  [exchange(): lax.all_to_all(rows, ('macro', 'micro'), split_axis=0, concat_axis=0, til...]
  transfers between devices with their start and end apart: 2 -> 4, of which waited for: 2 -> 2; matrix products, arithmetic and copies ran while one was open for 2% -> 3% of each run, Pallas kernels for 17% -> 23%
where the time goes in v10:
time: 30 us; the launch traced here: 29.6 us
  starting transfers between devices  13.9 us (46%)
  Pallas kernels  11.6 us (39%)
  waiting for transfers between devices  2.65 us (9%)
  local copies, waits for them, and re-layouts  0.76 us (3%)
  between operations  0.72 us (2%)
    all_to_all x2, starting transfers between devices, exchange(): lax.all_to_all(rows, ('macro', 'micro'), split_axis=0, concat_axis=0, til...  9.1 us
    ppermute x1, starting transfers between devices, shards(): y_low = lax.ppermute(y_last, 'tile', up)  3.48 us
    pallas_call x1, Pallas kernels, advance(): pl.pallas_call(functools.partial(micro_kernel, capacity, parts, rows, gro...  3.17 us
    all_to_all x2, waiting for transfers between devices, exchange(): lax.all_to_all(rows, ('macro', 'micro'), split_axis=0, concat_axis=0, til...  2.64 us
    pallas_call x1, Pallas kernels, flow_step(): pl.pallas_call(functools.partial(flow_kernel, size_x, size_y, size_z, chu...  2.46 us
    pallas_call x1, Pallas kernels, gather_rows(): pl.pallas_call(functools.partial(gather_kernel, capacity, size_x, size_y,...  2.24 us
    pallas_call x1, Pallas kernels, add_polymer(): pl.pallas_call(functools.partial(polymer_kernel, size_x, size_y, size_z,...  1.78 us
    ppermute x1, starting transfers between devices, shards(): y_high = lax.ppermute(y_first, 'tile', down)  1.29 us
  transfers between devices with their start and end apart: 4, of which 2 were waited for; matrix products, arithmetic and copies ran while one was open for 3% of the time, Pallas kernels for 23%

profile of v10, /device:TPU:0, one launch (start us, length us, event | category | flops | bytes accessed | tf_op | source)
XLA Modules:
  0.0 29.6 jit_solution(11276184788243824491)
XLA Ops:
  0.6 2.2 %gather_rows.1 = (f32[512,128]{1,0:T(8,128)}, s32[32]{0:T(128)S(1)}, f32[32,128]{1,0:T(8,128)S(1)}, f32[7,24,128]{2,1,0:T(8,128)S(1)}, f32[7,24,128]{2,1,0:T(8,128)S(1)}) custom-call(s32[32]{0:T(128)} %cell_ref.1, s32[32]{0:T(128)} %bitcast.11, f32[3,192,128]{2,1,0:T(8,128)} %bitcast.6, f32[192,128]{1,0:T(8,128)} %bitcast.8), custom_call_target="tpu_custom_call" | custom-call | flops 400000 | bytes 3000000 | tf_op jit(solution)/shard_map/gather_rows/pallas_call | solution.py:171
  2.9 5.2 %all-to-all-start = ((f32[8,64,128]{2,1,0:T(8,128)}), f32[8,64,128]{2,1,0:T(8,128)S(1)}, u32[]{:S(2)}, u32[]{:S(2)}) async-start(f32[8,64,128]{2,1,0:T(8,128)} %bitcast.3), calls=%async_computation | async-start | bytes 524288 | tf_op jit(solution)/shard_map/all_to_all | solution.py:769
  8.1 3.5 %collective-permute-start = (f32[7,24,128]{2,1,0:T(8,128)S(1)}, f32[7,24,128]{2,1,0:T(8,128)S(1)}, u32[]{:S(2)}, u32[]{:S(2)}) collective-permute-start(f32[7,24,128]{2,1,0:T(8,128)S(1)} %get-tuple-element.25), channel_id=1, source_target_pairs={{0,2},{2,4},{4,6},{1,3},{3,5},{5,7},{8,10},{10,12},{12,14},{9,11},... | collective-permute-start | bytes 258056 | tf_op jit(solution)/shard_map/ppermute | solution.py:774
  11.5 1.3 %collective-permute-start.1 = (f32[7,24,128]{2,1,0:T(8,128)S(1)}, f32[7,24,128]{2,1,0:T(8,128)S(1)}, u32[]{:S(2)}, u32[]{:S(2)}) collective-permute-start(f32[7,24,128]{2,1,0:T(8,128)S(1)} %get-tuple-element.26), channel_id=1, source_target_pairs={{2,0},{4,2},{6,4},{3,1},{5,3},{7,5},{10,8},{12,10},{14,12},{11,9},... | collective-permute-start | bytes 258056 | tf_op jit(solution)/shard_map/ppermute | solution.py:775
  12.8 1.3 %first_block.1 = (f32[3,32,512]{2,1,0:T(8,128)S(1)}, bf16[8,3,32,512]{3,2,1,0:T(8,128)(2,1)S(1)}) custom-call(s32[32]{0:T(128)S(1)} %get-tuple-element.21.after_ref.position_ref, f32[3,64,512]{2,1,0:T(8,128)} %conform_ref.3, bf16[16,3,64,512]{3,2,1,0:T(8,128)(2,1)} %noise_ref.3), custom_call_target="tpu_custom_call" | custom-call | bytes 3000000 | tf_op jit(solution)/shard_map/first_block/pallas_call | solution.py:348
  14.1 0.0 copy-start
  14.1 0.0 copy-start.1
  14.1 0.0 copy-start.2
  14.1 0.8 %all-to-all-done.rate_ref.chunk_ref = f32[8,64,128]{2,1,0:T(8,128)S(1)} async-done(((f32[8,64,128]{2,1,0:T(8,128)}), f32[8,64,128]{2,1,0:T(8,128)S(1)}, u32[]{:S(2)}, u32[]{:S(2)}) %all-to-all-start) | async-done | bytes 262176 | tf_op jit(solution)/shard_map/all_to_all | solution.py:769
  15.0 3.2 %advance.1 = (f32[3,64,512]{2,1,0:T(8,128)S(1)}, f32[8,16,128]{2,1,0:T(8,128)S(1)}) custom-call(f32[3,64,512]{2,1,0:T(8,128)} %conform_ref.3, bf16[16,3,64,512]{3,2,1,0:T(8,128)(2,1)} %noise_ref.3, f32[8,64,128]{2,1,0:T(8,128)S(1)} %all-to-all-done.rate_ref.chunk_ref, f32[3,32,512]{2,1,0:T(8,128)S(1)} %get-tuple-element.22.first_conform_ref, ...), custom_call_target="tpu_custom_call" | custom-call | flops 20000000 | bytes 5000000 | tf_op jit(solution)/shard_map/advance/pallas_call | solution.py:370
  18.2 0.0 collective-permute-done.y_low_ref
  18.2 0.0 collective-permute-done.1.y_high_ref
  18.2 0.7 %add_lines.1 = f32[8,16,128]{2,1,0:T(8,128)} custom-call(f32[8,16,128]{2,1,0:T(8,128)S(1)} %get-tuple-element.24.chunk_ref, f32[7,24,128]{2,1,0:T(8,128)S(1)} %collective-permute-done.y_low_ref, f32[7,24,128]{2,1,0:T(8,128)S(1)} %collective-permute-done.1.y_high_ref), custom_call_target="tpu_custom_call" | custom-call | flops 20000 | bytes 400000 | tf_op jit(solution)/shard_map/add_lines/pallas_call | solution.py:420
  18.9 3.9 %all-to-all-start.1 = ((f32[8,16,128]{2,1,0:T(8,128)}), f32[8,16,128]{2,1,0:T(8,128)S(1)}, u32[]{:S(2)}, u32[]{:S(2)}) async-start(f32[8,16,128]{2,1,0:T(8,128)} %add_lines.1), calls=%async_computation.1 | async-start | bytes 131072 | tf_op jit(solution)/shard_map/all_to_all | solution.py:769
  22.8 0.7 %copy.9 = f32[3,64,512]{2,1,0:T(8,128)} copy(f32[3,64,512]{2,1,0:T(8,128)S(1)} %get-tuple-element.38) | data formatting | bytes 786432
  23.6 0.0 copy-done
  23.6 0.0 copy-done.1
  23.6 0.0 copy-done.2
  23.6 2.5 %flow_step.1 = (f32[3,192,128]{2,1,0:T(8,128)S(1)}, f32[8,128]{1,0:T(8,128)S(1)}, f32[4,24,128]{2,1,0:T(8,128)S(1)}, f32[2,32,128]{2,1,0:T(8,128)S(1)}, bf16[32,...) custom-call(s32[32]{0:T(128)S(1)} %copy-done.2, s32[32]{0:T(128)S(1)} %get-tuple-element.21.after_ref.position_ref, ...), custom_call_target="tpu_custom_call" | custom-call | flops 4000000 | bytes 3000000 | tf_op jit(solution)/shard_map/flow_step/pallas_call | solution.py:640
  26.1 1.8 %all-to-all-done.1 = f32[8,16,128]{2,1,0:T(8,128)S(1)} async-done(((f32[8,16,128]{2,1,0:T(8,128)}), f32[8,16,128]{2,1,0:T(8,128)S(1)}, u32[]{:S(2)}, u32[]{:S(2)}) %all-to-all-start.1) | async-done | bytes 65568 | tf_op jit(solution)/shard_map/all_to_all | solution.py:769
  27.9 1.8 %add_polymer.1 = (f32[3,192,128]{2,1,0:T(8,128)}, f32[6,32]{1,0:T(8,128)}) custom-call(f32[128,128]{1,0:T(8,128)S(1)} %bitcast.10, f32[32,128]{1,0:T(8,128)S(1)} %get-tuple-element.27.viscous_ref, f32[8,128]{1,0:T(8,128)S(1)} %get-tuple-element.28.corner_ref, f32[4,24,128]{2,1,0:T(8,128)S(1)} %get-tuple-element.29.edge_ref, ...), custom_call_target="tpu_custom_call" | custom-call | flops 400000 | bytes 3000000 | tf_op jit(solution)/shard_map/add_polymer/pallas_call | solution.py:741
Async XLA Ops:
  2.9 12.1 %all-to-all-start = ((f32[8,64,128]{2,1,0:T(8,128)}), f32[8,64,128]{2,1,0:T(8,128)S(1)}, u32[]{:S(2)}, u32[]{:S(2)}) async-start(f32[8,64,128]{2,1,0:T(8,128)} %bitcast.3), calls=%async_computation | async-start | bytes 524288 | tf_op jit(solution)/shard_map/all_to_all | solution.py:769
  8.1 10.1 %collective-permute-start = (f32[7,24,128]{2,1,0:T(8,128)S(1)}, f32[7,24,128]{2,1,0:T(8,128)S(1)}, u32[]{:S(2)}, u32[]{:S(2)}) collective-permute-start(f32[7,24,128]{2,1,0:T(8,128)S(1)} %get-tuple-element.25), channel_id=1, source_target_pairs={{0,2},{2,4},{4,6},{1,3},{3,5},{5,7},{8,10},{10,12},{12,14},{9,11},... | collective-permute-start | bytes 258056 | tf_op jit(solution)/shard_map/ppermute | solution.py:774
  11.5 6.6 %collective-permute-start.1 = (f32[7,24,128]{2,1,0:T(8,128)S(1)}, f32[7,24,128]{2,1,0:T(8,128)S(1)}, u32[]{:S(2)}, u32[]{:S(2)}) collective-permute-start(f32[7,24,128]{2,1,0:T(8,128)S(1)} %get-tuple-element.26), channel_id=1, source_target_pairs={{2,0},{4,2},{6,4},{3,1},{5,3},{7,5},{10,8},{12,10},{14,12},{11,9},... | collective-permute-start | bytes 258056 | tf_op jit(solution)/shard_map/ppermute | solution.py:775
  14.1 9.5 %copy-start = (f32[3,24,8,128]{3,2,1,0:T(8,128)S(1)}, f32[3,24,8,128]{3,2,1,0:T(8,128)}, u32[]{:S(2)}) copy-start(f32[3,24,8,128]{3,2,1,0:T(8,128)} %param.6) | copy-start | bytes 884740
  14.1 9.5 %copy-start.1 = (f32[24,8,128]{2,1,0:T(8,128)S(1)}, f32[24,8,128]{2,1,0:T(8,128)}, u32[]{:S(2)}) copy-start(f32[24,8,128]{2,1,0:T(8,128)} %param.7) | copy-start | bytes 294916
  14.1 9.5 %copy-start.2 = (s32[32]{0:T(128)S(1)}, s32[32]{0:T(128)}, u32[]{:S(2)}) copy-start(s32[32]{0:T(128)} %cell_ref.1) | copy-start | bytes 388
  18.9 8.9 %all-to-all-start.1 = ((f32[8,16,128]{2,1,0:T(8,128)}), f32[8,16,128]{2,1,0:T(8,128)S(1)}, u32[]{:S(2)}, u32[]{:S(2)}) async-start(f32[8,16,128]{2,1,0:T(8,128)} %add_lines.1), calls=%async_computation.1 | async-start | bytes 131072 | tf_op jit(solution)/shard_map/all_to_all | solution.py:769

commit v11 on v10

--- a/solution.py
+++ b/solution.py
@@ -33,6 +33,10 @@
 line_rows = 8
 
 
+block_slots = 32
+first_share = 2
+
+
 def limit(mebibytes):
     return pltpu.CompilerParams(vmem_limit_bytes=mebibytes * 1024 * 1024)
 
@@ -58,7 +62,7 @@
 
 def gather_kernel(
     capacity, size_x, size_y, size_z, macro_count, cell_in, owner_in, velocity_in, viscosity_in,
-    chunk_ref, position_ref, viscous_ref, y_low_ref, y_high_ref,
+    conform_in, noise_in, chunk_ref, position_ref, viscous_ref, y_low_ref, y_high_ref, conform_ref, noise_ref,
     cell_ref, owner_ref, velocity_ref, viscosity_ref, masked, gradients, target, count, sems,
 ):
     flags = cell_ref.shape[0]
@@ -67,7 +71,8 @@
         for number, (source, into) in enumerate(
             (
                 (cell_in, cell_ref), (owner_in, owner_ref), (velocity_in, velocity_ref),
-                (viscosity_in, viscosity_ref),
+                (viscosity_in, viscosity_ref), (conform_in.at[:, 0:block_slots, :], conform_ref),
+                (noise_in.at[0 : noise_ref.shape[0], :, 0:block_slots, :], noise_ref),
             )
         )
     ]
@@ -88,7 +93,7 @@
         count[owner] = rank + 1
         target[j] = owner * chunk_rows + rank
         position_ref[j] = owner * (slot_rows + line_rows) + rank
-    for copy in copies[2:]:
+    for copy in copies[2:4]:
         copy.wait()
     planes = velocity_ref.reshape(3, size_x, size_y, size_z)
     layers = viscosity_ref.reshape(size_x, size_y, size_z)
@@ -161,24 +166,29 @@
 
     for j in range(flags):
         chunk_ref[pl.ds(target[j], 1), :] = gradients[j : j + 1, :]
-
-
-def gather_rows(flag_cell, owner, velocity, viscosity, capacity, owner_count):
+    for copy in copies[4:]:
+        copy.wait()
+
+
+def gather_rows(flag_cell, owner, velocity, viscosity, conformations, increments, capacity, owner_count):
     size_x, size_y, size_z = viscosity.shape
     flags = flag_cell.shape[0]
     chunk_rows = slot_rows + item_count * size_y
     face = jax.ShapeDtypeStruct((item_count, size_x, size_z), jnp.float32)
+    steps, _, _, dumbbells = increments.shape
     return pl.pallas_call(
         functools.partial(gather_kernel, capacity, size_x, size_y, size_z, owner_count // 2),
         out_shape=(
-            pltpu.VMEM((owner_count * chunk_rows, 128), jnp.float32),
+            jax.ShapeDtypeStruct((owner_count * chunk_rows, 128), jnp.float32),
             jax.ShapeDtypeStruct((flags,), jnp.int32),
             jax.ShapeDtypeStruct((flags, 128), jnp.float32),
             face,
             face,
+            pltpu.VMEM((3, block_slots, dumbbells), jnp.float32),
+            pltpu.VMEM((steps // first_share, 3, block_slots, dumbbells), jnp.bfloat16),
         ),
-        in_specs=[pl.BlockSpec(memory_space=pltpu.HBM)] * 4,
-        out_specs=(VMEM, SMEM, VMEM, VMEM, VMEM),
+        in_specs=[pl.BlockSpec(memory_space=pltpu.HBM)] * 6,
+        out_specs=(VMEM, SMEM, VMEM, VMEM, VMEM, VMEM, VMEM),
         scratch_shapes=[
             pltpu.SMEM((flags,), jnp.int32),
             pltpu.SMEM((flags,), jnp.int32),
@@ -188,7 +198,7 @@
             pltpu.VMEM((flags, 128), jnp.float32),
             pltpu.SMEM((flags,), jnp.int32),
             pltpu.SMEM((owner_count,), jnp.int32),
-            pltpu.SemaphoreType.DMA((4,)),
+            pltpu.SemaphoreType.DMA((6,)),
         ],
         compiler_params=limit(8),
         cost_estimate=pl.CostEstimate(flops=400000, bytes_accessed=3000000, transcendentals=0),
@@ -198,6 +208,8 @@
         far(owner),
         far(velocity.reshape(3, size_x * size_y, size_z)),
         far(viscosity.reshape(size_x * size_y, size_z)),
+        far(conformations),
+        far(increments),
     )
 
 
@@ -325,39 +337,6 @@
         packed = jnp.where(lane == k, polymer_weight * (mean - (1.0 if a == b else 0.0)), packed)
     for owner in range(owners):
         chunk_ref[owner, 0:capacity, :] = packed[owner * capacity : (owner + 1) * capacity]
-
-
-block_slots = 32
-first_share = 2
-
-
-def first_kernel(rows, after_ref, conform_ref, noise_ref, conform_out, noise_out, sems):
-    copies = (
-        pltpu.make_async_copy(conform_ref.at[:, 0:rows, :], conform_out, sems.at[0]),
-        pltpu.make_async_copy(noise_ref.at[0 : noise_out.shape[0], :, 0:rows, :], noise_out, sems.at[1]),
-    )
-    for copy in copies:
-        copy.start()
-    for copy in copies:
-        copy.wait()
-
-
-def first_block(after, conformations, increments):
-    steps, _, _, dumbbells = increments.shape
-    whole = pl.BlockSpec(memory_space=pltpu.HBM)
-    return pl.pallas_call(
-        functools.partial(first_kernel, block_slots),
-        out_shape=(
-            pltpu.VMEM((3, block_slots, dumbbells), jnp.float32),
-            pltpu.VMEM((steps // first_share, 3, block_slots, dumbbells), jnp.bfloat16),
-        ),
-        in_specs=[pl.BlockSpec(memory_space=pl.ANY), whole, whole],
-        out_specs=(VMEM, VMEM),
-        scratch_shapes=[pltpu.SemaphoreType.DMA((2,))],
-        compiler_params=limit(4),
-        cost_estimate=pl.CostEstimate(flops=0, bytes_accessed=3000000, transcendentals=0),
-        name="first_block",
-    )(after, far(conformations), far(increments))
 
 
 def advance(conformations, increments, chunks, first_conform, first_noise, capacity):
@@ -419,7 +398,7 @@
 def add_lines(chunks, y_low, y_high):
     return pl.pallas_call(
         functools.partial(lines_kernel, chunks.shape[0] // 2),
-        out_shape=pltpu.VMEM(chunks.shape, jnp.float32),
+        out_shape=jax.ShapeDtypeStruct(chunks.shape, jnp.float32),
         in_specs=[VMEM, VMEM, VMEM],
         out_specs=VMEM,
         compiler_params=limit(4),
@@ -761,8 +740,8 @@
     capacity = conformations.shape[1] // owner_count
     size_x, size_y, size_z = viscosity.shape
     assert capacity <= slot_rows and size_y == 8 and size_z == 128 and size_x % 8 == 0 and size_x <= 48
-    chunks, position, viscous, y_first, y_last = gather_rows(
-        flag_cell, flag_owner.reshape(-1), velocity, viscosity, capacity, owner_count
+    chunks, position, viscous, y_first, y_last, first_conform, first_noise = gather_rows(
+        flag_cell, flag_owner.reshape(-1), velocity, viscosity, conformations, increments, capacity, owner_count
     )
 
     def exchange(rows):
@@ -773,7 +752,6 @@
     down = [(target, source) for source, target in up]
     y_low = lax.ppermute(y_last, "tile", up)
     y_high = lax.ppermute(y_first, "tile", down)
-    first_conform, first_noise = first_block(position, conformations, increments)
     last_state, polymer = advance(
         conformations, increments, received, first_conform, first_noise, capacity
     )

time: 30 us -> 30.2 us (level)
  waiting for transfers between devices: 2.65 us -> 3.96 us
  Pallas kernels: 11.6 us -> 10.4 us
    all_to_all x2, waiting for transfers between devices: 2.64 us -> 3.95 us  [exchange(): lax.all_to_all(rows, ('macro', 'micro'), split_axis=0, concat_axis=0, til...]
    pallas_call x1 -> x0, Pallas kernels: 1.26 us -> none  [first_block(): pl.pallas_call(functools.partial(first_kernel, block_slots), out_shape=(p...]
  transfers between devices with their start and end apart: 4 -> 4, of which waited for: 2 -> 2; matrix products, arithmetic and copies ran while one was open for 3% -> 3% of each run, Pallas kernels for 23% -> 19%
where the time goes in v11:
time: 30.2 us; the launch traced here: 29.8 us
  starting transfers between devices  14 us (46%)
  Pallas kernels  10.4 us (34%)
  waiting for transfers between devices  3.96 us (13%)
  local copies, waits for them, and re-layouts  0.76 us (3%)
  between operations  0.71 us (2%)
    all_to_all x2, starting transfers between devices, exchange(): lax.all_to_all(rows, ('macro', 'micro'), split_axis=0, concat_axis=0, til...  9.23 us
    all_to_all x2, waiting for transfers between devices, exchange(): lax.all_to_all(rows, ('macro', 'micro'), split_axis=0, concat_axis=0, til...  3.95 us
    ppermute x1, starting transfers between devices, shards(): y_low = lax.ppermute(y_last, 'tile', up)  3.48 us
    pallas_call x1, Pallas kernels, advance(): pl.pallas_call(functools.partial(micro_kernel, capacity, parts, rows, gro...  3.17 us
    pallas_call x1, Pallas kernels, flow_step(): pl.pallas_call(functools.partial(flow_kernel, size_x, size_y, size_z, chu...  2.46 us
    pallas_call x1, Pallas kernels, gather_rows(): pl.pallas_call(functools.partial(gather_kernel, capacity, size_x, size_y,...  2.26 us
    pallas_call x1, Pallas kernels, add_polymer(): pl.pallas_call(functools.partial(polymer_kernel, size_x, size_y, size_z,...  1.78 us
    ppermute x1, starting transfers between devices, shards(): y_high = lax.ppermute(y_first, 'tile', down)  1.29 us
  transfers between devices with their start and end apart: 4, of which 2 were waited for; matrix products, arithmetic and copies ran while one was open for 3% of the time, Pallas kernels for 19%

profile of v11, /device:TPU:0, one launch (start us, length us, event | category | flops | bytes accessed | tf_op | source)
XLA Modules:
  0.0 29.8 jit_solution(7993030436522086057)
XLA Ops:
  0.6 2.3 %gather_rows.1 = (f32[512,128]{1,0:T(8,128)}, s32[32]{0:T(128)S(1)}, f32[32,128]{1,0:T(8,128)S(1)}, f32[7,24,128]{2,1,0:T(8,128)S(1)}, f32[7,24,128]{2,1,0:T(8,1...) custom-call(s32[32]{0:T(128)} %cell_ref.1, s32[32]{0:T(128)} %bitcast.11, ...), custom_call_target="tpu_custom_call" | custom-call | flops 400000 | bytes 3000000 | tf_op jit(solution)/shard_map/gather_rows/pallas_call | solution.py:179
  2.9 0.0 copy-start
  2.9 0.0 copy-start.1
  2.9 0.0 copy-start.2
  2.9 5.3 %all-to-all-start = ((f32[8,64,128]{2,1,0:T(8,128)}), f32[8,64,128]{2,1,0:T(8,128)S(1)}, u32[]{:S(2)}, u32[]{:S(2)}) async-start(f32[8,64,128]{2,1,0:T(8,128)} %bitcast.3), calls=%async_computation | async-start | bytes 524288 | tf_op jit(solution)/shard_map/all_to_all | solution.py:748
  8.2 3.5 %collective-permute-start = (f32[7,24,128]{2,1,0:T(8,128)S(1)}, f32[7,24,128]{2,1,0:T(8,128)S(1)}, u32[]{:S(2)}, u32[]{:S(2)}) collective-permute-start(f32[7,24,128]{2,1,0:T(8,128)S(1)} %get-tuple-element.24), channel_id=1, source_target_pairs={{0,2},{2,4},{4,6},{1,3},{3,5},{5,7},{8,10},{10,12},{12,14},{9,11},... | collective-permute-start | bytes 258056 | tf_op jit(solution)/shard_map/ppermute | solution.py:753
  11.7 1.3 %collective-permute-start.1 = (f32[7,24,128]{2,1,0:T(8,128)S(1)}, f32[7,24,128]{2,1,0:T(8,128)S(1)}, u32[]{:S(2)}, u32[]{:S(2)}) collective-permute-start(f32[7,24,128]{2,1,0:T(8,128)S(1)} %get-tuple-element.25), channel_id=1, source_target_pairs={{2,0},{4,2},{6,4},{3,1},{5,3},{7,5},{10,8},{12,10},{14,12},{11,9},... | collective-permute-start | bytes 258056 | tf_op jit(solution)/shard_map/ppermute | solution.py:754
  13.0 2.2 %all-to-all-done.rate_ref.chunk_ref = f32[8,64,128]{2,1,0:T(8,128)S(1)} async-done(((f32[8,64,128]{2,1,0:T(8,128)}), f32[8,64,128]{2,1,0:T(8,128)S(1)}, u32[]{:S(2)}, u32[]{:S(2)}) %all-to-all-start) | async-done | bytes 262176 | tf_op jit(solution)/shard_map/all_to_all | solution.py:748
  15.2 3.2 %advance.1 = (f32[3,64,512]{2,1,0:T(8,128)S(1)}, f32[8,16,128]{2,1,0:T(8,128)S(1)}) custom-call(f32[3,64,512]{2,1,0:T(8,128)} %conform_ref.1, bf16[16,3,64,512]{3,2,1,0:T(8,128)(2,1)} %noise_ref.1, f32[8,64,128]{2,1,0:T(8,128)S(1)} %all-to-all-done.rate_ref.chunk_ref, f32[3,32,512]{2,1,0:T(8,128)S(1)} %get-tuple-element.21.first_conform_ref, ...), custom_call_target="tpu_custom_call" | custom-call | flops 20000000 | bytes 5000000 | tf_op jit(solution)/shard_map/advance/pallas_call | solution.py:349
  18.4 0.0 collective-permute-done.y_low_ref
  18.4 0.0 collective-permute-done.1.y_high_ref
  18.4 0.7 %add_lines.1 = f32[8,16,128]{2,1,0:T(8,128)} custom-call(f32[8,16,128]{2,1,0:T(8,128)S(1)} %get-tuple-element.23.chunk_ref, f32[7,24,128]{2,1,0:T(8,128)S(1)} %collective-permute-done.y_low_ref, f32[7,24,128]{2,1,0:T(8,128)S(1)} %collective-permute-done.1.y_high_ref), custom_call_target="tpu_custom_call" | custom-call | flops 20000 | bytes 400000 | tf_op jit(solution)/shard_map/add_lines/pallas_call | solution.py:399
  19.1 3.9 %all-to-all-start.1 = ((f32[8,16,128]{2,1,0:T(8,128)}), f32[8,16,128]{2,1,0:T(8,128)S(1)}, u32[]{:S(2)}, u32[]{:S(2)}) async-start(f32[8,16,128]{2,1,0:T(8,128)} %add_lines.1), calls=%async_computation.1 | async-start | bytes 131072 | tf_op jit(solution)/shard_map/all_to_all | solution.py:748
  23.0 0.7 %copy.9 = f32[3,64,512]{2,1,0:T(8,128)} copy(f32[3,64,512]{2,1,0:T(8,128)S(1)} %get-tuple-element.38) | data formatting | bytes 786432
  23.8 0.0 copy-done
  23.8 0.0 copy-done.1
  23.8 0.0 copy-done.2
  23.8 2.5 %flow_step.1 = (f32[3,192,128]{2,1,0:T(8,128)S(1)}, f32[8,128]{1,0:T(8,128)S(1)}, f32[4,24,128]{2,1,0:T(8,128)S(1)}, f32[2,32,128]{2,1,0:T(8,128)S(1)}, bf16[32,...) custom-call(s32[32]{0:T(128)S(1)} %copy-done.2, s32[32]{0:T(128)S(1)} %get-tuple-element.27.position_ref, ...), custom_call_target="tpu_custom_call" | custom-call | flops 4000000 | bytes 3000000 | tf_op jit(solution)/shard_map/flow_step/pallas_call | solution.py:619
  26.3 1.8 %all-to-all-done.1 = f32[8,16,128]{2,1,0:T(8,128)S(1)} async-done(((f32[8,16,128]{2,1,0:T(8,128)}), f32[8,16,128]{2,1,0:T(8,128)S(1)}, u32[]{:S(2)}, u32[]{:S(2)}) %all-to-all-start.1) | async-done | bytes 65568 | tf_op jit(solution)/shard_map/all_to_all | solution.py:748
  28.1 1.8 %add_polymer.1 = (f32[3,192,128]{2,1,0:T(8,128)}, f32[6,32]{1,0:T(8,128)}) custom-call(f32[128,128]{1,0:T(8,128)S(1)} %bitcast.10, f32[32,128]{1,0:T(8,128)S(1)} %get-tuple-element.26.viscous_ref, f32[8,128]{1,0:T(8,128)S(1)} %get-tuple-element.28.corner_ref, f32[4,24,128]{2,1,0:T(8,128)S(1)} %get-tuple-element.29.edge_ref, ...), custom_call_target="tpu_custom_call" | custom-call | flops 400000 | bytes 3000000 | tf_op jit(solution)/shard_map/add_polymer/pallas_call | solution.py:720
Async XLA Ops:
  2.9 20.9 %copy-start = (f32[3,24,8,128]{3,2,1,0:T(8,128)S(1)}, f32[3,24,8,128]{3,2,1,0:T(8,128)}, u32[]{:S(2)}) copy-start(f32[3,24,8,128]{3,2,1,0:T(8,128)} %param.6) | copy-start | bytes 884740
  2.9 20.9 %copy-start.1 = (f32[24,8,128]{2,1,0:T(8,128)S(1)}, f32[24,8,128]{2,1,0:T(8,128)}, u32[]{:S(2)}) copy-start(f32[24,8,128]{2,1,0:T(8,128)} %param.7) | copy-start | bytes 294916
  2.9 20.9 %copy-start.2 = (s32[32]{0:T(128)S(1)}, s32[32]{0:T(128)}, u32[]{:S(2)}) copy-start(s32[32]{0:T(128)} %cell_ref.1) | copy-start | bytes 388
  2.9 12.2 %all-to-all-start = ((f32[8,64,128]{2,1,0:T(8,128)}), f32[8,64,128]{2,1,0:T(8,128)S(1)}, u32[]{:S(2)}, u32[]{:S(2)}) async-start(f32[8,64,128]{2,1,0:T(8,128)} %bitcast.3), calls=%async_computation | async-start | bytes 524288 | tf_op jit(solution)/shard_map/all_to_all | solution.py:748
  8.2 10.1 %collective-permute-start = (f32[7,24,128]{2,1,0:T(8,128)S(1)}, f32[7,24,128]{2,1,0:T(8,128)S(1)}, u32[]{:S(2)}, u32[]{:S(2)}) collective-permute-start(f32[7,24,128]{2,1,0:T(8,128)S(1)} %get-tuple-element.24), channel_id=1, source_target_pairs={{0,2},{2,4},{4,6},{1,3},{3,5},{5,7},{8,10},{10,12},{12,14},{9,11},... | collective-permute-start | bytes 258056 | tf_op jit(solution)/shard_map/ppermute | solution.py:753
  11.7 6.6 %collective-permute-start.1 = (f32[7,24,128]{2,1,0:T(8,128)S(1)}, f32[7,24,128]{2,1,0:T(8,128)S(1)}, u32[]{:S(2)}, u32[]{:S(2)}) collective-permute-start(f32[7,24,128]{2,1,0:T(8,128)S(1)} %get-tuple-element.25), channel_id=1, source_target_pairs={{2,0},{4,2},{6,4},{3,1},{5,3},{7,5},{10,8},{12,10},{14,12},{11,9},... | collective-permute-start | bytes 258056 | tf_op jit(solution)/shard_map/ppermute | solution.py:754
  19.1 8.9 %all-to-all-start.1 = ((f32[8,16,128]{2,1,0:T(8,128)}), f32[8,16,128]{2,1,0:T(8,128)S(1)}, u32[]{:S(2)}, u32[]{:S(2)}) async-start(f32[8,16,128]{2,1,0:T(8,128)} %add_lines.1), calls=%async_computation.1 | async-start | bytes 131072 | tf_op jit(solution)/shard_map/all_to_all | solution.py:748

commit v12 on v11

--- a/solution.py
+++ b/solution.py
@@ -30,7 +30,9 @@
 
 slot_rows = 8
 item_count = 7
-line_rows = 8
+back_rows = 8
+polymer_row = 4
+line_lane = 64
 
 
 block_slots = 32
@@ -92,7 +94,7 @@
         rank = count[owner]
         count[owner] = rank + 1
         target[j] = owner * chunk_rows + rank
-        position_ref[j] = owner * (slot_rows + line_rows) + rank
+        position_ref[j] = owner * slot_rows + rank
     for copy in copies[2:4]:
         copy.wait()
     planes = velocity_ref.reshape(3, size_x, size_y, size_z)
@@ -174,7 +176,7 @@
     size_x, size_y, size_z = viscosity.shape
     flags = flag_cell.shape[0]
     chunk_rows = slot_rows + item_count * size_y
-    face = jax.ShapeDtypeStruct((item_count, size_x, size_z), jnp.float32)
+    face = pltpu.HBM((item_count, size_x, size_z), jnp.float32)
     steps, _, _, dumbbells = increments.shape
     return pl.pallas_call(
         functools.partial(gather_kernel, capacity, size_x, size_y, size_z, owner_count // 2),
@@ -330,13 +332,16 @@
 
     lax.fori_loop(0, blocks, advance_block, 0)
     lane = lanes_of((slots, 128))
+    rank = lax.broadcasted_iota(jnp.int32, (slots, 128), 0) & (capacity - 1)
     packed = jnp.zeros((slots, 128), jnp.float32)
     weight = extent * noise_weight * noise_weight / dumbbells
     for k, (a, b) in enumerate(stress_pairs):
         mean = jnp.sum(sums_ref[k], axis=1, keepdims=True) * weight
-        packed = jnp.where(lane == k, polymer_weight * (mean - (1.0 if a == b else 0.0)), packed)
+        packed = jnp.where(lane == 8 * rank + k, polymer_weight * (mean - (1.0 if a == b else 0.0)), packed)
     for owner in range(owners):
-        chunk_ref[owner, 0:capacity, :] = packed[owner * capacity : (owner + 1) * capacity]
+        chunk_ref[owner, polymer_row : polymer_row + 1, :] = jnp.sum(
+            packed[owner * capacity : (owner + 1) * capacity], axis=0, keepdims=True
+        )
 
 
 def advance(conformations, increments, chunks, first_conform, first_noise, capacity):
@@ -350,7 +355,7 @@
         functools.partial(micro_kernel, capacity, parts, rows, groups),
         out_shape=(
             pltpu.VMEM(conformations.shape, jnp.float32),
-            jax.ShapeDtypeStruct((owners, slot_rows + line_rows, 128), jnp.float32),
+            jax.ShapeDtypeStruct((owners, back_rows, 128), jnp.float32),
         ),
         in_specs=[whole, whole, VMEM, VMEM, VMEM],
         out_specs=(VMEM, VMEM),
@@ -379,20 +384,21 @@
         x = 0 if side == 0 else size_x - 1
         for u in range(2):
             for a in range(2):
-                at = slot_rows + 2 * u + a
+                at = 2 * u + a
                 out_ref[2 * beside + core, at : at + 1, :] = sides[u][a, x : x + 1, :]
 
     lane = lanes_of((8, size_z))
     source = jnp.where(core == 0, size_z - 1, 0)
-    total = jnp.zeros((8, size_z), jnp.float32)
+    other = 2 * macro + 1 - core
+    total = chunk_ref[other]
     for i in range(size_x // 8):
         for u in range(2):
             for a in range(2):
-                at = 4 * i + 2 * u + a
+                at = line_lane + 4 * i + 2 * u + a
                 total = jnp.where(
                     lane == at, rolled(sides[u][1 + a, 8 * i : 8 * i + 8, :], at - source), total
                 )
-    out_ref[2 * macro + 1 - core, slot_rows:, :] = total
+    out_ref[other] = total
 
 
 def add_lines(chunks, y_low, y_high):
@@ -414,13 +420,14 @@
     flags = cell_ref.shape[0]
     weight = 0.5 * macro_step
     row_count = spread_ref.shape[0]
-    back_rows = pick_ref.shape[1] // 3
+    returned = pick_ref.shape[1] // 4
     lane = lanes_of((1, size_z))
     row_lane = lanes_of((1, rows.shape[1]))
-    slot_lane = lanes_of((flags, back_rows))
-    flag_row = lax.broadcasted_iota(jnp.int32, (flags, back_rows), 0)
+    slot_lane = lanes_of((flags, returned))
+    flag_row = lax.broadcasted_iota(jnp.int32, (flags, returned), 0)
     rows[3 * flags :, :] = jnp.zeros((product_depth - 3 * flags, rows.shape[1]), jnp.float32)
-    slot = jnp.zeros((flags, back_rows), jnp.int32)
+    slot = jnp.zeros((flags, returned), jnp.int32)
+    group = lax.shift_right_logical(lane, 3)
     for j in range(flags):
         cell = cell_ref[j]
         row = lax.div(cell, size_z)
@@ -434,12 +441,16 @@
                 row_lane == row - shift, 1.0, jnp.where(row_lane == row + shift, -1.0, 0.0)
             )
         rows[2 * flags + j : 2 * flags + j + 1, :] = jnp.where(row_lane == row, 1.0, 0.0)
-        slot = jnp.where(flag_row == j, position_ref[j], slot)
+        owner = lax.div(position_ref[j], slot_rows)
+        rank = position_ref[j] - owner * slot_rows
+        lines_ref[2, j : j + 1, :] = jnp.where(group == rank, 1.0, 0.0)
+        slot = jnp.where(flag_row == j, owner * back_rows + polymer_row, slot)
     spread = rows[...].T[:row_count].astype(jnp.bfloat16)
     pick = jnp.where(slot_lane == slot, 1.0, 0.0).astype(jnp.bfloat16)
     for piece in range(3):
         spread_ref[:, piece * product_depth : (piece + 1) * product_depth] = spread
-        pick_ref[:, piece * back_rows : (piece + 1) * back_rows] = pick
+        pick_ref[:, piece * returned : (piece + 1) * returned] = pick
+    pick_ref[:, 3 * returned :] = jnp.zeros((flags, returned), jnp.bfloat16)
 
 
 def flow_kernel(
@@ -612,7 +623,7 @@
 def flow_step(flag_cell, position, velocity, viscosity, chunks, y_low, y_high):
     size_x, size_y, size_z = viscosity.shape
     flags = flag_cell.shape[0]
-    back_rows = chunks.shape[0] * (slot_rows + line_rows)
+    returned = chunks.shape[0] * back_rows
     row_count = size_x * size_y
     planes = (size_x, size_y, size_z)
     wide = (size_x + 2, size_y, size_z)
@@ -622,8 +633,8 @@
             jax.ShapeDtypeStruct((3, size_x * size_y, size_z), jnp.float32),
             jax.ShapeDtypeStruct((8, size_z), jnp.float32),
             jax.ShapeDtypeStruct((4, size_x, size_z), jnp.float32),
-            jax.ShapeDtypeStruct((2, flags, size_z), jnp.float32),
-            jax.ShapeDtypeStruct((flags, 3 * back_rows), jnp.bfloat16),
+            jax.ShapeDtypeStruct((3, flags, size_z), jnp.float32),
+            jax.ShapeDtypeStruct((flags, 4 * returned), jnp.bfloat16),
             jax.ShapeDtypeStruct((row_count, 3 * product_depth), jnp.bfloat16),
         ),
         in_specs=[SMEM] * 2 + [VMEM] * 5,
@@ -660,13 +671,21 @@
     spread_ref, partial_ref, out_ref, flag_ref, field, write_sem,
 ):
     flags = viscous_ref.shape[0]
-    chunk_rows = slot_rows + line_rows
     macro, core = place_of()
-    values = jnp.dot(
-        pick_ref[...], jnp.concatenate(pieces(chunk_ref[...]), axis=0), preferred_element_type=jnp.float32
-    )
+    chunks = chunk_ref[...]
+    split = jnp.concatenate((*pieces(chunks), jnp.zeros(chunks.shape, jnp.bfloat16)), axis=0)
+    values = jnp.dot(pick_ref[...], split, preferred_element_type=jnp.float32) * lines_ref[2]
     here, beside_z = lines_ref[0], lines_ref[1]
-    columns = [jnp.broadcast_to(values[:, k : k + 1], (flags, size_z)) for k in range(6)]
+    lane = lanes_of((flags, 128))
+    columns = [
+        jnp.broadcast_to(
+            jnp.sum(jnp.where((lane & 7) == k, values, 0.0), axis=1, keepdims=True), (flags, size_z)
+        )
+        for k in range(6)
+    ]
+    stress = viscous_ref[...]
+    for k in range(6):
+        stress = jnp.where(lane == k, stress + columns[k], stress)
     unused = jnp.zeros((product_depth - 3 * flags, size_z), jnp.float32)
     split = [
         pieces(
@@ -680,13 +699,13 @@
         )
         for a in range(3)
     ]
-    flag_ref[...] = (viscous_ref[...] + values).T[0:6, :]
+    flag_ref[...] = stress.T[0:6, :]
 
     field[...] = partial_ref[...]
     for s in range(2):
         inside = macro > 0 if s == 0 else macro < macro_count - 1
         beside = jnp.maximum(macro - 1, 0) if s == 0 else jnp.minimum(macro + 1, macro_count - 1)
-        start = (2 * beside + core) * chunk_rows + slot_rows
+        start = (2 * beside + core) * back_rows
         x = 0 if s == 0 else size_x - 1
         for u in range(2):
             at = x * size_y + (0 if u == 0 else size_y - 1)
@@ -694,14 +713,14 @@
                 number = 4 * s + 2 * u + a
                 line = corner_ref[number : number + 1, :] * chunk_ref[pl.ds(start + 2 * u + a, 1), :]
                 field[1 - a, at : at + 1, :] += jnp.where(inside, line, 0.0)
-    start = pl.multiple_of((2 * macro + 1 - core) * chunk_rows + slot_rows, 8)
-    packed = chunk_ref[pl.ds(start, line_rows), :]
+    start = pl.multiple_of((2 * macro + 1 - core) * back_rows, 8)
+    packed = chunk_ref[pl.ds(start, back_rows), :]
     end = jnp.where(core == 0, size_z - 1, 0)
     for u in range(2):
         y = 0 if u == 0 else size_y - 1
         for a in range(2):
             for i in range(size_x // 8):
-                line = rolled(packed, end - (4 * i + 2 * u + a)) * edge_ref[2 * u + a, 8 * i : 8 * i + 8, :]
+                line = rolled(packed, end - (line_lane + 4 * i + 2 * u + a)) * edge_ref[2 * u + a, 8 * i : 8 * i + 8, :]
                 at = pl.ds(8 * i * size_y + y, 8, stride=size_y)
                 field[2 - a, at, :] += line
     copies = [pltpu.make_async_copy(field.at[a], out_ref.at[a], write_sem.at[a]) for a in range(3)]

time: 30.2 us -> 30.3 us (level)
  transfers between devices with their start and end apart: 4 -> 4, of which waited for: 2 -> 3; matrix products, arithmetic and copies ran while one was open for 3% -> 2% of each run, Pallas kernels for 19% -> 19%
where the time goes in v12:
time: 30.3 us; the launch traced here: 29.9 us
  starting transfers between devices  14.1 us (47%)
  Pallas kernels  10.4 us (34%)
  waiting for transfers between devices  3.88 us (13%)
  local copies, waits for them, and re-layouts  0.76 us (3%)
  between operations  0.7 us (2%)
    all_to_all x2, starting transfers between devices, exchange(): lax.all_to_all(rows, ('macro', 'micro'), split_axis=0, concat_axis=0, til...  9.34 us
    all_to_all x2, waiting for transfers between devices, exchange(): lax.all_to_all(rows, ('macro', 'micro'), split_axis=0, concat_axis=0, til...  3.78 us
    ppermute x1, starting transfers between devices, shards(): y_low = lax.ppermute(y_last, 'tile', up)  3.47 us
    pallas_call x1, Pallas kernels, advance(): pl.pallas_call(functools.partial(micro_kernel, capacity, parts, rows, gro...  3.19 us
    pallas_call x1, Pallas kernels, flow_step(): pl.pallas_call(functools.partial(flow_kernel, size_x, size_y, size_z, chu...  2.46 us
    pallas_call x1, Pallas kernels, gather_rows(): pl.pallas_call(functools.partial(gather_kernel, capacity, size_x, size_y,...  2.3 us
    pallas_call x1, Pallas kernels, add_polymer(): pl.pallas_call(functools.partial(polymer_kernel, size_x, size_y, size_z,...  1.78 us
    ppermute x1, starting transfers between devices, shards(): y_high = lax.ppermute(y_first, 'tile', down)  1.29 us
  transfers between devices with their start and end apart: 4, of which 3 were waited for; matrix products, arithmetic and copies ran while one was open for 2% of the time, Pallas kernels for 19%

profile of v12, /device:TPU:0, one launch (start us, length us, event | category | flops | bytes accessed | tf_op | source)
XLA Modules:
  0.0 29.9 jit_solution(637632219117418324)
XLA Ops:
  0.6 2.3 %gather_rows.1 = (f32[512,128]{1,0:T(8,128)}, s32[32]{0:T(128)S(1)}, f32[32,128]{1,0:T(8,128)S(1)}, f32[7,24,128]{2,1,0:T(8,128)}, f32[7,24,128]{2,1,0:T(8,128)}...) custom-call(s32[32]{0:T(128)} %cell_ref.1, s32[32]{0:T(128)} %bitcast.11, f32[3,192,128]{2,1,0:T(8,128)} %bitcast.6, ...), custom_call_target="tpu_custom_call" | custom-call | flops 400000 | bytes 3000000 | tf_op jit(solution)/shard_map/gather_rows/pallas_call | solution.py:181
  2.9 0.0 copy-start
  2.9 0.0 copy-start.1
  3.0 0.0 copy-start.2
  3.0 5.3 %all-to-all-start = ((f32[8,64,128]{2,1,0:T(8,128)}), f32[8,64,128]{2,1,0:T(8,128)S(1)}, u32[]{:S(2)}, u32[]{:S(2)}) async-start(f32[8,64,128]{2,1,0:T(8,128)} %bitcast.3), calls=%async_computation | async-start | bytes 524288 | tf_op jit(solution)/shard_map/all_to_all | solution.py:767
  8.3 3.5 %collective-permute-start = (f32[7,24,128]{2,1,0:T(8,128)}, f32[7,24,128]{2,1,0:T(8,128)S(1)}, u32[]{:S(2)}, u32[]{:S(2)}) collective-permute-start(f32[7,24,128]{2,1,0:T(8,128)} %get-tuple-element.24), channel_id=1, source_target_pairs={{0,2},{2,4},{4,6},{1,3},{3,5},{5,7},{8,10},{10,12},{12,14},{9,11},... | collective-permute-start | bytes 258056 | tf_op jit(solution)/shard_map/ppermute | solution.py:772
  11.8 1.3 %collective-permute-start.1 = (f32[7,24,128]{2,1,0:T(8,128)}, f32[7,24,128]{2,1,0:T(8,128)S(1)}, u32[]{:S(2)}, u32[]{:S(2)}) collective-permute-start(f32[7,24,128]{2,1,0:T(8,128)} %get-tuple-element.25), channel_id=1, source_target_pairs={{2,0},{4,2},{6,4},{3,1},{5,3},{7,5},{10,8},{12,10},{14,12},{11,9},... | collective-permute-start | bytes 258056 | tf_op jit(solution)/shard_map/ppermute | solution.py:773
  13.1 2.2 %all-to-all-done.rate_ref.chunk_ref = f32[8,64,128]{2,1,0:T(8,128)S(1)} async-done(((f32[8,64,128]{2,1,0:T(8,128)}), f32[8,64,128]{2,1,0:T(8,128)S(1)}, u32[]{:S(2)}, u32[]{:S(2)}) %all-to-all-start) | async-done | bytes 262176 | tf_op jit(solution)/shard_map/all_to_all | solution.py:767
  15.2 3.2 %advance.1 = (f32[3,64,512]{2,1,0:T(8,128)S(1)}, f32[8,8,128]{2,1,0:T(8,128)S(1)}) custom-call(f32[3,64,512]{2,1,0:T(8,128)} %conform_ref.1, bf16[16,3,64,512]{3,2,1,0:T(8,128)(2,1)} %noise_ref.1, f32[8,64,128]{2,1,0:T(8,128)S(1)} %all-to-all-done.rate_ref.chunk_ref, f32[3,32,512]{2,1,0:T(8,128)S(1)} %get-tuple-element.21.first_conform_ref, ...), custom_call_target="tpu_custom_call" | custom-call | flops 20000000 | bytes 5000000 | tf_op jit(solution)/shard_map/advance/pallas_call | solution.py:354
  18.4 0.0 collective-permute-done.y_low_ref
  18.4 0.1 collective-permute-done.1.y_high_ref
  18.5 0.7 %add_lines.1 = f32[8,8,128]{2,1,0:T(8,128)} custom-call(f32[8,8,128]{2,1,0:T(8,128)S(1)} %get-tuple-element.23.chunk_ref, f32[7,24,128]{2,1,0:T(8,128)S(1)} %collective-permute-done.y_low_ref, f32[7,24,128]{2,1,0:T(8,128)S(1)} %collective-permute-done.1.y_high_ref), custom_call_target="tpu_custom_call" | custom-call | flops 20000 | bytes 400000 | tf_op jit(solution)/shard_map/add_lines/pallas_call | solution.py:405
  19.2 4.0 %all-to-all-start.1 = ((f32[8,8,128]{2,1,0:T(8,128)}), f32[8,8,128]{2,1,0:T(8,128)S(1)}, u32[]{:S(2)}, u32[]{:S(2)}) async-start(f32[8,8,128]{2,1,0:T(8,128)} %add_lines.1), calls=%async_computation.1 | async-start | bytes 65536 | tf_op jit(solution)/shard_map/all_to_all | solution.py:767
  23.3 0.7 %copy.9 = f32[3,64,512]{2,1,0:T(8,128)} copy(f32[3,64,512]{2,1,0:T(8,128)S(1)} %get-tuple-element.38) | data formatting | bytes 786432
  24.0 0.0 copy-done
  24.0 0.0 copy-done.1
  24.0 0.0 copy-done.2
  24.0 2.5 %flow_step.1 = (f32[3,192,128]{2,1,0:T(8,128)S(1)}, f32[8,128]{1,0:T(8,128)S(1)}, f32[4,24,128]{2,1,0:T(8,128)S(1)}, f32[3,32,128]{2,1,0:T(8,128)S(1)}, bf16[32,...) custom-call(s32[32]{0:T(128)S(1)} %copy-done.2, s32[32]{0:T(128)S(1)} %get-tuple-element.27.position_ref, ...), custom_call_target="tpu_custom_call" | custom-call | flops 4000000 | bytes 3000000 | tf_op jit(solution)/shard_map/flow_step/pallas_call | solution.py:630
  26.5 1.6 %all-to-all-done.1 = f32[8,8,128]{2,1,0:T(8,128)S(1)} async-done(((f32[8,8,128]{2,1,0:T(8,128)}), f32[8,8,128]{2,1,0:T(8,128)S(1)}, u32[]{:S(2)}, u32[]{:S(2)}) %all-to-all-start.1) | async-done | bytes 32800 | tf_op jit(solution)/shard_map/all_to_all | solution.py:767
  28.1 1.8 %add_polymer.1 = (f32[3,192,128]{2,1,0:T(8,128)}, f32[6,32]{1,0:T(8,128)}) custom-call(f32[64,128]{1,0:T(8,128)S(1)} %bitcast.10, f32[32,128]{1,0:T(8,128)S(1)} %get-tuple-element.26.viscous_ref, f32[8,128]{1,0:T(8,128)S(1)} %get-tuple-element.28.corner_ref, f32[4,24,128]{2,1,0:T(8,128)S(1)} %get-tuple-element.29.edge_ref, ...), custom_call_target="tpu_custom_call" | custom-call | flops 400000 | bytes 3000000 | tf_op jit(solution)/shard_map/add_polymer/pallas_call | solution.py:739
Async XLA Ops:
  2.9 21.1 %copy-start = (f32[3,24,8,128]{3,2,1,0:T(8,128)S(1)}, f32[3,24,8,128]{3,2,1,0:T(8,128)}, u32[]{:S(2)}) copy-start(f32[3,24,8,128]{3,2,1,0:T(8,128)} %param.6) | copy-start | bytes 884740
  2.9 21.1 %copy-start.1 = (f32[24,8,128]{2,1,0:T(8,128)S(1)}, f32[24,8,128]{2,1,0:T(8,128)}, u32[]{:S(2)}) copy-start(f32[24,8,128]{2,1,0:T(8,128)} %param.7) | copy-start | bytes 294916
  3.0 21.1 %copy-start.2 = (s32[32]{0:T(128)S(1)}, s32[32]{0:T(128)}, u32[]{:S(2)}) copy-start(s32[32]{0:T(128)} %cell_ref.1) | copy-start | bytes 388
  3.0 12.3 %all-to-all-start = ((f32[8,64,128]{2,1,0:T(8,128)}), f32[8,64,128]{2,1,0:T(8,128)S(1)}, u32[]{:S(2)}, u32[]{:S(2)}) async-start(f32[8,64,128]{2,1,0:T(8,128)} %bitcast.3), calls=%async_computation | async-start | bytes 524288 | tf_op jit(solution)/shard_map/all_to_all | solution.py:767
  8.3 10.1 %collective-permute-start = (f32[7,24,128]{2,1,0:T(8,128)}, f32[7,24,128]{2,1,0:T(8,128)S(1)}, u32[]{:S(2)}, u32[]{:S(2)}) collective-permute-start(f32[7,24,128]{2,1,0:T(8,128)} %get-tuple-element.24), channel_id=1, source_target_pairs={{0,2},{2,4},{4,6},{1,3},{3,5},{5,7},{8,10},{10,12},{12,14},{9,11},... | collective-permute-start | bytes 258056 | tf_op jit(solution)/shard_map/ppermute | solution.py:772
  11.8 6.8 %collective-permute-start.1 = (f32[7,24,128]{2,1,0:T(8,128)}, f32[7,24,128]{2,1,0:T(8,128)S(1)}, u32[]{:S(2)}, u32[]{:S(2)}) collective-permute-start(f32[7,24,128]{2,1,0:T(8,128)} %get-tuple-element.25), channel_id=1, source_target_pairs={{2,0},{4,2},{6,4},{3,1},{5,3},{7,5},{10,8},{12,10},{14,12},{11,9},... | collective-permute-start | bytes 258056 | tf_op jit(solution)/shard_map/ppermute | solution.py:773
  19.2 8.9 %all-to-all-start.1 = ((f32[8,8,128]{2,1,0:T(8,128)}), f32[8,8,128]{2,1,0:T(8,128)S(1)}, u32[]{:S(2)}, u32[]{:S(2)}) async-start(f32[8,8,128]{2,1,0:T(8,128)} %add_lines.1), calls=%async_computation.1 | async-start | bytes 65536 | tf_op jit(solution)/shard_map/all_to_all | solution.py:767

commit v13 on v12

--- a/solution.py
+++ b/solution.py
@@ -64,7 +64,7 @@
 
 def gather_kernel(
     capacity, size_x, size_y, size_z, macro_count, cell_in, owner_in, velocity_in, viscosity_in,
-    conform_in, noise_in, chunk_ref, position_ref, viscous_ref, y_low_ref, y_high_ref, conform_ref, noise_ref,
+    conform_in, noise_in, chunk_ref, position_ref, viscous_ref, first_ref, second_ref, conform_ref, noise_ref,
     cell_ref, owner_ref, velocity_ref, viscosity_ref, masked, gradients, target, count, sems,
 ):
     flags = cell_ref.shape[0]
@@ -115,13 +115,17 @@
             masked[3 * a + 2, j : j + 1, :] = planes[a, x, at, :] * along_z
         masked[9, j : j + 1, :] = layers[x, at, :] * here
 
-    for side, ref in enumerate((y_low_ref, y_high_ref)):
-        for layer in range(2):
-            y = layer if side == 0 else size_y - 1 - layer
-            for a in range(3):
-                ref[3 * layer + a] = velocity_ref[a, pl.ds(y, size_x, stride=size_y), :]
-        y = 0 if side == 0 else size_y - 1
-        ref[6] = viscosity_ref[pl.ds(y, size_x, stride=size_y), :]
+    even = lax.axis_index("tile") & 1 == 0
+
+    def put(number, ref, low, high):
+        rows = [ref[pl.ds(y, size_x, stride=size_y), :] for y in (low, high)]
+        first_ref[number] = jnp.where(even, rows[1], rows[0])
+        second_ref[number] = jnp.where(even, rows[0], rows[1])
+
+    for layer in range(2):
+        for a in range(3):
+            put(3 * layer + a, velocity_ref.at[a], layer, size_y - 1 - layer)
+    put(6, viscosity_ref, 0, size_y - 1)
 
     for side in range(2):
         beside = neighbour(macro, side, macro_count)
@@ -176,7 +180,7 @@
     size_x, size_y, size_z = viscosity.shape
     flags = flag_cell.shape[0]
     chunk_rows = slot_rows + item_count * size_y
-    face = pltpu.HBM((item_count, size_x, size_z), jnp.float32)
+    face = jax.ShapeDtypeStruct((item_count, size_x, size_z), jnp.float32)
     steps, _, _, dumbbells = increments.shape
     return pl.pallas_call(
         functools.partial(gather_kernel, capacity, size_x, size_y, size_z, owner_count // 2),
@@ -374,9 +378,12 @@
     )(far(conformations), far(increments), chunks, first_conform, first_noise)
 
 
-def lines_kernel(macro_count, chunk_ref, y_low_ref, y_high_ref, out_ref):
+def lines_kernel(macro_count, chunk_ref, first_ref, second_ref, out_ref, y_low_ref, y_high_ref):
     out_ref[...] = chunk_ref[...]
     macro, core = place_of()
+    even = lax.axis_index("tile") & 1 == 0
+    y_low_ref[...] = jnp.where(even, second_ref[...], first_ref[...])
+    y_high_ref[...] = jnp.where(even, first_ref[...], second_ref[...])
     sides = (y_low_ref, y_high_ref)
     size_x, size_z = y_low_ref.shape[1:]
     for side in range(2):
@@ -401,16 +408,17 @@
     out_ref[other] = total
 
 
-def add_lines(chunks, y_low, y_high):
+def add_lines(chunks, first, second):
+    face = jax.ShapeDtypeStruct(first.shape, jnp.float32)
     return pl.pallas_call(
         functools.partial(lines_kernel, chunks.shape[0] // 2),
-        out_shape=jax.ShapeDtypeStruct(chunks.shape, jnp.float32),
+        out_shape=(jax.ShapeDtypeStruct(chunks.shape, jnp.float32), face, face),
         in_specs=[VMEM, VMEM, VMEM],
-        out_specs=VMEM,
+        out_specs=(VMEM, VMEM, VMEM),
         compiler_params=limit(4),
         cost_estimate=pl.CostEstimate(flops=20000, bytes_accessed=400000, transcendentals=0),
         name="add_lines",
-    )(chunks, y_low, y_high)
+    )(chunks, first, second)
 
 
 product_depth = 128
@@ -759,7 +767,7 @@
     capacity = conformations.shape[1] // owner_count
     size_x, size_y, size_z = viscosity.shape
     assert capacity <= slot_rows and size_y == 8 and size_z == 128 and size_x % 8 == 0 and size_x <= 48
-    chunks, position, viscous, y_first, y_last, first_conform, first_noise = gather_rows(
+    chunks, position, viscous, first, second, first_conform, first_noise = gather_rows(
         flag_cell, flag_owner.reshape(-1), velocity, viscosity, conformations, increments, capacity, owner_count
     )
 
@@ -767,14 +775,17 @@
         return lax.all_to_all(rows, ("macro", "micro"), split_axis=0, concat_axis=0, tiled=True)
 
     received = exchange(chunks.reshape(owner_count, -1, 128))
-    up = [(i, i + 1) for i in range(tile_count - 1)]
-    down = [(target, source) for source, target in up]
-    y_low = lax.ppermute(y_last, "tile", up)
-    y_high = lax.ppermute(y_first, "tile", down)
+    swaps = []
+    for start in range(2):
+        pairs = [(i, i + 1) for i in range(start, tile_count - 1, 2)]
+        swaps.append(pairs + [(high, low) for low, high in pairs])
+    first = lax.ppermute(first, "tile", swaps[0])
+    second = lax.ppermute(second, "tile", swaps[1])
     last_state, polymer = advance(
         conformations, increments, received, first_conform, first_noise, capacity
     )
-    returned = exchange(add_lines(polymer, y_low, y_high))
+    polymer, y_low, y_high = add_lines(polymer, first, second)
+    returned = exchange(polymer)
     partial, corners, edges, lines, pick, spread = flow_step(
         flag_cell, position, velocity, viscosity, received, y_low, y_high
     )

time: 30.3 us -> 29.4 us (0.970)
  starting transfers between devices: 14.1 us -> 10.9 us
  waiting for transfers between devices: 3.88 us -> 6.26 us
    ppermute x2, starting transfers between devices: 4.76 us -> 2.23 us  [the longest x1 1.57 us: shards(): first = lax.ppermute(first, 'tile', swaps[0])]
    all_to_all x2, waiting for transfers between devices: 3.78 us -> 6.25 us  [exchange(): lax.all_to_all(rows, ('macro', 'micro'), split_axis=0, concat_axis=0, til...]
    all_to_all x2, starting transfers between devices: 9.34 us -> 8.66 us  [exchange(): lax.all_to_all(rows, ('macro', 'micro'), split_axis=0, concat_axis=0, til...]
  transfers between devices with their start and end apart: 4 -> 4, of which waited for: 3 -> 2; matrix products, arithmetic and copies ran while one was open for 2% -> 3% of each run, Pallas kernels for 19% -> 19%
where the time goes in v13:
time: 29.4 us; the launch traced here: 29 us
  starting transfers between devices  10.9 us (37%)
  Pallas kernels  10.4 us (35%)
  waiting for transfers between devices  6.26 us (21%)
  local copies, waits for them, and re-layouts  0.77 us (3%)
  between operations  0.71 us (2%)
    all_to_all x2, starting transfers between devices, exchange(): lax.all_to_all(rows, ('macro', 'micro'), split_axis=0, concat_axis=0, til...  8.66 us
    all_to_all x2, waiting for transfers between devices, exchange(): lax.all_to_all(rows, ('macro', 'micro'), split_axis=0, concat_axis=0, til...  6.25 us
    pallas_call x1, Pallas kernels, advance(): pl.pallas_call(functools.partial(micro_kernel, capacity, parts, rows, gro...  3.19 us
    pallas_call x1, Pallas kernels, flow_step(): pl.pallas_call(functools.partial(flow_kernel, size_x, size_y, size_z, chu...  2.46 us
    pallas_call x1, Pallas kernels, gather_rows(): pl.pallas_call(functools.partial(gather_kernel, capacity, size_x, size_y,...  2.25 us
    pallas_call x1, Pallas kernels, add_polymer(): pl.pallas_call(functools.partial(polymer_kernel, size_x, size_y, size_z,...  1.78 us
    ppermute x1, starting transfers between devices, shards(): first = lax.ppermute(first, 'tile', swaps[0])  1.57 us
    unnamed x7, local copies, waits for them, and re-layouts  0.77 us
  transfers between devices with their start and end apart: 4, of which 2 were waited for; matrix products, arithmetic and copies ran while one was open for 3% of the time, Pallas kernels for 19%

profile of v13, /device:TPU:0, one launch (start us, length us, event | category | flops | bytes accessed | tf_op | source)
XLA Modules:
  0.0 29.0 jit_solution(8598407007685985607)
XLA Ops:
  0.6 2.3 %gather_rows.1 = (f32[512,128]{1,0:T(8,128)}, s32[32]{0:T(128)S(1)}, f32[32,128]{1,0:T(8,128)S(1)}, f32[7,24,128]{2,1,0:T(8,128)S(1)}, f32[7,24,128]{2,1,0:T(8,1...) custom-call(s32[32]{0:T(128)} %cell_ref.1, s32[32]{0:T(128)} %bitcast.11, ...), custom_call_target="tpu_custom_call" | custom-call | flops 400000 | bytes 3000000 | tf_op jit(solution)/shard_map/gather_rows/pallas_call | solution.py:185
  2.9 0.0 copy-start
  2.9 0.0 copy-start.1
  2.9 0.0 copy-start.2
  2.9 5.3 %all-to-all-start = ((f32[8,64,128]{2,1,0:T(8,128)}), f32[8,64,128]{2,1,0:T(8,128)S(1)}, u32[]{:S(2)}, u32[]{:S(2)}) async-start(f32[8,64,128]{2,1,0:T(8,128)} %bitcast.3), calls=%async_computation | async-start | bytes 524288 | tf_op jit(solution)/shard_map/all_to_all | solution.py:775
  8.2 1.6 %collective-permute-start = (f32[7,24,128]{2,1,0:T(8,128)S(1)}, f32[7,24,128]{2,1,0:T(8,128)S(1)}, u32[]{:S(2)}, u32[]{:S(2)}) collective-permute-start(f32[7,24,128]{2,1,0:T(8,128)S(1)} %get-tuple-element.27), channel_id=1, source_target_pairs={{0,2},{4,6},{2,0},{6,4},{1,3},{5,7},{3,1},{7,5},{8,10},{12,14},{10... | collective-permute-start | bytes 258056 | tf_op jit(solution)/shard_map/ppermute | solution.py:782
  9.8 0.7 %collective-permute-start.1 = (f32[7,24,128]{2,1,0:T(8,128)S(1)}, f32[7,24,128]{2,1,0:T(8,128)S(1)}, u32[]{:S(2)}, u32[]{:S(2)}) collective-permute-start(f32[7,24,128]{2,1,0:T(8,128)S(1)} %get-tuple-element.28), channel_id=1, source_target_pairs={{2,4},{4,2},{3,5},{5,3},{10,12},{12,10},{11,13},{13,11},{18,20},{2... | collective-permute-start | bytes 258056 | tf_op jit(solution)/shard_map/ppermute | solution.py:783
  10.5 4.7 %all-to-all-done.rate_ref.chunk_ref = f32[8,64,128]{2,1,0:T(8,128)S(1)} async-done(((f32[8,64,128]{2,1,0:T(8,128)}), f32[8,64,128]{2,1,0:T(8,128)S(1)}, u32[]{:S(2)}, u32[]{:S(2)}) %all-to-all-start) | async-done | bytes 262176 | tf_op jit(solution)/shard_map/all_to_all | solution.py:775
  15.2 3.2 %advance.1 = (f32[3,64,512]{2,1,0:T(8,128)S(1)}, f32[8,8,128]{2,1,0:T(8,128)S(1)}) custom-call(f32[3,64,512]{2,1,0:T(8,128)} %conform_ref.1, bf16[16,3,64,512]{3,2,1,0:T(8,128)(2,1)} %noise_ref.1, f32[8,64,128]{2,1,0:T(8,128)S(1)} %all-to-all-done.rate_ref.chunk_ref, f32[3,32,512]{2,1,0:T(8,128)S(1)} %get-tuple-element.24.first_conform_ref, ...), custom_call_target="tpu_custom_call" | custom-call | flops 20000000 | bytes 5000000 | tf_op jit(solution)/shard_map/advance/pallas_call | solution.py:358
  18.4 0.0 collective-permute-done.first_ref
  18.4 0.0 collective-permute-done.1.second_ref
  18.4 0.7 %add_lines.1 = (f32[8,8,128]{2,1,0:T(8,128)}, f32[7,24,128]{2,1,0:T(8,128)S(1)}, f32[7,24,128]{2,1,0:T(8,128)S(1)}) custom-call(f32[8,8,128]{2,1,0:T(8,128)S(1)} %get-tuple-element.26.chunk_ref, f32[7,24,128]{2,1,0:T(8,128)S(1)} %collective-permute-done.first_ref, f32[7,24,128]{2,1,0:T(8,128)S(1)} %collective-permute-done.1.second_ref), custom_call_target="tpu_custom_call" | custom-call | flops 20000 | bytes 400000 | tf_op jit(solution)/shard_map/add_lines/pallas_call | solution.py:413
  19.1 3.3 %all-to-all-start.1 = ((f32[8,8,128]{2,1,0:T(8,128)}), f32[8,8,128]{2,1,0:T(8,128)S(1)}, u32[]{:S(2)}, u32[]{:S(2)}) async-start(f32[8,8,128]{2,1,0:T(8,128)} %get-tuple-element.29), calls=%async_computation.1 | async-start | bytes 65536 | tf_op jit(solution)/shard_map/all_to_all | solution.py:775
  22.5 0.7 %copy.9 = f32[3,64,512]{2,1,0:T(8,128)} copy(f32[3,64,512]{2,1,0:T(8,128)S(1)} %get-tuple-element.44) | data formatting | bytes 786432
  23.2 0.0 copy-done
  23.2 0.0 copy-done.1
  23.2 0.0 copy-done.2
  23.2 2.5 %flow_step.1 = (f32[3,192,128]{2,1,0:T(8,128)S(1)}, f32[8,128]{1,0:T(8,128)S(1)}, f32[4,24,128]{2,1,0:T(8,128)S(1)}, f32[3,32,128]{2,1,0:T(8,128)S(1)}, bf16[32,...) custom-call(s32[32]{0:T(128)S(1)} %copy-done.2, s32[32]{0:T(128)S(1)} %get-tuple-element.31.position_ref, ...), custom_call_target="tpu_custom_call" | custom-call | flops 4000000 | bytes 3000000 | tf_op jit(solution)/shard_map/flow_step/pallas_call | solution.py:638
  25.7 1.5 %all-to-all-done.1 = f32[8,8,128]{2,1,0:T(8,128)S(1)} async-done(((f32[8,8,128]{2,1,0:T(8,128)}), f32[8,8,128]{2,1,0:T(8,128)S(1)}, u32[]{:S(2)}, u32[]{:S(2)}) %all-to-all-start.1) | async-done | bytes 32800 | tf_op jit(solution)/shard_map/all_to_all | solution.py:775
  27.2 1.8 %add_polymer.1 = (f32[3,192,128]{2,1,0:T(8,128)}, f32[6,32]{1,0:T(8,128)}) custom-call(f32[64,128]{1,0:T(8,128)S(1)} %bitcast.10, f32[32,128]{1,0:T(8,128)S(1)} %get-tuple-element.30.viscous_ref, f32[8,128]{1,0:T(8,128)S(1)} %get-tuple-element.34.corner_ref, f32[4,24,128]{2,1,0:T(8,128)S(1)} %get-tuple-element.35.edge_ref, ...), custom_call_target="tpu_custom_call" | custom-call | flops 400000 | bytes 3000000 | tf_op jit(solution)/shard_map/add_polymer/pallas_call | solution.py:747
Async XLA Ops:
  2.9 20.3 %copy-start = (f32[3,24,8,128]{3,2,1,0:T(8,128)S(1)}, f32[3,24,8,128]{3,2,1,0:T(8,128)}, u32[]{:S(2)}) copy-start(f32[3,24,8,128]{3,2,1,0:T(8,128)} %param.6) | copy-start | bytes 884740
  2.9 20.3 %copy-start.1 = (f32[24,8,128]{2,1,0:T(8,128)S(1)}, f32[24,8,128]{2,1,0:T(8,128)}, u32[]{:S(2)}) copy-start(f32[24,8,128]{2,1,0:T(8,128)} %param.7) | copy-start | bytes 294916
  2.9 20.3 %copy-start.2 = (s32[32]{0:T(128)S(1)}, s32[32]{0:T(128)}, u32[]{:S(2)}) copy-start(s32[32]{0:T(128)} %cell_ref.1) | copy-start | bytes 388
  2.9 12.3 %all-to-all-start = ((f32[8,64,128]{2,1,0:T(8,128)}), f32[8,64,128]{2,1,0:T(8,128)S(1)}, u32[]{:S(2)}, u32[]{:S(2)}) async-start(f32[8,64,128]{2,1,0:T(8,128)} %bitcast.3), calls=%async_computation | async-start | bytes 524288 | tf_op jit(solution)/shard_map/all_to_all | solution.py:775
  8.2 10.1 %collective-permute-start = (f32[7,24,128]{2,1,0:T(8,128)S(1)}, f32[7,24,128]{2,1,0:T(8,128)S(1)}, u32[]{:S(2)}, u32[]{:S(2)}) collective-permute-start(f32[7,24,128]{2,1,0:T(8,128)S(1)} %get-tuple-element.27), channel_id=1, source_target_pairs={{0,2},{4,6},{2,0},{6,4},{1,3},{5,7},{3,1},{7,5},{8,10},{12,14},{10... | collective-permute-start | bytes 258056 | tf_op jit(solution)/shard_map/ppermute | solution.py:782
  9.8 8.6 %collective-permute-start.1 = (f32[7,24,128]{2,1,0:T(8,128)S(1)}, f32[7,24,128]{2,1,0:T(8,128)S(1)}, u32[]{:S(2)}, u32[]{:S(2)}) collective-permute-start(f32[7,24,128]{2,1,0:T(8,128)S(1)} %get-tuple-element.28), channel_id=1, source_target_pairs={{2,4},{4,2},{3,5},{5,3},{10,12},{12,10},{11,13},{13,11},{18,20},{2... | collective-permute-start | bytes 258056 | tf_op jit(solution)/shard_map/ppermute | solution.py:783
  19.1 8.1 %all-to-all-start.1 = ((f32[8,8,128]{2,1,0:T(8,128)}), f32[8,8,128]{2,1,0:T(8,128)S(1)}, u32[]{:S(2)}, u32[]{:S(2)}) async-start(f32[8,8,128]{2,1,0:T(8,128)} %get-tuple-element.29), calls=%async_computation.1 | async-start | bytes 65536 | tf_op jit(solution)/shard_map/all_to_all | solution.py:775

commit v14 on v13

--- a/solution.py
+++ b/solution.py
@@ -29,6 +29,8 @@
 
 
 slot_rows = 8
+face_rows = 16
+corner_lane = 64
 item_count = 7
 back_rows = 8
 polymer_row = 4
@@ -64,7 +66,7 @@
 
 def gather_kernel(
     capacity, size_x, size_y, size_z, macro_count, cell_in, owner_in, velocity_in, viscosity_in,
-    conform_in, noise_in, chunk_ref, position_ref, viscous_ref, first_ref, second_ref, conform_ref, noise_ref,
+    conform_in, noise_in, chunk_ref, position_ref, viscous_ref, first_ref, second_ref, first_x_ref, second_x_ref, conform_ref, noise_ref,
     cell_ref, owner_ref, velocity_ref, viscosity_ref, masked, gradients, target, count, sems,
 ):
     flags = cell_ref.shape[0]
@@ -80,7 +82,7 @@
     ]
     for copy in copies:
         copy.start()
-    chunk_rows = slot_rows + item_count * size_y
+    chunk_rows = slot_rows + face_rows
     macro, core = place_of()
     lane = lanes_of((1, size_z))
 
@@ -127,22 +129,17 @@
             put(3 * layer + a, velocity_ref.at[a], layer, size_y - 1 - layer)
     put(6, viscosity_ref, 0, size_y - 1)
 
-    for side in range(2):
-        beside = neighbour(macro, side, macro_count)
-        first = pl.multiple_of((2 * beside + core) * chunk_rows + slot_rows, 8)
-        other = pl.multiple_of((2 * beside + 1 - core) * chunk_rows + slot_rows, 8)
-        for layer in range(2):
-            x = layer if side == 0 else size_x - 1 - layer
-            for a in range(3):
-                chunk_ref[pl.ds(first + (3 * layer + a) * size_y, size_y), :] = velocity_ref[
-                    a, x * size_y : (x + 1) * size_y, :
-                ]
-        x = 0 if side == 0 else size_x - 1
-        chunk_ref[pl.ds(first + 6 * size_y, size_y), :] = viscosity_ref[x * size_y : (x + 1) * size_y, :]
-        for number, a in enumerate((0, 2)):
-            chunk_ref[pl.ds(other + number * size_y, size_y), :] = velocity_ref[
-                a, x * size_y : (x + 1) * size_y, :
-            ]
+    even_x = macro & 1 == 0
+
+    def put_x(number, ref, low, high):
+        planes = [ref[x * size_y : (x + 1) * size_y, :] for x in (low, high)]
+        first_x_ref[number] = jnp.where(even_x, planes[1], planes[0])
+        second_x_ref[number] = jnp.where(even_x, planes[0], planes[1])
+
+    for layer in range(2):
+        for a in range(3):
+            put_x(3 * layer + a, velocity_ref.at[a], layer, size_x - 1 - layer)
+    put_x(6, viscosity_ref, 0, size_x - 1)
 
     group = size_z // 8
     lane2 = lanes_of((size_y, size_z))
@@ -172,6 +169,18 @@
 
     for j in range(flags):
         chunk_ref[pl.ds(target[j], 1), :] = gradients[j : j + 1, :]
+
+    edge = jnp.where(core == 0, size_z - 1, 0)
+    for side in range(2):
+        beside = neighbour(macro, side, macro_count)
+        rows = pl.ds(pl.multiple_of((2 * beside + 1 - core) * chunk_rows, 8), slot_rows)
+        x = 0 if side == 0 else size_x - 1
+        value = chunk_ref[rows, :]
+        for number, a in enumerate((0, 2)):
+            plane = velocity_ref[a, x * size_y : (x + 1) * size_y, :]
+            at = corner_lane + number
+            value = jnp.where(lane2 == at, rolled(plane, at - edge), value)
+        chunk_ref[rows, :] = value
     for copy in copies[4:]:
         copy.wait()
 
@@ -179,8 +188,9 @@
 def gather_rows(flag_cell, owner, velocity, viscosity, conformations, increments, capacity, owner_count):
     size_x, size_y, size_z = viscosity.shape
     flags = flag_cell.shape[0]
-    chunk_rows = slot_rows + item_count * size_y
+    chunk_rows = slot_rows + face_rows
     face = jax.ShapeDtypeStruct((item_count, size_x, size_z), jnp.float32)
+    face_x = jax.ShapeDtypeStruct((item_count, size_y, size_z), jnp.float32)
     steps, _, _, dumbbells = increments.shape
     return pl.pallas_call(
         functools.partial(gather_kernel, capacity, size_x, size_y, size_z, owner_count // 2),
@@ -190,11 +200,13 @@
             jax.ShapeDtypeStruct((flags, 128), jnp.float32),
             face,
             face,
+            face_x,
+            face_x,
             pltpu.VMEM((3, block_slots, dumbbells), jnp.float32),
             pltpu.VMEM((steps // first_share, 3, block_slots, dumbbells), jnp.bfloat16),
         ),
         in_specs=[pl.BlockSpec(memory_space=pltpu.HBM)] * 6,
-        out_specs=(VMEM, SMEM, VMEM, VMEM, VMEM, VMEM, VMEM),
+        out_specs=(VMEM, SMEM) + (VMEM,) * 7,
         scratch_shapes=[
             pltpu.SMEM((flags,), jnp.int32),
             pltpu.SMEM((flags,), jnp.int32),
@@ -463,7 +475,7 @@
 
 def flow_kernel(
     size_x, size_y, size_z, macro_count, cell_ref, position_ref, velocity_ref, viscosity_ref, chunk_ref,
-    y_low_ref, y_high_ref, out_ref, corner_ref, edge_ref, lines_ref, pick_ref, spread_ref,
+    y_low_ref, y_high_ref, first_x_ref, second_x_ref, out_ref, corner_ref, edge_ref, lines_ref, pick_ref, spread_ref,
     padded, stress_x, stress_rest, faces, ghost_y, ghost_z, rows,
 ):
     macro, core = place_of()
@@ -494,29 +506,16 @@
             row == 0, low, pltpu.roll(value, 1, 0)
         )
 
-    x_faces, x_others = [], []
+    even = macro & 1 == 0
+    x_faces, x_others = [[], []], []
+    for i in range(item_count):
+        first, second = first_x_ref[i], second_x_ref[i]
+        x_faces[0].append(jnp.where(even, second, first))
+        x_faces[1].append(jnp.where(even, first, second))
     for s in range(2):
-        beside = jnp.maximum(macro - 1, 0) if s == 0 else jnp.minimum(macro + 1, macro_count - 1)
-        x_faces.append(
-            [
-                kept(chunk_ref[2 * beside + core, slot_rows + i * size_y : slot_rows + (i + 1) * size_y, :], inside[s])
-                for i in range(item_count)
-            ]
-        )
-        x_others.append(
-            [
-                kept(
-                    rolled(
-                        chunk_ref[
-                            2 * beside + 1 - core, slot_rows + i * size_y : slot_rows + (i + 1) * size_y, :
-                        ],
-                        2 * end + 1,
-                    ),
-                    inside[s],
-                )
-                for i in range(2)
-            ]
-        )
+        beside = neighbour(macro, s, macro_count)
+        corner = chunk_ref[2 * beside + 1 - core, 0:slot_rows, :]
+        x_others.append([kept(rolled(corner, end - (corner_lane + i)), inside[s]) for i in range(2)])
 
     group = size_z // 8
     packed = [
@@ -628,7 +627,7 @@
     lax.fori_loop(0, size_x, step_plane, 0, unroll=6)
 
 
-def flow_step(flag_cell, position, velocity, viscosity, chunks, y_low, y_high):
+def flow_step(flag_cell, position, velocity, viscosity, chunks, y_low, y_high, first_x, second_x):
     size_x, size_y, size_z = viscosity.shape
     flags = flag_cell.shape[0]
     returned = chunks.shape[0] * back_rows
@@ -645,7 +644,7 @@
             jax.ShapeDtypeStruct((flags, 4 * returned), jnp.bfloat16),
             jax.ShapeDtypeStruct((row_count, 3 * product_depth), jnp.bfloat16),
         ),
-        in_specs=[SMEM] * 2 + [VMEM] * 5,
+        in_specs=[SMEM] * 2 + [VMEM] * 7,
         out_specs=(VMEM,) * 6,
         scratch_shapes=[
             pltpu.VMEM((3, *wide), jnp.float32),
@@ -663,7 +662,7 @@
         flag_cell, position,
         velocity.reshape(3, size_x * size_y, size_z),
         viscosity.reshape(size_x * size_y, size_z),
-        chunks, y_low, y_high,
+        chunks, y_low, y_high, first_x, second_x,
     )
 
 
@@ -761,13 +760,12 @@
 
 def shards(velocity, viscosity, flag_cell, flag_owner, conformations, increments):
     macro_count = lax.axis_size("macro")
-    tile_count = lax.axis_size("tile")
     assert lax.axis_size("micro") == 2
     owner_count = 2 * macro_count
     capacity = conformations.shape[1] // owner_count
     size_x, size_y, size_z = viscosity.shape
-    assert capacity <= slot_rows and size_y == 8 and size_z == 128 and size_x % 8 == 0 and size_x <= 48
-    chunks, position, viscous, first, second, first_conform, first_noise = gather_rows(
+    assert capacity <= slot_rows and size_y == 8 and size_z == 128 and size_x % 8 == 0 and size_x <= 32
+    chunks, position, viscous, first, second, first_x, second_x, first_conform, first_noise = gather_rows(
         flag_cell, flag_owner.reshape(-1), velocity, viscosity, conformations, increments, capacity, owner_count
     )
 
@@ -775,19 +773,25 @@
         return lax.all_to_all(rows, ("macro", "micro"), split_axis=0, concat_axis=0, tiled=True)
 
     received = exchange(chunks.reshape(owner_count, -1, 128))
-    swaps = []
-    for start in range(2):
-        pairs = [(i, i + 1) for i in range(start, tile_count - 1, 2)]
-        swaps.append(pairs + [(high, low) for low, high in pairs])
-    first = lax.ppermute(first, "tile", swaps[0])
-    second = lax.ppermute(second, "tile", swaps[1])
+
+    def swaps(axis):
+        result = []
+        for start in range(2):
+            pairs = [(i, i + 1) for i in range(start, lax.axis_size(axis) - 1, 2)]
+            result.append(pairs + [(high, low) for low, high in pairs])
+        return result
+
+    first, second = [lax.ppermute(face, "tile", pairs) for face, pairs in zip((first, second), swaps("tile"))]
+    first_x, second_x = [
+        lax.ppermute(face, "macro", pairs) for face, pairs in zip((first_x, second_x), swaps("macro"))
+    ]
     last_state, polymer = advance(
         conformations, increments, received, first_conform, first_noise, capacity
     )
     polymer, y_low, y_high = add_lines(polymer, first, second)
     returned = exchange(polymer)
     partial, corners, edges, lines, pick, spread = flow_step(
-        flag_cell, position, velocity, viscosity, received, y_low, y_high
+        flag_cell, position, velocity, viscosity, received, y_low, y_high, first_x, second_x
     )
     velocity_next, flag_stress = add_polymer(
         returned, viscous, corners, edges, lines, pick, spread, partial, viscosity.shape

time: 29.4 us -> 31 us (1.054)
  the two profiles are of different devices: /device:TPU:0 before, /device:TPU:8 now
where the time goes in v14:
time: 31 us; the launch traced here: 30.6 us
  starting transfers between devices  17.1 us (55%)
  Pallas kernels  10.4 us (34%)
  waiting for transfers between devices  1.6 us (5%)
  local copies, waits for them, and re-layouts  0.76 us (2%)
  between operations  0.74 us (2%)
    all_to_all x2, starting transfers between devices, exchange(): lax.all_to_all(rows, ('macro', 'micro'), split_axis=0, concat_axis=0, til...  9.32 us
    ppermute x2, starting transfers between devices, shards(): lax.ppermute(face, 'tile', pairs)  5.05 us
    pallas_call x1, Pallas kernels, advance(): pl.pallas_call(functools.partial(micro_kernel, capacity, parts, rows, gro...  3.19 us
    ppermute x2, starting transfers between devices, shards(): lax.ppermute(face, 'macro', pairs)  2.74 us
    pallas_call x1, Pallas kernels, flow_step(): pl.pallas_call(functools.partial(flow_kernel, size_x, size_y, size_z, chu...  2.47 us
    pallas_call x1, Pallas kernels, gather_rows(): pl.pallas_call(functools.partial(gather_kernel, capacity, size_x, size_y,...  2.27 us
    pallas_call x1, Pallas kernels, add_polymer(): pl.pallas_call(functools.partial(polymer_kernel, size_x, size_y, size_z,...  1.78 us
    all_to_all x2, waiting for transfers between devices, exchange(): lax.all_to_all(rows, ('macro', 'micro'), split_axis=0, concat_axis=0, til...  1.59 us
  transfers between devices with their start and end apart: 6, of which 1 were waited for; matrix products, arithmetic and copies ran while one was open for 2% of the time, Pallas kernels for 21%

profile of v14, /device:TPU:8, one launch (start us, length us, event | category | flops | bytes accessed | tf_op | source)
XLA Modules:
  0.0 30.6 jit_solution(17532705335305332112)
XLA Ops:
  0.6 2.3 %gather_rows.1 = (f32[192,128]{1,0:T(8,128)}, s32[32]{0:T(128)S(1)}, f32[32,128]{1,0:T(8,128)S(1)}, f32[7,24,128]{2,1,0:T(8,128)S(1)}, f32[7,24,128]{2,1,0:T(8,1...) custom-call(s32[32]{0:T(128)} %cell_ref.1, ...), custom_call_target="tpu_custom_call" | custom-call | flops 400000 | bytes 3000000 | tf_op jit(solution)/shard_map/gather_rows/pallas_call | solution.py:195
  2.9 0.0 copy-start
  2.9 0.0 copy-start.1
  2.9 0.0 copy-start.2
  2.9 3.9 %all-to-all-start = ((f32[8,24,128]{2,1,0:T(8,128)}), f32[8,24,128]{2,1,0:T(8,128)S(1)}, u32[]{:S(2)}, u32[]{:S(2)}) async-start(f32[8,24,128]{2,1,0:T(8,128)} %bitcast.3), calls=%async_computation | async-start | bytes 196608 | tf_op jit(solution)/shard_map/all_to_all | solution.py:773
  6.8 0.4 %collective-permute-start = (f32[7,24,128]{2,1,0:T(8,128)S(1)}, f32[7,24,128]{2,1,0:T(8,128)S(1)}, u32[]{:S(2)}, u32[]{:S(2)}) collective-permute-start(f32[7,24,128]{2,1,0:T(8,128)S(1)} %get-tuple-element.29), channel_id=1, source_target_pairs={{0,2},{4,6},{2,0},{6,4},{1,3},{5,7},{3,1},{7,5},{8,10},{12,14},{10... | collective-permute-start | bytes 258056 | tf_op jit(solution)/shard_map/ppermute | solution.py:784
  7.3 4.6 %collective-permute-start.1 = (f32[7,24,128]{2,1,0:T(8,128)S(1)}, f32[7,24,128]{2,1,0:T(8,128)S(1)}, u32[]{:S(2)}, u32[]{:S(2)}) collective-permute-start(f32[7,24,128]{2,1,0:T(8,128)S(1)} %get-tuple-element.30), channel_id=1, source_target_pairs={{2,4},{4,2},{3,5},{5,3},{10,12},{12,10},{11,13},{13,11},{18,20},{2... | collective-permute-start | bytes 258056 | tf_op jit(solution)/shard_map/ppermute | solution.py:784
  11.9 2.1 %collective-permute-start.2 = (f32[7,8,128]{2,1,0:T(8,128)S(1)}, f32[7,8,128]{2,1,0:T(8,128)S(1)}, u32[]{:S(2)}, u32[]{:S(2)}) collective-permute-start(f32[7,8,128]{2,1,0:T(8,128)S(1)} %get-tuple-element.36), channel_id=1, source_target_pairs={{0,8},{16,24},{8,0},{24,16},{1,9},{17,25},{9,1},{25,17},{2,10},{18... | collective-permute-start | bytes 86024 | tf_op jit(solution)/shard_map/ppermute | solution.py:786
  14.0 0.7 %collective-permute-start.3 = (f32[7,8,128]{2,1,0:T(8,128)S(1)}, f32[7,8,128]{2,1,0:T(8,128)S(1)}, u32[]{:S(2)}, u32[]{:S(2)}) collective-permute-start(f32[7,8,128]{2,1,0:T(8,128)S(1)} %get-tuple-element.37), channel_id=1, source_target_pairs={{8,16},{16,8},{9,17},{17,9},{10,18},{18,10},{11,19},{19,11},{12,20... | collective-permute-start | bytes 86024 | tf_op jit(solution)/shard_map/ppermute | solution.py:786
  14.6 0.0 all-to-all-done.rate_ref.chunk_ref
  14.6 3.2 %advance.1 = (f32[3,64,512]{2,1,0:T(8,128)S(1)}, f32[8,8,128]{2,1,0:T(8,128)S(1)}) custom-call(f32[3,64,512]{2,1,0:T(8,128)} %conform_ref.1, bf16[16,3,64,512]{3,2,1,0:T(8,128)(2,1)} %noise_ref.1, f32[8,24,128]{2,1,0:T(8,128)S(1)} %all-to-all-done.rate_ref.chunk_ref, f32[3,32,512]{2,1,0:T(8,128)S(1)} %get-tuple-element.26.first_conform_ref, ...), custom_call_target="tpu_custom_call" | custom-call | flops 20000000 | bytes 5000000 | tf_op jit(solution)/shard_map/advance/pallas_call | solution.py:370
  17.8 0.0 collective-permute-done.first_ref
  17.8 0.0 collective-permute-done.1.second_ref
  17.8 0.7 %add_lines.1 = (f32[8,8,128]{2,1,0:T(8,128)}, f32[7,24,128]{2,1,0:T(8,128)S(1)}, f32[7,24,128]{2,1,0:T(8,128)S(1)}) custom-call(f32[8,8,128]{2,1,0:T(8,128)S(1)} %get-tuple-element.28.chunk_ref, f32[7,24,128]{2,1,0:T(8,128)S(1)} %collective-permute-done.first_ref, f32[7,24,128]{2,1,0:T(8,128)S(1)} %collective-permute-done.1.second_ref), custom_call_target="tpu_custom_call" | custom-call | flops 20000 | bytes 400000 | tf_op jit(solution)/shard_map/add_lines/pallas_call | solution.py:425
  18.6 5.4 %all-to-all-start.1 = ((f32[8,8,128]{2,1,0:T(8,128)}), f32[8,8,128]{2,1,0:T(8,128)S(1)}, u32[]{:S(2)}, u32[]{:S(2)}) async-start(f32[8,8,128]{2,1,0:T(8,128)} %get-tuple-element.31), calls=%async_computation.1 | async-start | bytes 65536 | tf_op jit(solution)/shard_map/all_to_all | solution.py:773
  24.0 0.7 %copy.9 = f32[3,64,512]{2,1,0:T(8,128)} copy(f32[3,64,512]{2,1,0:T(8,128)S(1)} %get-tuple-element.48) | data formatting | bytes 786432
  24.8 0.0 collective-permute-done.2.first_x_ref
  24.8 0.0 collective-permute-done.3.second_x_ref
  24.8 0.0 copy-done
  24.8 0.0 copy-done.1
  24.8 0.0 copy-done.2
  24.8 2.5 %flow_step.1 = (f32[3,192,128]{2,1,0:T(8,128)S(1)}, f32[8,128]{1,0:T(8,128)S(1)}, f32[4,24,128]{2,1,0:T(8,128)S(1)}, f32[3,32,128]{2,1,0:T(8,128)S(1)}, bf16[32,...) custom-call(s32[32]{0:T(128)S(1)} %copy-done.2, s32[32]{0:T(128)S(1)} %get-tuple-element.33.position_ref, ...), custom_call_target="tpu_custom_call" | custom-call | flops 4000000 | bytes 3000000 | tf_op jit(solution)/shard_map/flow_step/pallas_call | solution.py:637
  27.3 1.6 %all-to-all-done.1 = f32[8,8,128]{2,1,0:T(8,128)S(1)} async-done(((f32[8,8,128]{2,1,0:T(8,128)}), f32[8,8,128]{2,1,0:T(8,128)S(1)}, u32[]{:S(2)}, u32[]{:S(2)}) %all-to-all-start.1) | async-done | bytes 32800 | tf_op jit(solution)/shard_map/all_to_all | solution.py:773
  28.9 1.8 %add_polymer.1 = (f32[3,192,128]{2,1,0:T(8,128)}, f32[6,32]{1,0:T(8,128)}) custom-call(f32[64,128]{1,0:T(8,128)S(1)} %bitcast.10, f32[32,128]{1,0:T(8,128)S(1)} %get-tuple-element.32.viscous_ref, f32[8,128]{1,0:T(8,128)S(1)} %get-tuple-element.38.corner_ref, f32[4,24,128]{2,1,0:T(8,128)S(1)} %get-tuple-element.39.edge_ref, ...), custom_call_target="tpu_custom_call" | custom-call | flops 400000 | bytes 3000000 | tf_op jit(solution)/shard_map/add_polymer/pallas_call | solution.py:746
Async XLA Ops:
  2.9 21.9 %copy-start = (f32[3,24,8,128]{3,2,1,0:T(8,128)S(1)}, f32[3,24,8,128]{3,2,1,0:T(8,128)}, u32[]{:S(2)}) copy-start(f32[3,24,8,128]{3,2,1,0:T(8,128)} %param.6) | copy-start | bytes 884740
  2.9 21.9 %copy-start.1 = (f32[24,8,128]{2,1,0:T(8,128)S(1)}, f32[24,8,128]{2,1,0:T(8,128)}, u32[]{:S(2)}) copy-start(f32[24,8,128]{2,1,0:T(8,128)} %param.7) | copy-start | bytes 294916
  2.9 21.9 %copy-start.2 = (s32[32]{0:T(128)S(1)}, s32[32]{0:T(128)}, u32[]{:S(2)}) copy-start(s32[32]{0:T(128)} %cell_ref.1) | copy-start | bytes 388
  2.9 11.7 %all-to-all-start = ((f32[8,24,128]{2,1,0:T(8,128)}), f32[8,24,128]{2,1,0:T(8,128)S(1)}, u32[]{:S(2)}, u32[]{:S(2)}) async-start(f32[8,24,128]{2,1,0:T(8,128)} %bitcast.3), calls=%async_computation | async-start | bytes 196608 | tf_op jit(solution)/shard_map/all_to_all | solution.py:773
  6.8 11.0 %collective-permute-start = (f32[7,24,128]{2,1,0:T(8,128)S(1)}, f32[7,24,128]{2,1,0:T(8,128)S(1)}, u32[]{:S(2)}, u32[]{:S(2)}) collective-permute-start(f32[7,24,128]{2,1,0:T(8,128)S(1)} %get-tuple-element.29), channel_id=1, source_target_pairs={{0,2},{4,6},{2,0},{6,4},{1,3},{5,7},{3,1},{7,5},{8,10},{12,14},{10... | collective-permute-start | bytes 258056 | tf_op jit(solution)/shard_map/ppermute | solution.py:784
  7.3 10.6 %collective-permute-start.1 = (f32[7,24,128]{2,1,0:T(8,128)S(1)}, f32[7,24,128]{2,1,0:T(8,128)S(1)}, u32[]{:S(2)}, u32[]{:S(2)}) collective-permute-start(f32[7,24,128]{2,1,0:T(8,128)S(1)} %get-tuple-element.30), channel_id=1, source_target_pairs={{2,4},{4,2},{3,5},{5,3},{10,12},{12,10},{11,13},{13,11},{18,20},{2... | collective-permute-start | bytes 258056 | tf_op jit(solution)/shard_map/ppermute | solution.py:784
  11.9 12.9 %collective-permute-start.2 = (f32[7,8,128]{2,1,0:T(8,128)S(1)}, f32[7,8,128]{2,1,0:T(8,128)S(1)}, u32[]{:S(2)}, u32[]{:S(2)}) collective-permute-start(f32[7,8,128]{2,1,0:T(8,128)S(1)} %get-tuple-element.36), channel_id=1, source_target_pairs={{0,8},{16,24},{8,0},{24,16},{1,9},{17,25},{9,1},{25,17},{2,10},{18... | collective-permute-start | bytes 86024 | tf_op jit(solution)/shard_map/ppermute | solution.py:786
  14.0 10.8 %collective-permute-start.3 = (f32[7,8,128]{2,1,0:T(8,128)S(1)}, f32[7,8,128]{2,1,0:T(8,128)S(1)}, u32[]{:S(2)}, u32[]{:S(2)}) collective-permute-start(f32[7,8,128]{2,1,0:T(8,128)S(1)} %get-tuple-element.37), channel_id=1, source_target_pairs={{8,16},{16,8},{9,17},{17,9},{10,18},{18,10},{11,19},{19,11},{12,20... | collective-permute-start | bytes 86024 | tf_op jit(solution)/shard_map/ppermute | solution.py:786
  18.6 10.3 %all-to-all-start.1 = ((f32[8,8,128]{2,1,0:T(8,128)}), f32[8,8,128]{2,1,0:T(8,128)S(1)}, u32[]{:S(2)}, u32[]{:S(2)}) async-start(f32[8,8,128]{2,1,0:T(8,128)} %get-tuple-element.31), calls=%async_computation.1 | async-start | bytes 65536 | tf_op jit(solution)/shard_map/all_to_all | solution.py:773

commit v15 on v13

--- a/solution.py
+++ b/solution.py
@@ -29,6 +29,8 @@
 
 
 slot_rows = 8
+face_rows = 32
+corner_lane = 64
 item_count = 7
 back_rows = 8
 polymer_row = 4
@@ -80,7 +82,7 @@
     ]
     for copy in copies:
         copy.start()
-    chunk_rows = slot_rows + item_count * size_y
+    chunk_rows = slot_rows + face_rows
     macro, core = place_of()
     lane = lanes_of((1, size_z))
 
@@ -129,20 +131,14 @@
 
     for side in range(2):
         beside = neighbour(macro, side, macro_count)
-        first = pl.multiple_of((2 * beside + core) * chunk_rows + slot_rows, 8)
+        same = pl.multiple_of((2 * beside + core) * chunk_rows + slot_rows, 8)
         other = pl.multiple_of((2 * beside + 1 - core) * chunk_rows + slot_rows, 8)
-        for layer in range(2):
+        for layer, start in enumerate((same, other)):
             x = layer if side == 0 else size_x - 1 - layer
             for a in range(3):
-                chunk_ref[pl.ds(first + (3 * layer + a) * size_y, size_y), :] = velocity_ref[
-                    a, x * size_y : (x + 1) * size_y, :
-                ]
+                chunk_ref[pl.ds(start + a * size_y, size_y), :] = velocity_ref[a, x * size_y : (x + 1) * size_y, :]
         x = 0 if side == 0 else size_x - 1
-        chunk_ref[pl.ds(first + 6 * size_y, size_y), :] = viscosity_ref[x * size_y : (x + 1) * size_y, :]
-        for number, a in enumerate((0, 2)):
-            chunk_ref[pl.ds(other + number * size_y, size_y), :] = velocity_ref[
-                a, x * size_y : (x + 1) * size_y, :
-            ]
+        chunk_ref[pl.ds(other + 3 * size_y, size_y), :] = viscosity_ref[x * size_y : (x + 1) * size_y, :]
 
     group = size_z // 8
     lane2 = lanes_of((size_y, size_z))
@@ -172,6 +168,18 @@
 
     for j in range(flags):
         chunk_ref[pl.ds(target[j], 1), :] = gradients[j : j + 1, :]
+
+    edge = jnp.where(core == 0, size_z - 1, 0)
+    for side in range(2):
+        beside = neighbour(macro, side, macro_count)
+        rows = pl.ds(pl.multiple_of((2 * beside + 1 - core) * chunk_rows, 8), slot_rows)
+        x = 0 if side == 0 else size_x - 1
+        value = chunk_ref[rows, :]
+        for number, a in enumerate((0, 2)):
+            plane = velocity_ref[a, x * size_y : (x + 1) * size_y, :]
+            at = corner_lane + number
+            value = jnp.where(lane2 == at, rolled(plane, at - edge), value)
+        chunk_ref[rows, :] = value
     for copy in copies[4:]:
         copy.wait()
 
@@ -179,7 +187,7 @@
 def gather_rows(flag_cell, owner, velocity, viscosity, conformations, increments, capacity, owner_count):
     size_x, size_y, size_z = viscosity.shape
     flags = flag_cell.shape[0]
-    chunk_rows = slot_rows + item_count * size_y
+    chunk_rows = slot_rows + face_rows
     face = jax.ShapeDtypeStruct((item_count, size_x, size_z), jnp.float32)
     steps, _, _, dumbbells = increments.shape
     return pl.pallas_call(
@@ -378,9 +386,14 @@
     )(far(conformations), far(increments), chunks, first_conform, first_noise)
 
 
-def lines_kernel(macro_count, chunk_ref, first_ref, second_ref, out_ref, y_low_ref, y_high_ref):
+def lines_kernel(
+    macro_count, chunk_ref, received_ref, first_ref, second_ref, out_ref, y_low_ref, y_high_ref, handed_ref
+):
     out_ref[...] = chunk_ref[...]
     macro, core = place_of()
+    for side in range(2):
+        beside = neighbour(macro, side, macro_count)
+        handed_ref[side] = received_ref[2 * beside + 1 - core, slot_rows:, :]
     even = lax.axis_index("tile") & 1 == 0
     y_low_ref[...] = jnp.where(even, second_ref[...], first_ref[...])
     y_high_ref[...] = jnp.where(even, first_ref[...], second_ref[...])
@@ -408,17 +421,20 @@
     out_ref[other] = total
 
 
-def add_lines(chunks, first, second):
+def add_lines(chunks, received, first, second):
     face = jax.ShapeDtypeStruct(first.shape, jnp.float32)
     return pl.pallas_call(
         functools.partial(lines_kernel, chunks.shape[0] // 2),
-        out_shape=(jax.ShapeDtypeStruct(chunks.shape, jnp.float32), face, face),
-        in_specs=[VMEM, VMEM, VMEM],
-        out_specs=(VMEM, VMEM, VMEM),
+        out_shape=(
+            jax.ShapeDtypeStruct(chunks.shape, jnp.float32), face, face,
+            jax.ShapeDtypeStruct((2, face_rows, 128), jnp.float32),
+        ),
+        in_specs=[VMEM] * 4,
+        out_specs=(VMEM,) * 4,
         compiler_params=limit(4),
         cost_estimate=pl.CostEstimate(flops=20000, bytes_accessed=400000, transcendentals=0),
         name="add_lines",
-    )(chunks, first, second)
+    )(chunks, received, first, second)
 
 
 product_depth = 128
@@ -463,7 +479,7 @@
 
 def flow_kernel(
     size_x, size_y, size_z, macro_count, cell_ref, position_ref, velocity_ref, viscosity_ref, chunk_ref,
-    y_low_ref, y_high_ref, out_ref, corner_ref, edge_ref, lines_ref, pick_ref, spread_ref,
+    y_low_ref, y_high_ref, handed_ref, out_ref, corner_ref, edge_ref, lines_ref, pick_ref, spread_ref,
     padded, stress_x, stress_rest, faces, ghost_y, ghost_z, rows,
 ):
     macro, core = place_of()
@@ -496,27 +512,13 @@
 
     x_faces, x_others = [], []
     for s in range(2):
-        beside = jnp.maximum(macro - 1, 0) if s == 0 else jnp.minimum(macro + 1, macro_count - 1)
-        x_faces.append(
-            [
-                kept(chunk_ref[2 * beside + core, slot_rows + i * size_y : slot_rows + (i + 1) * size_y, :], inside[s])
-                for i in range(item_count)
-            ]
-        )
-        x_others.append(
-            [
-                kept(
-                    rolled(
-                        chunk_ref[
-                            2 * beside + 1 - core, slot_rows + i * size_y : slot_rows + (i + 1) * size_y, :
-                        ],
-                        2 * end + 1,
-                    ),
-                    inside[s],
-                )
-                for i in range(2)
-            ]
-        )
+        beside = neighbour(macro, s, macro_count)
+        outer = chunk_ref[2 * beside + core, slot_rows : slot_rows + 3 * size_y, :]
+        items = [outer[i * size_y : (i + 1) * size_y] for i in range(3)]
+        items += [handed_ref[s, i * size_y : (i + 1) * size_y, :] for i in range(4)]
+        x_faces.append([kept(item, inside[s]) for item in items])
+        corner = chunk_ref[2 * beside + 1 - core, 0:slot_rows, :]
+        x_others.append([kept(rolled(corner, end - (corner_lane + i)), inside[s]) for i in range(2)])
 
     group = size_z // 8
     packed = [
@@ -628,7 +630,7 @@
     lax.fori_loop(0, size_x, step_plane, 0, unroll=6)
 
 
-def flow_step(flag_cell, position, velocity, viscosity, chunks, y_low, y_high):
+def flow_step(flag_cell, position, velocity, viscosity, chunks, y_low, y_high, handed):
     size_x, size_y, size_z = viscosity.shape
     flags = flag_cell.shape[0]
     returned = chunks.shape[0] * back_rows
@@ -645,7 +647,7 @@
             jax.ShapeDtypeStruct((flags, 4 * returned), jnp.bfloat16),
             jax.ShapeDtypeStruct((row_count, 3 * product_depth), jnp.bfloat16),
         ),
-        in_specs=[SMEM] * 2 + [VMEM] * 5,
+        in_specs=[SMEM] * 2 + [VMEM] * 6,
         out_specs=(VMEM,) * 6,
         scratch_shapes=[
             pltpu.VMEM((3, *wide), jnp.float32),
@@ -663,7 +665,7 @@
         flag_cell, position,
         velocity.reshape(3, size_x * size_y, size_z),
         viscosity.reshape(size_x * size_y, size_z),
-        chunks, y_low, y_high,
+        chunks, y_low, y_high, handed,
     )
 
 
@@ -784,10 +786,11 @@
     last_state, polymer = advance(
         conformations, increments, received, first_conform, first_noise, capacity
     )
-    polymer, y_low, y_high = add_lines(polymer, first, second)
+    polymer, y_low, y_high, handed = add_lines(polymer, received, first, second)
     returned = exchange(polymer)
+    handed = lax.ppermute(handed, "micro", [(0, 1), (1, 0)])
     partial, corners, edges, lines, pick, spread = flow_step(
-        flag_cell, position, velocity, viscosity, received, y_low, y_high
+        flag_cell, position, velocity, viscosity, received, y_low, y_high, handed
     )
     velocity_next, flag_stress = add_polymer(
         returned, viscous, corners, edges, lines, pick, spread, partial, viscosity.shape

time: 29.4 us -> 28.3 us (0.963)
  waiting for transfers between devices: 6.26 us -> 5.18 us
    all_to_all x2, waiting for transfers between devices: 6.25 us -> 5.17 us  [exchange(): lax.all_to_all(rows, ('macro', 'micro'), split_axis=0, concat_axis=0, til...]
  transfers between devices with their start and end apart: 4 -> 5, of which waited for: 2 -> 2; matrix products, arithmetic and copies ran while one was open for 3% -> 3% of each run, Pallas kernels for 19% -> 20%
where the time goes in v15:
time: 28.3 us; the launch traced here: 28 us
  starting transfers between devices  10.9 us (39%)
  Pallas kernels  10.4 us (37%)
  waiting for transfers between devices  5.18 us (18%)
  local copies, waits for them, and re-layouts  0.77 us (3%)
  between operations  0.72 us (3%)
    all_to_all x2, starting transfers between devices, exchange(): lax.all_to_all(rows, ('macro', 'micro'), split_axis=0, concat_axis=0, til...  8.66 us
    all_to_all x2, waiting for transfers between devices, exchange(): lax.all_to_all(rows, ('macro', 'micro'), split_axis=0, concat_axis=0, til...  5.17 us
    pallas_call x1, Pallas kernels, advance(): pl.pallas_call(functools.partial(micro_kernel, capacity, parts, rows, gro...  3.19 us
    pallas_call x1, Pallas kernels, flow_step(): pl.pallas_call(functools.partial(flow_kernel, size_x, size_y, size_z, chu...  2.47 us
    pallas_call x1, Pallas kernels, gather_rows(): pl.pallas_call(functools.partial(gather_kernel, capacity, size_x, size_y,...  2.29 us
    pallas_call x1, Pallas kernels, add_polymer(): pl.pallas_call(functools.partial(polymer_kernel, size_x, size_y, size_z,...  1.78 us
    ppermute x1, starting transfers between devices, shards(): first = lax.ppermute(first, 'tile', swaps[0])  1.58 us
    unnamed x7, local copies, waits for them, and re-layouts  0.77 us
  transfers between devices with their start and end apart: 5, of which 2 were waited for; matrix products, arithmetic and copies ran while one was open for 3% of the time, Pallas kernels for 20%

profile of v15, /device:TPU:0, one launch (start us, length us, event | category | flops | bytes accessed | tf_op | source)
XLA Modules:
  0.0 28.0 jit_solution(7111039351597845376)
XLA Ops:
  0.6 2.3 %gather_rows.1 = (f32[320,128]{1,0:T(8,128)}, s32[32]{0:T(128)S(1)}, f32[32,128]{1,0:T(8,128)S(1)}, f32[7,24,128]{2,1,0:T(8,128)S(1)}, f32[7,24,128]{2,1,0:T(8,1...) custom-call(s32[32]{0:T(128)} %cell_ref.1, s32[32]{0:T(128)} %bitcast.11, ...), custom_call_target="tpu_custom_call" | custom-call | flops 400000 | bytes 3000000 | tf_op jit(solution)/shard_map/gather_rows/pallas_call | solution.py:193
  2.9 0.0 copy-start
  2.9 0.0 copy-start.1
  3.0 0.0 copy-start.2
  3.0 5.3 %all-to-all-start = ((f32[8,40,128]{2,1,0:T(8,128)}), f32[8,40,128]{2,1,0:T(8,128)S(1)}, u32[]{:S(2)}, u32[]{:S(2)}) async-start(f32[8,40,128]{2,1,0:T(8,128)} %bitcast.3), calls=%async_computation | async-start | bytes 327680 | tf_op jit(solution)/shard_map/all_to_all | solution.py:777
  8.3 1.6 %collective-permute-start = (f32[7,24,128]{2,1,0:T(8,128)S(1)}, f32[7,24,128]{2,1,0:T(8,128)S(1)}, u32[]{:S(2)}, u32[]{:S(2)}) collective-permute-start(f32[7,24,128]{2,1,0:T(8,128)S(1)} %get-tuple-element.28), channel_id=1, source_target_pairs={{0,2},{4,6},{2,0},{6,4},{1,3},{5,7},{3,1},{7,5},{8,10},{12,14},{10... | collective-permute-start | bytes 258056 | tf_op jit(solution)/shard_map/ppermute | solution.py:784
  9.9 0.7 %collective-permute-start.1 = (f32[7,24,128]{2,1,0:T(8,128)S(1)}, f32[7,24,128]{2,1,0:T(8,128)S(1)}, u32[]{:S(2)}, u32[]{:S(2)}) collective-permute-start(f32[7,24,128]{2,1,0:T(8,128)S(1)} %get-tuple-element.29), channel_id=1, source_target_pairs={{2,4},{4,2},{3,5},{5,3},{10,12},{12,10},{11,13},{13,11},{18,20},{2... | collective-permute-start | bytes 258056 | tf_op jit(solution)/shard_map/ppermute | solution.py:785
  10.5 3.6 %all-to-all-done.rate_ref.received_ref.chunk_ref = f32[8,40,128]{2,1,0:T(8,128)S(1)} async-done(((f32[8,40,128]{2,1,0:T(8,128)}), f32[8,40,128]{2,1,0:T(8,128)S(1)}, u32[]{:S(2)}, u32[]{:S(2)}) %all-to-all-start) | async-done | bytes 163872 | tf_op jit(solution)/shard_map/all_to_all | solution.py:777
  14.2 3.2 %advance.1 = (f32[3,64,512]{2,1,0:T(8,128)S(1)}, f32[8,8,128]{2,1,0:T(8,128)S(1)}) custom-call(f32[3,64,512]{2,1,0:T(8,128)} %conform_ref.1, bf16[16,3,64,512]{3,2,1,0:T(8,128)(2,1)} %noise_ref.1, f32[8,40,128]{2,1,0:T(8,128)S(1)} %all-to-all-done.rate_ref.received_ref.chunk_ref, f32[3,32,512]{2,1,0:T(8,128)S(1)} %get-tuple-element.25.first_conform_ref, ...), custom_call_target="tpu_custom_call" | custom-call | flops 20000000 | bytes 5000000 | tf_op jit(solution)/shard_map/advance/pallas_call | solution.py:366
  17.4 0.0 collective-permute-done.first_ref
  17.4 0.0 collective-permute-done.1.second_ref
  17.4 0.7 %add_lines.1 = (f32[8,8,128]{2,1,0:T(8,128)}, f32[7,24,128]{2,1,0:T(8,128)S(1)}, f32[7,24,128]{2,1,0:T(8,128)S(1)}, f32[2,32,128]{2,1,0:T(8,128)S(1)}) custom-call(f32[8,8,128]{2,1,0:T(8,128)S(1)} %get-tuple-element.27.chunk_ref, f32[8,40,128]{2,1,0:T(8,128)S(1)} %all-to-all-done.rate_ref.received_ref.chunk_ref, ...), custom_call_target="tpu_custom_call" | custom-call | flops 20000 | bytes 400000 | tf_op jit(solution)/shard_map/add_lines/pallas_call | solution.py:426
  18.1 0.0 collective-permute-start.2
  18.1 3.3 %all-to-all-start.1 = ((f32[8,8,128]{2,1,0:T(8,128)}), f32[8,8,128]{2,1,0:T(8,128)S(1)}, u32[]{:S(2)}, u32[]{:S(2)}) async-start(f32[8,8,128]{2,1,0:T(8,128)} %get-tuple-element.30), calls=%async_computation.1 | async-start | bytes 65536 | tf_op jit(solution)/shard_map/all_to_all | solution.py:777
  21.5 0.7 %copy.9 = f32[3,64,512]{2,1,0:T(8,128)} copy(f32[3,64,512]{2,1,0:T(8,128)S(1)} %get-tuple-element.46) | data formatting | bytes 786432
  22.2 0.0 collective-permute-done.2.handed_ref
  22.2 0.0 copy-done
  22.2 0.0 copy-done.1
  22.2 0.0 copy-done.2
  22.2 2.5 %flow_step.1 = (f32[3,192,128]{2,1,0:T(8,128)S(1)}, f32[8,128]{1,0:T(8,128)S(1)}, f32[4,24,128]{2,1,0:T(8,128)S(1)}, f32[3,32,128]{2,1,0:T(8,128)S(1)}, bf16[32,...) custom-call(s32[32]{0:T(128)S(1)} %copy-done.2, s32[32]{0:T(128)S(1)} %get-tuple-element.32.position_ref, ...), custom_call_target="tpu_custom_call" | custom-call | flops 4000000 | bytes 3000000 | tf_op jit(solution)/shard_map/flow_step/pallas_call | solution.py:640
  24.7 1.5 %all-to-all-done.1 = f32[8,8,128]{2,1,0:T(8,128)S(1)} async-done(((f32[8,8,128]{2,1,0:T(8,128)}), f32[8,8,128]{2,1,0:T(8,128)S(1)}, u32[]{:S(2)}, u32[]{:S(2)}) %all-to-all-start.1) | async-done | bytes 32800 | tf_op jit(solution)/shard_map/all_to_all | solution.py:777
  26.2 1.8 %add_polymer.1 = (f32[3,192,128]{2,1,0:T(8,128)}, f32[6,32]{1,0:T(8,128)}) custom-call(f32[64,128]{1,0:T(8,128)S(1)} %bitcast.10, f32[32,128]{1,0:T(8,128)S(1)} %get-tuple-element.31.viscous_ref, f32[8,128]{1,0:T(8,128)S(1)} %get-tuple-element.36.corner_ref, f32[4,24,128]{2,1,0:T(8,128)S(1)} %get-tuple-element.37.edge_ref, ...), custom_call_target="tpu_custom_call" | custom-call | flops 400000 | bytes 3000000 | tf_op jit(solution)/shard_map/add_polymer/pallas_call | solution.py:749
Async XLA Ops:
  2.9 19.3 %copy-start = (f32[3,24,8,128]{3,2,1,0:T(8,128)S(1)}, f32[3,24,8,128]{3,2,1,0:T(8,128)}, u32[]{:S(2)}) copy-start(f32[3,24,8,128]{3,2,1,0:T(8,128)} %param.6) | copy-start | bytes 884740
  2.9 19.3 %copy-start.1 = (f32[24,8,128]{2,1,0:T(8,128)S(1)}, f32[24,8,128]{2,1,0:T(8,128)}, u32[]{:S(2)}) copy-start(f32[24,8,128]{2,1,0:T(8,128)} %param.7) | copy-start | bytes 294916
  3.0 19.3 %copy-start.2 = (s32[32]{0:T(128)S(1)}, s32[32]{0:T(128)}, u32[]{:S(2)}) copy-start(s32[32]{0:T(128)} %cell_ref.1) | copy-start | bytes 388
  3.0 11.2 %all-to-all-start = ((f32[8,40,128]{2,1,0:T(8,128)}), f32[8,40,128]{2,1,0:T(8,128)S(1)}, u32[]{:S(2)}, u32[]{:S(2)}) async-start(f32[8,40,128]{2,1,0:T(8,128)} %bitcast.3), calls=%async_computation | async-start | bytes 327680 | tf_op jit(solution)/shard_map/all_to_all | solution.py:777
  8.3 9.1 %collective-permute-start = (f32[7,24,128]{2,1,0:T(8,128)S(1)}, f32[7,24,128]{2,1,0:T(8,128)S(1)}, u32[]{:S(2)}, u32[]{:S(2)}) collective-permute-start(f32[7,24,128]{2,1,0:T(8,128)S(1)} %get-tuple-element.28), channel_id=1, source_target_pairs={{0,2},{4,6},{2,0},{6,4},{1,3},{5,7},{3,1},{7,5},{8,10},{12,14},{10... | collective-permute-start | bytes 258056 | tf_op jit(solution)/shard_map/ppermute | solution.py:784
  9.9 7.5 %collective-permute-start.1 = (f32[7,24,128]{2,1,0:T(8,128)S(1)}, f32[7,24,128]{2,1,0:T(8,128)S(1)}, u32[]{:S(2)}, u32[]{:S(2)}) collective-permute-start(f32[7,24,128]{2,1,0:T(8,128)S(1)} %get-tuple-element.29), channel_id=1, source_target_pairs={{2,4},{4,2},{3,5},{5,3},{10,12},{12,10},{11,13},{13,11},{18,20},{2... | collective-permute-start | bytes 258056 | tf_op jit(solution)/shard_map/ppermute | solution.py:785
  18.1 4.1 %collective-permute-start.2 = (f32[2,32,128]{2,1,0:T(8,128)S(1)}, f32[2,32,128]{2,1,0:T(8,128)S(1)}, u32[]{:S(2)}, u32[]{:S(2)}) collective-permute-start(f32[2,32,128]{2,1,0:T(8,128)S(1)} %get-tuple-element.35), channel_id=1, source_target_pairs={{0,1},{1,0},{2,3},{3,2},{4,5},{5,4},{6,7},{7,6},{8,9},{9,8},{10,11... | collective-permute-start | bytes 98312 | tf_op jit(solution)/shard_map/ppermute | solution.py:791
  18.1 8.1 %all-to-all-start.1 = ((f32[8,8,128]{2,1,0:T(8,128)}), f32[8,8,128]{2,1,0:T(8,128)S(1)}, u32[]{:S(2)}, u32[]{:S(2)}) async-start(f32[8,8,128]{2,1,0:T(8,128)} %get-tuple-element.30), calls=%async_computation.1 | async-start | bytes 65536 | tf_op jit(solution)/shard_map/all_to_all | solution.py:777

commit v16 on v15

--- a/solution.py
+++ b/solution.py
@@ -440,7 +440,7 @@
 product_depth = 128
 
 
-def one_hots(size_y, size_z, cell_ref, position_ref, lines_ref, pick_ref, spread_ref, rows):
+def one_hots(core, size_y, size_z, cell_ref, position_ref, lines_ref, pick_ref, spread_ref, rows):
     flags = cell_ref.shape[0]
     weight = 0.5 * macro_step
     row_count = spread_ref.shape[0]
@@ -468,7 +468,9 @@
         owner = lax.div(position_ref[j], slot_rows)
         rank = position_ref[j] - owner * slot_rows
         lines_ref[2, j : j + 1, :] = jnp.where(group == rank, 1.0, 0.0)
-        slot = jnp.where(flag_row == j, owner * back_rows + polymer_row, slot)
+        chip, sender = lax.div(owner, 2), owner & 1
+        row = jnp.where(sender == core, 0, returned // 2) + (2 * chip + core) * back_rows + polymer_row
+        slot = jnp.where(flag_row == j, row, slot)
     spread = rows[...].T[:row_count].astype(jnp.bfloat16)
     pick = jnp.where(slot_lane == slot, 1.0, 0.0).astype(jnp.bfloat16)
     for piece in range(3):
@@ -483,7 +485,7 @@
     padded, stress_x, stress_rest, faces, ghost_y, ghost_z, rows,
 ):
     macro, core = place_of()
-    one_hots(size_y, size_z, cell_ref, position_ref, lines_ref, pick_ref, spread_ref, rows)
+    one_hots(core, size_y, size_z, cell_ref, position_ref, lines_ref, pick_ref, spread_ref, rows)
     inside = (macro > 0, macro < macro_count - 1)
     sign_z = jnp.where(core == 0, 1.0, -1.0)
     end = jnp.where(core == 0, size_z - 1, 0)
@@ -633,7 +635,7 @@
 def flow_step(flag_cell, position, velocity, viscosity, chunks, y_low, y_high, handed):
     size_x, size_y, size_z = viscosity.shape
     flags = flag_cell.shape[0]
-    returned = chunks.shape[0] * back_rows
+    returned = 2 * chunks.shape[0] * back_rows
     row_count = size_x * size_y
     planes = (size_x, size_y, size_z)
     wide = (size_x + 2, size_y, size_z)
@@ -677,12 +679,12 @@
 
 
 def polymer_kernel(
-    size_x, size_y, size_z, macro_count, chunk_ref, viscous_ref, corner_ref, edge_ref, lines_ref, pick_ref,
+    size_x, size_y, size_z, macro_count, own_ref, other_ref, viscous_ref, corner_ref, edge_ref, lines_ref, pick_ref,
     spread_ref, partial_ref, out_ref, flag_ref, field, write_sem,
 ):
     flags = viscous_ref.shape[0]
     macro, core = place_of()
-    chunks = chunk_ref[...]
+    chunks = jnp.concatenate([own_ref[...], other_ref[...]], axis=0)
     split = jnp.concatenate((*pieces(chunks), jnp.zeros(chunks.shape, jnp.bfloat16)), axis=0)
     values = jnp.dot(pick_ref[...], split, preferred_element_type=jnp.float32) * lines_ref[2]
     here, beside_z = lines_ref[0], lines_ref[1]
@@ -721,10 +723,10 @@
             at = x * size_y + (0 if u == 0 else size_y - 1)
             for a in range(2):
                 number = 4 * s + 2 * u + a
-                line = corner_ref[number : number + 1, :] * chunk_ref[pl.ds(start + 2 * u + a, 1), :]
+                line = corner_ref[number : number + 1, :] * own_ref[pl.ds(start + 2 * u + a, 1), :]
                 field[1 - a, at : at + 1, :] += jnp.where(inside, line, 0.0)
-    start = pl.multiple_of((2 * macro + 1 - core) * back_rows, 8)
-    packed = chunk_ref[pl.ds(start, back_rows), :]
+    start = pl.multiple_of((2 * macro + core) * back_rows, 8)
+    packed = other_ref[pl.ds(start, back_rows), :]
     end = jnp.where(core == 0, size_z - 1, 0)
     for u in range(2):
         y = 0 if u == 0 else size_y - 1
@@ -743,22 +745,22 @@
         copy.wait()
 
 
-def add_polymer(chunks, viscous, corners, edges, lines, pick, spread, partial, shape):
+def add_polymer(own, other, viscous, corners, edges, lines, pick, spread, partial, shape):
     flags = viscous.shape[0]
     size_x, size_y, size_z = shape
     return pl.pallas_call(
-        functools.partial(polymer_kernel, size_x, size_y, size_z, chunks.shape[0] // 2),
+        functools.partial(polymer_kernel, size_x, size_y, size_z, own.shape[0]),
         out_shape=(
             jax.ShapeDtypeStruct(partial.shape, jnp.float32),
             jax.ShapeDtypeStruct((6, flags), jnp.float32),
         ),
-        in_specs=[VMEM] * 8,
+        in_specs=[VMEM] * 9,
         out_specs=(pl.BlockSpec(memory_space=pltpu.HBM), VMEM),
         scratch_shapes=[pltpu.VMEM(partial.shape, jnp.float32), pltpu.SemaphoreType.DMA((3,))],
         compiler_params=limit(8),
         cost_estimate=pl.CostEstimate(flops=400000, bytes_accessed=3000000, transcendentals=0),
         name="add_polymer",
-    )(chunks.reshape(-1, 128), viscous, corners, edges, lines, pick, spread, partial)
+    )(own.reshape(-1, 128), other.reshape(-1, 128), viscous, corners, edges, lines, pick, spread, partial)
 
 
 def shards(velocity, viscosity, flag_cell, flag_owner, conformations, increments):
@@ -787,13 +789,16 @@
         conformations, increments, received, first_conform, first_noise, capacity
     )
     polymer, y_low, y_high, handed = add_lines(polymer, received, first, second)
-    returned = exchange(polymer)
+    returned = lax.all_to_all(
+        polymer.reshape(macro_count, 2 * back_rows, 128), "macro", split_axis=0, concat_axis=0, tiled=True
+    )
+    other = lax.ppermute(returned, "micro", [(0, 1), (1, 0)])
     handed = lax.ppermute(handed, "micro", [(0, 1), (1, 0)])
     partial, corners, edges, lines, pick, spread = flow_step(
         flag_cell, position, velocity, viscosity, received, y_low, y_high, handed
     )
     velocity_next, flag_stress = add_polymer(
-        returned, viscous, corners, edges, lines, pick, spread, partial, viscosity.shape
+        returned, other, viscous, corners, edges, lines, pick, spread, partial, viscosity.shape
     )
     return (velocity_next.reshape(velocity.shape), last_state, flag_stress)
 

time: 28.3 us -> 31.8 us (1.12)
  waiting for transfers between devices: 5.18 us -> 8.3 us
    all_to_all x0 -> x1, waiting for transfers between devices: none -> 4.64 us  [shards(): lax.all_to_all(polymer.reshape(macro_count, 2 * back_rows, 128), 'macro',...]
    all_to_all x2 -> x1, starting transfers between devices: 8.66 us -> 5.31 us  [exchange(): lax.all_to_all(rows, ('macro', 'micro'), split_axis=0, concat_axis=0, til...]
    all_to_all x0 -> x1, starting transfers between devices: none -> 3.26 us  [shards(): lax.all_to_all(polymer.reshape(macro_count, 2 * back_rows, 128), 'macro',...]
    all_to_all x2 -> x1, waiting for transfers between devices: 5.17 us -> 3.64 us  [exchange(): lax.all_to_all(rows, ('macro', 'micro'), split_axis=0, concat_axis=0, til...]
  transfers between devices with their start and end apart: 5 -> 6, of which waited for: 2 -> 2; matrix products, arithmetic and copies ran while one was open for 3% -> 2% of each run, Pallas kernels for 20% -> 19%
where the time goes in v16:
time: 31.8 us; the launch traced here: 31.4 us
  starting transfers between devices  10.9 us (34%)
  Pallas kernels  10.7 us (34%)
  waiting for transfers between devices  8.3 us (26%)
  local copies, waits for them, and re-layouts  0.77 us (2%)
  between operations  0.74 us (2%)
    all_to_all x1, starting transfers between devices, exchange(): lax.all_to_all(rows, ('macro', 'micro'), split_axis=0, concat_axis=0, til...  5.31 us
    all_to_all x1, waiting for transfers between devices, shards(): lax.all_to_all(polymer.reshape(macro_count, 2 * back_rows, 128), 'macro',...  4.64 us
    all_to_all x1, waiting for transfers between devices, exchange(): lax.all_to_all(rows, ('macro', 'micro'), split_axis=0, concat_axis=0, til...  3.64 us
    all_to_all x1, starting transfers between devices, shards(): lax.all_to_all(polymer.reshape(macro_count, 2 * back_rows, 128), 'macro',...  3.26 us
    pallas_call x1, Pallas kernels, advance(): pl.pallas_call(functools.partial(micro_kernel, capacity, parts, rows, gro...  3.19 us
    pallas_call x1, Pallas kernels, flow_step(): pl.pallas_call(functools.partial(flow_kernel, size_x, size_y, size_z, chu...  2.68 us
    pallas_call x1, Pallas kernels, gather_rows(): pl.pallas_call(functools.partial(gather_kernel, capacity, size_x, size_y,...  2.3 us
    pallas_call x1, Pallas kernels, add_polymer(): pl.pallas_call(functools.partial(polymer_kernel, size_x, size_y, size_z,...  1.8 us
  transfers between devices with their start and end apart: 6, of which 2 were waited for; matrix products, arithmetic and copies ran while one was open for 2% of the time, Pallas kernels for 19%

profile of v16, /device:TPU:0, one launch (start us, length us, event | category | flops | bytes accessed | tf_op | source)
XLA Modules:
  0.0 31.4 jit_solution(2116787582870293815)
XLA Ops:
  0.6 2.3 %gather_rows.1 = (f32[320,128]{1,0:T(8,128)}, s32[32]{0:T(128)S(1)}, f32[32,128]{1,0:T(8,128)S(1)}, f32[7,24,128]{2,1,0:T(8,128)S(1)}, f32[7,24,128]{2,1,0:T(8,1...) custom-call(s32[32]{0:T(128)} %cell_ref.1, s32[32]{0:T(128)} %bitcast.14, ...), custom_call_target="tpu_custom_call" | custom-call | flops 400000 | bytes 3000000 | tf_op jit(solution)/shard_map/gather_rows/pallas_call | solution.py:193
  2.9 0.0 copy-start
  2.9 0.0 copy-start.1
  3.0 0.0 copy-start.2
  3.0 5.3 %all-to-all-start = ((f32[8,40,128]{2,1,0:T(8,128)}), f32[8,40,128]{2,1,0:T(8,128)S(1)}, u32[]{:S(2)}, u32[]{:S(2)}) async-start(f32[8,40,128]{2,1,0:T(8,128)} %bitcast.3), calls=%async_computation | async-start | bytes 327680 | tf_op jit(solution)/shard_map/all_to_all | solution.py:779
  8.3 1.6 %collective-permute-start = (f32[7,24,128]{2,1,0:T(8,128)S(1)}, f32[7,24,128]{2,1,0:T(8,128)S(1)}, u32[]{:S(2)}, u32[]{:S(2)}) collective-permute-start(f32[7,24,128]{2,1,0:T(8,128)S(1)} %get-tuple-element.28), channel_id=1, source_target_pairs={{0,2},{4,6},{2,0},{6,4},{1,3},{5,7},{3,1},{7,5},{8,10},{12,14},{10... | collective-permute-start | bytes 258056 | tf_op jit(solution)/shard_map/ppermute | solution.py:786
  9.9 0.7 %collective-permute-start.1 = (f32[7,24,128]{2,1,0:T(8,128)S(1)}, f32[7,24,128]{2,1,0:T(8,128)S(1)}, u32[]{:S(2)}, u32[]{:S(2)}) collective-permute-start(f32[7,24,128]{2,1,0:T(8,128)S(1)} %get-tuple-element.29), channel_id=1, source_target_pairs={{2,4},{4,2},{3,5},{5,3},{10,12},{12,10},{11,13},{13,11},{18,20},{2... | collective-permute-start | bytes 258056 | tf_op jit(solution)/shard_map/ppermute | solution.py:787
  10.5 3.6 %all-to-all-done.rate_ref.received_ref.chunk_ref = f32[8,40,128]{2,1,0:T(8,128)S(1)} async-done(((f32[8,40,128]{2,1,0:T(8,128)}), f32[8,40,128]{2,1,0:T(8,128)S(1)}, u32[]{:S(2)}, u32[]{:S(2)}) %all-to-all-start) | async-done | bytes 163872 | tf_op jit(solution)/shard_map/all_to_all | solution.py:779
  14.2 3.2 %advance.1 = (f32[3,64,512]{2,1,0:T(8,128)S(1)}, f32[8,8,128]{2,1,0:T(8,128)S(1)}) custom-call(f32[3,64,512]{2,1,0:T(8,128)} %conform_ref.1, bf16[16,3,64,512]{3,2,1,0:T(8,128)(2,1)} %noise_ref.1, f32[8,40,128]{2,1,0:T(8,128)S(1)} %all-to-all-done.rate_ref.received_ref.chunk_ref, f32[3,32,512]{2,1,0:T(8,128)S(1)} %get-tuple-element.25.first_conform_ref, ...), custom_call_target="tpu_custom_call" | custom-call | flops 20000000 | bytes 5000000 | tf_op jit(solution)/shard_map/advance/pallas_call | solution.py:366
  17.4 0.0 collective-permute-done.first_ref
  17.4 0.0 collective-permute-done.1.second_ref
  17.4 0.7 %add_lines.1 = (f32[8,8,128]{2,1,0:T(8,128)}, f32[7,24,128]{2,1,0:T(8,128)S(1)}, f32[7,24,128]{2,1,0:T(8,128)S(1)}, f32[2,32,128]{2,1,0:T(8,128)S(1)}) custom-call(f32[8,8,128]{2,1,0:T(8,128)S(1)} %get-tuple-element.27.chunk_ref, f32[8,40,128]{2,1,0:T(8,128)S(1)} %all-to-all-done.rate_ref.received_ref.chunk_ref, ...), custom_call_target="tpu_custom_call" | custom-call | flops 20000 | bytes 400000 | tf_op jit(solution)/shard_map/add_lines/pallas_call | solution.py:426
  18.1 3.3 %all-to-all-start.1 = ((f32[4,16,128]{2,1,0:T(8,128)}), f32[4,16,128]{2,1,0:T(8,128)S(1)}, u32[]{:S(2)}, u32[]{:S(2)}) async-start(f32[4,16,128]{2,1,0:T(8,128)} %bitcast.4), calls=%async_computation.1 | async-start | bytes 65536 | tf_op jit(solution)/shard_map/all_to_all | solution.py:792
  21.4 0.1 collective-permute-start.3
  21.5 4.6 %all-to-all-done.1 = f32[4,16,128]{2,1,0:T(8,128)S(1)} async-done(((f32[4,16,128]{2,1,0:T(8,128)}), f32[4,16,128]{2,1,0:T(8,128)S(1)}, u32[]{:S(2)}, u32[]{:S(2)}) %all-to-all-start.1) | async-done | bytes 32800 | tf_op jit(solution)/shard_map/all_to_all | solution.py:792
  26.1 0.0 collective-permute-start.2
  26.1 0.7 %copy.9 = f32[3,64,512]{2,1,0:T(8,128)} copy(f32[3,64,512]{2,1,0:T(8,128)S(1)} %get-tuple-element.46) | data formatting | bytes 786432
  26.8 0.0 collective-permute-done.3.handed_ref
  26.9 0.0 copy-done
  26.9 0.0 copy-done.1
  26.9 0.0 copy-done.2
  26.9 2.7 %flow_step.1 = (f32[3,192,128]{2,1,0:T(8,128)S(1)}, f32[8,128]{1,0:T(8,128)S(1)}, f32[4,24,128]{2,1,0:T(8,128)S(1)}, f32[3,32,128]{2,1,0:T(8,128)S(1)}, bf16[32,...) custom-call(s32[32]{0:T(128)S(1)} %copy-done.2, s32[32]{0:T(128)S(1)} %get-tuple-element.32.position_ref, ...), custom_call_target="tpu_custom_call" | custom-call | flops 4000000 | bytes 3000000 | tf_op jit(solution)/shard_map/flow_step/pallas_call | solution.py:642
  29.6 0.0 collective-permute-done.2
  29.6 1.8 %add_polymer.1 = (f32[3,192,128]{2,1,0:T(8,128)}, f32[6,32]{1,0:T(8,128)}) custom-call(f32[64,128]{1,0:T(8,128)S(1)} %bitcast.12, f32[64,128]{1,0:T(8,128)S(1)} %bitcast.13, f32[32,128]{1,0:T(8,128)S(1)} %get-tuple-element.31.viscous_ref, f32[8,128]{1,0:T(8,128)S(1)} %get-tuple-element.36.corner_ref, f32[4,24,128]{2,1,0:T(8,128)S(1)} %get-tuple-element.37.edge_ref, ...), custom_call_target="tpu_custom_call" | custom-call | flops 400000 | bytes 3000000 | tf_op jit(solution)/shard_map/add_polymer/pallas_call | solution.py:751
Async XLA Ops:
  2.9 23.9 %copy-start = (f32[3,24,8,128]{3,2,1,0:T(8,128)S(1)}, f32[3,24,8,128]{3,2,1,0:T(8,128)}, u32[]{:S(2)}) copy-start(f32[3,24,8,128]{3,2,1,0:T(8,128)} %param.6) | copy-start | bytes 884740
  2.9 23.9 %copy-start.1 = (f32[24,8,128]{2,1,0:T(8,128)S(1)}, f32[24,8,128]{2,1,0:T(8,128)}, u32[]{:S(2)}) copy-start(f32[24,8,128]{2,1,0:T(8,128)} %param.7) | copy-start | bytes 294916
  3.0 23.9 %copy-start.2 = (s32[32]{0:T(128)S(1)}, s32[32]{0:T(128)}, u32[]{:S(2)}) copy-start(s32[32]{0:T(128)} %cell_ref.1) | copy-start | bytes 388
  3.0 11.2 %all-to-all-start = ((f32[8,40,128]{2,1,0:T(8,128)}), f32[8,40,128]{2,1,0:T(8,128)S(1)}, u32[]{:S(2)}, u32[]{:S(2)}) async-start(f32[8,40,128]{2,1,0:T(8,128)} %bitcast.3), calls=%async_computation | async-start | bytes 327680 | tf_op jit(solution)/shard_map/all_to_all | solution.py:779
  8.3 9.1 %collective-permute-start = (f32[7,24,128]{2,1,0:T(8,128)S(1)}, f32[7,24,128]{2,1,0:T(8,128)S(1)}, u32[]{:S(2)}, u32[]{:S(2)}) collective-permute-start(f32[7,24,128]{2,1,0:T(8,128)S(1)} %get-tuple-element.28), channel_id=1, source_target_pairs={{0,2},{4,6},{2,0},{6,4},{1,3},{5,7},{3,1},{7,5},{8,10},{12,14},{10... | collective-permute-start | bytes 258056 | tf_op jit(solution)/shard_map/ppermute | solution.py:786
  9.9 7.5 %collective-permute-start.1 = (f32[7,24,128]{2,1,0:T(8,128)S(1)}, f32[7,24,128]{2,1,0:T(8,128)S(1)}, u32[]{:S(2)}, u32[]{:S(2)}) collective-permute-start(f32[7,24,128]{2,1,0:T(8,128)S(1)} %get-tuple-element.29), channel_id=1, source_target_pairs={{2,4},{4,2},{3,5},{5,3},{10,12},{12,10},{11,13},{13,11},{18,20},{2... | collective-permute-start | bytes 258056 | tf_op jit(solution)/shard_map/ppermute | solution.py:787
  18.1 8.0 %all-to-all-start.1 = ((f32[4,16,128]{2,1,0:T(8,128)}), f32[4,16,128]{2,1,0:T(8,128)S(1)}, u32[]{:S(2)}, u32[]{:S(2)}) async-start(f32[4,16,128]{2,1,0:T(8,128)} %bitcast.4), calls=%async_computation.1 | async-start | bytes 65536 | tf_op jit(solution)/shard_map/all_to_all | solution.py:792
  21.4 5.5 %collective-permute-start.3 = (f32[2,32,128]{2,1,0:T(8,128)S(1)}, f32[2,32,128]{2,1,0:T(8,128)S(1)}, u32[]{:S(2)}, u32[]{:S(2)}) collective-permute-start(f32[2,32,128]{2,1,0:T(8,128)S(1)} %get-tuple-element.35), channel_id=1, source_target_pairs={{0,1},{1,0},{2,3},{3,2},{4,5},{5,4},{6,7},{7,6},{8,9},{9,8},{10,11... | collective-permute-start | bytes 98312 | tf_op jit(solution)/shard_map/ppermute | solution.py:796
  26.1 3.5 %collective-permute-start.2 = (f32[4,16,128]{2,1,0:T(8,128)S(1)}, f32[4,16,128]{2,1,0:T(8,128)S(1)}, u32[]{:S(2)}, u32[]{:S(2)}) collective-permute-start(f32[4,16,128]{2,1,0:T(8,128)S(1)} %all-to-all-done.1), channel_id=1, source_target_pairs={{0,1},{1,0},{2,3},{3,2},{4,5},{5,4},{6,7},{7,6},{8,9},{9,8},{10,11... | collective-permute-start | bytes 98312 | tf_op jit(solution)/shard_map/ppermute | solution.py:795

commit v17 on v15

--- a/solution.py
+++ b/solution.py
@@ -29,8 +29,9 @@
 
 
 slot_rows = 8
-face_rows = 32
-corner_lane = 64
+chunk_rows = 32
+half_face = 28
+handed_rows = 48
 item_count = 7
 back_rows = 8
 polymer_row = 4
@@ -67,7 +68,7 @@
 def gather_kernel(
     capacity, size_x, size_y, size_z, macro_count, cell_in, owner_in, velocity_in, viscosity_in,
     conform_in, noise_in, chunk_ref, position_ref, viscous_ref, first_ref, second_ref, conform_ref, noise_ref,
-    cell_ref, owner_ref, velocity_ref, viscosity_ref, masked, gradients, target, count, sems,
+    cell_ref, owner_ref, velocity_ref, viscosity_ref, masked, gradients, paired, target, count, sems,
 ):
     flags = cell_ref.shape[0]
     copies = [
@@ -82,20 +83,20 @@
     ]
     for copy in copies:
         copy.start()
-    chunk_rows = slot_rows + face_rows
+    paired_rows = paired.shape[0] // 2
     macro, core = place_of()
     lane = lanes_of((1, size_z))
 
     for owner in range(count.shape[0]):
         count[owner] = 0
-        chunk_ref[owner * chunk_rows : owner * chunk_rows + slot_rows, :] = jnp.zeros((slot_rows, 128), jnp.float32)
+    paired[...] = jnp.zeros_like(paired)
     for copy in copies[:2]:
         copy.wait()
     for j in range(flags):
         owner = owner_ref[j]
         rank = count[owner]
         count[owner] = rank + 1
-        target[j] = owner * chunk_rows + rank
+        target[j] = (rank & 1) * paired_rows + owner * (slot_rows // 2) + lax.shift_right_logical(rank, 1)
         position_ref[j] = owner * slot_rows + rank
     for copy in copies[2:4]:
         copy.wait()
@@ -131,18 +132,18 @@
 
     for side in range(2):
         beside = neighbour(macro, side, macro_count)
-        same = pl.multiple_of((2 * beside + core) * chunk_rows + slot_rows, 8)
-        other = pl.multiple_of((2 * beside + 1 - core) * chunk_rows + slot_rows, 8)
-        for layer, start in enumerate((same, other)):
+        for layer, owner in enumerate((2 * beside + core, 2 * beside + 1 - core)):
+            start = pl.multiple_of(owner * chunk_rows, 8)
             x = layer if side == 0 else size_x - 1 - layer
             for a in range(3):
                 chunk_ref[pl.ds(start + a * size_y, size_y), :] = velocity_ref[a, x * size_y : (x + 1) * size_y, :]
-        x = 0 if side == 0 else size_x - 1
-        chunk_ref[pl.ds(other + 3 * size_y, size_y), :] = viscosity_ref[x * size_y : (x + 1) * size_y, :]
+            x = 0 if side == 0 else size_x - 1
+            half = x * size_y + layer * (size_y // 2)
+            chunk_ref[pl.ds(start + 3 * size_y, size_y // 2), :] = viscosity_ref[half : half + size_y // 2, :]
 
     group = size_z // 8
     lane2 = lanes_of((size_y, size_z))
-    first = pl.multiple_of((2 * macro + 1 - core) * chunk_rows + slot_rows, 8)
+    first = pl.multiple_of((2 * macro + 1 - core) * chunk_rows, 8)
     source = jnp.where(core == 0, size_z - 2, 0)
     for block in range(-(-size_x // group)):
         total = jnp.zeros((size_y, size_z), jnp.float32)
@@ -167,19 +168,12 @@
     viscous_ref[...] = stress
 
     for j in range(flags):
-        chunk_ref[pl.ds(target[j], 1), :] = gradients[j : j + 1, :]
-
-    edge = jnp.where(core == 0, size_z - 1, 0)
-    for side in range(2):
-        beside = neighbour(macro, side, macro_count)
-        rows = pl.ds(pl.multiple_of((2 * beside + 1 - core) * chunk_rows, 8), slot_rows)
-        x = 0 if side == 0 else size_x - 1
-        value = chunk_ref[rows, :]
-        for number, a in enumerate((0, 2)):
-            plane = velocity_ref[a, x * size_y : (x + 1) * size_y, :]
-            at = corner_lane + number
-            value = jnp.where(lane2 == at, rolled(plane, at - edge), value)
-        chunk_ref[rows, :] = value
+        paired[pl.ds(target[j], 1), :] = gradients[j : j + 1, :]
+    rows = paired[0:paired_rows, :] + rolled(paired[paired_rows:, :], 64)
+    for owner in range(count.shape[0]):
+        chunk_ref[owner * chunk_rows + half_face : (owner + 1) * chunk_rows, :] = rows[
+            owner * (slot_rows // 2) : (owner + 1) * (slot_rows // 2)
+        ]
     for copy in copies[4:]:
         copy.wait()
 
@@ -187,7 +181,6 @@
 def gather_rows(flag_cell, owner, velocity, viscosity, conformations, increments, capacity, owner_count):
     size_x, size_y, size_z = viscosity.shape
     flags = flag_cell.shape[0]
-    chunk_rows = slot_rows + face_rows
     face = jax.ShapeDtypeStruct((item_count, size_x, size_z), jnp.float32)
     steps, _, _, dumbbells = increments.shape
     return pl.pallas_call(
@@ -210,6 +203,7 @@
             pltpu.VMEM((size_x * size_y, size_z), jnp.float32),
             pltpu.VMEM((10, flags, size_z), jnp.float32),
             pltpu.VMEM((flags, 128), jnp.float32),
+            pltpu.VMEM((owner_count * slot_rows, 128), jnp.float32),
             pltpu.SMEM((flags,), jnp.int32),
             pltpu.SMEM((owner_count,), jnp.int32),
             pltpu.SemaphoreType.DMA((6,)),
@@ -266,7 +260,9 @@
     for step in range(steps // first_share):
         noise[step, :, 0:rows, :] = first_noise_ref[step]
     for owner in range(owners):
-        rate[owner * capacity : (owner + 1) * capacity, :] = rate_ref[owner, 0:capacity, :]
+        packed = rate_ref[owner, half_face : half_face + capacity // 2, :]
+        rate[pl.ds(owner * capacity, capacity // 2, stride=2), :] = packed
+        rate[pl.ds(owner * capacity + 1, capacity // 2, stride=2), :] = rolled(packed, 64)
         chunk_ref[owner] = jnp.zeros(chunk_ref.shape[1:], jnp.float32)
     for a in range(3):
         for b in range(3):
@@ -393,7 +389,11 @@
     macro, core = place_of()
     for side in range(2):
         beside = neighbour(macro, side, macro_count)
-        handed_ref[side] = received_ref[2 * beside + 1 - core, slot_rows:, :]
+        handed_ref[side, 0:chunk_rows, :] = received_ref[2 * beside + 1 - core]
+        for number, a in enumerate((0, 2)):
+            handed_ref[side, chunk_rows + number * 8 : chunk_rows + (number + 1) * 8, :] = received_ref[
+                2 * beside + core, a * 8 : (a + 1) * 8, :
+            ]
     even = lax.axis_index("tile") & 1 == 0
     y_low_ref[...] = jnp.where(even, second_ref[...], first_ref[...])
     y_high_ref[...] = jnp.where(even, first_ref[...], second_ref[...])
@@ -427,7 +427,7 @@
         functools.partial(lines_kernel, chunks.shape[0] // 2),
         out_shape=(
             jax.ShapeDtypeStruct(chunks.shape, jnp.float32), face, face,
-            jax.ShapeDtypeStruct((2, face_rows, 128), jnp.float32),
+            jax.ShapeDtypeStruct((2, handed_rows, 128), jnp.float32),
         ),
         in_specs=[VMEM] * 4,
         out_specs=(VMEM,) * 4,
@@ -480,7 +480,7 @@
 def flow_kernel(
     size_x, size_y, size_z, macro_count, cell_ref, position_ref, velocity_ref, viscosity_ref, chunk_ref,
     y_low_ref, y_high_ref, handed_ref, out_ref, corner_ref, edge_ref, lines_ref, pick_ref, spread_ref,
-    padded, stress_x, stress_rest, faces, ghost_y, ghost_z, rows,
+    padded, stress_x, stress_rest, faces, ghost_y, ghost_z, rows, halves,
 ):
     macro, core = place_of()
     one_hots(size_y, size_z, cell_ref, position_ref, lines_ref, pick_ref, spread_ref, rows)
@@ -511,18 +511,22 @@
         )
 
     x_faces, x_others = [], []
+    half = size_y // 2
     for s in range(2):
         beside = neighbour(macro, s, macro_count)
-        outer = chunk_ref[2 * beside + core, slot_rows : slot_rows + 3 * size_y, :]
+        outer = chunk_ref[2 * beside + core]
         items = [outer[i * size_y : (i + 1) * size_y] for i in range(3)]
-        items += [handed_ref[s, i * size_y : (i + 1) * size_y, :] for i in range(4)]
+        items += [handed_ref[s, i * size_y : (i + 1) * size_y, :] for i in range(3)]
+        halves[s, 0:half, :] = chunk_ref[2 * beside + core, 3 * size_y : 3 * size_y + half, :]
+        halves[s, half:, :] = handed_ref[s, 3 * size_y : 3 * size_y + half, :]
+        items.append(halves[s])
         x_faces.append([kept(item, inside[s]) for item in items])
-        corner = chunk_ref[2 * beside + 1 - core, 0:slot_rows, :]
-        x_others.append([kept(rolled(corner, end - (corner_lane + i)), inside[s]) for i in range(2)])
+        corners = [handed_ref[s, chunk_rows + i * size_y : chunk_rows + (i + 1) * size_y, :] for i in range(2)]
+        x_others.append([kept(rolled(corner, 2 * end + 1), inside[s]) for corner in corners])
 
     group = size_z // 8
     packed = [
-        chunk_ref[2 * macro + 1 - core, slot_rows + i * size_y : slot_rows + (i + 1) * size_y, :]
+        chunk_ref[2 * macro + 1 - core, i * size_y : (i + 1) * size_y, :]
         for i in range(-(-size_x // group))
     ]
     for i, value in enumerate(packed):
@@ -657,6 +661,7 @@
             pltpu.VMEM((6, size_x, size_z), jnp.float32),
             pltpu.VMEM((3, *planes), jnp.float32),
             pltpu.VMEM((product_depth, -(-row_count // 128) * 128), jnp.float32),
+            pltpu.VMEM((2, size_y, size_z), jnp.float32),
         ],
         compiler_params=limit(12),
         cost_estimate=pl.CostEstimate(flops=4000000, bytes_accessed=3000000, transcendentals=0),
@@ -768,7 +773,7 @@
     owner_count = 2 * macro_count
     capacity = conformations.shape[1] // owner_count
     size_x, size_y, size_z = viscosity.shape
-    assert capacity <= slot_rows and size_y == 8 and size_z == 128 and size_x % 8 == 0 and size_x <= 48
+    assert capacity <= slot_rows and capacity % 2 == 0 and size_y == 8 and size_z == 128 and size_x % 8 == 0 and size_x <= 48
     chunks, position, viscous, first, second, first_conform, first_noise = gather_rows(
         flag_cell, flag_owner.reshape(-1), velocity, viscosity, conformations, increments, capacity, owner_count
     )

time: 28.3 us -> 28 us (0.989)
  waiting for transfers between devices: 5.18 us -> 4.83 us
    all_to_all x2, waiting for transfers between devices: 5.17 us -> 4.82 us  [exchange(): lax.all_to_all(rows, ('macro', 'micro'), split_axis=0, concat_axis=0, til...]
where the time goes in v17:
time: 28 us; the launch traced here: 27.6 us
  starting transfers between devices  10.9 us (39%)
  Pallas kernels  10.4 us (37%)
  waiting for transfers between devices  4.83 us (17%)
  local copies, waits for them, and re-layouts  0.77 us (3%)
  between operations  0.72 us (3%)
    all_to_all x2, starting transfers between devices, exchange(): lax.all_to_all(rows, ('macro', 'micro'), split_axis=0, concat_axis=0, til...  8.65 us
    all_to_all x2, waiting for transfers between devices, exchange(): lax.all_to_all(rows, ('macro', 'micro'), split_axis=0, concat_axis=0, til...  4.82 us
    pallas_call x1, Pallas kernels, advance(): pl.pallas_call(functools.partial(micro_kernel, capacity, parts, rows, gro...  3.19 us
    pallas_call x1, Pallas kernels, flow_step(): pl.pallas_call(functools.partial(flow_kernel, size_x, size_y, size_z, chu...  2.47 us
    pallas_call x1, Pallas kernels, gather_rows(): pl.pallas_call(functools.partial(gather_kernel, capacity, size_x, size_y,...  2.22 us
    pallas_call x1, Pallas kernels, add_polymer(): pl.pallas_call(functools.partial(polymer_kernel, size_x, size_y, size_z,...  1.78 us
    ppermute x1, starting transfers between devices, shards(): first = lax.ppermute(first, 'tile', swaps[0])  1.58 us
    unnamed x7, local copies, waits for them, and re-layouts  0.77 us
  transfers between devices with their start and end apart: 5, of which 2 were waited for; matrix products, arithmetic and copies ran while one was open for 3% of the time, Pallas kernels for 20%

profile of v17, /device:TPU:0, one launch (start us, length us, event | category | flops | bytes accessed | tf_op | source)
XLA Modules:
  0.0 27.6 jit_solution(16729426869158626882)
XLA Ops:
  0.6 2.2 %gather_rows.1 = (f32[256,128]{1,0:T(8,128)}, s32[32]{0:T(128)S(1)}, f32[32,128]{1,0:T(8,128)S(1)}, f32[7,24,128]{2,1,0:T(8,128)S(1)}, f32[7,24,128]{2,1,0:T(8,1...) custom-call(s32[32]{0:T(128)} %cell_ref.1, s32[32]{0:T(128)} %bitcast.11, ...), custom_call_target="tpu_custom_call" | custom-call | flops 400000 | bytes 3000000 | tf_op jit(solution)/shard_map/gather_rows/pallas_call | solution.py:186
  2.9 0.0 copy-start
  2.9 0.0 copy-start.1
  2.9 0.0 copy-start.2
  2.9 5.3 %all-to-all-start = ((f32[8,32,128]{2,1,0:T(8,128)}), f32[8,32,128]{2,1,0:T(8,128)S(1)}, u32[]{:S(2)}, u32[]{:S(2)}) async-start(f32[8,32,128]{2,1,0:T(8,128)} %bitcast.3), calls=%async_computation | async-start | bytes 262144 | tf_op jit(solution)/shard_map/all_to_all | solution.py:782
  8.2 1.6 %collective-permute-start = (f32[7,24,128]{2,1,0:T(8,128)S(1)}, f32[7,24,128]{2,1,0:T(8,128)S(1)}, u32[]{:S(2)}, u32[]{:S(2)}) collective-permute-start(f32[7,24,128]{2,1,0:T(8,128)S(1)} %get-tuple-element.28), channel_id=1, source_target_pairs={{0,2},{4,6},{2,0},{6,4},{1,3},{5,7},{3,1},{7,5},{8,10},{12,14},{10... | collective-permute-start | bytes 258056 | tf_op jit(solution)/shard_map/ppermute | solution.py:789
  9.8 0.7 %collective-permute-start.1 = (f32[7,24,128]{2,1,0:T(8,128)S(1)}, f32[7,24,128]{2,1,0:T(8,128)S(1)}, u32[]{:S(2)}, u32[]{:S(2)}) collective-permute-start(f32[7,24,128]{2,1,0:T(8,128)S(1)} %get-tuple-element.29), channel_id=1, source_target_pairs={{2,4},{4,2},{3,5},{5,3},{10,12},{12,10},{11,13},{13,11},{18,20},{2... | collective-permute-start | bytes 258056 | tf_op jit(solution)/shard_map/ppermute | solution.py:790
  10.4 3.3 %all-to-all-done.rate_ref.received_ref.chunk_ref = f32[8,32,128]{2,1,0:T(8,128)S(1)} async-done(((f32[8,32,128]{2,1,0:T(8,128)}), f32[8,32,128]{2,1,0:T(8,128)S(1)}, u32[]{:S(2)}, u32[]{:S(2)}) %all-to-all-start) | async-done | bytes 131104 | tf_op jit(solution)/shard_map/all_to_all | solution.py:782
  13.7 3.2 %advance.1 = (f32[3,64,512]{2,1,0:T(8,128)S(1)}, f32[8,8,128]{2,1,0:T(8,128)S(1)}) custom-call(f32[3,64,512]{2,1,0:T(8,128)} %conform_ref.1, bf16[16,3,64,512]{3,2,1,0:T(8,128)(2,1)} %noise_ref.1, f32[8,32,128]{2,1,0:T(8,128)S(1)} %all-to-all-done.rate_ref.received_ref.chunk_ref, f32[3,32,512]{2,1,0:T(8,128)S(1)} %get-tuple-element.25.first_conform_ref, ...), custom_call_target="tpu_custom_call" | custom-call | flops 20000000 | bytes 5000000 | tf_op jit(solution)/shard_map/advance/pallas_call | solution.py:362
  16.9 0.0 collective-permute-done.first_ref
  16.9 0.0 collective-permute-done.1.second_ref
  17.0 0.7 %add_lines.1 = (f32[8,8,128]{2,1,0:T(8,128)}, f32[7,24,128]{2,1,0:T(8,128)S(1)}, f32[7,24,128]{2,1,0:T(8,128)S(1)}, f32[2,48,128]{2,1,0:T(8,128)S(1)}) custom-call(f32[8,8,128]{2,1,0:T(8,128)S(1)} %get-tuple-element.27.chunk_ref, f32[8,32,128]{2,1,0:T(8,128)S(1)} %all-to-all-done.rate_ref.received_ref.chunk_ref, ...), custom_call_target="tpu_custom_call" | custom-call | flops 20000 | bytes 400000 | tf_op jit(solution)/shard_map/add_lines/pallas_call | solution.py:426
  17.7 0.0 collective-permute-start.2
  17.7 3.3 %all-to-all-start.1 = ((f32[8,8,128]{2,1,0:T(8,128)}), f32[8,8,128]{2,1,0:T(8,128)S(1)}, u32[]{:S(2)}, u32[]{:S(2)}) async-start(f32[8,8,128]{2,1,0:T(8,128)} %get-tuple-element.30), calls=%async_computation.1 | async-start | bytes 65536 | tf_op jit(solution)/shard_map/all_to_all | solution.py:782
  21.0 0.7 %copy.9 = f32[3,64,512]{2,1,0:T(8,128)} copy(f32[3,64,512]{2,1,0:T(8,128)S(1)} %get-tuple-element.46) | data formatting | bytes 786432
  21.8 0.0 collective-permute-done.2.handed_ref
  21.8 0.0 copy-done
  21.8 0.0 copy-done.1
  21.8 0.0 copy-done.2
  21.8 2.5 %flow_step.1 = (f32[3,192,128]{2,1,0:T(8,128)S(1)}, f32[8,128]{1,0:T(8,128)S(1)}, f32[4,24,128]{2,1,0:T(8,128)S(1)}, f32[3,32,128]{2,1,0:T(8,128)S(1)}, bf16[32,...) custom-call(s32[32]{0:T(128)S(1)} %copy-done.2, s32[32]{0:T(128)S(1)} %get-tuple-element.32.position_ref, ...), custom_call_target="tpu_custom_call" | custom-call | flops 4000000 | bytes 3000000 | tf_op jit(solution)/shard_map/flow_step/pallas_call | solution.py:644
  24.3 1.5 %all-to-all-done.1 = f32[8,8,128]{2,1,0:T(8,128)S(1)} async-done(((f32[8,8,128]{2,1,0:T(8,128)}), f32[8,8,128]{2,1,0:T(8,128)S(1)}, u32[]{:S(2)}, u32[]{:S(2)}) %all-to-all-start.1) | async-done | bytes 32800 | tf_op jit(solution)/shard_map/all_to_all | solution.py:782
  25.8 1.8 %add_polymer.1 = (f32[3,192,128]{2,1,0:T(8,128)}, f32[6,32]{1,0:T(8,128)}) custom-call(f32[64,128]{1,0:T(8,128)S(1)} %bitcast.10, f32[32,128]{1,0:T(8,128)S(1)} %get-tuple-element.31.viscous_ref, f32[8,128]{1,0:T(8,128)S(1)} %get-tuple-element.36.corner_ref, f32[4,24,128]{2,1,0:T(8,128)S(1)} %get-tuple-element.37.edge_ref, ...), custom_call_target="tpu_custom_call" | custom-call | flops 400000 | bytes 3000000 | tf_op jit(solution)/shard_map/add_polymer/pallas_call | solution.py:754
Async XLA Ops:
  2.9 18.9 %copy-start = (f32[3,24,8,128]{3,2,1,0:T(8,128)S(1)}, f32[3,24,8,128]{3,2,1,0:T(8,128)}, u32[]{:S(2)}) copy-start(f32[3,24,8,128]{3,2,1,0:T(8,128)} %param.6) | copy-start | bytes 884740
  2.9 18.9 %copy-start.1 = (f32[24,8,128]{2,1,0:T(8,128)S(1)}, f32[24,8,128]{2,1,0:T(8,128)}, u32[]{:S(2)}) copy-start(f32[24,8,128]{2,1,0:T(8,128)} %param.7) | copy-start | bytes 294916
  2.9 18.9 %copy-start.2 = (s32[32]{0:T(128)S(1)}, s32[32]{0:T(128)}, u32[]{:S(2)}) copy-start(s32[32]{0:T(128)} %cell_ref.1) | copy-start | bytes 388
  2.9 10.8 %all-to-all-start = ((f32[8,32,128]{2,1,0:T(8,128)}), f32[8,32,128]{2,1,0:T(8,128)S(1)}, u32[]{:S(2)}, u32[]{:S(2)}) async-start(f32[8,32,128]{2,1,0:T(8,128)} %bitcast.3), calls=%async_computation | async-start | bytes 262144 | tf_op jit(solution)/shard_map/all_to_all | solution.py:782
  8.2 8.7 %collective-permute-start = (f32[7,24,128]{2,1,0:T(8,128)S(1)}, f32[7,24,128]{2,1,0:T(8,128)S(1)}, u32[]{:S(2)}, u32[]{:S(2)}) collective-permute-start(f32[7,24,128]{2,1,0:T(8,128)S(1)} %get-tuple-element.28), channel_id=1, source_target_pairs={{0,2},{4,6},{2,0},{6,4},{1,3},{5,7},{3,1},{7,5},{8,10},{12,14},{10... | collective-permute-start | bytes 258056 | tf_op jit(solution)/shard_map/ppermute | solution.py:789
  9.8 7.2 %collective-permute-start.1 = (f32[7,24,128]{2,1,0:T(8,128)S(1)}, f32[7,24,128]{2,1,0:T(8,128)S(1)}, u32[]{:S(2)}, u32[]{:S(2)}) collective-permute-start(f32[7,24,128]{2,1,0:T(8,128)S(1)} %get-tuple-element.29), channel_id=1, source_target_pairs={{2,4},{4,2},{3,5},{5,3},{10,12},{12,10},{11,13},{13,11},{18,20},{2... | collective-permute-start | bytes 258056 | tf_op jit(solution)/shard_map/ppermute | solution.py:790
  17.7 4.1 %collective-permute-start.2 = (f32[2,48,128]{2,1,0:T(8,128)S(1)}, f32[2,48,128]{2,1,0:T(8,128)S(1)}, u32[]{:S(2)}, u32[]{:S(2)}) collective-permute-start(f32[2,48,128]{2,1,0:T(8,128)S(1)} %get-tuple-element.35), channel_id=1, source_target_pairs={{0,1},{1,0},{2,3},{3,2},{4,5},{5,4},{6,7},{7,6},{8,9},{9,8},{10,11... | collective-permute-start | bytes 147464 | tf_op jit(solution)/shard_map/ppermute | solution.py:796
  17.7 8.1 %all-to-all-start.1 = ((f32[8,8,128]{2,1,0:T(8,128)}), f32[8,8,128]{2,1,0:T(8,128)S(1)}, u32[]{:S(2)}, u32[]{:S(2)}) async-start(f32[8,8,128]{2,1,0:T(8,128)} %get-tuple-element.30), calls=%async_computation.1 | async-start | bytes 65536 | tf_op jit(solution)/shard_map/all_to_all | solution.py:782

commit v18 on v17

--- a/solution.py
+++ b/solution.py
@@ -67,8 +67,8 @@
 
 def gather_kernel(
     capacity, size_x, size_y, size_z, macro_count, cell_in, owner_in, velocity_in, viscosity_in,
-    conform_in, noise_in, chunk_ref, position_ref, viscous_ref, first_ref, second_ref, conform_ref, noise_ref,
-    cell_ref, owner_ref, velocity_ref, viscosity_ref, masked, gradients, paired, target, count, sems,
+    conform_in, noise_in, chunk_out, position_ref, viscous_ref, first_ref, second_ref, conform_ref, noise_ref,
+    cell_ref, owner_ref, velocity_ref, viscosity_ref, masked, gradients, paired, chunk_ref, target, count, sems, write_sem,
 ):
     flags = cell_ref.shape[0]
     copies = [
@@ -118,18 +118,6 @@
             masked[3 * a + 2, j : j + 1, :] = planes[a, x, at, :] * along_z
         masked[9, j : j + 1, :] = layers[x, at, :] * here
 
-    even = lax.axis_index("tile") & 1 == 0
-
-    def put(number, ref, low, high):
-        rows = [ref[pl.ds(y, size_x, stride=size_y), :] for y in (low, high)]
-        first_ref[number] = jnp.where(even, rows[1], rows[0])
-        second_ref[number] = jnp.where(even, rows[0], rows[1])
-
-    for layer in range(2):
-        for a in range(3):
-            put(3 * layer + a, velocity_ref.at[a], layer, size_y - 1 - layer)
-    put(6, viscosity_ref, 0, size_y - 1)
-
     for side in range(2):
         beside = neighbour(macro, side, macro_count)
         for layer, owner in enumerate((2 * beside + core, 2 * beside + 1 - core)):
@@ -162,11 +150,6 @@
     for c in range(9):
         packed = jnp.where(wide == c, columns[c], packed)
     gradients[...] = packed
-    stress = jnp.zeros((flags, 128), jnp.float32)
-    for k, (a, b) in enumerate(stress_pairs):
-        stress = jnp.where(wide == k, viscous * (columns[3 * a + b] + columns[3 * b + a]), stress)
-    viscous_ref[...] = stress
-
     for j in range(flags):
         paired[pl.ds(target[j], 1), :] = gradients[j : j + 1, :]
     rows = paired[0:paired_rows, :] + rolled(paired[paired_rows:, :], 64)
@@ -174,8 +157,29 @@
         chunk_ref[owner * chunk_rows + half_face : (owner + 1) * chunk_rows, :] = rows[
             owner * (slot_rows // 2) : (owner + 1) * (slot_rows // 2)
         ]
+    write = pltpu.make_async_copy(chunk_ref, chunk_out, write_sem)
+    write.start()
+
+    stress = jnp.zeros((flags, 128), jnp.float32)
+    for k, (a, b) in enumerate(stress_pairs):
+        stress = jnp.where(wide == k, viscous * (columns[3 * a + b] + columns[3 * b + a]), stress)
+    viscous_ref[...] = stress
+
+    even = lax.axis_index("tile") & 1 == 0
+
+    def put(number, ref, low, high):
+        rows = [ref[pl.ds(y, size_x, stride=size_y), :] for y in (low, high)]
+        first_ref[number] = jnp.where(even, rows[1], rows[0])
+        second_ref[number] = jnp.where(even, rows[0], rows[1])
+
+    for layer in range(2):
+        for a in range(3):
+            put(3 * layer + a, velocity_ref.at[a], layer, size_y - 1 - layer)
+    put(6, viscosity_ref, 0, size_y - 1)
+
     for copy in copies[4:]:
         copy.wait()
+    write.wait()
 
 
 def gather_rows(flag_cell, owner, velocity, viscosity, conformations, increments, capacity, owner_count):
@@ -195,7 +199,7 @@
             pltpu.VMEM((steps // first_share, 3, block_slots, dumbbells), jnp.bfloat16),
         ),
         in_specs=[pl.BlockSpec(memory_space=pltpu.HBM)] * 6,
-        out_specs=(VMEM, SMEM, VMEM, VMEM, VMEM, VMEM, VMEM),
+        out_specs=(pl.BlockSpec(memory_space=pltpu.HBM), SMEM) + (VMEM,) * 5,
         scratch_shapes=[
             pltpu.SMEM((flags,), jnp.int32),
             pltpu.SMEM((flags,), jnp.int32),
@@ -204,9 +208,11 @@
             pltpu.VMEM((10, flags, size_z), jnp.float32),
             pltpu.VMEM((flags, 128), jnp.float32),
             pltpu.VMEM((owner_count * slot_rows, 128), jnp.float32),
+            pltpu.VMEM((owner_count * chunk_rows, 128), jnp.float32),
             pltpu.SMEM((flags,), jnp.int32),
             pltpu.SMEM((owner_count,), jnp.int32),
             pltpu.SemaphoreType.DMA((6,)),
+            pltpu.SemaphoreType.DMA,
         ],
         compiler_params=limit(8),
         cost_estimate=pl.CostEstimate(flops=400000, bytes_accessed=3000000, transcendentals=0),
@@ -383,29 +389,25 @@
 
 
 def lines_kernel(
-    macro_count, chunk_ref, received_ref, first_ref, second_ref, out_ref, y_low_ref, y_high_ref, handed_ref
+    macro_count, chunk_ref, received_ref, first_ref, second_ref, chunk_out, y_low_ref, y_high_ref, handed_ref,
+    out_ref, write_sem,
 ):
+    macro, core = place_of()
+    even = lax.axis_index("tile") & 1 == 0
+    size_x, size_z = first_ref.shape[1:]
     out_ref[...] = chunk_ref[...]
-    macro, core = place_of()
-    for side in range(2):
-        beside = neighbour(macro, side, macro_count)
-        handed_ref[side, 0:chunk_rows, :] = received_ref[2 * beside + 1 - core]
-        for number, a in enumerate((0, 2)):
-            handed_ref[side, chunk_rows + number * 8 : chunk_rows + (number + 1) * 8, :] = received_ref[
-                2 * beside + core, a * 8 : (a + 1) * 8, :
-            ]
-    even = lax.axis_index("tile") & 1 == 0
-    y_low_ref[...] = jnp.where(even, second_ref[...], first_ref[...])
-    y_high_ref[...] = jnp.where(even, first_ref[...], second_ref[...])
-    sides = (y_low_ref, y_high_ref)
-    size_x, size_z = y_low_ref.shape[1:]
+
+    def side_of(u, item, at):
+        first, second = first_ref[item, at, :], second_ref[item, at, :]
+        return jnp.where(even, second, first) if u == 0 else jnp.where(even, first, second)
+
     for side in range(2):
         beside = neighbour(macro, side, macro_count)
         x = 0 if side == 0 else size_x - 1
         for u in range(2):
             for a in range(2):
                 at = 2 * u + a
-                out_ref[2 * beside + core, at : at + 1, :] = sides[u][a, x : x + 1, :]
+                out_ref[2 * beside + core, at : at + 1, :] = side_of(u, a, slice(x, x + 1))
 
     lane = lanes_of((8, size_z))
     source = jnp.where(core == 0, size_z - 1, 0)
@@ -415,10 +417,22 @@
         for u in range(2):
             for a in range(2):
                 at = line_lane + 4 * i + 2 * u + a
-                total = jnp.where(
-                    lane == at, rolled(sides[u][1 + a, 8 * i : 8 * i + 8, :], at - source), total
-                )
+                value = side_of(u, 1 + a, slice(8 * i, 8 * i + 8))
+                total = jnp.where(lane == at, rolled(value, at - source), total)
     out_ref[other] = total
+    write = pltpu.make_async_copy(out_ref, chunk_out, write_sem)
+    write.start()
+
+    for side in range(2):
+        beside = neighbour(macro, side, macro_count)
+        handed_ref[side, 0:chunk_rows, :] = received_ref[2 * beside + 1 - core]
+        for number, a in enumerate((0, 2)):
+            handed_ref[side, chunk_rows + number * 8 : chunk_rows + (number + 1) * 8, :] = received_ref[
+                2 * beside + core, a * 8 : (a + 1) * 8, :
+            ]
+    y_low_ref[...] = jnp.where(even, second_ref[...], first_ref[...])
+    y_high_ref[...] = jnp.where(even, first_ref[...], second_ref[...])
+    write.wait()
 
 
 def add_lines(chunks, received, first, second):
@@ -430,7 +444,8 @@
             jax.ShapeDtypeStruct((2, handed_rows, 128), jnp.float32),
         ),
         in_specs=[VMEM] * 4,
-        out_specs=(VMEM,) * 4,
+        out_specs=(pl.BlockSpec(memory_space=pltpu.HBM),) + (VMEM,) * 3,
+        scratch_shapes=[pltpu.VMEM(chunks.shape, jnp.float32), pltpu.SemaphoreType.DMA],
         compiler_params=limit(4),
         cost_estimate=pl.CostEstimate(flops=20000, bytes_accessed=400000, transcendentals=0),
         name="add_lines",

time: 28 us -> 28.6 us (1.021)
  Pallas kernels: 10.4 us -> 11 us
    pallas_call x1, Pallas kernels: 2.22 us -> 2.82 us  [gather_rows(): pl.pallas_call(functools.partial(gather_kernel, capacity, size_x, size_y,...]
where the time goes in v18:
time: 28.6 us; the launch traced here: 28.3 us
  Pallas kernels  11 us (38%)
  starting transfers between devices  11 us (38%)
  waiting for transfers between devices  4.83 us (17%)
  local copies, waits for them, and re-layouts  0.77 us (3%)
  between operations  0.74 us (3%)
    all_to_all x2, starting transfers between devices, exchange(): lax.all_to_all(rows, ('macro', 'micro'), split_axis=0, concat_axis=0, til...  8.67 us
    all_to_all x2, waiting for transfers between devices, exchange(): lax.all_to_all(rows, ('macro', 'micro'), split_axis=0, concat_axis=0, til...  4.82 us
    pallas_call x1, Pallas kernels, advance(): pl.pallas_call(functools.partial(micro_kernel, capacity, parts, rows, gro...  3.19 us
    pallas_call x1, Pallas kernels, gather_rows(): pl.pallas_call(functools.partial(gather_kernel, capacity, size_x, size_y,...  2.82 us
    pallas_call x1, Pallas kernels, flow_step(): pl.pallas_call(functools.partial(flow_kernel, size_x, size_y, size_z, chu...  2.47 us
    pallas_call x1, Pallas kernels, add_polymer(): pl.pallas_call(functools.partial(polymer_kernel, size_x, size_y, size_z,...  1.78 us
    ppermute x1, starting transfers between devices, shards(): first = lax.ppermute(first, 'tile', swaps[0])  1.57 us
    unnamed x7, local copies, waits for them, and re-layouts  0.77 us
  transfers between devices with their start and end apart: 5, of which 2 were waited for; matrix products, arithmetic and copies ran while one was open for 3% of the time, Pallas kernels for 20%

profile of v18, /device:TPU:0, one launch (start us, length us, event | category | flops | bytes accessed | tf_op | source)
XLA Modules:
  0.0 28.3 jit_solution(16529092519152864023)
XLA Ops:
  0.6 2.8 %gather_rows.1 = (f32[256,128]{1,0:T(8,128)}, s32[32]{0:T(128)S(1)}, f32[32,128]{1,0:T(8,128)S(1)}, f32[7,24,128]{2,1,0:T(8,128)S(1)}, f32[7,24,128]{2,1,0:T(8,1...) custom-call(s32[32]{0:T(128)} %cell_ref.1, s32[32]{0:T(128)} %bitcast.11, ...), custom_call_target="tpu_custom_call" | custom-call | flops 400000 | bytes 3000000 | tf_op jit(solution)/shard_map/gather_rows/pallas_call | solution.py:190
  3.5 0.0 copy-start
  3.5 0.0 copy-start.1
  3.5 0.0 copy-start.2
  3.5 5.3 %all-to-all-start = ((f32[8,32,128]{2,1,0:T(8,128)}), f32[8,32,128]{2,1,0:T(8,128)S(1)}, u32[]{:S(2)}, u32[]{:S(2)}) async-start(f32[8,32,128]{2,1,0:T(8,128)} %bitcast.3), calls=%async_computation | async-start | bytes 262144 | tf_op jit(solution)/shard_map/all_to_all | solution.py:797
  8.8 1.6 %collective-permute-start = (f32[7,24,128]{2,1,0:T(8,128)S(1)}, f32[7,24,128]{2,1,0:T(8,128)S(1)}, u32[]{:S(2)}, u32[]{:S(2)}) collective-permute-start(f32[7,24,128]{2,1,0:T(8,128)S(1)} %get-tuple-element.28), channel_id=1, source_target_pairs={{0,2},{4,6},{2,0},{6,4},{1,3},{5,7},{3,1},{7,5},{8,10},{12,14},{10... | collective-permute-start | bytes 258056 | tf_op jit(solution)/shard_map/ppermute | solution.py:804
  10.4 0.7 %collective-permute-start.1 = (f32[7,24,128]{2,1,0:T(8,128)S(1)}, f32[7,24,128]{2,1,0:T(8,128)S(1)}, u32[]{:S(2)}, u32[]{:S(2)}) collective-permute-start(f32[7,24,128]{2,1,0:T(8,128)S(1)} %get-tuple-element.29), channel_id=1, source_target_pairs={{2,4},{4,2},{3,5},{5,3},{10,12},{12,10},{11,13},{13,11},{18,20},{2... | collective-permute-start | bytes 258056 | tf_op jit(solution)/shard_map/ppermute | solution.py:805
  11.0 3.3 %all-to-all-done.rate_ref.received_ref.chunk_ref = f32[8,32,128]{2,1,0:T(8,128)S(1)} async-done(((f32[8,32,128]{2,1,0:T(8,128)}), f32[8,32,128]{2,1,0:T(8,128)S(1)}, u32[]{:S(2)}, u32[]{:S(2)}) %all-to-all-start) | async-done | bytes 131104 | tf_op jit(solution)/shard_map/all_to_all | solution.py:797
  14.3 3.2 %advance.1 = (f32[3,64,512]{2,1,0:T(8,128)S(1)}, f32[8,8,128]{2,1,0:T(8,128)S(1)}) custom-call(f32[3,64,512]{2,1,0:T(8,128)} %conform_ref.1, bf16[16,3,64,512]{3,2,1,0:T(8,128)(2,1)} %noise_ref.1, f32[8,32,128]{2,1,0:T(8,128)S(1)} %all-to-all-done.rate_ref.received_ref.chunk_ref, f32[3,32,512]{2,1,0:T(8,128)S(1)} %get-tuple-element.25.first_conform_ref, ...), custom_call_target="tpu_custom_call" | custom-call | flops 20000000 | bytes 5000000 | tf_op jit(solution)/shard_map/advance/pallas_call | solution.py:368
  17.5 0.0 collective-permute-done.first_ref
  17.5 0.0 collective-permute-done.1.second_ref
  17.6 0.7 %add_lines.1 = (f32[8,8,128]{2,1,0:T(8,128)}, f32[7,24,128]{2,1,0:T(8,128)S(1)}, f32[7,24,128]{2,1,0:T(8,128)S(1)}, f32[2,48,128]{2,1,0:T(8,128)S(1)}) custom-call(f32[8,8,128]{2,1,0:T(8,128)S(1)} %get-tuple-element.27.chunk_ref, f32[8,32,128]{2,1,0:T(8,128)S(1)} %all-to-all-done.rate_ref.received_ref.chunk_ref, ...), custom_call_target="tpu_custom_call" | custom-call | flops 20000 | bytes 400000 | tf_op jit(solution)/shard_map/add_lines/pallas_call | solution.py:440
  18.3 0.1 collective-permute-start.2
  18.4 3.4 %all-to-all-start.1 = ((f32[8,8,128]{2,1,0:T(8,128)}), f32[8,8,128]{2,1,0:T(8,128)S(1)}, u32[]{:S(2)}, u32[]{:S(2)}) async-start(f32[8,8,128]{2,1,0:T(8,128)} %get-tuple-element.30), calls=%async_computation.1 | async-start | bytes 65536 | tf_op jit(solution)/shard_map/all_to_all | solution.py:797
  21.7 0.7 %copy.9 = f32[3,64,512]{2,1,0:T(8,128)} copy(f32[3,64,512]{2,1,0:T(8,128)S(1)} %get-tuple-element.46) | data formatting | bytes 786432
  22.5 0.0 collective-permute-done.2.handed_ref
  22.5 0.0 copy-done
  22.5 0.0 copy-done.1
  22.5 0.0 copy-done.2
  22.5 2.5 %flow_step.1 = (f32[3,192,128]{2,1,0:T(8,128)S(1)}, f32[8,128]{1,0:T(8,128)S(1)}, f32[4,24,128]{2,1,0:T(8,128)S(1)}, f32[3,32,128]{2,1,0:T(8,128)S(1)}, bf16[32,...) custom-call(s32[32]{0:T(128)S(1)} %copy-done.2, s32[32]{0:T(128)S(1)} %get-tuple-element.32.position_ref, ...), custom_call_target="tpu_custom_call" | custom-call | flops 4000000 | bytes 3000000 | tf_op jit(solution)/shard_map/flow_step/pallas_call | solution.py:659
  25.0 1.5 %all-to-all-done.1 = f32[8,8,128]{2,1,0:T(8,128)S(1)} async-done(((f32[8,8,128]{2,1,0:T(8,128)}), f32[8,8,128]{2,1,0:T(8,128)S(1)}, u32[]{:S(2)}, u32[]{:S(2)}) %all-to-all-start.1) | async-done | bytes 32800 | tf_op jit(solution)/shard_map/all_to_all | solution.py:797
  26.5 1.8 %add_polymer.1 = (f32[3,192,128]{2,1,0:T(8,128)}, f32[6,32]{1,0:T(8,128)}) custom-call(f32[64,128]{1,0:T(8,128)S(1)} %bitcast.10, f32[32,128]{1,0:T(8,128)S(1)} %get-tuple-element.31.viscous_ref, f32[8,128]{1,0:T(8,128)S(1)} %get-tuple-element.36.corner_ref, f32[4,24,128]{2,1,0:T(8,128)S(1)} %get-tuple-element.37.edge_ref, ...), custom_call_target="tpu_custom_call" | custom-call | flops 400000 | bytes 3000000 | tf_op jit(solution)/shard_map/add_polymer/pallas_call | solution.py:769
Async XLA Ops:
  3.5 19.0 %copy-start = (f32[3,24,8,128]{3,2,1,0:T(8,128)S(1)}, f32[3,24,8,128]{3,2,1,0:T(8,128)}, u32[]{:S(2)}) copy-start(f32[3,24,8,128]{3,2,1,0:T(8,128)} %param.6) | copy-start | bytes 884740
  3.5 19.0 %copy-start.1 = (f32[24,8,128]{2,1,0:T(8,128)S(1)}, f32[24,8,128]{2,1,0:T(8,128)}, u32[]{:S(2)}) copy-start(f32[24,8,128]{2,1,0:T(8,128)} %param.7) | copy-start | bytes 294916
  3.5 19.0 %copy-start.2 = (s32[32]{0:T(128)S(1)}, s32[32]{0:T(128)}, u32[]{:S(2)}) copy-start(s32[32]{0:T(128)} %cell_ref.1) | copy-start | bytes 388
  3.5 10.8 %all-to-all-start = ((f32[8,32,128]{2,1,0:T(8,128)}), f32[8,32,128]{2,1,0:T(8,128)S(1)}, u32[]{:S(2)}, u32[]{:S(2)}) async-start(f32[8,32,128]{2,1,0:T(8,128)} %bitcast.3), calls=%async_computation | async-start | bytes 262144 | tf_op jit(solution)/shard_map/all_to_all | solution.py:797
  8.8 8.7 %collective-permute-start = (f32[7,24,128]{2,1,0:T(8,128)S(1)}, f32[7,24,128]{2,1,0:T(8,128)S(1)}, u32[]{:S(2)}, u32[]{:S(2)}) collective-permute-start(f32[7,24,128]{2,1,0:T(8,128)S(1)} %get-tuple-element.28), channel_id=1, source_target_pairs={{0,2},{4,6},{2,0},{6,4},{1,3},{5,7},{3,1},{7,5},{8,10},{12,14},{10... | collective-permute-start | bytes 258056 | tf_op jit(solution)/shard_map/ppermute | solution.py:804
  10.4 7.2 %collective-permute-start.1 = (f32[7,24,128]{2,1,0:T(8,128)S(1)}, f32[7,24,128]{2,1,0:T(8,128)S(1)}, u32[]{:S(2)}, u32[]{:S(2)}) collective-permute-start(f32[7,24,128]{2,1,0:T(8,128)S(1)} %get-tuple-element.29), channel_id=1, source_target_pairs={{2,4},{4,2},{3,5},{5,3},{10,12},{12,10},{11,13},{13,11},{18,20},{2... | collective-permute-start | bytes 258056 | tf_op jit(solution)/shard_map/ppermute | solution.py:805
  18.3 4.2 %collective-permute-start.2 = (f32[2,48,128]{2,1,0:T(8,128)S(1)}, f32[2,48,128]{2,1,0:T(8,128)S(1)}, u32[]{:S(2)}, u32[]{:S(2)}) collective-permute-start(f32[2,48,128]{2,1,0:T(8,128)S(1)} %get-tuple-element.35), channel_id=1, source_target_pairs={{0,1},{1,0},{2,3},{3,2},{4,5},{5,4},{6,7},{7,6},{8,9},{9,8},{10,11... | collective-permute-start | bytes 147464 | tf_op jit(solution)/shard_map/ppermute | solution.py:811
  18.4 8.1 %all-to-all-start.1 = ((f32[8,8,128]{2,1,0:T(8,128)}), f32[8,8,128]{2,1,0:T(8,128)S(1)}, u32[]{:S(2)}, u32[]{:S(2)}) async-start(f32[8,8,128]{2,1,0:T(8,128)} %get-tuple-element.30), calls=%async_computation.1 | async-start | bytes 65536 | tf_op jit(solution)/shard_map/all_to_all | solution.py:797

commit v19 on v17

--- a/solution.py
+++ b/solution.py
@@ -683,7 +683,7 @@
 
 def polymer_kernel(
     size_x, size_y, size_z, macro_count, chunk_ref, viscous_ref, corner_ref, edge_ref, lines_ref, pick_ref,
-    spread_ref, partial_ref, out_ref, flag_ref, field, write_sem,
+    spread_ref, partial_ref, out_ref, flag_ref,
 ):
     flags = viscous_ref.shape[0]
     macro, core = place_of()
@@ -716,7 +716,7 @@
     ]
     flag_ref[...] = stress.T[0:6, :]
 
-    field[...] = partial_ref[...]
+    out_ref[...] = partial_ref[...]
     for s in range(2):
         inside = macro > 0 if s == 0 else macro < macro_count - 1
         beside = jnp.maximum(macro - 1, 0) if s == 0 else jnp.minimum(macro + 1, macro_count - 1)
@@ -727,7 +727,7 @@
             for a in range(2):
                 number = 4 * s + 2 * u + a
                 line = corner_ref[number : number + 1, :] * chunk_ref[pl.ds(start + 2 * u + a, 1), :]
-                field[1 - a, at : at + 1, :] += jnp.where(inside, line, 0.0)
+                out_ref[1 - a, at : at + 1, :] += jnp.where(inside, line, 0.0)
     start = pl.multiple_of((2 * macro + 1 - core) * back_rows, 8)
     packed = chunk_ref[pl.ds(start, back_rows), :]
     end = jnp.where(core == 0, size_z - 1, 0)
@@ -737,15 +737,11 @@
             for i in range(size_x // 8):
                 line = rolled(packed, end - (line_lane + 4 * i + 2 * u + a)) * edge_ref[2 * u + a, 8 * i : 8 * i + 8, :]
                 at = pl.ds(8 * i * size_y + y, 8, stride=size_y)
-                field[2 - a, at, :] += line
-    copies = [pltpu.make_async_copy(field.at[a], out_ref.at[a], write_sem.at[a]) for a in range(3)]
+                out_ref[2 - a, at, :] += line
     for a in range(3):
-        field[a] += jnp.dot(
+        out_ref[a] += jnp.dot(
             spread_ref[...], jnp.concatenate(split[a], axis=0), preferred_element_type=jnp.float32
         )
-        copies[a].start()
-    for copy in copies:
-        copy.wait()
 
 
 def add_polymer(chunks, viscous, corners, edges, lines, pick, spread, partial, shape):
@@ -758,8 +754,7 @@
             jax.ShapeDtypeStruct((6, flags), jnp.float32),
         ),
         in_specs=[VMEM] * 8,
-        out_specs=(pl.BlockSpec(memory_space=pltpu.HBM), VMEM),
-        scratch_shapes=[pltpu.VMEM(partial.shape, jnp.float32), pltpu.SemaphoreType.DMA((3,))],
+        out_specs=(VMEM, VMEM),
         compiler_params=limit(8),
         cost_estimate=pl.CostEstimate(flops=400000, bytes_accessed=3000000, transcendentals=0),
         name="add_polymer",

time: 28 us -> 27.4 us (0.979)
  Pallas kernels: 10.4 us -> 9.84 us
    pallas_call x1, Pallas kernels: 1.78 us -> 1.24 us  [add_polymer(): pl.pallas_call(functools.partial(polymer_kernel, size_x, size_y, size_z,...]
  transfers between devices with their start and end apart: 5 -> 5, of which waited for: 2 -> 2; matrix products, arithmetic and copies ran while one was open for 3% -> 3% of each run, Pallas kernels for 20% -> 21%
where the time goes in v19:
time: 27.4 us; the launch traced here: 27 us
  starting transfers between devices  10.9 us (40%)
  Pallas kernels  9.84 us (36%)
  waiting for transfers between devices  4.83 us (18%)
  local copies, waits for them, and re-layouts  0.77 us (3%)
  between operations  0.72 us (3%)
    all_to_all x2, starting transfers between devices, exchange(): lax.all_to_all(rows, ('macro', 'micro'), split_axis=0, concat_axis=0, til...  8.65 us
    all_to_all x2, waiting for transfers between devices, exchange(): lax.all_to_all(rows, ('macro', 'micro'), split_axis=0, concat_axis=0, til...  4.83 us
    pallas_call x1, Pallas kernels, advance(): pl.pallas_call(functools.partial(micro_kernel, capacity, parts, rows, gro...  3.19 us
    pallas_call x1, Pallas kernels, flow_step(): pl.pallas_call(functools.partial(flow_kernel, size_x, size_y, size_z, chu...  2.47 us
    pallas_call x1, Pallas kernels, gather_rows(): pl.pallas_call(functools.partial(gather_kernel, capacity, size_x, size_y,...  2.23 us
    ppermute x1, starting transfers between devices, shards(): first = lax.ppermute(first, 'tile', swaps[0])  1.57 us
    pallas_call x1, Pallas kernels, add_polymer(): pl.pallas_call(functools.partial(polymer_kernel, size_x, size_y, size_z,...  1.24 us
    unnamed x7, local copies, waits for them, and re-layouts  0.77 us
  transfers between devices with their start and end apart: 5, of which 2 were waited for; matrix products, arithmetic and copies ran while one was open for 3% of the time, Pallas kernels for 21%

profile of v19, /device:TPU:0, one launch (start us, length us, event | category | flops | bytes accessed | tf_op | source)
XLA Modules:
  0.0 27.0 jit_solution(12632996691362601146)
XLA Ops:
  0.6 2.2 %gather_rows.1 = (f32[256,128]{1,0:T(8,128)}, s32[32]{0:T(128)S(1)}, f32[32,128]{1,0:T(8,128)S(1)}, f32[7,24,128]{2,1,0:T(8,128)S(1)}, f32[7,24,128]{2,1,0:T(8,1...) custom-call(s32[32]{0:T(128)} %cell_ref.1, s32[32]{0:T(128)} %bitcast.11, ...), custom_call_target="tpu_custom_call" | custom-call | flops 400000 | bytes 3000000 | tf_op jit(solution)/shard_map/gather_rows/pallas_call | solution.py:186
  2.9 0.0 copy-start
  2.9 0.0 copy-start.1
  2.9 0.0 copy-start.2
  2.9 5.3 %all-to-all-start = ((f32[8,32,128]{2,1,0:T(8,128)}), f32[8,32,128]{2,1,0:T(8,128)S(1)}, u32[]{:S(2)}, u32[]{:S(2)}) async-start(f32[8,32,128]{2,1,0:T(8,128)} %bitcast.3), calls=%async_computation | async-start | bytes 262144 | tf_op jit(solution)/shard_map/all_to_all | solution.py:777
  8.2 1.6 %collective-permute-start = (f32[7,24,128]{2,1,0:T(8,128)S(1)}, f32[7,24,128]{2,1,0:T(8,128)S(1)}, u32[]{:S(2)}, u32[]{:S(2)}) collective-permute-start(f32[7,24,128]{2,1,0:T(8,128)S(1)} %get-tuple-element.28), channel_id=1, source_target_pairs={{0,2},{4,6},{2,0},{6,4},{1,3},{5,7},{3,1},{7,5},{8,10},{12,14},{10... | collective-permute-start | bytes 258056 | tf_op jit(solution)/shard_map/ppermute | solution.py:784
  9.8 0.7 %collective-permute-start.1 = (f32[7,24,128]{2,1,0:T(8,128)S(1)}, f32[7,24,128]{2,1,0:T(8,128)S(1)}, u32[]{:S(2)}, u32[]{:S(2)}) collective-permute-start(f32[7,24,128]{2,1,0:T(8,128)S(1)} %get-tuple-element.29), channel_id=1, source_target_pairs={{2,4},{4,2},{3,5},{5,3},{10,12},{12,10},{11,13},{13,11},{18,20},{2... | collective-permute-start | bytes 258056 | tf_op jit(solution)/shard_map/ppermute | solution.py:785
  10.4 3.3 %all-to-all-done.rate_ref.received_ref.chunk_ref = f32[8,32,128]{2,1,0:T(8,128)S(1)} async-done(((f32[8,32,128]{2,1,0:T(8,128)}), f32[8,32,128]{2,1,0:T(8,128)S(1)}, u32[]{:S(2)}, u32[]{:S(2)}) %all-to-all-start) | async-done | bytes 131104 | tf_op jit(solution)/shard_map/all_to_all | solution.py:777
  13.7 3.2 %advance.1 = (f32[3,64,512]{2,1,0:T(8,128)S(1)}, f32[8,8,128]{2,1,0:T(8,128)S(1)}) custom-call(f32[3,64,512]{2,1,0:T(8,128)} %conform_ref.1, bf16[16,3,64,512]{3,2,1,0:T(8,128)(2,1)} %noise_ref.1, f32[8,32,128]{2,1,0:T(8,128)S(1)} %all-to-all-done.rate_ref.received_ref.chunk_ref, f32[3,32,512]{2,1,0:T(8,128)S(1)} %get-tuple-element.25.first_conform_ref, ...), custom_call_target="tpu_custom_call" | custom-call | flops 20000000 | bytes 5000000 | tf_op jit(solution)/shard_map/advance/pallas_call | solution.py:362
  16.9 0.0 collective-permute-done.first_ref
  16.9 0.0 collective-permute-done.1.second_ref
  17.0 0.7 %add_lines.1 = (f32[8,8,128]{2,1,0:T(8,128)}, f32[7,24,128]{2,1,0:T(8,128)S(1)}, f32[7,24,128]{2,1,0:T(8,128)S(1)}, f32[2,48,128]{2,1,0:T(8,128)S(1)}) custom-call(f32[8,8,128]{2,1,0:T(8,128)S(1)} %get-tuple-element.27.chunk_ref, f32[8,32,128]{2,1,0:T(8,128)S(1)} %all-to-all-done.rate_ref.received_ref.chunk_ref, ...), custom_call_target="tpu_custom_call" | custom-call | flops 20000 | bytes 400000 | tf_op jit(solution)/shard_map/add_lines/pallas_call | solution.py:426
  17.7 0.0 collective-permute-start.2
  17.7 3.3 %all-to-all-start.1 = ((f32[8,8,128]{2,1,0:T(8,128)}), f32[8,8,128]{2,1,0:T(8,128)S(1)}, u32[]{:S(2)}, u32[]{:S(2)}) async-start(f32[8,8,128]{2,1,0:T(8,128)} %get-tuple-element.30), calls=%async_computation.1 | async-start | bytes 65536 | tf_op jit(solution)/shard_map/all_to_all | solution.py:777
  21.0 0.7 %copy.9 = f32[3,64,512]{2,1,0:T(8,128)} copy(f32[3,64,512]{2,1,0:T(8,128)S(1)} %get-tuple-element.46) | data formatting | bytes 786432
  21.8 0.0 collective-permute-done.2.handed_ref
  21.8 0.0 copy-done
  21.8 0.0 copy-done.1
  21.8 0.0 copy-done.2
  21.8 2.5 %flow_step.1 = (f32[3,192,128]{2,1,0:T(8,128)S(1)}, f32[8,128]{1,0:T(8,128)S(1)}, f32[4,24,128]{2,1,0:T(8,128)S(1)}, f32[3,32,128]{2,1,0:T(8,128)S(1)}, bf16[32,...) custom-call(s32[32]{0:T(128)S(1)} %copy-done.2, s32[32]{0:T(128)S(1)} %get-tuple-element.32.position_ref, ...), custom_call_target="tpu_custom_call" | custom-call | flops 4000000 | bytes 3000000 | tf_op jit(solution)/shard_map/flow_step/pallas_call | solution.py:644
  24.3 1.5 %all-to-all-done.1 = f32[8,8,128]{2,1,0:T(8,128)S(1)} async-done(((f32[8,8,128]{2,1,0:T(8,128)}), f32[8,8,128]{2,1,0:T(8,128)S(1)}, u32[]{:S(2)}, u32[]{:S(2)}) %all-to-all-start.1) | async-done | bytes 32800 | tf_op jit(solution)/shard_map/all_to_all | solution.py:777
  25.8 1.2 %add_polymer.1 = (f32[3,192,128]{2,1,0:T(8,128)}, f32[6,32]{1,0:T(8,128)}) custom-call(f32[64,128]{1,0:T(8,128)S(1)} %bitcast.10, f32[32,128]{1,0:T(8,128)S(1)} %get-tuple-element.31.viscous_ref, f32[8,128]{1,0:T(8,128)S(1)} %get-tuple-element.36.corner_ref, f32[4,24,128]{2,1,0:T(8,128)S(1)} %get-tuple-element.37.edge_ref, ...), custom_call_target="tpu_custom_call" | custom-call | flops 400000 | bytes 3000000 | tf_op jit(solution)/shard_map/add_polymer/pallas_call | solution.py:750
Async XLA Ops:
  2.9 18.9 %copy-start = (f32[3,24,8,128]{3,2,1,0:T(8,128)S(1)}, f32[3,24,8,128]{3,2,1,0:T(8,128)}, u32[]{:S(2)}) copy-start(f32[3,24,8,128]{3,2,1,0:T(8,128)} %param.6) | copy-start | bytes 884740
  2.9 18.9 %copy-start.1 = (f32[24,8,128]{2,1,0:T(8,128)S(1)}, f32[24,8,128]{2,1,0:T(8,128)}, u32[]{:S(2)}) copy-start(f32[24,8,128]{2,1,0:T(8,128)} %param.7) | copy-start | bytes 294916
  2.9 18.9 %copy-start.2 = (s32[32]{0:T(128)S(1)}, s32[32]{0:T(128)}, u32[]{:S(2)}) copy-start(s32[32]{0:T(128)} %cell_ref.1) | copy-start | bytes 388
  2.9 10.8 %all-to-all-start = ((f32[8,32,128]{2,1,0:T(8,128)}), f32[8,32,128]{2,1,0:T(8,128)S(1)}, u32[]{:S(2)}, u32[]{:S(2)}) async-start(f32[8,32,128]{2,1,0:T(8,128)} %bitcast.3), calls=%async_computation | async-start | bytes 262144 | tf_op jit(solution)/shard_map/all_to_all | solution.py:777
  8.2 8.7 %collective-permute-start = (f32[7,24,128]{2,1,0:T(8,128)S(1)}, f32[7,24,128]{2,1,0:T(8,128)S(1)}, u32[]{:S(2)}, u32[]{:S(2)}) collective-permute-start(f32[7,24,128]{2,1,0:T(8,128)S(1)} %get-tuple-element.28), channel_id=1, source_target_pairs={{0,2},{4,6},{2,0},{6,4},{1,3},{5,7},{3,1},{7,5},{8,10},{12,14},{10... | collective-permute-start | bytes 258056 | tf_op jit(solution)/shard_map/ppermute | solution.py:784
  9.8 7.2 %collective-permute-start.1 = (f32[7,24,128]{2,1,0:T(8,128)S(1)}, f32[7,24,128]{2,1,0:T(8,128)S(1)}, u32[]{:S(2)}, u32[]{:S(2)}) collective-permute-start(f32[7,24,128]{2,1,0:T(8,128)S(1)} %get-tuple-element.29), channel_id=1, source_target_pairs={{2,4},{4,2},{3,5},{5,3},{10,12},{12,10},{11,13},{13,11},{18,20},{2... | collective-permute-start | bytes 258056 | tf_op jit(solution)/shard_map/ppermute | solution.py:785
  17.7 4.1 %collective-permute-start.2 = (f32[2,48,128]{2,1,0:T(8,128)S(1)}, f32[2,48,128]{2,1,0:T(8,128)S(1)}, u32[]{:S(2)}, u32[]{:S(2)}) collective-permute-start(f32[2,48,128]{2,1,0:T(8,128)S(1)} %get-tuple-element.35), channel_id=1, source_target_pairs={{0,1},{1,0},{2,3},{3,2},{4,5},{5,4},{6,7},{7,6},{8,9},{9,8},{10,11... | collective-permute-start | bytes 147464 | tf_op jit(solution)/shard_map/ppermute | solution.py:791
  17.7 8.1 %all-to-all-start.1 = ((f32[8,8,128]{2,1,0:T(8,128)}), f32[8,8,128]{2,1,0:T(8,128)S(1)}, u32[]{:S(2)}, u32[]{:S(2)}) async-start(f32[8,8,128]{2,1,0:T(8,128)} %get-tuple-element.30), calls=%async_computation.1 | async-start | bytes 65536 | tf_op jit(solution)/shard_map/all_to_all | solution.py:777

commit v20 on v19

--- a/solution.py
+++ b/solution.py
@@ -35,7 +35,6 @@
 item_count = 7
 back_rows = 8
 polymer_row = 4
-line_lane = 64
 
 
 block_slots = 32
@@ -407,18 +406,10 @@
                 at = 2 * u + a
                 out_ref[2 * beside + core, at : at + 1, :] = sides[u][a, x : x + 1, :]
 
-    lane = lanes_of((8, size_z))
-    source = jnp.where(core == 0, size_z - 1, 0)
-    other = 2 * macro + 1 - core
-    total = chunk_ref[other]
-    for i in range(size_x // 8):
-        for u in range(2):
-            for a in range(2):
-                at = line_lane + 4 * i + 2 * u + a
-                total = jnp.where(
-                    lane == at, rolled(sides[u][1 + a, 8 * i : 8 * i + 8, :], at - source), total
-                )
-    out_ref[other] = total
+    for u in range(2):
+        for number in range(2):
+            start = handed_rows + number * size_x
+            handed_ref[u, start : start + size_x, :] = sides[u][1 + number]
 
 
 def add_lines(chunks, received, first, second):
@@ -427,7 +418,7 @@
         functools.partial(lines_kernel, chunks.shape[0] // 2),
         out_shape=(
             jax.ShapeDtypeStruct(chunks.shape, jnp.float32), face, face,
-            jax.ShapeDtypeStruct((2, handed_rows, 128), jnp.float32),
+            jax.ShapeDtypeStruct((2, handed_rows + 2 * first.shape[1], 128), jnp.float32),
         ),
         in_specs=[VMEM] * 4,
         out_specs=(VMEM,) * 4,
@@ -479,8 +470,8 @@
 
 def flow_kernel(
     size_x, size_y, size_z, macro_count, cell_ref, position_ref, velocity_ref, viscosity_ref, chunk_ref,
-    y_low_ref, y_high_ref, handed_ref, out_ref, corner_ref, edge_ref, lines_ref, pick_ref, spread_ref,
-    padded, stress_x, stress_rest, faces, ghost_y, ghost_z, rows, halves,
+    y_low_ref, y_high_ref, handed_ref, out_ref, corner_ref, lines_ref, pick_ref, spread_ref,
+    padded, stress_x, stress_rest, faces, ghost_y, ghost_z, rows, halves, beyond,
 ):
     macro, core = place_of()
     one_hots(size_y, size_z, cell_ref, position_ref, lines_ref, pick_ref, spread_ref, rows)
@@ -523,6 +514,12 @@
         x_faces.append([kept(item, inside[s]) for item in items])
         corners = [handed_ref[s, chunk_rows + i * size_y : chunk_rows + (i + 1) * size_y, :] for i in range(2)]
         x_others.append([kept(rolled(corner, 2 * end + 1), inside[s]) for corner in corners])
+
+    y_others = []
+    for u in range(2):
+        start = handed_rows + size_x
+        y_others.append(rolled(handed_ref[u, handed_rows:start, :], 2 * end + 1))
+        beyond[u] = rolled(handed_ref[u, start : start + size_x, :], 2 * end + 1)
 
     group = size_z // 8
     packed = [
@@ -576,7 +573,8 @@
         weight = (0.5 * faces[3, x + 1]) * at_end
         normal = [(faces[4 + a, x + 1] - centre[a]) * sign_z for a in range(3)]
         ghost_z[0, x] = weight * (normal[0] + (faces[2, x + 2] - faces[2, x]))
-        ghost_z[1, x] = weight * (normal[1] + difference_rows(faces[2, x + 1]))
+        slope = difference_rows(faces[2, x + 1], beyond[0, pl.ds(x, 1), :], beyond[1, pl.ds(x, 1), :])
+        ghost_z[1, x] = weight * (normal[1] + slope)
         ghost_z[2, x] = weight * (2.0 * normal[2])
         return carry
 
@@ -605,16 +603,13 @@
         ]
         ghost_y[3 * u] = weight * (normal[0] + difference_rows(ref[1]))
         ghost_y[3 * u + 1] = weight * (2.0 * normal[1])
-        ghost_y[3 * u + 2] = weight * (normal[2] + difference_z(ref[1]))
+        wide = lanes_of((size_x, size_z))
+        across = jnp.where(wide == end, y_others[u] * sign_z, 0.0)
+        ghost_y[3 * u + 2] = weight * (normal[2] + (difference_z(ref[1]) + across))
         for s in range(2):
             x, sign_x = (0, -1.0) if s == 0 else (size_x - 1, 1.0)
             number = 4 * s + 2 * u + 1
             corner_ref[number : number + 1, :] = (0.5 * macro_step * sign * sign_x) * weight[x : x + 1, :]
-        wide = lanes_of((size_x, size_z))
-        scale = jnp.where(wide == end, (0.5 * macro_step * sign) * sign_z, 0.0)
-        edge_ref[2 * u] = scale * weight
-        for x in range(size_x):
-            edge_ref[2 * u + 1, x : x + 1, :] = scale[x : x + 1, :] * (0.5 * faces[3, x + 1, y : y + 1, :])
 
     columns = {(0, 1): (stress_x, 1, 1), (1, 1): (stress_rest, 0, 0), (2, 1): (stress_rest, 2, 0)}
     columns_z = {0: (stress_x, 2, 1), 1: (stress_rest, 2, 0), 2: (stress_rest, 1, 0)}
@@ -646,13 +641,12 @@
         out_shape=(
             jax.ShapeDtypeStruct((3, size_x * size_y, size_z), jnp.float32),
             jax.ShapeDtypeStruct((8, size_z), jnp.float32),
-            jax.ShapeDtypeStruct((4, size_x, size_z), jnp.float32),
             jax.ShapeDtypeStruct((3, flags, size_z), jnp.float32),
             jax.ShapeDtypeStruct((flags, 4 * returned), jnp.bfloat16),
             jax.ShapeDtypeStruct((row_count, 3 * product_depth), jnp.bfloat16),
         ),
         in_specs=[SMEM] * 2 + [VMEM] * 6,
-        out_specs=(VMEM,) * 6,
+        out_specs=(VMEM,) * 5,
         scratch_shapes=[
             pltpu.VMEM((3, *wide), jnp.float32),
             pltpu.VMEM((3, *wide), jnp.float32),
@@ -662,6 +656,7 @@
             pltpu.VMEM((3, *planes), jnp.float32),
             pltpu.VMEM((product_depth, -(-row_count // 128) * 128), jnp.float32),
             pltpu.VMEM((2, size_y, size_z), jnp.float32),
+            pltpu.VMEM((2, size_x, size_z), jnp.float32),
         ],
         compiler_params=limit(12),
         cost_estimate=pl.CostEstimate(flops=4000000, bytes_accessed=3000000, transcendentals=0),
@@ -682,7 +677,7 @@
 
 
 def polymer_kernel(
-    size_x, size_y, size_z, macro_count, chunk_ref, viscous_ref, corner_ref, edge_ref, lines_ref, pick_ref,
+    size_x, size_y, size_z, macro_count, chunk_ref, viscous_ref, corner_ref, lines_ref, pick_ref,
     spread_ref, partial_ref, out_ref, flag_ref,
 ):
     flags = viscous_ref.shape[0]
@@ -728,23 +723,13 @@
                 number = 4 * s + 2 * u + a
                 line = corner_ref[number : number + 1, :] * chunk_ref[pl.ds(start + 2 * u + a, 1), :]
                 out_ref[1 - a, at : at + 1, :] += jnp.where(inside, line, 0.0)
-    start = pl.multiple_of((2 * macro + 1 - core) * back_rows, 8)
-    packed = chunk_ref[pl.ds(start, back_rows), :]
-    end = jnp.where(core == 0, size_z - 1, 0)
-    for u in range(2):
-        y = 0 if u == 0 else size_y - 1
-        for a in range(2):
-            for i in range(size_x // 8):
-                line = rolled(packed, end - (line_lane + 4 * i + 2 * u + a)) * edge_ref[2 * u + a, 8 * i : 8 * i + 8, :]
-                at = pl.ds(8 * i * size_y + y, 8, stride=size_y)
-                out_ref[2 - a, at, :] += line
     for a in range(3):
         out_ref[a] += jnp.dot(
             spread_ref[...], jnp.concatenate(split[a], axis=0), preferred_element_type=jnp.float32
         )
 
 
-def add_polymer(chunks, viscous, corners, edges, lines, pick, spread, partial, shape):
+def add_polymer(chunks, viscous, corners, lines, pick, spread, partial, shape):
     flags = viscous.shape[0]
     size_x, size_y, size_z = shape
     return pl.pallas_call(
@@ -753,12 +738,12 @@
             jax.ShapeDtypeStruct(partial.shape, jnp.float32),
             jax.ShapeDtypeStruct((6, flags), jnp.float32),
         ),
-        in_specs=[VMEM] * 8,
+        in_specs=[VMEM] * 7,
         out_specs=(VMEM, VMEM),
         compiler_params=limit(8),
         cost_estimate=pl.CostEstimate(flops=400000, bytes_accessed=3000000, transcendentals=0),
         name="add_polymer",
-    )(chunks.reshape(-1, 128), viscous, corners, edges, lines, pick, spread, partial)
+    )(chunks.reshape(-1, 128), viscous, corners, lines, pick, spread, partial)
 
 
 def shards(velocity, viscosity, flag_cell, flag_owner, conformations, increments):
@@ -789,11 +774,11 @@
     polymer, y_low, y_high, handed = add_lines(polymer, received, first, second)
     returned = exchange(polymer)
     handed = lax.ppermute(handed, "micro", [(0, 1), (1, 0)])
-    partial, corners, edges, lines, pick, spread = flow_step(
+    partial, corners, lines, pick, spread = flow_step(
         flag_cell, position, velocity, viscosity, received, y_low, y_high, handed
     )
     velocity_next, flag_stress = add_polymer(
-        returned, viscous, corners, edges, lines, pick, spread, partial, viscosity.shape
+        returned, viscous, corners, lines, pick, spread, partial, viscosity.shape
     )
     return (velocity_next.reshape(velocity.shape), last_state, flag_stress)
 

time: 27.4 us -> 27.4 us (level)
  no operation moved by 1% of the time
where the time goes in v20:
time: 27.4 us; the launch traced here: 27 us
  starting transfers between devices  10.9 us (40%)
  Pallas kernels  9.79 us (36%)
  waiting for transfers between devices  4.8 us (18%)
  local copies, waits for them, and re-layouts  0.77 us (3%)
  between operations  0.72 us (3%)
    all_to_all x2, starting transfers between devices, exchange(): lax.all_to_all(rows, ('macro', 'micro'), split_axis=0, concat_axis=0, til...  8.66 us
    all_to_all x2, waiting for transfers between devices, exchange(): lax.all_to_all(rows, ('macro', 'micro'), split_axis=0, concat_axis=0, til...  4.8 us
    pallas_call x1, Pallas kernels, advance(): pl.pallas_call(functools.partial(micro_kernel, capacity, parts, rows, gro...  3.19 us
    pallas_call x1, Pallas kernels, flow_step(): pl.pallas_call(functools.partial(flow_kernel, size_x, size_y, size_z, chu...  2.49 us
    pallas_call x1, Pallas kernels, gather_rows(): pl.pallas_call(functools.partial(gather_kernel, capacity, size_x, size_y,...  2.22 us
    ppermute x1, starting transfers between devices, shards(): first = lax.ppermute(first, 'tile', swaps[0])  1.58 us
    pallas_call x1, Pallas kernels, add_polymer(): pl.pallas_call(functools.partial(polymer_kernel, size_x, size_y, size_z,...  1.23 us
    unnamed x7, local copies, waits for them, and re-layouts  0.77 us
  transfers between devices with their start and end apart: 5, of which 2 were waited for; matrix products, arithmetic and copies ran while one was open for 3% of the time, Pallas kernels for 21%

profile of v20, /device:TPU:0, one launch (start us, length us, event | category | flops | bytes accessed | tf_op | source)
XLA Modules:
  0.0 27.0 jit_solution(9666002927536445660)
XLA Ops:
  0.6 2.2 %gather_rows.1 = (f32[256,128]{1,0:T(8,128)}, s32[32]{0:T(128)S(1)}, f32[32,128]{1,0:T(8,128)S(1)}, f32[7,24,128]{2,1,0:T(8,128)S(1)}, f32[7,24,128]{2,1,0:T(8,1...) custom-call(s32[32]{0:T(128)} %cell_ref.1, s32[32]{0:T(128)} %bitcast.11, ...), custom_call_target="tpu_custom_call" | custom-call | flops 400000 | bytes 3000000 | tf_op jit(solution)/shard_map/gather_rows/pallas_call | solution.py:185
  2.9 0.0 copy-start
  2.9 0.0 copy-start.1
  2.9 0.0 copy-start.2
  2.9 5.3 %all-to-all-start = ((f32[8,32,128]{2,1,0:T(8,128)}), f32[8,32,128]{2,1,0:T(8,128)S(1)}, u32[]{:S(2)}, u32[]{:S(2)}) async-start(f32[8,32,128]{2,1,0:T(8,128)} %bitcast.3), calls=%async_computation | async-start | bytes 262144 | tf_op jit(solution)/shard_map/all_to_all | solution.py:762
  8.2 1.6 %collective-permute-start = (f32[7,24,128]{2,1,0:T(8,128)S(1)}, f32[7,24,128]{2,1,0:T(8,128)S(1)}, u32[]{:S(2)}, u32[]{:S(2)}) collective-permute-start(f32[7,24,128]{2,1,0:T(8,128)S(1)} %get-tuple-element.27), channel_id=1, source_target_pairs={{0,2},{4,6},{2,0},{6,4},{1,3},{5,7},{3,1},{7,5},{8,10},{12,14},{10... | collective-permute-start | bytes 258056 | tf_op jit(solution)/shard_map/ppermute | solution.py:769
  9.8 0.7 %collective-permute-start.1 = (f32[7,24,128]{2,1,0:T(8,128)S(1)}, f32[7,24,128]{2,1,0:T(8,128)S(1)}, u32[]{:S(2)}, u32[]{:S(2)}) collective-permute-start(f32[7,24,128]{2,1,0:T(8,128)S(1)} %get-tuple-element.28), channel_id=1, source_target_pairs={{2,4},{4,2},{3,5},{5,3},{10,12},{12,10},{11,13},{13,11},{18,20},{2... | collective-permute-start | bytes 258056 | tf_op jit(solution)/shard_map/ppermute | solution.py:770
  10.4 3.3 %all-to-all-done.rate_ref.received_ref.chunk_ref = f32[8,32,128]{2,1,0:T(8,128)S(1)} async-done(((f32[8,32,128]{2,1,0:T(8,128)}), f32[8,32,128]{2,1,0:T(8,128)S(1)}, u32[]{:S(2)}, u32[]{:S(2)}) %all-to-all-start) | async-done | bytes 131104 | tf_op jit(solution)/shard_map/all_to_all | solution.py:762
  13.7 3.2 %advance.1 = (f32[3,64,512]{2,1,0:T(8,128)S(1)}, f32[8,8,128]{2,1,0:T(8,128)S(1)}) custom-call(f32[3,64,512]{2,1,0:T(8,128)} %conform_ref.1, bf16[16,3,64,512]{3,2,1,0:T(8,128)(2,1)} %noise_ref.1, f32[8,32,128]{2,1,0:T(8,128)S(1)} %all-to-all-done.rate_ref.received_ref.chunk_ref, f32[3,32,512]{2,1,0:T(8,128)S(1)} %get-tuple-element.24.first_conform_ref, ...), custom_call_target="tpu_custom_call" | custom-call | flops 20000000 | bytes 5000000 | tf_op jit(solution)/shard_map/advance/pallas_call | solution.py:361
  16.9 0.0 collective-permute-done.first_ref
  16.9 0.0 collective-permute-done.1.second_ref
  17.0 0.7 %add_lines.1 = (f32[8,8,128]{2,1,0:T(8,128)}, f32[7,24,128]{2,1,0:T(8,128)S(1)}, f32[7,24,128]{2,1,0:T(8,128)S(1)}, f32[2,96,128]{2,1,0:T(8,128)S(1)}) custom-call(f32[8,8,128]{2,1,0:T(8,128)S(1)} %get-tuple-element.26.chunk_ref, f32[8,32,128]{2,1,0:T(8,128)S(1)} %all-to-all-done.rate_ref.received_ref.chunk_ref, ...), custom_call_target="tpu_custom_call" | custom-call | flops 20000 | bytes 400000 | tf_op jit(solution)/shard_map/add_lines/pallas_call | solution.py:417
  17.6 0.0 collective-permute-start.2
  17.6 3.3 %all-to-all-start.1 = ((f32[8,8,128]{2,1,0:T(8,128)}), f32[8,8,128]{2,1,0:T(8,128)S(1)}, u32[]{:S(2)}, u32[]{:S(2)}) async-start(f32[8,8,128]{2,1,0:T(8,128)} %get-tuple-element.29), calls=%async_computation.1 | async-start | bytes 65536 | tf_op jit(solution)/shard_map/all_to_all | solution.py:762
  21.0 0.7 %copy.9 = f32[3,64,512]{2,1,0:T(8,128)} copy(f32[3,64,512]{2,1,0:T(8,128)S(1)} %get-tuple-element.44) | data formatting | bytes 786432
  21.7 0.0 collective-permute-done.2.handed_ref
  21.7 0.0 copy-done
  21.7 0.0 copy-done.1
  21.7 0.0 copy-done.2
  21.7 2.5 %flow_step.1 = (f32[3,192,128]{2,1,0:T(8,128)S(1)}, f32[8,128]{1,0:T(8,128)S(1)}, f32[3,32,128]{2,1,0:T(8,128)S(1)}, bf16[32,256]{1,0:T(8,128)(2,1)S(1)}, bf16[192,384]{1,0:T(8,128)(2,1)S(1)}) custom-call(s32[32]{0:T(128)S(1)} %copy-done.2, s32[32]{0:T(128)S(1)} %get-tuple-element.31.position_ref, f32[3,192,128]{2,1,0:T(8,128)S(1)} %bitcast.7, ...), custom_call_target="tpu_custom_call" | custom-call | flops 4000000 | bytes 3000000 | tf_op jit(solution)/shard_map/flow_step/pallas_call | solution.py:639
  24.2 1.5 %all-to-all-done.1 = f32[8,8,128]{2,1,0:T(8,128)S(1)} async-done(((f32[8,8,128]{2,1,0:T(8,128)}), f32[8,8,128]{2,1,0:T(8,128)S(1)}, u32[]{:S(2)}, u32[]{:S(2)}) %all-to-all-start.1) | async-done | bytes 32800 | tf_op jit(solution)/shard_map/all_to_all | solution.py:762
  25.7 1.2 %add_polymer.1 = (f32[3,192,128]{2,1,0:T(8,128)}, f32[6,32]{1,0:T(8,128)}) custom-call(f32[64,128]{1,0:T(8,128)S(1)} %bitcast.10, f32[32,128]{1,0:T(8,128)S(1)} %get-tuple-element.30.viscous_ref, f32[8,128]{1,0:T(8,128)S(1)} %get-tuple-element.35.corner_ref, f32[3,32,128]{2,1,0:T(8,128)S(1)} %get-tuple-element.36.lines_ref, ...), custom_call_target="tpu_custom_call" | custom-call | flops 400000 | bytes 3000000 | tf_op jit(solution)/shard_map/add_polymer/pallas_call | solution.py:735
Async XLA Ops:
  2.9 18.9 %copy-start = (f32[3,24,8,128]{3,2,1,0:T(8,128)S(1)}, f32[3,24,8,128]{3,2,1,0:T(8,128)}, u32[]{:S(2)}) copy-start(f32[3,24,8,128]{3,2,1,0:T(8,128)} %param.6) | copy-start | bytes 884740
  2.9 18.9 %copy-start.1 = (f32[24,8,128]{2,1,0:T(8,128)S(1)}, f32[24,8,128]{2,1,0:T(8,128)}, u32[]{:S(2)}) copy-start(f32[24,8,128]{2,1,0:T(8,128)} %param.7) | copy-start | bytes 294916
  2.9 18.8 %copy-start.2 = (s32[32]{0:T(128)S(1)}, s32[32]{0:T(128)}, u32[]{:S(2)}) copy-start(s32[32]{0:T(128)} %cell_ref.1) | copy-start | bytes 388
  2.9 10.8 %all-to-all-start = ((f32[8,32,128]{2,1,0:T(8,128)}), f32[8,32,128]{2,1,0:T(8,128)S(1)}, u32[]{:S(2)}, u32[]{:S(2)}) async-start(f32[8,32,128]{2,1,0:T(8,128)} %bitcast.3), calls=%async_computation | async-start | bytes 262144 | tf_op jit(solution)/shard_map/all_to_all | solution.py:762
  8.2 8.7 %collective-permute-start = (f32[7,24,128]{2,1,0:T(8,128)S(1)}, f32[7,24,128]{2,1,0:T(8,128)S(1)}, u32[]{:S(2)}, u32[]{:S(2)}) collective-permute-start(f32[7,24,128]{2,1,0:T(8,128)S(1)} %get-tuple-element.27), channel_id=1, source_target_pairs={{0,2},{4,6},{2,0},{6,4},{1,3},{5,7},{3,1},{7,5},{8,10},{12,14},{10... | collective-permute-start | bytes 258056 | tf_op jit(solution)/shard_map/ppermute | solution.py:769
  9.8 7.2 %collective-permute-start.1 = (f32[7,24,128]{2,1,0:T(8,128)S(1)}, f32[7,24,128]{2,1,0:T(8,128)S(1)}, u32[]{:S(2)}, u32[]{:S(2)}) collective-permute-start(f32[7,24,128]{2,1,0:T(8,128)S(1)} %get-tuple-element.28), channel_id=1, source_target_pairs={{2,4},{4,2},{3,5},{5,3},{10,12},{12,10},{11,13},{13,11},{18,20},{2... | collective-permute-start | bytes 258056 | tf_op jit(solution)/shard_map/ppermute | solution.py:770
  17.6 4.1 %collective-permute-start.2 = (f32[2,96,128]{2,1,0:T(8,128)S(1)}, f32[2,96,128]{2,1,0:T(8,128)S(1)}, u32[]{:S(2)}, u32[]{:S(2)}) collective-permute-start(f32[2,96,128]{2,1,0:T(8,128)S(1)} %get-tuple-element.34), channel_id=1, source_target_pairs={{0,1},{1,0},{2,3},{3,2},{4,5},{5,4},{6,7},{7,6},{8,9},{9,8},{10,11... | collective-permute-start | bytes 294920 | tf_op jit(solution)/shard_map/ppermute | solution.py:776
  17.6 8.1 %all-to-all-start.1 = ((f32[8,8,128]{2,1,0:T(8,128)}), f32[8,8,128]{2,1,0:T(8,128)S(1)}, u32[]{:S(2)}, u32[]{:S(2)}) async-start(f32[8,8,128]{2,1,0:T(8,128)} %get-tuple-element.29), calls=%async_computation.1 | async-start | bytes 65536 | tf_op jit(solution)/shard_map/all_to_all | solution.py:762

commit v21 on v20

--- a/solution.py
+++ b/solution.py
@@ -381,11 +381,16 @@
     )(far(conformations), far(increments), chunks, first_conform, first_noise)
 
 
-def lines_kernel(
-    macro_count, chunk_ref, received_ref, first_ref, second_ref, out_ref, y_low_ref, y_high_ref, handed_ref
-):
+def lines_kernel(macro_count, chunk_ref, received_ref, first_ref, second_ref, out_ref, handed_ref):
     out_ref[...] = chunk_ref[...]
     macro, core = place_of()
+    even = lax.axis_index("tile") & 1 == 0
+    size_x = first_ref.shape[1]
+
+    def side_of(u, item, at):
+        first, second = first_ref[item, at, :], second_ref[item, at, :]
+        return jnp.where(even, second, first) if u == 0 else jnp.where(even, first, second)
+
     for side in range(2):
         beside = neighbour(macro, side, macro_count)
         handed_ref[side, 0:chunk_rows, :] = received_ref[2 * beside + 1 - core]
@@ -393,35 +398,26 @@
             handed_ref[side, chunk_rows + number * 8 : chunk_rows + (number + 1) * 8, :] = received_ref[
                 2 * beside + core, a * 8 : (a + 1) * 8, :
             ]
-    even = lax.axis_index("tile") & 1 == 0
-    y_low_ref[...] = jnp.where(even, second_ref[...], first_ref[...])
-    y_high_ref[...] = jnp.where(even, first_ref[...], second_ref[...])
-    sides = (y_low_ref, y_high_ref)
-    size_x, size_z = y_low_ref.shape[1:]
-    for side in range(2):
-        beside = neighbour(macro, side, macro_count)
         x = 0 if side == 0 else size_x - 1
         for u in range(2):
             for a in range(2):
                 at = 2 * u + a
-                out_ref[2 * beside + core, at : at + 1, :] = sides[u][a, x : x + 1, :]
-
+                out_ref[2 * beside + core, at : at + 1, :] = side_of(u, a, slice(x, x + 1))
     for u in range(2):
         for number in range(2):
             start = handed_rows + number * size_x
-            handed_ref[u, start : start + size_x, :] = sides[u][1 + number]
+            handed_ref[u, start : start + size_x, :] = side_of(u, 1 + number, slice(0, size_x))
 
 
 def add_lines(chunks, received, first, second):
-    face = jax.ShapeDtypeStruct(first.shape, jnp.float32)
     return pl.pallas_call(
         functools.partial(lines_kernel, chunks.shape[0] // 2),
         out_shape=(
-            jax.ShapeDtypeStruct(chunks.shape, jnp.float32), face, face,
+            jax.ShapeDtypeStruct(chunks.shape, jnp.float32),
             jax.ShapeDtypeStruct((2, handed_rows + 2 * first.shape[1], 128), jnp.float32),
         ),
         in_specs=[VMEM] * 4,
-        out_specs=(VMEM,) * 4,
+        out_specs=(VMEM,) * 2,
         compiler_params=limit(4),
         cost_estimate=pl.CostEstimate(flops=20000, bytes_accessed=400000, transcendentals=0),
         name="add_lines",
@@ -470,10 +466,14 @@
 
 def flow_kernel(
     size_x, size_y, size_z, macro_count, cell_ref, position_ref, velocity_ref, viscosity_ref, chunk_ref,
-    y_low_ref, y_high_ref, handed_ref, out_ref, corner_ref, lines_ref, pick_ref, spread_ref,
+    first_ref, second_ref, handed_ref, out_ref, corner_ref, lines_ref, pick_ref, spread_ref,
     padded, stress_x, stress_rest, faces, ghost_y, ghost_z, rows, halves, beyond,
+    y_low_ref, y_high_ref,
 ):
     macro, core = place_of()
+    even = lax.axis_index("tile") & 1 == 0
+    y_low_ref[...] = jnp.where(even, second_ref[...], first_ref[...])
+    y_high_ref[...] = jnp.where(even, first_ref[...], second_ref[...])
     one_hots(size_y, size_z, cell_ref, position_ref, lines_ref, pick_ref, spread_ref, rows)
     inside = (macro > 0, macro < macro_count - 1)
     sign_z = jnp.where(core == 0, 1.0, -1.0)
@@ -629,7 +629,7 @@
     lax.fori_loop(0, size_x, step_plane, 0, unroll=6)
 
 
-def flow_step(flag_cell, position, velocity, viscosity, chunks, y_low, y_high, handed):
+def flow_step(flag_cell, position, velocity, viscosity, chunks, first, second, handed):
     size_x, size_y, size_z = viscosity.shape
     flags = flag_cell.shape[0]
     returned = chunks.shape[0] * back_rows
@@ -657,6 +657,8 @@
             pltpu.VMEM((product_depth, -(-row_count // 128) * 128), jnp.float32),
             pltpu.VMEM((2, size_y, size_z), jnp.float32),
             pltpu.VMEM((2, size_x, size_z), jnp.float32),
+            pltpu.VMEM(first.shape, jnp.float32),
+            pltpu.VMEM(first.shape, jnp.float32),
         ],
         compiler_params=limit(12),
         cost_estimate=pl.CostEstimate(flops=4000000, bytes_accessed=3000000, transcendentals=0),
@@ -665,7 +667,7 @@
         flag_cell, position,
         velocity.reshape(3, size_x * size_y, size_z),
         viscosity.reshape(size_x * size_y, size_z),
-        chunks, y_low, y_high, handed,
+        chunks, first, second, handed,
     )
 
 
@@ -771,11 +773,11 @@
     last_state, polymer = advance(
         conformations, increments, received, first_conform, first_noise, capacity
     )
-    polymer, y_low, y_high, handed = add_lines(polymer, received, first, second)
+    polymer, handed = add_lines(polymer, received, first, second)
     returned = exchange(polymer)
     handed = lax.ppermute(handed, "micro", [(0, 1), (1, 0)])
     partial, corners, lines, pick, spread = flow_step(
-        flag_cell, position, velocity, viscosity, received, y_low, y_high, handed
+        flag_cell, position, velocity, viscosity, received, first, second, handed
     )
     velocity_next, flag_stress = add_polymer(
         returned, viscous, corners, lines, pick, spread, partial, viscosity.shape

time: 27.4 us -> 27.3 us (level)
  no operation moved by 1% of the time
where the time goes in v21:
time: 27.3 us; the launch traced here: 26.9 us
  starting transfers between devices  10.9 us (40%)
  Pallas kernels  9.78 us (36%)
  waiting for transfers between devices  4.79 us (18%)
  local copies, waits for them, and re-layouts  0.77 us (3%)
  between operations  0.72 us (3%)
    all_to_all x2, starting transfers between devices, exchange(): lax.all_to_all(rows, ('macro', 'micro'), split_axis=0, concat_axis=0, til...  8.65 us
    all_to_all x2, waiting for transfers between devices, exchange(): lax.all_to_all(rows, ('macro', 'micro'), split_axis=0, concat_axis=0, til...  4.79 us
    pallas_call x1, Pallas kernels, advance(): pl.pallas_call(functools.partial(micro_kernel, capacity, parts, rows, gro...  3.19 us
    pallas_call x1, Pallas kernels, flow_step(): pl.pallas_call(functools.partial(flow_kernel, size_x, size_y, size_z, chu...  2.5 us
    pallas_call x1, Pallas kernels, gather_rows(): pl.pallas_call(functools.partial(gather_kernel, capacity, size_x, size_y,...  2.22 us
    ppermute x1, starting transfers between devices, shards(): first = lax.ppermute(first, 'tile', swaps[0])  1.58 us
    pallas_call x1, Pallas kernels, add_polymer(): pl.pallas_call(functools.partial(polymer_kernel, size_x, size_y, size_z,...  1.22 us
    unnamed x7, local copies, waits for them, and re-layouts  0.77 us
  transfers between devices with their start and end apart: 5, of which 2 were waited for; matrix products, arithmetic and copies ran while one was open for 3% of the time, Pallas kernels for 21%

profile of v21, /device:TPU:0, one launch (start us, length us, event | category | flops | bytes accessed | tf_op | source)
XLA Modules:
  0.0 26.9 jit_solution(4265236536308836896)
XLA Ops:
  0.6 2.2 %gather_rows.1 = (f32[256,128]{1,0:T(8,128)}, s32[32]{0:T(128)S(1)}, f32[32,128]{1,0:T(8,128)S(1)}, f32[7,24,128]{2,1,0:T(8,128)S(1)}, f32[7,24,128]{2,1,0:T(8,1...) custom-call(s32[32]{0:T(128)} %cell_ref.1, s32[32]{0:T(128)} %bitcast.11, ...), custom_call_target="tpu_custom_call" | custom-call | flops 400000 | bytes 3000000 | tf_op jit(solution)/shard_map/gather_rows/pallas_call | solution.py:185
  2.9 0.0 copy-start
  2.9 0.0 copy-start.1
  2.9 0.0 copy-start.2
  2.9 5.3 %all-to-all-start = ((f32[8,32,128]{2,1,0:T(8,128)}), f32[8,32,128]{2,1,0:T(8,128)S(1)}, u32[]{:S(2)}, u32[]{:S(2)}) async-start(f32[8,32,128]{2,1,0:T(8,128)} %bitcast.3), calls=%async_computation | async-start | bytes 262144 | tf_op jit(solution)/shard_map/all_to_all | solution.py:764
  8.2 1.6 %collective-permute-start = (f32[7,24,128]{2,1,0:T(8,128)S(1)}, f32[7,24,128]{2,1,0:T(8,128)S(1)}, u32[]{:S(2)}, u32[]{:S(2)}) collective-permute-start(f32[7,24,128]{2,1,0:T(8,128)S(1)} %get-tuple-element.25), channel_id=1, source_target_pairs={{0,2},{4,6},{2,0},{6,4},{1,3},{5,7},{3,1},{7,5},{8,10},{12,14},{10... | collective-permute-start | bytes 258056 | tf_op jit(solution)/shard_map/ppermute | solution.py:771
  9.8 0.7 %collective-permute-start.1 = (f32[7,24,128]{2,1,0:T(8,128)S(1)}, f32[7,24,128]{2,1,0:T(8,128)S(1)}, u32[]{:S(2)}, u32[]{:S(2)}) collective-permute-start(f32[7,24,128]{2,1,0:T(8,128)S(1)} %get-tuple-element.26), channel_id=1, source_target_pairs={{2,4},{4,2},{3,5},{5,3},{10,12},{12,10},{11,13},{13,11},{18,20},{2... | collective-permute-start | bytes 258056 | tf_op jit(solution)/shard_map/ppermute | solution.py:772
  10.5 3.3 %all-to-all-done.rate_ref.received_ref.chunk_ref = f32[8,32,128]{2,1,0:T(8,128)S(1)} async-done(((f32[8,32,128]{2,1,0:T(8,128)}), f32[8,32,128]{2,1,0:T(8,128)S(1)}, u32[]{:S(2)}, u32[]{:S(2)}) %all-to-all-start) | async-done | bytes 131104 | tf_op jit(solution)/shard_map/all_to_all | solution.py:764
  13.7 3.2 %advance.1 = (f32[3,64,512]{2,1,0:T(8,128)S(1)}, f32[8,8,128]{2,1,0:T(8,128)S(1)}) custom-call(f32[3,64,512]{2,1,0:T(8,128)} %conform_ref.1, bf16[16,3,64,512]{3,2,1,0:T(8,128)(2,1)} %noise_ref.1, f32[8,32,128]{2,1,0:T(8,128)S(1)} %all-to-all-done.rate_ref.received_ref.chunk_ref, f32[3,32,512]{2,1,0:T(8,128)S(1)} %get-tuple-element.22.first_conform_ref, ...), custom_call_target="tpu_custom_call" | custom-call | flops 20000000 | bytes 5000000 | tf_op jit(solution)/shard_map/advance/pallas_call | solution.py:361
  16.9 0.0 collective-permute-done.first_ref
  16.9 0.0 collective-permute-done.1.second_ref
  17.0 0.6 %add_lines.1 = (f32[8,8,128]{2,1,0:T(8,128)}, f32[2,96,128]{2,1,0:T(8,128)S(1)}) custom-call(f32[8,8,128]{2,1,0:T(8,128)S(1)} %get-tuple-element.24.chunk_ref, f32[8,32,128]{2,1,0:T(8,128)S(1)} %all-to-all-done.rate_ref.received_ref.chunk_ref, f32[7,24,128]{2,1,0:T(8,128)S(1)} %collective-permute-done.first_ref, ...), custom_call_target="tpu_custom_call" | custom-call | flops 20000 | bytes 400000 | tf_op jit(solution)/shard_map/add_lines/pallas_call | solution.py:413
  17.6 0.0 collective-permute-start.2
  17.6 3.3 %all-to-all-start.1 = ((f32[8,8,128]{2,1,0:T(8,128)}), f32[8,8,128]{2,1,0:T(8,128)S(1)}, u32[]{:S(2)}, u32[]{:S(2)}) async-start(f32[8,8,128]{2,1,0:T(8,128)} %get-tuple-element.27), calls=%async_computation.1 | async-start | bytes 65536 | tf_op jit(solution)/shard_map/all_to_all | solution.py:764
  21.0 0.7 %copy.9 = f32[3,64,512]{2,1,0:T(8,128)} copy(f32[3,64,512]{2,1,0:T(8,128)S(1)} %get-tuple-element.40) | data formatting | bytes 786432
  21.7 0.0 collective-permute-done.2.handed_ref
  21.7 0.0 copy-done
  21.7 0.0 copy-done.1
  21.7 0.0 copy-done.2
  21.7 2.5 %flow_step.1 = (f32[3,192,128]{2,1,0:T(8,128)S(1)}, f32[8,128]{1,0:T(8,128)S(1)}, f32[3,32,128]{2,1,0:T(8,128)S(1)}, bf16[32,256]{1,0:T(8,128)(2,1)S(1)}, bf16[192,384]{1,0:T(8,128)(2,1)S(1)}) custom-call(s32[32]{0:T(128)S(1)} %copy-done.2, s32[32]{0:T(128)S(1)} %get-tuple-element.29.position_ref, f32[3,192,128]{2,1,0:T(8,128)S(1)} %bitcast.7, ...), custom_call_target="tpu_custom_call" | custom-call | flops 4000000 | bytes 3000000 | tf_op jit(solution)/shard_map/flow_step/pallas_call | solution.py:639
  24.2 1.5 %all-to-all-done.1 = f32[8,8,128]{2,1,0:T(8,128)S(1)} async-done(((f32[8,8,128]{2,1,0:T(8,128)}), f32[8,8,128]{2,1,0:T(8,128)S(1)}, u32[]{:S(2)}, u32[]{:S(2)}) %all-to-all-start.1) | async-done | bytes 32800 | tf_op jit(solution)/shard_map/all_to_all | solution.py:764
  25.7 1.2 %add_polymer.1 = (f32[3,192,128]{2,1,0:T(8,128)}, f32[6,32]{1,0:T(8,128)}) custom-call(f32[64,128]{1,0:T(8,128)S(1)} %bitcast.10, f32[32,128]{1,0:T(8,128)S(1)} %get-tuple-element.28.viscous_ref, f32[8,128]{1,0:T(8,128)S(1)} %get-tuple-element.31.corner_ref, f32[3,32,128]{2,1,0:T(8,128)S(1)} %get-tuple-element.32.lines_ref, ...), custom_call_target="tpu_custom_call" | custom-call | flops 400000 | bytes 3000000 | tf_op jit(solution)/shard_map/add_polymer/pallas_call | solution.py:737
Async XLA Ops:
  2.9 18.8 %copy-start = (f32[3,24,8,128]{3,2,1,0:T(8,128)S(1)}, f32[3,24,8,128]{3,2,1,0:T(8,128)}, u32[]{:S(2)}) copy-start(f32[3,24,8,128]{3,2,1,0:T(8,128)} %param.6) | copy-start | bytes 884740
  2.9 18.8 %copy-start.1 = (f32[24,8,128]{2,1,0:T(8,128)S(1)}, f32[24,8,128]{2,1,0:T(8,128)}, u32[]{:S(2)}) copy-start(f32[24,8,128]{2,1,0:T(8,128)} %param.7) | copy-start | bytes 294916
  2.9 18.8 %copy-start.2 = (s32[32]{0:T(128)S(1)}, s32[32]{0:T(128)}, u32[]{:S(2)}) copy-start(s32[32]{0:T(128)} %cell_ref.1) | copy-start | bytes 388
  2.9 10.8 %all-to-all-start = ((f32[8,32,128]{2,1,0:T(8,128)}), f32[8,32,128]{2,1,0:T(8,128)S(1)}, u32[]{:S(2)}, u32[]{:S(2)}) async-start(f32[8,32,128]{2,1,0:T(8,128)} %bitcast.3), calls=%async_computation | async-start | bytes 262144 | tf_op jit(solution)/shard_map/all_to_all | solution.py:764
  8.2 8.7 %collective-permute-start = (f32[7,24,128]{2,1,0:T(8,128)S(1)}, f32[7,24,128]{2,1,0:T(8,128)S(1)}, u32[]{:S(2)}, u32[]{:S(2)}) collective-permute-start(f32[7,24,128]{2,1,0:T(8,128)S(1)} %get-tuple-element.25), channel_id=1, source_target_pairs={{0,2},{4,6},{2,0},{6,4},{1,3},{5,7},{3,1},{7,5},{8,10},{12,14},{10... | collective-permute-start | bytes 258056 | tf_op jit(solution)/shard_map/ppermute | solution.py:771
  9.8 7.2 %collective-permute-start.1 = (f32[7,24,128]{2,1,0:T(8,128)S(1)}, f32[7,24,128]{2,1,0:T(8,128)S(1)}, u32[]{:S(2)}, u32[]{:S(2)}) collective-permute-start(f32[7,24,128]{2,1,0:T(8,128)S(1)} %get-tuple-element.26), channel_id=1, source_target_pairs={{2,4},{4,2},{3,5},{5,3},{10,12},{12,10},{11,13},{13,11},{18,20},{2... | collective-permute-start | bytes 258056 | tf_op jit(solution)/shard_map/ppermute | solution.py:772
  17.6 4.1 %collective-permute-start.2 = (f32[2,96,128]{2,1,0:T(8,128)S(1)}, f32[2,96,128]{2,1,0:T(8,128)S(1)}, u32[]{:S(2)}, u32[]{:S(2)}) collective-permute-start(f32[2,96,128]{2,1,0:T(8,128)S(1)} %get-tuple-element.30), channel_id=1, source_target_pairs={{0,1},{1,0},{2,3},{3,2},{4,5},{5,4},{6,7},{7,6},{8,9},{9,8},{10,11... | collective-permute-start | bytes 294920 | tf_op jit(solution)/shard_map/ppermute | solution.py:778
  17.6 8.1 %all-to-all-start.1 = ((f32[8,8,128]{2,1,0:T(8,128)}), f32[8,8,128]{2,1,0:T(8,128)S(1)}, u32[]{:S(2)}, u32[]{:S(2)}) async-start(f32[8,8,128]{2,1,0:T(8,128)} %get-tuple-element.27), calls=%async_computation.1 | async-start | bytes 65536 | tf_op jit(solution)/shard_map/all_to_all | solution.py:764

commit v22 on v21

--- a/solution.py
+++ b/solution.py
@@ -255,9 +255,6 @@
             read(block).start()
         for group in range(early if block == 0 else 0, groups):
             read_noise(block, group).start()
-    conform[:, 0:rows, :] = first_conform_ref[...]
-    for step in range(steps // first_share):
-        noise[step, :, 0:rows, :] = first_noise_ref[step]
     for owner in range(owners):
         packed = rate_ref[owner, half_face : half_face + capacity // 2, :]
         rate[pl.ds(owner * capacity, capacity // 2, stride=2), :] = packed
@@ -282,8 +279,9 @@
             result = [result[i // 2] * level[i ^ 1] for i in range(len(level))]
         return result
 
-    def advance_block(block, carry):
-        ats = [pl.ds(pl.multiple_of(block * rows + 16 * half, 16), 16) for half in range(rows // 16)]
+    def advance_block(block):
+        ats = [pl.ds(block * rows + 16 * half, 16) for half in range(rows // 16)]
+        ahead = [pl.ds(16 * half, 16) for half in range(rows // 16)]
         rates = [
             [[rate_wide.at[3 * a + b, at, :] for b in range(3)] for a in range(3)] for at in ats
         ]
@@ -296,29 +294,27 @@
                 table = rates[half]
                 for a in range(3):
                     b, c = [other for other in range(3) if other != a]
-                    kick = noise[step, a, ats[half], lanes].astype(jnp.float32)
+                    if block == 0 and step < steps // first_share:
+                        kick = first_noise_ref[step, a, ahead[half], lanes]
+                    else:
+                        kick = noise[step, a, ats[half], lanes]
+                    kick = kick.astype(jnp.float32)
                     rest = (table[a][b][...] * q[b] + table[a][c][...] * q[c]) + kick
                     updated.append((table[a][a][...] - springs[piece]) * q[a] + rest)
             return tuple(updated)
 
         def advance_group(group, state):
-            if group < early:
-
-                @pl.when(block > 0)
-                def _():
-                    read_noise(block, group).wait()
-
-            else:
+            if block > 0 or group >= early:
                 read_noise(block, group).wait()
             for step in range(span):
                 state = substep(group * span + step, state)
             return state
 
-        @pl.when(block > 0)
-        def _():
+        if block > 0:
             read(block).wait()
-
-        state = tuple(conform[a, ats[half], lanes] * scale for half, lanes in pieces for a in range(3))
+            state = tuple(conform[a, ats[half], lanes] * scale for half, lanes in pieces for a in range(3))
+        else:
+            state = tuple(first_conform_ref[a, ahead[half], lanes] * scale for half, lanes in pieces for a in range(3))
         for group in range(groups):
             state = advance_group(group, state)
         inverse = inverses(state, 1.0)
@@ -335,9 +331,9 @@
                     sums[k] = term if sums[k] is None else sums[k] + term
             for k in range(6):
                 sums_ref[k, at, :] = sums[k]
-        return carry
-
-    lax.fori_loop(0, blocks, advance_block, 0)
+
+    for block in range(blocks):
+        advance_block(block)
     lane = lanes_of((slots, 128))
     rank = lax.broadcasted_iota(jnp.int32, (slots, 128), 0) & (capacity - 1)
     packed = jnp.zeros((slots, 128), jnp.float32)

time: 27.3 us -> 27.3 us (level)
  no operation moved by 1% of the time
where the time goes in v22:
time: 27.3 us; the launch traced here: 26.9 us
  starting transfers between devices  10.9 us (40%)
  Pallas kernels  9.74 us (36%)
  waiting for transfers between devices  4.79 us (18%)
  local copies, waits for them, and re-layouts  0.77 us (3%)
  between operations  0.72 us (3%)
    all_to_all x2, starting transfers between devices, exchange(): lax.all_to_all(rows, ('macro', 'micro'), split_axis=0, concat_axis=0, til...  8.66 us
    all_to_all x2, waiting for transfers between devices, exchange(): lax.all_to_all(rows, ('macro', 'micro'), split_axis=0, concat_axis=0, til...  4.79 us
    pallas_call x1, Pallas kernels, advance(): pl.pallas_call(functools.partial(micro_kernel, capacity, parts, rows, gro...  3.15 us
    pallas_call x1, Pallas kernels, flow_step(): pl.pallas_call(functools.partial(flow_kernel, size_x, size_y, size_z, chu...  2.5 us
    pallas_call x1, Pallas kernels, gather_rows(): pl.pallas_call(functools.partial(gather_kernel, capacity, size_x, size_y,...  2.22 us
    ppermute x1, starting transfers between devices, shards(): first = lax.ppermute(first, 'tile', swaps[0])  1.58 us
    pallas_call x1, Pallas kernels, add_polymer(): pl.pallas_call(functools.partial(polymer_kernel, size_x, size_y, size_z,...  1.22 us
    unnamed x7, local copies, waits for them, and re-layouts  0.77 us
  transfers between devices with their start and end apart: 5, of which 2 were waited for; matrix products, arithmetic and copies ran while one was open for 3% of the time, Pallas kernels for 21%

profile of v22, /device:TPU:0, one launch (start us, length us, event | category | flops | bytes accessed | tf_op | source)
XLA Modules:
  0.0 26.9 jit_solution(6954110764056456412)
XLA Ops:
  0.6 2.2 %gather_rows.1 = (f32[256,128]{1,0:T(8,128)}, s32[32]{0:T(128)S(1)}, f32[32,128]{1,0:T(8,128)S(1)}, f32[7,24,128]{2,1,0:T(8,128)S(1)}, f32[7,24,128]{2,1,0:T(8,1...) custom-call(s32[32]{0:T(128)} %cell_ref.1, s32[32]{0:T(128)} %bitcast.11, ...), custom_call_target="tpu_custom_call" | custom-call | flops 400000 | bytes 3000000 | tf_op jit(solution)/shard_map/gather_rows/pallas_call | solution.py:185
  2.9 0.0 copy-start
  2.9 0.0 copy-start.1
  2.9 0.0 copy-start.2
  2.9 5.3 %all-to-all-start = ((f32[8,32,128]{2,1,0:T(8,128)}), f32[8,32,128]{2,1,0:T(8,128)S(1)}, u32[]{:S(2)}, u32[]{:S(2)}) async-start(f32[8,32,128]{2,1,0:T(8,128)} %bitcast.3), calls=%async_computation | async-start | bytes 262144 | tf_op jit(solution)/shard_map/all_to_all | solution.py:760
  8.2 1.6 %collective-permute-start = (f32[7,24,128]{2,1,0:T(8,128)S(1)}, f32[7,24,128]{2,1,0:T(8,128)S(1)}, u32[]{:S(2)}, u32[]{:S(2)}) collective-permute-start(f32[7,24,128]{2,1,0:T(8,128)S(1)} %get-tuple-element.25), channel_id=1, source_target_pairs={{0,2},{4,6},{2,0},{6,4},{1,3},{5,7},{3,1},{7,5},{8,10},{12,14},{10... | collective-permute-start | bytes 258056 | tf_op jit(solution)/shard_map/ppermute | solution.py:767
  9.8 0.7 %collective-permute-start.1 = (f32[7,24,128]{2,1,0:T(8,128)S(1)}, f32[7,24,128]{2,1,0:T(8,128)S(1)}, u32[]{:S(2)}, u32[]{:S(2)}) collective-permute-start(f32[7,24,128]{2,1,0:T(8,128)S(1)} %get-tuple-element.26), channel_id=1, source_target_pairs={{2,4},{4,2},{3,5},{5,3},{10,12},{12,10},{11,13},{13,11},{18,20},{2... | collective-permute-start | bytes 258056 | tf_op jit(solution)/shard_map/ppermute | solution.py:768
  10.5 3.3 %all-to-all-done.rate_ref.received_ref.chunk_ref = f32[8,32,128]{2,1,0:T(8,128)S(1)} async-done(((f32[8,32,128]{2,1,0:T(8,128)}), f32[8,32,128]{2,1,0:T(8,128)S(1)}, u32[]{:S(2)}, u32[]{:S(2)}) %all-to-all-start) | async-done | bytes 131104 | tf_op jit(solution)/shard_map/all_to_all | solution.py:760
  13.7 3.1 %advance.1 = (f32[3,64,512]{2,1,0:T(8,128)S(1)}, f32[8,8,128]{2,1,0:T(8,128)S(1)}) custom-call(f32[3,64,512]{2,1,0:T(8,128)} %conform_ref.1, bf16[16,3,64,512]{3,2,1,0:T(8,128)(2,1)} %noise_ref.1, f32[8,32,128]{2,1,0:T(8,128)S(1)} %all-to-all-done.rate_ref.received_ref.chunk_ref, f32[3,32,512]{2,1,0:T(8,128)S(1)} %get-tuple-element.22.first_conform_ref, ...), custom_call_target="tpu_custom_call" | custom-call | flops 20000000 | bytes 5000000 | tf_op jit(solution)/shard_map/advance/pallas_call | solution.py:357
  16.9 0.0 collective-permute-done.first_ref
  16.9 0.0 collective-permute-done.1.second_ref
  16.9 0.6 %add_lines.1 = (f32[8,8,128]{2,1,0:T(8,128)}, f32[2,96,128]{2,1,0:T(8,128)S(1)}) custom-call(f32[8,8,128]{2,1,0:T(8,128)S(1)} %get-tuple-element.24.chunk_ref, f32[8,32,128]{2,1,0:T(8,128)S(1)} %all-to-all-done.rate_ref.received_ref.chunk_ref, f32[7,24,128]{2,1,0:T(8,128)S(1)} %collective-permute-done.first_ref, ...), custom_call_target="tpu_custom_call" | custom-call | flops 20000 | bytes 400000 | tf_op jit(solution)/shard_map/add_lines/pallas_call | solution.py:409
  17.6 0.0 collective-permute-start.2
  17.6 3.3 %all-to-all-start.1 = ((f32[8,8,128]{2,1,0:T(8,128)}), f32[8,8,128]{2,1,0:T(8,128)S(1)}, u32[]{:S(2)}, u32[]{:S(2)}) async-start(f32[8,8,128]{2,1,0:T(8,128)} %get-tuple-element.27), calls=%async_computation.1 | async-start | bytes 65536 | tf_op jit(solution)/shard_map/all_to_all | solution.py:760
  20.9 0.7 %copy.9 = f32[3,64,512]{2,1,0:T(8,128)} copy(f32[3,64,512]{2,1,0:T(8,128)S(1)} %get-tuple-element.40) | data formatting | bytes 786432
  21.7 0.0 collective-permute-done.2.handed_ref
  21.7 0.0 copy-done
  21.7 0.0 copy-done.1
  21.7 0.0 copy-done.2
  21.7 2.5 %flow_step.1 = (f32[3,192,128]{2,1,0:T(8,128)S(1)}, f32[8,128]{1,0:T(8,128)S(1)}, f32[3,32,128]{2,1,0:T(8,128)S(1)}, bf16[32,256]{1,0:T(8,128)(2,1)S(1)}, bf16[192,384]{1,0:T(8,128)(2,1)S(1)}) custom-call(s32[32]{0:T(128)S(1)} %copy-done.2, s32[32]{0:T(128)S(1)} %get-tuple-element.29.position_ref, f32[3,192,128]{2,1,0:T(8,128)S(1)} %bitcast.7, ...), custom_call_target="tpu_custom_call" | custom-call | flops 4000000 | bytes 3000000 | tf_op jit(solution)/shard_map/flow_step/pallas_call | solution.py:635
  24.2 1.5 %all-to-all-done.1 = f32[8,8,128]{2,1,0:T(8,128)S(1)} async-done(((f32[8,8,128]{2,1,0:T(8,128)}), f32[8,8,128]{2,1,0:T(8,128)S(1)}, u32[]{:S(2)}, u32[]{:S(2)}) %all-to-all-start.1) | async-done | bytes 32800 | tf_op jit(solution)/shard_map/all_to_all | solution.py:760
  25.7 1.2 %add_polymer.1 = (f32[3,192,128]{2,1,0:T(8,128)}, f32[6,32]{1,0:T(8,128)}) custom-call(f32[64,128]{1,0:T(8,128)S(1)} %bitcast.10, f32[32,128]{1,0:T(8,128)S(1)} %get-tuple-element.28.viscous_ref, f32[8,128]{1,0:T(8,128)S(1)} %get-tuple-element.31.corner_ref, f32[3,32,128]{2,1,0:T(8,128)S(1)} %get-tuple-element.32.lines_ref, ...), custom_call_target="tpu_custom_call" | custom-call | flops 400000 | bytes 3000000 | tf_op jit(solution)/shard_map/add_polymer/pallas_call | solution.py:733
Async XLA Ops:
  2.9 18.8 %copy-start = (f32[3,24,8,128]{3,2,1,0:T(8,128)S(1)}, f32[3,24,8,128]{3,2,1,0:T(8,128)}, u32[]{:S(2)}) copy-start(f32[3,24,8,128]{3,2,1,0:T(8,128)} %param.6) | copy-start | bytes 884740
  2.9 18.8 %copy-start.1 = (f32[24,8,128]{2,1,0:T(8,128)S(1)}, f32[24,8,128]{2,1,0:T(8,128)}, u32[]{:S(2)}) copy-start(f32[24,8,128]{2,1,0:T(8,128)} %param.7) | copy-start | bytes 294916
  2.9 18.8 %copy-start.2 = (s32[32]{0:T(128)S(1)}, s32[32]{0:T(128)}, u32[]{:S(2)}) copy-start(s32[32]{0:T(128)} %cell_ref.1) | copy-start | bytes 388
  2.9 10.8 %all-to-all-start = ((f32[8,32,128]{2,1,0:T(8,128)}), f32[8,32,128]{2,1,0:T(8,128)S(1)}, u32[]{:S(2)}, u32[]{:S(2)}) async-start(f32[8,32,128]{2,1,0:T(8,128)} %bitcast.3), calls=%async_computation | async-start | bytes 262144 | tf_op jit(solution)/shard_map/all_to_all | solution.py:760
  8.2 8.7 %collective-permute-start = (f32[7,24,128]{2,1,0:T(8,128)S(1)}, f32[7,24,128]{2,1,0:T(8,128)S(1)}, u32[]{:S(2)}, u32[]{:S(2)}) collective-permute-start(f32[7,24,128]{2,1,0:T(8,128)S(1)} %get-tuple-element.25), channel_id=1, source_target_pairs={{0,2},{4,6},{2,0},{6,4},{1,3},{5,7},{3,1},{7,5},{8,10},{12,14},{10... | collective-permute-start | bytes 258056 | tf_op jit(solution)/shard_map/ppermute | solution.py:767
  9.8 7.1 %collective-permute-start.1 = (f32[7,24,128]{2,1,0:T(8,128)S(1)}, f32[7,24,128]{2,1,0:T(8,128)S(1)}, u32[]{:S(2)}, u32[]{:S(2)}) collective-permute-start(f32[7,24,128]{2,1,0:T(8,128)S(1)} %get-tuple-element.26), channel_id=1, source_target_pairs={{2,4},{4,2},{3,5},{5,3},{10,12},{12,10},{11,13},{13,11},{18,20},{2... | collective-permute-start | bytes 258056 | tf_op jit(solution)/shard_map/ppermute | solution.py:768
  17.6 4.1 %collective-permute-start.2 = (f32[2,96,128]{2,1,0:T(8,128)S(1)}, f32[2,96,128]{2,1,0:T(8,128)S(1)}, u32[]{:S(2)}, u32[]{:S(2)}) collective-permute-start(f32[2,96,128]{2,1,0:T(8,128)S(1)} %get-tuple-element.30), channel_id=1, source_target_pairs={{0,1},{1,0},{2,3},{3,2},{4,5},{5,4},{6,7},{7,6},{8,9},{9,8},{10,11... | collective-permute-start | bytes 294920 | tf_op jit(solution)/shard_map/ppermute | solution.py:774
  17.6 8.1 %all-to-all-start.1 = ((f32[8,8,128]{2,1,0:T(8,128)}), f32[8,8,128]{2,1,0:T(8,128)S(1)}, u32[]{:S(2)}, u32[]{:S(2)}) async-start(f32[8,8,128]{2,1,0:T(8,128)} %get-tuple-element.27), calls=%async_computation.1 | async-start | bytes 65536 | tf_op jit(solution)/shard_map/all_to_all | solution.py:760

commit v23 on v21

--- a/solution.py
+++ b/solution.py
@@ -713,7 +713,11 @@
     ]
     flag_ref[...] = stress.T[0:6, :]
 
-    out_ref[...] = partial_ref[...]
+    for a in range(3):
+        out_ref[a] = partial_ref[a] + jnp.dot(
+            spread_ref[...], jnp.concatenate(split[a], axis=0), preferred_element_type=jnp.float32
+        )
+
     for s in range(2):
         inside = macro > 0 if s == 0 else macro < macro_count - 1
         beside = jnp.maximum(macro - 1, 0) if s == 0 else jnp.minimum(macro + 1, macro_count - 1)
@@ -725,10 +729,6 @@
                 number = 4 * s + 2 * u + a
                 line = corner_ref[number : number + 1, :] * chunk_ref[pl.ds(start + 2 * u + a, 1), :]
                 out_ref[1 - a, at : at + 1, :] += jnp.where(inside, line, 0.0)
-    for a in range(3):
-        out_ref[a] += jnp.dot(
-            spread_ref[...], jnp.concatenate(split[a], axis=0), preferred_element_type=jnp.float32
-        )
 
 
 def add_polymer(chunks, viscous, corners, lines, pick, spread, partial, shape):

time: 27.3 us -> 27.3 us (level)
  no operation moved by 1% of the time
where the time goes in v23:
time: 27.3 us; the launch traced here: 26.9 us
  starting transfers between devices  10.9 us (40%)
  Pallas kernels  9.78 us (36%)
  waiting for transfers between devices  4.79 us (18%)
  local copies, waits for them, and re-layouts  0.77 us (3%)
  between operations  0.72 us (3%)
    all_to_all x2, starting transfers between devices, exchange(): lax.all_to_all(rows, ('macro', 'micro'), split_axis=0, concat_axis=0, til...  8.65 us
    all_to_all x2, waiting for transfers between devices, exchange(): lax.all_to_all(rows, ('macro', 'micro'), split_axis=0, concat_axis=0, til...  4.78 us
    pallas_call x1, Pallas kernels, advance(): pl.pallas_call(functools.partial(micro_kernel, capacity, parts, rows, gro...  3.19 us
    pallas_call x1, Pallas kernels, flow_step(): pl.pallas_call(functools.partial(flow_kernel, size_x, size_y, size_z, chu...  2.5 us
    pallas_call x1, Pallas kernels, gather_rows(): pl.pallas_call(functools.partial(gather_kernel, capacity, size_x, size_y,...  2.22 us
    ppermute x1, starting transfers between devices, shards(): first = lax.ppermute(first, 'tile', swaps[0])  1.58 us
    pallas_call x1, Pallas kernels, add_polymer(): pl.pallas_call(functools.partial(polymer_kernel, size_x, size_y, size_z,...  1.22 us
    unnamed x7, local copies, waits for them, and re-layouts  0.77 us
  transfers between devices with their start and end apart: 5, of which 2 were waited for; matrix products, arithmetic and copies ran while one was open for 3% of the time, Pallas kernels for 21%

profile of v23, /device:TPU:0, one launch (start us, length us, event | category | flops | bytes accessed | tf_op | source)
XLA Modules:
  0.0 26.9 jit_solution(13650248423119013116)
XLA Ops:
  0.6 2.2 %gather_rows.1 = (f32[256,128]{1,0:T(8,128)}, s32[32]{0:T(128)S(1)}, f32[32,128]{1,0:T(8,128)S(1)}, f32[7,24,128]{2,1,0:T(8,128)S(1)}, f32[7,24,128]{2,1,0:T(8,1...) custom-call(s32[32]{0:T(128)} %cell_ref.1, s32[32]{0:T(128)} %bitcast.11, ...), custom_call_target="tpu_custom_call" | custom-call | flops 400000 | bytes 3000000 | tf_op jit(solution)/shard_map/gather_rows/pallas_call | solution.py:185
  2.9 0.0 copy-start
  2.9 0.0 copy-start.1
  2.9 0.0 copy-start.2
  2.9 5.3 %all-to-all-start = ((f32[8,32,128]{2,1,0:T(8,128)}), f32[8,32,128]{2,1,0:T(8,128)S(1)}, u32[]{:S(2)}, u32[]{:S(2)}) async-start(f32[8,32,128]{2,1,0:T(8,128)} %bitcast.3), calls=%async_computation | async-start | bytes 262144 | tf_op jit(solution)/shard_map/all_to_all | solution.py:764
  8.2 1.6 %collective-permute-start = (f32[7,24,128]{2,1,0:T(8,128)S(1)}, f32[7,24,128]{2,1,0:T(8,128)S(1)}, u32[]{:S(2)}, u32[]{:S(2)}) collective-permute-start(f32[7,24,128]{2,1,0:T(8,128)S(1)} %get-tuple-element.25), channel_id=1, source_target_pairs={{0,2},{4,6},{2,0},{6,4},{1,3},{5,7},{3,1},{7,5},{8,10},{12,14},{10... | collective-permute-start | bytes 258056 | tf_op jit(solution)/shard_map/ppermute | solution.py:771
  9.8 0.7 %collective-permute-start.1 = (f32[7,24,128]{2,1,0:T(8,128)S(1)}, f32[7,24,128]{2,1,0:T(8,128)S(1)}, u32[]{:S(2)}, u32[]{:S(2)}) collective-permute-start(f32[7,24,128]{2,1,0:T(8,128)S(1)} %get-tuple-element.26), channel_id=1, source_target_pairs={{2,4},{4,2},{3,5},{5,3},{10,12},{12,10},{11,13},{13,11},{18,20},{2... | collective-permute-start | bytes 258056 | tf_op jit(solution)/shard_map/ppermute | solution.py:772
  10.5 3.3 %all-to-all-done.rate_ref.received_ref.chunk_ref = f32[8,32,128]{2,1,0:T(8,128)S(1)} async-done(((f32[8,32,128]{2,1,0:T(8,128)}), f32[8,32,128]{2,1,0:T(8,128)S(1)}, u32[]{:S(2)}, u32[]{:S(2)}) %all-to-all-start) | async-done | bytes 131104 | tf_op jit(solution)/shard_map/all_to_all | solution.py:764
  13.7 3.2 %advance.1 = (f32[3,64,512]{2,1,0:T(8,128)S(1)}, f32[8,8,128]{2,1,0:T(8,128)S(1)}) custom-call(f32[3,64,512]{2,1,0:T(8,128)} %conform_ref.1, bf16[16,3,64,512]{3,2,1,0:T(8,128)(2,1)} %noise_ref.1, f32[8,32,128]{2,1,0:T(8,128)S(1)} %all-to-all-done.rate_ref.received_ref.chunk_ref, f32[3,32,512]{2,1,0:T(8,128)S(1)} %get-tuple-element.22.first_conform_ref, ...), custom_call_target="tpu_custom_call" | custom-call | flops 20000000 | bytes 5000000 | tf_op jit(solution)/shard_map/advance/pallas_call | solution.py:361
  16.9 0.0 collective-permute-done.first_ref
  16.9 0.0 collective-permute-done.1.second_ref
  17.0 0.6 %add_lines.1 = (f32[8,8,128]{2,1,0:T(8,128)}, f32[2,96,128]{2,1,0:T(8,128)S(1)}) custom-call(f32[8,8,128]{2,1,0:T(8,128)S(1)} %get-tuple-element.24.chunk_ref, f32[8,32,128]{2,1,0:T(8,128)S(1)} %all-to-all-done.rate_ref.received_ref.chunk_ref, f32[7,24,128]{2,1,0:T(8,128)S(1)} %collective-permute-done.first_ref, ...), custom_call_target="tpu_custom_call" | custom-call | flops 20000 | bytes 400000 | tf_op jit(solution)/shard_map/add_lines/pallas_call | solution.py:413
  17.6 0.0 collective-permute-start.2
  17.6 3.3 %all-to-all-start.1 = ((f32[8,8,128]{2,1,0:T(8,128)}), f32[8,8,128]{2,1,0:T(8,128)S(1)}, u32[]{:S(2)}, u32[]{:S(2)}) async-start(f32[8,8,128]{2,1,0:T(8,128)} %get-tuple-element.27), calls=%async_computation.1 | async-start | bytes 65536 | tf_op jit(solution)/shard_map/all_to_all | solution.py:764
  21.0 0.7 %copy.9 = f32[3,64,512]{2,1,0:T(8,128)} copy(f32[3,64,512]{2,1,0:T(8,128)S(1)} %get-tuple-element.40) | data formatting | bytes 786432
  21.7 0.0 collective-permute-done.2.handed_ref
  21.7 0.0 copy-done
  21.7 0.0 copy-done.1
  21.7 0.0 copy-done.2
  21.7 2.5 %flow_step.1 = (f32[3,192,128]{2,1,0:T(8,128)S(1)}, f32[8,128]{1,0:T(8,128)S(1)}, f32[3,32,128]{2,1,0:T(8,128)S(1)}, bf16[32,256]{1,0:T(8,128)(2,1)S(1)}, bf16[192,384]{1,0:T(8,128)(2,1)S(1)}) custom-call(s32[32]{0:T(128)S(1)} %copy-done.2, s32[32]{0:T(128)S(1)} %get-tuple-element.29.position_ref, f32[3,192,128]{2,1,0:T(8,128)S(1)} %bitcast.7, ...), custom_call_target="tpu_custom_call" | custom-call | flops 4000000 | bytes 3000000 | tf_op jit(solution)/shard_map/flow_step/pallas_call | solution.py:639
  24.2 1.5 %all-to-all-done.1 = f32[8,8,128]{2,1,0:T(8,128)S(1)} async-done(((f32[8,8,128]{2,1,0:T(8,128)}), f32[8,8,128]{2,1,0:T(8,128)S(1)}, u32[]{:S(2)}, u32[]{:S(2)}) %all-to-all-start.1) | async-done | bytes 32800 | tf_op jit(solution)/shard_map/all_to_all | solution.py:764
  25.7 1.2 %add_polymer.1 = (f32[3,192,128]{2,1,0:T(8,128)}, f32[6,32]{1,0:T(8,128)}) custom-call(f32[64,128]{1,0:T(8,128)S(1)} %bitcast.10, f32[32,128]{1,0:T(8,128)S(1)} %get-tuple-element.28.viscous_ref, f32[8,128]{1,0:T(8,128)S(1)} %get-tuple-element.31.corner_ref, f32[3,32,128]{2,1,0:T(8,128)S(1)} %get-tuple-element.32.lines_ref, ...), custom_call_target="tpu_custom_call" | custom-call | flops 400000 | bytes 3000000 | tf_op jit(solution)/shard_map/add_polymer/pallas_call | solution.py:737
Async XLA Ops:
  2.9 18.8 %copy-start = (f32[3,24,8,128]{3,2,1,0:T(8,128)S(1)}, f32[3,24,8,128]{3,2,1,0:T(8,128)}, u32[]{:S(2)}) copy-start(f32[3,24,8,128]{3,2,1,0:T(8,128)} %param.6) | copy-start | bytes 884740
  2.9 18.8 %copy-start.1 = (f32[24,8,128]{2,1,0:T(8,128)S(1)}, f32[24,8,128]{2,1,0:T(8,128)}, u32[]{:S(2)}) copy-start(f32[24,8,128]{2,1,0:T(8,128)} %param.7) | copy-start | bytes 294916
  2.9 18.8 %copy-start.2 = (s32[32]{0:T(128)S(1)}, s32[32]{0:T(128)}, u32[]{:S(2)}) copy-start(s32[32]{0:T(128)} %cell_ref.1) | copy-start | bytes 388
  2.9 10.8 %all-to-all-start = ((f32[8,32,128]{2,1,0:T(8,128)}), f32[8,32,128]{2,1,0:T(8,128)S(1)}, u32[]{:S(2)}, u32[]{:S(2)}) async-start(f32[8,32,128]{2,1,0:T(8,128)} %bitcast.3), calls=%async_computation | async-start | bytes 262144 | tf_op jit(solution)/shard_map/all_to_all | solution.py:764
  8.2 8.7 %collective-permute-start = (f32[7,24,128]{2,1,0:T(8,128)S(1)}, f32[7,24,128]{2,1,0:T(8,128)S(1)}, u32[]{:S(2)}, u32[]{:S(2)}) collective-permute-start(f32[7,24,128]{2,1,0:T(8,128)S(1)} %get-tuple-element.25), channel_id=1, source_target_pairs={{0,2},{4,6},{2,0},{6,4},{1,3},{5,7},{3,1},{7,5},{8,10},{12,14},{10... | collective-permute-start | bytes 258056 | tf_op jit(solution)/shard_map/ppermute | solution.py:771
  9.8 7.2 %collective-permute-start.1 = (f32[7,24,128]{2,1,0:T(8,128)S(1)}, f32[7,24,128]{2,1,0:T(8,128)S(1)}, u32[]{:S(2)}, u32[]{:S(2)}) collective-permute-start(f32[7,24,128]{2,1,0:T(8,128)S(1)} %get-tuple-element.26), channel_id=1, source_target_pairs={{2,4},{4,2},{3,5},{5,3},{10,12},{12,10},{11,13},{13,11},{18,20},{2... | collective-permute-start | bytes 258056 | tf_op jit(solution)/shard_map/ppermute | solution.py:772
  17.6 4.1 %collective-permute-start.2 = (f32[2,96,128]{2,1,0:T(8,128)S(1)}, f32[2,96,128]{2,1,0:T(8,128)S(1)}, u32[]{:S(2)}, u32[]{:S(2)}) collective-permute-start(f32[2,96,128]{2,1,0:T(8,128)S(1)} %get-tuple-element.30), channel_id=1, source_target_pairs={{0,1},{1,0},{2,3},{3,2},{4,5},{5,4},{6,7},{7,6},{8,9},{9,8},{10,11... | collective-permute-start | bytes 294920 | tf_op jit(solution)/shard_map/ppermute | solution.py:778
  17.6 8.1 %all-to-all-start.1 = ((f32[8,8,128]{2,1,0:T(8,128)}), f32[8,8,128]{2,1,0:T(8,128)S(1)}, u32[]{:S(2)}, u32[]{:S(2)}) async-start(f32[8,8,128]{2,1,0:T(8,128)} %get-tuple-element.27), calls=%async_computation.1 | async-start | bytes 65536 | tf_op jit(solution)/shard_map/all_to_all | solution.py:764
